TPU v7x, 32 devices: a whole 2x2x4 slice. The times are simulated.
32 devices in a mesh: dp: 8 (over z, y), tensor: 4 (over x, core).
Axes of the slice: x: 2, y: 2, z: 4, core: 2. Of those that a mesh axis runs over, the one named last changes fastest.
Arguments:
- inputs: bfloat16 [32, 512, 512], P('dp', 'tensor'), may hold values from -6 to 6
- segment_ids: int32 [32, 512], P('dp'), may hold values from 0 to 22, as said below
- cotangent: bfloat16 [32, 512, 512], P('dp', 'tensor'), may hold values from -6 to 6
- attn_proj: float32 [3, 512, 512], P(None, 'dp', 'tensor'), may hold values from -0.25 to 0.25
- out_proj: float32 [512, 512], P(('tensor', 'dp')), may hold values from -2 to 2
- up_proj: float32 [512, 2048], P('dp', 'tensor'), may hold values from -0.25 to 0.25
- down_proj: float32 [2048, 512], P(('tensor', 'dp')), may hold values from -0.125 to 0.125
- pos_table: float32 [512, 512], P(('tensor', 'dp')), may hold values from -4 to 4
- norm_params: float32 [4, 512], P(None, 'dp'), may hold values from -1 to 1.6, as said below
- first_attn: float32 [3, 512, 512], P(None, 'dp', 'tensor'), may hold values from -32 to 32
- second_attn: float32 [3, 512, 512], P(None, 'dp', 'tensor'), may hold values from 137.6256 to 557.056
- first_out: float32 [512, 512], P(('tensor', 'dp')), may hold values from -5 to 5
- second_out: float32 [512, 512], P(('tensor', 'dp')), may hold values from 3.11296 to 12.45184
- first_up: float32 [512, 2048], P('dp', 'tensor'), may hold values from -16 to 16
- second_up: float32 [512, 2048], P('dp', 'tensor'), may hold values from 27.8528 to 111.4112
- first_down: float32 [2048, 512], P(('tensor', 'dp')), may hold values from -32 to 32
- second_down: float32 [2048, 512], P(('tensor', 'dp')), may hold values from 137.6256 to 557.056
- first_pos: float32 [512, 512], P(('tensor', 'dp')), may hold values from -4 to 4
- second_pos: float32 [512, 512], P(('tensor', 'dp')), may hold values from 1.696 to 6.72
- first_norm: float32 [4, 512], P(None, 'dp'), may hold values from -80 to 80
- second_norm: float32 [4, 512], P(None, 'dp'), may hold values from 868.352 to 3440.64
Outputs:
- outputs: bfloat16 [32, 512, 512], P('dp', 'tensor')
- grad_input: float32 [32, 512, 512], P('dp', 'tensor')
- new_attn_proj: float32 [3, 512, 512], P(None, 'dp', 'tensor')
- new_first_attn: float32 [3, 512, 512], P(None, 'dp', 'tensor')
- new_second_attn: float32 [3, 512, 512], P(None, 'dp', 'tensor')
- new_out_proj: float32 [512, 512], P(('tensor', 'dp'))
- new_first_out: float32 [512, 512], P(('tensor', 'dp'))
- new_second_out: float32 [512, 512], P(('tensor', 'dp'))
- new_up_proj: float32 [512, 2048], P('dp', 'tensor')
- new_first_up: float32 [512, 2048], P('dp', 'tensor')
- new_second_up: float32 [512, 2048], P('dp', 'tensor')
- new_down_proj: float32 [2048, 512], P(('tensor', 'dp'))
- new_first_down: float32 [2048, 512], P(('tensor', 'dp'))
- new_second_down: float32 [2048, 512], P(('tensor', 'dp'))
- new_pos_table: float32 [512, 512], P(('tensor', 'dp'))
- new_first_pos: float32 [512, 512], P(('tensor', 'dp'))
- new_second_pos: float32 [512, 512], P(('tensor', 'dp'))
- new_norm_params: float32 [4, 512], P(None, 'dp')
- new_first_norm: float32 [4, 512], P(None, 'dp')
- new_second_norm: float32 [4, 512], P(None, 'dp')
Inputs may be any that keep to these rules, and one draw needn't show every extreme that they name: `segment_ids`: within each window ids start at 0 and never fall; characters with the same id in a window are one document; every window's last id is the largest allowed. `norm_params`: rows 0 and 2 are gains, rows 1 and 3 shifts.
All inputs are finite; a program needn't handle non-finite values.
Results may differ from a plain program's by a relative error of at most 0.018.
The roundings to bfloat16 on the way count: a program that leaves them out, or rounds other values in their place, can miss the bound.
Values may be sent and summed in bfloat16 or wider, within the bound.
No kernel may reach another device: no remote copies, remote signals or barrier semaphores. Data moves between devices by JAX's collectives and lax.ppermute only.
A program may use at most 64 MiB of HBM per device.

v0:
```python
import jax
import jax.numpy as jnp
from jax import lax
from jax.sharding import PartitionSpec as P

HD = 64
STEP = 10


NORM_EPS = 1e-05
NEG_FILL = -1e30
BETA_ONE = 0.9
BETA_TWO = 0.95
ADAM_EPS = 1e-08
RATES = (0.03, 0.2, 0.03, 0.02, 0.3, 0.3)
DECAYS = (0.1, 0.1, 0.1, 0.1, 0.1, 0.0)


def split_up(array, dim, devices):
    before, after = (array.shape[:dim], array.shape[dim + 1 :])
    return jnp.moveaxis(array.reshape(*before, devices, -1, *after), dim, 0)


def sent_and_summed(array, axis, dim):
    tiles = split_up(array, dim, lax.axis_size(axis))
    arrived = lax.all_to_all(tiles, axis, split_axis=0, concat_axis=0, tiled=True)
    return arrived.astype(jnp.float32).sum(axis=0)


def side_by_side(arrays, axis, dim, along):
    widths = [a.shape[along] for a in arrays]
    both = jnp.concatenate(arrays, axis=along)
    filled = sent_and_summed(both, axis, dim)
    return tuple(jnp.split(filled, [sum(widths[:k]) for k in range(1, len(widths))], axis=along))


def normalize(values, norm_gain, norm_shift):
    center = values - jnp.mean(values, axis=-1, keepdims=True)
    spread = jnp.mean(center * center, axis=-1, keepdims=True)
    return center * lax.rsqrt(spread + NORM_EPS) * norm_gain + norm_shift


def window_scores(query_rows, key_rows, segments):
    score_scale = query_rows.shape[-1] ** (-0.5)
    places = jnp.arange(segments.shape[0])
    allowed = (segments[:, None] == segments[None, :]) & (places[:, None] >= places[None, :])
    scores = (
        jnp.einsum("qhd,khd->hqk", query_rows, key_rows, preferred_element_type=jnp.float32)
        * score_scale
    )
    return jnp.where(allowed[None], scores, NEG_FILL)


def window_forward(window_item):
    query_rows, key_rows, value_rows, segments = window_item
    scores = window_scores(query_rows, key_rows, segments)
    row_peak = jnp.max(scores, axis=-1, keepdims=True)
    exponents = jnp.exp(scores - row_peak)
    exp_total = jnp.sum(exponents, axis=-1, keepdims=True)
    probabilities = (exponents / exp_total).astype(jnp.bfloat16)
    mixed_rows = jnp.einsum(
        "hqk,khd->qhd", probabilities, value_rows, preferred_element_type=jnp.float32
    )
    return (mixed_rows.astype(jnp.bfloat16), row_peak + jnp.log(exp_total))


def window_backward(window_item):
    query_rows, key_rows, value_rows, segments, log_total, grad_mixed = window_item
    score_scale = query_rows.shape[-1] ** (-0.5)
    scores = window_scores(query_rows, key_rows, segments)
    probabilities = jnp.exp(scores - log_total)
    grad_probs = jnp.einsum(
        "qhd,khd->hqk", grad_mixed, value_rows, preferred_element_type=jnp.float32
    )
    row_dot = jnp.sum(probabilities * grad_probs, axis=-1, keepdims=True)
    grad_scores = (probabilities * (grad_probs - row_dot)).astype(jnp.bfloat16)
    grad_query = (
        jnp.einsum("hqk,khd->qhd", grad_scores, key_rows, preferred_element_type=jnp.float32)
        * score_scale
    )
    grad_key = (
        jnp.einsum("hqk,qhd->khd", grad_scores, query_rows, preferred_element_type=jnp.float32)
        * score_scale
    )
    grad_value = jnp.einsum(
        "hqk,qhd->khd",
        probabilities.astype(jnp.bfloat16),
        grad_mixed,
        preferred_element_type=jnp.float32,
    )
    return (
        grad_query.astype(jnp.bfloat16),
        grad_key.astype(jnp.bfloat16),
        grad_value.astype(jnp.bfloat16),
    )


def adam_step(weight, gradient, moment_one, second, step_rate, decay_rate):
    first_new = BETA_ONE * moment_one + (1.0 - BETA_ONE) * gradient
    second_new = BETA_TWO * second + (1.0 - BETA_TWO) * gradient * gradient
    fixed_first = first_new / (1.0 - BETA_ONE**STEP)
    fixed_second = second_new / (1.0 - BETA_TWO**STEP)
    weight_new = weight - step_rate * (
        fixed_first / (jnp.sqrt(fixed_second) + ADAM_EPS) + decay_rate * weight
    )
    return (weight_new, first_new, second_new)


def body(
    inputs,
    segment_ids,
    cotangent,
    attn_proj,
    out_proj,
    up_proj,
    down_proj,
    pos_table,
    norm_params,
    first_attn,
    second_attn,
    first_out,
    second_out,
    first_up,
    second_up,
    first_down,
    second_down,
    first_pos,
    second_pos,
    first_norm,
    second_norm,
):
    window_count, shard_rows, model_width = inputs.shape
    window = shard_rows * lax.axis_size("tensor")
    attn_low, out_low, up_low, down_low = (
        lax.all_gather(attn_proj.astype(jnp.bfloat16), "dp", axis=1, tiled=True),
        lax.all_gather(out_proj.astype(jnp.bfloat16), "dp", axis=0, tiled=True),
        lax.all_gather(up_proj.astype(jnp.bfloat16), "dp", axis=0, tiled=True),
        lax.all_gather(down_proj.astype(jnp.bfloat16), "dp", axis=0, tiled=True),
    )
    pos_rows, norm_full = (
        lax.all_gather(pos_table, "dp", axis=0, tiled=True),
        lax.all_gather(norm_params, "dp", axis=1, tiled=True),
    )
    group_width = attn_low.shape[2]
    group_heads = group_width // HD

    def project(gathered):
        projected = jnp.einsum(
            "bld,tdc->tblc", gathered, attn_low, preferred_element_type=jnp.float32
        )
        return projected.astype(jnp.bfloat16).reshape(3, window_count, window, group_heads, HD)

    hidden = inputs.astype(jnp.float32) + pos_rows[None]
    sent_hidden = hidden.astype(jnp.bfloat16)
    gathered_hidden = lax.all_gather(sent_hidden, "tensor", axis=1, tiled=True)
    projected = project(gathered_hidden)
    mixed_rows, log_total = lax.map(
        window_forward, (projected[0], projected[1], projected[2], segment_ids)
    )
    mixed_flat = mixed_rows.reshape(window_count, window, group_width)
    attn_part = jnp.einsum("blc,cd->bld", mixed_flat, out_low, preferred_element_type=jnp.float32)
    attn_sum = lax.psum_scatter(
        attn_part.astype(jnp.bfloat16), "tensor", scatter_dimension=1, tiled=True
    ).astype(jnp.float32)
    residual_one = hidden + attn_sum
    normed_one = normalize(residual_one, norm_full[0], norm_full[1])
    sent_normed = normed_one.astype(jnp.bfloat16)
    gathered_normed = lax.all_gather(sent_normed, "tensor", axis=1, tiled=True)
    pre_active = jnp.einsum(
        "bld,df->blf", gathered_normed, up_low, preferred_element_type=jnp.float32
    )
    active = jax.nn.gelu(pre_active).astype(jnp.bfloat16)
    ffn_part = jnp.einsum("blf,fd->bld", active, down_low, preferred_element_type=jnp.float32)
    ffn_sum = lax.psum_scatter(
        ffn_part.astype(jnp.bfloat16), "tensor", scatter_dimension=1, tiled=True
    ).astype(jnp.float32)
    residual_two = normed_one + ffn_sum
    result, norm_two_pull = jax.vjp(normalize, residual_two, norm_full[2], norm_full[3])
    grad_two, gain_two_grad, shift_two_grad = norm_two_pull(cotangent.astype(jnp.float32))
    grad_ffn = lax.all_gather(grad_two.astype(jnp.bfloat16), "tensor", axis=1, tiled=True)
    active_again, gelu_pull = jax.vjp(
        jax.nn.gelu,
        jnp.einsum("bld,df->blf", gathered_normed, up_low, preferred_element_type=jnp.float32),
    )
    grad_down = jnp.einsum(
        "blf,bld->fd",
        active_again.astype(jnp.bfloat16),
        grad_ffn,
        preferred_element_type=jnp.float32,
    )
    grad_active = jnp.einsum("bld,fd->blf", grad_ffn, down_low, preferred_element_type=jnp.float32)
    grad_pre = gelu_pull(grad_active)[0].astype(jnp.bfloat16)
    grad_up = jnp.einsum(
        "bld,blf->df", gathered_normed, grad_pre, preferred_element_type=jnp.float32
    )
    back_ffn = jnp.einsum("blf,df->bld", grad_pre, up_low, preferred_element_type=jnp.float32)
    grad_first = grad_two + lax.psum_scatter(
        back_ffn.astype(jnp.bfloat16), "tensor", scatter_dimension=1, tiled=True
    ).astype(jnp.float32)
    unused_norm, norm_one_pull = jax.vjp(normalize, residual_one, norm_full[0], norm_full[1])
    grad_one, gain_one_grad, shift_one_grad = norm_one_pull(grad_first)
    grad_branch = lax.all_gather(grad_one.astype(jnp.bfloat16), "tensor", axis=1, tiled=True)
    projected_again = project(gathered_hidden)
    grad_out = jnp.einsum(
        "blc,bld->cd", mixed_flat, grad_branch, preferred_element_type=jnp.float32
    )
    grad_mixed = jnp.einsum(
        "bld,cd->blc", grad_branch, out_low, preferred_element_type=jnp.float32
    ).astype(jnp.bfloat16)
    grad_mixed = grad_mixed.reshape(window_count, window, group_heads, HD)
    grad_parts = lax.map(
        window_backward,
        (
            projected_again[0],
            projected_again[1],
            projected_again[2],
            segment_ids,
            log_total,
            grad_mixed,
        ),
    )
    stacked = jnp.stack(
        [grad_piece.reshape(window_count, window, group_width) for grad_piece in grad_parts]
    )
    grad_attn_proj = jnp.einsum(
        "bld,tblc->tdc", gathered_hidden, stacked, preferred_element_type=jnp.float32
    )
    back_attn = jnp.einsum("tblc,tdc->bld", stacked, attn_low, preferred_element_type=jnp.float32)
    grad_input = grad_one + lax.psum_scatter(
        back_attn.astype(jnp.bfloat16), "tensor", scatter_dimension=1, tiled=True
    ).astype(jnp.float32)
    grad_pos = jnp.sum(grad_input, axis=0)
    grad_norm = jnp.stack([gain_one_grad, shift_one_grad, gain_two_grad, shift_two_grad])
    reduced = (
        sent_and_summed(grad_attn_proj.astype(jnp.bfloat16), "dp", 1),
        sent_and_summed(grad_out.astype(jnp.bfloat16), "dp", 0),
        *side_by_side((grad_up.astype(jnp.bfloat16), grad_down.astype(jnp.bfloat16)), "dp", 0, 1),
        sent_and_summed(grad_pos.astype(jnp.bfloat16), "dp", 0),
        sent_and_summed(grad_norm.astype(jnp.bfloat16), "dp", 1),
    )
    norm_reduced = lax.psum(reduced[5], "tensor")
    masters = (attn_proj, out_proj, up_proj, down_proj, pos_table, norm_params)
    gradients = (reduced[0], reduced[1], reduced[2], reduced[3], reduced[4], norm_reduced)
    firsts = (first_attn, first_out, first_up, first_down, first_pos, first_norm)
    seconds = (second_attn, second_out, second_up, second_down, second_pos, second_norm)
    updated = [
        adam_step(
            masters[index],
            gradients[index],
            firsts[index],
            seconds[index],
            RATES[index],
            DECAYS[index],
        )
        for index in range(6)
    ]
    return (
        result.astype(jnp.bfloat16),
        grad_input,
        updated[0][0],
        updated[0][1],
        updated[0][2],
        updated[1][0],
        updated[1][1],
        updated[1][2],
        updated[2][0],
        updated[2][1],
        updated[2][2],
        updated[3][0],
        updated[3][1],
        updated[3][2],
        updated[4][0],
        updated[4][1],
        updated[4][2],
        updated[5][0],
        updated[5][1],
        updated[5][2],
    )


def solution(mesh):
    placed = (
        P("dp", "tensor", None),
        P("dp", None),
        P("dp", "tensor", None),
        P(None, "dp", "tensor"),
        P(("tensor", "dp"), None),
        P("dp", "tensor"),
        P(("tensor", "dp"), None),
        P(("tensor", "dp"), None),
        P(None, "dp"),
        P(None, "dp", "tensor"),
        P(None, "dp", "tensor"),
        P(("tensor", "dp"), None),
        P(("tensor", "dp"), None),
        P("dp", "tensor"),
        P("dp", "tensor"),
        P(("tensor", "dp"), None),
        P(("tensor", "dp"), None),
        P(("tensor", "dp"), None),
        P(("tensor", "dp"), None),
        P(None, "dp"),
        P(None, "dp"),
    )
    return jax.shard_map(
        body,
        mesh=mesh,
        in_specs=placed,
        out_specs=(
            P("dp", "tensor", None),
            P("dp", "tensor", None),
            P(None, "dp", "tensor"),
            P(None, "dp", "tensor"),
            P(None, "dp", "tensor"),
            P(("tensor", "dp"), None),
            P(("tensor", "dp"), None),
            P(("tensor", "dp"), None),
            P("dp", "tensor"),
            P("dp", "tensor"),
            P("dp", "tensor"),
            P(("tensor", "dp"), None),
            P(("tensor", "dp"), None),
            P(("tensor", "dp"), None),
            P(("tensor", "dp"), None),
            P(("tensor", "dp"), None),
            P(("tensor", "dp"), None),
            P(None, "dp"),
            P(None, "dp"),
            P(None, "dp"),
        ),
        check_vma=False,
    )
```

profile of v0, /device:TPU:0, one launch (start us, length us, event | category | flops | bytes accessed | tf_op | source)
XLA Modules:
  0.0 491.9 jit_solution(2387497513203336973)
XLA Ops:
  7.3 32.7 %all_gather.30 = f32[128,512]{1,0:T(8,128)S(1)} all-gather(f32[16,512]{1,0:T(8,128)} %param.32), channel_id=1, replica_groups=mesh['dp'=8,'tensor'=4] {'dp'}, dimensions={0}, use_global_device_ids=true | all-gather | bytes 294912 | tf_op jit(solution)/shard_map/all_gather | solution.py:141
  42.1 30.6 %all_gather.33 = bf16[128,512]{1,0:T(8,128)(2,1)S(1)} all-gather(bf16[16,512]{1,0:T(8,128)(2,1)S(1)} %convert_element_type.151), channel_id=1, replica_groups=mesh['dp'=8,'tensor'=4] {'dp'}, dimensions={0}, use_global_device_ids=true | all-gather | bytes 147456 | tf_op jit(solution)/shard_map/all_gather | solution.py:136
  72.7 30.9 %all_gather.32 = bf16[3,512,128]{2,1,0:T(8,128)(2,1)S(1)} all-gather(bf16[3,64,128]{2,1,0:T(8,128)(2,1)S(1)} %convert_element_type.148), channel_id=1, replica_groups=mesh['dp'=8,'tensor'=4] {'dp'}, dimensions={1}, use_global_device_ids=true | all-gather | bytes 442368 | tf_op jit(solution)/shard_map/all_gather | solution.py:135
  107.7 10.9 %while.26 = (s32[]{:T(128)}, bf16[4,512,2,64]{1,3,2,0:T(8,128)(2,1)S(1)}, f32[4,2,512,1]{2,1,3,0:T(2,128)}, bf16[4,512,2,64]{1,3,2,0:T(8,128)(2,1)S(1)}, s32[4,5...) while((s32[]{:T(128)}, ...), condition=%wide.region_3.4_spmd, body=%wide.region_0.3_spmd.sunk | while | flops 141360128 | bytes 7905881 | solution.py:157
  121.6 26.0 %all-gather = f32[8,64,4]{1,2,0:T(4,128)S(1)} all-gather(f32[1,64,4]{1,2,0:T(4,128)S(1)} %bitcast.227), channel_id=1, replica_groups=mesh['dp'=8,'tensor'=4] {'dp'}, dimensions={0}, use_global_device_ids=true | all-gather | bytes 9216 | tf_op jit(solution)/shard_map/all_gather | solution.py:142
  148.3 5.8 %reduce-scatter.5.cloned.1.call-done = bf16[4,128,512]{2,1,0:T(8,128)(2,1)} async-done(((bf16[4,512,512]{2,1,0:T(8,128)(2,1)}), bf16[4,128,512]{2,1,0:T(8,128)(2,1)}) %reduce-scatter.5.cloned.1.call-update) | async-done | bytes 524304 | tf_op jit(solution)/shard_map/reduce_scatter | solution.py:162
  158.2 31.5 %all_gather.36 = bf16[512,512]{1,0:T(8,128)(2,1)S(1)} all-gather(bf16[64,512]{1,0:T(8,128)(2,1)S(1)} %convert_element_type.155), channel_id=1, replica_groups=mesh['dp'=8,'tensor'=4] {'dp'}, dimensions={0}, use_global_device_ids=true | all-gather | bytes 589824 | tf_op jit(solution)/shard_map/all_gather | solution.py:137
  189.6 31.2 %all_gather.37 = bf16[512,512]{1,0:T(8,128)(2,1)S(1)} all-gather(bf16[64,512]{1,0:T(8,128)(2,1)S(1)} %convert_element_type.157), channel_id=1, replica_groups=mesh['dp'=8,'tensor'=4] {'dp'}, dimensions={0}, use_global_device_ids=true | all-gather | bytes 589824 | tf_op jit(solution)/shard_map/all_gather | solution.py:138
  228.9 31.8 %reduce-scatter.7.cloned.1.call-done = bf16[4,128,512]{2,1,0:T(8,128)(2,1)} async-done(((bf16[4,512,512]{2,1,0:T(8,128)(2,1)}), bf16[4,128,512]{2,1,0:T(8,128)(2,1)}) %reduce-scatter.7.cloned.1.call-update) | async-done | bytes 524304 | tf_op jit(solution)/shard_map/reduce_scatter | solution.py:174
  267.4 22.5 %all-gather.10.cloned.1.call-done = bf16[4,512,512]{2,1,0:T(8,128)(2,1)} async-done(((bf16[4,128,512]{2,1,0:T(8,128)(2,1)}), bf16[4,512,512]{2,1,0:T(8,128)(2,1)}) %all-gather.10.cloned.1.call-update) | async-done | bytes 2097168 | tf_op jit(solution)/shard_map/all_gather | solution.py:180
  289.9 5.5 %fusion.53 = bf16[4,512,512]{2,1,0:T(8,128)(2,1)S(1)} fusion(f32[4,512,512]{2,1,0:T(8,128)} %copy-done.2, bf16[4,512,512]{2,1,0:T(8,128)(2,1)} %all-gather.10.cloned.1.call-done, bf16[512,512]{1,0:T(8,128)(2,1)S(1)} %copy-done.18), kind=kOutput, calls=%fused_computation.71 | convolution fusion | flops 1094713344 | bytes 8912896 | tf_op jit(solution)/shard_map/bld,fd->blf/dot_general | solution.py:191
  299.5 31.6 %reduce-scatter.9.cloned.1.call-done = bf16[4,128,512]{2,1,0:T(8,128)(2,1)} async-done(((bf16[4,512,512]{2,1,0:T(8,128)(2,1)}), bf16[4,128,512]{2,1,0:T(8,128)(2,1)}) %reduce-scatter.9.cloned.1.call-update) | async-done | bytes 524304 | tf_op jit(solution)/shard_map/reduce_scatter | solution.py:197
  336.6 4.9 fusion.65
  341.5 17.0 %all-gather.12.cloned.1.call-done = bf16[4,512,512]{2,1,0:T(8,128)(2,1)} async-done(((bf16[4,128,512]{2,1,0:T(8,128)(2,1)}), bf16[4,512,512]{2,1,0:T(8,128)(2,1)}) %all-gather.12.cloned.1.call-update) | async-done | bytes 2097168 | tf_op jit(solution)/shard_map/all_gather | solution.py:202
  362.7 25.2 %while.27 = (s32[]{:T(128)}, bf16[4,512,2,64]{1,3,2,0:T(8,128)(2,1)S(1)}, bf16[4,512,2,64]{1,3,2,0:T(8,128)(2,1)}, bf16[4,512,2,64]{1,3,2,0:T(8,128)(2,1)}, bf16...) while((s32[]{:T(128)}, ...), condition=%wide.region_17.18_spmd, body=%wide.region_15.17_spmd.sunk | while | flops 341376000 | bytes 17595508 | solution.py:211
  392.0 3.6 bitcast_convert_fusion
  401.6 5.6 %all-to-all-start.2 = ((bf16[8,64,1024]{2,1,0:T(8,128)(2,1)}), bf16[8,64,1024]{2,1,0:T(8,128)(2,1)}, u32[]{:S(2)}, u32[]{:S(2)}) async-start(bf16[8,64,1024]{2,1,0:T(8,128)(2,1)} %bitcast.210), calls=%async_computation.6 | async-start | bytes 2097152 | tf_op jit(solution)/shard_map/all_to_all | solution.py:26
  408.6 24.9 %all-to-all-done.2 = bf16[8,64,1024]{2,1,0:T(8,128)(2,1)} async-done(((bf16[8,64,1024]{2,1,0:T(8,128)(2,1)}), bf16[8,64,1024]{2,1,0:T(8,128)(2,1)}, u32[]{:S(2)}, u32[]{:S(2)}) %all-to-all-start.2) | async-done | bytes 1048608 | tf_op jit(solution)/shard_map/all_to_all | solution.py:26
  435.8 3.6 all-to-all-start.4
  441.6 4.2 all-to-all-done.4
  456.5 3.5 all-to-all-start
  461.1 5.8 %psum.7 = f32[4,64]{1,0:T(4,128)S(1)} all-reduce(f32[4,64]{1,0:T(4,128)S(1)} %convert_reduce_fusion.4), channel_id=1, replica_groups=mesh['dp'=8,'tensor'=4] {'tensor'}, use_global_device_ids=true, to_apply=%region_29.30 | all-reduce | flops 256 | bytes 2048 | tf_op jit(solution)/shard_map/psum | solution.py:241
  472.5 4.5 all-to-all-start.3
  477.8 6.6 %all-to-all-done.3 = bf16[8,16,512]{2,1,0:T(8,128)(2,1)S(1)} async-done(((bf16[8,16,512]{2,1,0:T(8,128)(2,1)}), bf16[8,16,512]{2,1,0:T(8,128)(2,1)S(1)}, u32[]{:S(2)}, u32[]{:S(2)}) %all-to-all-start.3) | async-done | bytes 131104 | tf_op jit(solution)/shard_map/all_to_all | solution.py:26
  (263 shorter events, 112.2 us)
Async XLA Ops:
  7.2 34.8 %copy-start.24 = (f32[3,64,128]{2,1,0:T(8,128)S(1)}, f32[3,64,128]{2,1,0:T(8,128)}, u32[]{:S(2)}) copy-start(f32[3,64,128]{2,1,0:T(8,128)} %param.28) | copy-start | bytes 294916
  7.2 34.8 %copy-start.31 = (f32[16,512]{1,0:T(8,128)S(1)}, f32[16,512]{1,0:T(8,128)}, u32[]{:S(2)}) copy-start(f32[16,512]{1,0:T(8,128)} %param.29) | copy-start | bytes 98308
  7.2 96.4 %all-gather.6.cloned.1.call-start = ((), (), s32[]{:S(2)}) async-start(), calls=%async_computation.9 | async-start | bytes 2621440 | tf_op jit(solution)/shard_map/all_gather | solution.py:155
  42.0 112.1 %reduce-scatter.5.cloned.1.call-start = ((), (), s32[]{:S(2)}) async-start(), calls=%async_computation.10 | async-start | bytes 2621440 | tf_op jit(solution)/shard_map/reduce_scatter | solution.py:162
  119.4 34.7 %copy-start = (bf16[4,128,512]{2,1,0:T(8,128)(2,1)S(1)}, bf16[4,128,512]{2,1,0:T(8,128)(2,1)}, u32[]{:S(2)}) copy-start(bf16[4,128,512]{2,1,0:T(8,128)(2,1)} %param.25) | copy-start | bytes 1572868
  121.5 99.3 %all-gather.8.cloned.1.call-start = ((), (), s32[]{:S(2)}) async-start(), calls=%async_computation.11 | async-start | bytes 2621440 | tf_op jit(solution)/shard_map/all_gather | solution.py:168
  148.3 112.5 %copy-start.36 = (f32[1,512]{1,0:T(1,128)}, f32[1,512]{1,0:T(1,128)S(1)}, u32[]{:S(2)}) copy-start(f32[1,512]{1,0:T(1,128)S(1)} %get-tuple-element.196) | copy-start | bytes 6148
  148.3 114.3 %copy-start.44 = (f32[1,512]{1,0:T(1,128)}, f32[1,512]{1,0:T(1,128)S(1)}, u32[]{:S(2)}) copy-start(f32[1,512]{1,0:T(1,128)S(1)} %get-tuple-element.193) | copy-start | bytes 6148
  158.0 102.7 %reduce-scatter.7.cloned.1.call-start = ((), (), s32[]{:S(2)}) async-start(), calls=%async_computation.12 | async-start | bytes 2621440 | tf_op jit(solution)/shard_map/reduce_scatter | solution.py:174
  228.9 33.7 %copy-start.9 = (bf16[4,128,512]{2,1,0:T(8,128)(2,1)S(1)}, bf16[4,128,512]{2,1,0:T(8,128)(2,1)}, u32[]{:S(2)}) copy-start(bf16[4,128,512]{2,1,0:T(8,128)(2,1)} %param.27) | copy-start | bytes 1572868
  228.9 61.0 %all-gather.10.cloned.1.call-start = ((), (), s32[]{:S(2)}) async-start(), calls=%async_computation.13 | async-start | bytes 2621440 | tf_op jit(solution)/shard_map/all_gather | solution.py:180
  267.1 64.0 %reduce-scatter.9.cloned.1.call-start = ((), (), s32[]{:S(2)}) async-start(), calls=%async_computation.14 | async-start | bytes 2621440 | tf_op jit(solution)/shard_map/reduce_scatter | solution.py:197
  299.5 31.6 %copy-start.43 = (f32[4,128]{1,0:T(4,128)S(1)}, f32[4,128]{1,0:T(4,128)}, u32[]{:S(2)}) copy-start(f32[4,128]{1,0:T(4,128)} %copy-done.42) | copy-start | bytes 6148
  299.5 34.0 %copy-start.46 = (f32[4,128]{1,0:T(4,128)S(1)}, f32[4,128]{1,0:T(4,128)}, u32[]{:S(2)}) copy-start(f32[4,128]{1,0:T(4,128)} %copy-done.45) | copy-start | bytes 6148
  299.5 59.1 %all-gather.12.cloned.1.call-start = ((), (), s32[]{:S(2)}) async-start(), calls=%async_computation.15 | async-start | bytes 2621440 | tf_op jit(solution)/shard_map/all_gather | solution.py:202
  335.8 133.8 %reduce-scatter.11.cloned.1.call-start = ((), (), s32[]{:S(2)}) async-start(), calls=%async_computation.16 | async-start | bytes 2621440 | tf_op jit(solution)/shard_map/reduce_scatter | solution.py:229
  401.6 33.4 %copy-start.50 = (bf16[512]{0:T(512)(128)(2,1)S(1)}, bf16[512]{0:T(512)(128)(2,1)}, u32[]{:S(2)}) copy-start(bf16[512]{0:T(512)(128)(2,1)} %get-tuple-element.117) | copy-start | bytes 3076
  401.6 33.4 %copy-start.49 = (bf16[512]{0:T(512)(128)(2,1)S(1)}, bf16[512]{0:T(512)(128)(2,1)}, u32[]{:S(2)}) copy-start(bf16[512]{0:T(512)(128)(2,1)} %get-tuple-element.119) | copy-start | bytes 3076
  401.6 37.9 %copy-start.3 = (bf16[4,512,512]{2,1,0:T(8,128)(2,1)S(1)}, bf16[4,512,512]{2,1,0:T(8,128)(2,1)}, u32[]{:S(2)}) copy-start(bf16[4,512,512]{2,1,0:T(8,128)(2,1)} %all-gather.12.cloned.1.call-done) | copy-start | bytes 6291460
  401.6 31.9 %all-to-all-start.2 = ((bf16[8,64,1024]{2,1,0:T(8,128)(2,1)}), bf16[8,64,1024]{2,1,0:T(8,128)(2,1)}, u32[]{:S(2)}, u32[]{:S(2)}) async-start(bf16[8,64,1024]{2,1,0:T(8,128)(2,1)} %bitcast.210), calls=%async_computation.6 | async-start | bytes 2097152 | tf_op jit(solution)/shard_map/all_to_all | solution.py:26
  435.8 10.0 %all-to-all-start.4 = ((bf16[8,2,128]{2,1,0:T(2,128)(2,1)}), bf16[8,2,128]{2,1,0:T(2,128)(2,1)S(1)}, u32[]{:S(2)}, u32[]{:S(2)}) async-start(bf16[8,2,128]{2,1,0:T(2,128)(2,1)} %reshape.277), calls=%async_computation.8 | async-start | bytes 8192 | tf_op jit(solution)/shard_map/all_to_all | solution.py:26
  445.8 10.7 %all-to-all-start.1 = ((bf16[8,16,512]{2,1,0:T(8,128)(2,1)}), bf16[8,16,512]{2,1,0:T(8,128)(2,1)S(1)}, u32[]{:S(2)}, u32[]{:S(2)}) async-start(bf16[8,16,512]{2,1,0:T(8,128)(2,1)} %bitcast.49), calls=%async_computation.5 | async-start | bytes 262144 | tf_op jit(solution)/shard_map/all_to_all | solution.py:26
  456.5 13.0 %all-to-all-start = ((bf16[8,3,64,128]{3,2,1,0:T(8,128)(2,1)}), bf16[8,3,64,128]{3,2,1,0:T(8,128)(2,1)S(1)}, u32[]{:S(2)}, u32[]{:S(2)}) async-start(bf16[8,3,64,128]{3,2,1,0:T(8,128)(2,1)} %copy.108), calls=%async_computation.4 | async-start | bytes 786432 | tf_op jit(solution)/shard_map/all_to_all | solution.py:26
  472.5 11.9 %all-to-all-start.3 = ((bf16[8,16,512]{2,1,0:T(8,128)(2,1)}), bf16[8,16,512]{2,1,0:T(8,128)(2,1)S(1)}, u32[]{:S(2)}, u32[]{:S(2)}) async-start(bf16[8,16,512]{2,1,0:T(8,128)(2,1)} %bitcast.53), calls=%async_computation.7 | async-start | bytes 262144 | tf_op jit(solution)/shard_map/all_to_all | solution.py:26
  (45 other events, 381.4 us)
Sparse Core Ops, SparseCore 0:
  42.1 23.5 all-gather.5
  121.6 32.3 reduce-scatter.4
  158.2 22.5 all-gather.7
  229.0 31.7 reduce-scatter.6
  267.2 22.5 all-gather.9
  299.6 31.4 reduce-scatter.8
  335.9 22.5 all-gather.11
  395.8 31.4 reduce-scatter.10
where the time goes:
time: 494 us; the launch traced here: 492 us
  blocking collectives  189 us (38%)
  waiting for transfers between devices  149 us (30%)
  matrix products  62.7 us (13%)
  other arithmetic  33.9 us (7%)
  local copies, waits for them, and re-layouts  21.3 us (4%)
  starting transfers between devices  21.1 us (4%)
  between operations  14.9 us (3%)
    all_to_all x5, waiting for transfers between devices, sent_and_summed(): lax.all_to_all(tiles, axis, split_axis=0, concat_axis=0, tiled=True)  40.1 us
    all_gather x1, blocking collectives, body(): lax.all_gather(pos_table, 'dp', axis=0, tiled=True)  32.7 us
    reduce_scatter x1, waiting for transfers between devices, body(): lax.psum_scatter(ffn_part.astype(jnp.bfloat16), 'tensor', scatter_dimensi...  31.8 us
    reduce_scatter x1, waiting for transfers between devices, body(): lax.psum_scatter(back_ffn.astype(jnp.bfloat16), 'tensor', scatter_dimensi...  31.6 us
    all_gather x1, blocking collectives, body(): lax.all_gather(up_proj.astype(jnp.bfloat16), 'dp', axis=0, tiled=True)  31.5 us
    all_gather x1, blocking collectives, body(): lax.all_gather(down_proj.astype(jnp.bfloat16), 'dp', axis=0, tiled=True)  31.2 us
    all_gather x1, blocking collectives, body(): lax.all_gather(attn_proj.astype(jnp.bfloat16), 'dp', axis=1, tiled=True)  30.9 us
    all_gather x1, blocking collectives, body(): lax.all_gather(out_proj.astype(jnp.bfloat16), 'dp', axis=0, tiled=True)  30.6 us
  transfers between devices with their start and end apart: 13, of which 10 were waited for; matrix products, arithmetic and copies ran while one was open for 5% of the time, Pallas kernels for 0%

commit v1 on v0

v1 whole, which is shorter than its diff:
```python
import functools

import jax
import jax.numpy as jnp
from jax import lax
from jax.experimental import pallas as pl
from jax.experimental.pallas import tpu as pltpu
from jax.sharding import PartitionSpec as P

HD = 64
STEP = 10
LANES = 128

NORM_EPS = 1e-05
NEG_FILL = -1e30
BETA_ONE = 0.9
BETA_TWO = 0.95
ADAM_EPS = 1e-08
RATES = (0.03, 0.2, 0.03, 0.02, 0.3, 0.3)
DECAYS = (0.1, 0.1, 0.1, 0.1, 0.1, 0.0)
GELU_A = 0.7978845608028654
GELU_B = 0.044715

F32 = jnp.float32
BF16 = jnp.bfloat16
AXES = ("dp", "tensor")

NN = (((1,), (0,)), ((), ()))
NT = (((1,), (1,)), ((), ()))


def mm(a, b, dims=NN):
    return lax.dot_general(a, b, dims, preferred_element_type=F32)


def swap(value, rd, rt):
    n_t = lax.axis_size("tensor")
    mask = rd * n_t + rt
    return lax.ppermute(value, AXES, [(i, i ^ mask) for i in range(lax.axis_size("dp") * n_t)])


def rows_at(start, size, step):
    return pl.ds(pl.multiple_of(start, step), size)


def fill_window(me_t, parts, out_ref):
    own, rx, c1, c3 = parts
    n = own.shape[1]
    out_ref[rows_at(me_t * n, n, n), :] = own[me_t]
    out_ref[rows_at((me_t ^ 1) * n, n, n), :] = c1[0]
    out_ref[rows_at((me_t ^ 2) * n, n, n), :] = rx[me_t & 1]
    out_ref[rows_at((me_t ^ 3) * n, n, n), :] = c3[0]


def attention_kernel(places, n_pieces, scal, *refs):
    own, rx, c1, c3, seg_row = refs[:5]
    pieces = refs[5 : 5 + n_pieces]
    hid_o, qkv_o, pt_o, mixt_o, w_o, nrm_o, x_s, pos_s, bias_s, nrm_s = refs[5 + n_pieces :]
    me_dp, me_t = scal[0], scal[1]
    win, width = x_s.shape
    groups = w_o.shape[0]
    fill_window(me_t, (own, rx, c1, c3), x_s)
    if places is None:
        w_o[...] = pieces[0][...]
        pos_s[...] = pieces[1][...]
        nrm_o[...] = pieces[2][...]
    else:
        n_dp = nrm_s.shape[0]
        per = width // n_dp
        pos_per = win // (n_dp * groups)
        for ref, (xr, yr, z0, c) in zip(pieces, places, strict=True):
            tr = xr * 2 + c
            for i in range(ref.shape[0]):
                src = me_dp ^ ((z0 + i) * 2 + yr)
                for t in range(3):
                    w_o[tr, rows_at(src * per, per, per), t * LANES : (t + 1) * LANES] = ref[i, t * per : (t + 1) * per]
                where = (me_t ^ tr) * (win // groups) + src * pos_per
                for k in range(width // LANES):
                    at = 3 * per + k * pos_per
                    pos_s[rows_at(where, pos_per, pos_per), k * LANES : (k + 1) * LANES] = ref[i, at : at + pos_per]
                if tr == 0:
                    at = 3 * per + width // LANES * pos_per
                    nrm_s[src] = ref[i, at : at + 16].astype(F32)
        low_lane = lax.broadcasted_iota(jnp.int32, (8, LANES), 1) < per
        for j in range(n_dp // 2):
            left = nrm_s[2 * j]
            right = nrm_s[2 * j + 1]
            both = jnp.where(low_lane, left[0:8] + left[8:16], right[0:8] + right[8:16])
            nrm_o[:, j * LANES : (j + 1) * LANES] = both

    seg = seg_row[...].astype(F32)
    seg_col = jnp.transpose(jnp.broadcast_to(seg, (LANES, win)))
    for i in range(win // LANES):
        key_seg = seg_col[i * LANES : (i + 1) * LANES, 0:1]
        key_at = lax.broadcasted_iota(jnp.int32, (LANES, win), 0) + i * LANES
        query_at = lax.broadcasted_iota(jnp.int32, (LANES, win), 1)
        counts = (key_seg == seg) & (query_at >= key_at)
        bias_s[i * LANES : (i + 1) * LANES, :] = jnp.where(counts, 0.0, NEG_FILL)

    hidden = x_s[...].astype(F32) + pos_s[...].astype(F32)
    hid_o[...] = hidden
    x_s[...] = hidden.astype(BF16)
    lane = lax.broadcasted_iota(jnp.int32, (win, LANES), 1)

    @pl.loop(0, groups)
    def _(g):
        qkv = mm(x_s[...], w_o[g]).astype(BF16)
        q = qkv[:, :LANES] * jnp.asarray(HD**-0.5, BF16)
        k = qkv[:, LANES : 2 * LANES]
        v = qkv[:, 2 * LANES :]
        qkv_o[g] = jnp.concatenate([q, k, v], axis=1)
        v_t = jnp.transpose(v)
        for h in range(LANES // HD):
            here = (lane >= h * HD) & (lane < (h + 1) * HD)
            k_h = jnp.where(here, k, jnp.zeros_like(k))
            for j in range(win // LANES):
                ext = (j + 1) * LANES
                cols = slice(j * LANES, ext)
                s = mm(k_h[:ext], q[cols], NT) + bias_s[:ext, cols]
                e = jnp.exp(s - jnp.max(s, axis=0, keepdims=True))
                p = (e * (1.0 / jnp.sum(e, axis=0, keepdims=True))).astype(BF16)
                pt_o[2 * g + h, :ext, cols] = p
                mixed = mm(v_t[h * HD : (h + 1) * HD, :ext], p)
                mixt_o[rows_at(g * LANES + h * HD, HD, HD), cols] = mixed.astype(BF16)


def norm_forward(v):
    center = v - jnp.mean(v, axis=-1, keepdims=True)
    rs = lax.rsqrt(jnp.mean(center * center, axis=-1, keepdims=True) + NORM_EPS)
    return center * rs, rs


def norm_backward(g, xhat, rs, gain):
    e = g * gain
    return rs * (e - jnp.mean(e, axis=-1, keepdims=True) - xhat * jnp.mean(e * xhat, axis=-1, keepdims=True))


def put_blocks(me_t, value, keep, s1, sx):
    n = keep.shape[0]
    for r, ref in ((0, keep), (1, s1.at[0]), (2, sx.at[0]), (3, sx.at[1])):
        ref[...] = value[rows_at((me_t ^ r) * n, n, n), :].astype(ref.dtype)


CHUNK = 64


def ffn_kernel(places, n_pieces, scal, *refs):
    own, rx, c1, c3, hid, mixt, nrm = refs[:7]
    pieces = refs[7 : 7 + n_pieces]
    rest = refs[7 + n_pieces :]
    res_k, res_1, res_x, gone_o, gm_o, gnorm_o = rest[:6]
    if places is None:
        gup_o, gdown_o, gout_o = rest[6:9]
        rest = rest[9:]
    else:
        keep_o, send_o = rest[6:8]
        rest = rest[8:]
    cot_s, out_s, up_s, down_s, a_s, b_s, xh1_s, r1_s, n1_s, sent_s, act_s, dg_s, low_s, xt_s = rest
    me_dp, me_t = scal[0], scal[1]
    win, width = hid.shape
    groups = up_s.shape[0]
    fill_window(me_t, (own, rx, c1, c3), cot_s)
    if places is None:
        up_s[...] = pieces[0][...]
        down_s[...] = pieces[1][...]
        out_s[...] = pieces[2][...]
        n_dp = 1
    else:
        n_dp = 2 * max(z0 + ref.shape[0] for ref, (_, _, z0, _) in zip(pieces, places, strict=True))
        per = width // n_dp
        out_per = LANES // n_dp
        for ref, (xr, yr, z0, c) in zip(pieces, places, strict=True):
            tr = xr * 2 + c
            for i in range(ref.shape[0]):
                src = me_dp ^ ((z0 + i) * 2 + yr)
                up_s[tr, rows_at(src * per, per, per), :] = ref[i, 0:per]
                down_s[tr, rows_at(src * per, per, per), :] = ref[i, per : 2 * per]
                out_s[rows_at(tr * LANES + src * out_per, out_per, out_per), :] = ref[i, 2 * per : 2 * per + out_per]

    def chunks(fn):
        @pl.loop(0, win // CHUNK)
        def _(i):
            fn(rows_at(i * CHUNK, CHUNK, CHUNK))

    a_s[...] = mm(jnp.transpose(mixt[...]), out_s[...])

    def norm_one(at):
        xhat, rs = norm_forward(hid[at, :] + a_s[at, :])
        xh1_s[at, :] = xhat
        r1_s[at, :] = jnp.broadcast_to(rs, (CHUNK, LANES))
        normed = xhat * nrm[0:1, :] + nrm[1:2, :]
        n1_s[at, :] = normed
        sent_s[at, :] = normed.astype(BF16)

    chunks(norm_one)

    @pl.loop(0, groups)
    def _(g):
        a_s[...] = mm(sent_s[...], up_s[g])

        def gelu(at):
            v = a_s[at, :]
            t = jnp.tanh(GELU_A * (v + GELU_B * v * v * v))
            act_s[g, at, :] = (0.5 * v * (1.0 + t)).astype(BF16)
            dg_s[g, at, :] = 0.5 * (1.0 + t) + 0.5 * v * (1.0 - t * t) * (GELU_A * (1.0 + 3.0 * GELU_B * v * v))

        chunks(gelu)
        n1_s[...] += mm(act_s[g], down_s[g])

    def norm_two(i, sums):
        at = rows_at(i * CHUNK, CHUNK, CHUNK)
        xhat, rs = norm_forward(n1_s[at, :])
        n1_s[at, :] = xhat * nrm[2:3, :] + nrm[3:4, :]
        g = cot_s[at, :].astype(F32)
        grad = norm_backward(g, xhat, rs, nrm[2:3, :])
        b_s[at, :] = grad
        low_s[at, :] = grad.astype(BF16)
        return (sums[0] + jnp.sum((g * xhat).reshape(-1, 8, width), axis=0), sums[1] + jnp.sum(g.reshape(-1, 8, width), axis=0))

    zero = jnp.zeros((8, width), F32)
    gain_two, shift_two = lax.fori_loop(0, win // CHUNK, norm_two, (zero, zero))
    put_blocks(me_t, n1_s, res_k, res_1, res_x)

    def put(c, xr, first, height, value):
        ref = keep_o if c == 0 else send_o
        each = value.shape[0] // n_dp
        for d in range(n_dp):
            rel = d ^ me_dp
            ref[xr * 2 + (rel & 1), rel >> 1, first : first + height, :] = value[d * each : (d + 1) * each].astype(BF16)

    xt_s[...] = jnp.transpose(sent_s[...])
    for xr in range(groups // 2):
        for c in range(2):
            g = xr * 2 + c
            gdown = mm(jnp.transpose(act_s[g]), low_s[...])
            a_s[...] = mm(low_s[...], down_s[g], NT)
            act_s[g] = (a_s[...] * dg_s[g]).astype(BF16)
            gup = mm(xt_s[...], act_s[g])
            if places is None:
                gdown_o[g] = gdown.astype(BF16)
                gup_o[g] = gup.astype(BF16)
            else:
                put(c, xr, 0, per, gup)
                put(c, xr, per, per, gdown)
            b_s[...] += mm(act_s[g], up_s[g], NT)

    def norm_one_back(i, sums):
        at = rows_at(i * CHUNK, CHUNK, CHUNK)
        g = b_s[at, :]
        xhat = xh1_s[at, :]
        grad = norm_backward(g, xhat, r1_s[at, 0:1], nrm[0:1, :])
        gone_o[at, :] = grad
        low_s[at, :] = grad.astype(BF16)
        return (sums[0] + jnp.sum((g * xhat).reshape(-1, 8, width), axis=0), sums[1] + jnp.sum(g.reshape(-1, 8, width), axis=0))

    gain_one, shift_one = lax.fori_loop(0, win // CHUNK, norm_one_back, (zero, zero))
    for k, total in enumerate((gain_one, shift_one, gain_two, shift_two)):
        gnorm_o[k : k + 1, :] = jnp.sum(total, axis=0, keepdims=True)
    gnorm_o[4:8, :] = jnp.zeros((4, width), F32)

    gout = mm(mixt[...], low_s[...])
    if places is None:
        gout_o[...] = gout.astype(BF16)
    else:
        for xr in range(groups // 2):
            for c in range(2):
                g = xr * 2 + c
                put(c, xr, 2 * per, out_per, gout[g * LANES : (g + 1) * LANES])
    gm = mm(low_s[...], out_s[...], NT).astype(BF16)
    for g in range(groups):
        gm_o[g] = gm[:, g * LANES : (g + 1) * LANES]


def attention_back_kernel(fast, scal, hid, qkv, pt, gm, w, gone, gnorm, *rest):
    gi_k, gi_1, gi_x = rest[:3]
    if fast:
        keep_o, send_o = rest[3:5]
    else:
        gattn_o, gpos_o = rest[3:5]
    ht_s, ds_s, dqkv_s, acc_s, dqt_s = rest[5:]
    me_dp, me_t = scal[0], scal[1]
    win, width = hid.shape
    groups = w.shape[0]
    blocks = win // LANES
    heads = LANES // HD
    ht_s[...] = jnp.transpose(hid[...].astype(BF16))
    acc_s[...] = gone[...]
    lane = lax.broadcasted_iota(jnp.int32, (win, LANES), 1)

    @pl.loop(0, groups)
    def _(g):
        q = qkv[g, :, :LANES]
        k = qkv[g, :, LANES : 2 * LANES]
        v = qkv[g, :, 2 * LANES :]
        d_mixed = gm[g]
        k_t = jnp.transpose(k)
        d_m_h = []
        q_h = []
        for h in range(heads):
            here = (lane >= h * HD) & (lane < (h + 1) * HD)
            q_h.append(jnp.where(here, q, jnp.zeros_like(q)))
            d_m_h.append(jnp.where(here, d_mixed, jnp.zeros_like(q)))
            for j in range(blocks):
                ext = (j + 1) * LANES
                cols = slice(j * LANES, ext)
                p = pt[2 * g + h, :ext, cols].astype(F32)
                dp = mm(v[:ext], d_m_h[h][cols], NT)
                ds = (p * (dp - jnp.sum(p * dp, axis=0, keepdims=True))).astype(BF16)
                ds_s[h, :ext, cols] = ds
                dqt_s[h * HD : (h + 1) * HD, cols] = mm(k_t[h * HD : (h + 1) * HD, :ext], ds) * (HD**-0.5)
        dqkv_s[g, :, :LANES] = jnp.transpose(dqt_s[...]).astype(BF16)
        for i in range(blocks):
            at = slice(i * LANES, (i + 1) * LANES)
            dk = jnp.zeros((LANES, LANES), F32)
            dv = jnp.zeros((LANES, LANES), F32)
            for h in range(heads):
                dk += mm(ds_s[h, at, i * LANES :], q_h[h][i * LANES :])
                dv += mm(pt[2 * g + h, at, i * LANES :], d_m_h[h][i * LANES :])
            dqkv_s[g, at, LANES : 2 * LANES] = dk.astype(BF16)
            dqkv_s[g, at, 2 * LANES :] = dv.astype(BF16)
        acc_s[...] += mm(dqkv_s[g], w[g], NT)

    put_blocks(me_t, acc_s, gi_k, gi_1, gi_x)
    if not fast:
        for g in range(groups):
            gattn_o[g] = mm(ht_s[...], dqkv_s[g]).astype(BF16)
        gpos_o[...] = acc_s[...].astype(BF16)
        return
    n_dp = 2 * keep_o.shape[1]
    per = width // n_dp
    pos_per = win // (n_dp * groups)
    for xr in range(groups // 2):
        for c in range(2):
            g = xr * 2 + c
            ref = keep_o if c == 0 else send_o
            grad = mm(ht_s[...], dqkv_s[g])
            for d in range(n_dp):
                rel = d ^ me_dp
                a, b = xr * 2 + (rel & 1), rel >> 1
                for t in range(3):
                    ref[a, b, t * per : (t + 1) * per, :] = grad[d * per : (d + 1) * per, t * LANES : (t + 1) * LANES].astype(BF16)
                where = (me_t ^ g) * (win // groups) + d * pos_per
                for k in range(width // LANES):
                    at = 3 * per + k * pos_per
                    ref[a, b, at : at + pos_per, :] = acc_s[rows_at(where, pos_per, pos_per), k * LANES : (k + 1) * LANES].astype(BF16)
                at = 3 * per + width // LANES * pos_per
                pair = d // 2 * LANES
                tile = gnorm[0:8, pair : pair + LANES]
                ref[a, b, at : at + 16, :] = jnp.concatenate([tile, tile], axis=0).astype(BF16)


def to_windows(value, me_t):
    x, c = me_t >> 1, me_t & 1
    rx = swap(lax.dynamic_slice_in_dim(value, 2 * (1 - x), 2, 0), 0, 2)
    c1 = swap(lax.dynamic_slice_in_dim(value, me_t ^ 1, 1, 0), 0, 1)
    c3 = swap(lax.dynamic_slice_in_dim(rx, 1 - c, 1, 0), 0, 1)
    return value, rx, c1, c3


def from_windows(keep, s1, sx, me_t):
    rx = swap(sx, 0, 2)
    r1 = swap(s1, 0, 1)[0]
    r3 = swap(rx[1:2], 0, 1)[0]
    flip = (me_t & 1) == 1
    low = [jnp.where(flip, r1, keep), jnp.where(flip, keep, r1)]
    high = [jnp.where(flip, r3, rx[0]), jnp.where(flip, rx[0], r3)]
    cross = (me_t >> 1) == 1
    return jnp.stack([jnp.where(cross, high[0], low[0]), jnp.where(cross, high[1], low[1]), jnp.where(cross, low[0], high[0]), jnp.where(cross, low[1], high[1])])


def gather(value, direct):
    nz = lax.axis_size("dp") // 2
    q = jnp.stack([value] + [swap(value, 2 * k, 0) for k in range(1, nz)])
    qx, qy = swap(q, 0, 2), swap(q, 1, 0)
    found = [(q, (0, 0, 0)), (qx, (1, 0, 0)), (qy, (0, 1, 0))]
    if direct:
        found.append((swap(q, 1, 2), (1, 1, 0)))
    else:
        half = nz // 2
        found.append((swap(qx[:half], 1, 0), (1, 1, 0)))
        found.append((swap(qy[half:], 0, 2), (1, 1, half)))
    out = []
    for array, place in found:
        out.append((array, (*place, 0)))
        out.append((swap(array, 0, 1), (*place, 1)))
    return out


def add(a, b):
    return (a.astype(F32) + b.astype(F32)).astype(BF16)


def scatter_sum(keep, send, direct):
    total = add(keep, swap(send, 0, 1))
    nz = total.shape[1]
    if direct:
        parts = [total[0], swap(total[2], 0, 2), swap(total[1], 1, 0), swap(total[3], 1, 2)]
        total = sum(p.astype(F32) for p in parts).astype(BF16)
    else:
        half = nz // 2
        a, b = total[:, :half], total[:, half:]
        a = add(a[:2], swap(a[2:], 0, 2))
        b = add(b[0::2], swap(b[1::2], 1, 0))
        a = add(a[0], swap(a[1], 1, 0))
        b = add(b[0], swap(b[1], 0, 2))
        total = jnp.concatenate([a, b])
    arrived = [total[0]] + [swap(total[k], 2 * k, 0) for k in range(1, nz)]
    return sum(p.astype(F32) for p in arrived)


def adam_step(weight, gradient, moment_one, second, step_rate, decay_rate):
    first_new = BETA_ONE * moment_one + (1.0 - BETA_ONE) * gradient
    second_new = BETA_TWO * second + (1.0 - BETA_TWO) * gradient * gradient
    fixed_first = first_new / (1.0 - BETA_ONE**STEP)
    fixed_second = second_new / (1.0 - BETA_TWO**STEP)
    weight_new = weight - step_rate * (fixed_first / (jnp.sqrt(fixed_second) + ADAM_EPS) + decay_rate * weight)
    return (weight_new, first_new, second_new)


def call(kernel, outs, scratch, args, mib, flops):
    vmem = pl.BlockSpec(memory_space=pltpu.VMEM)
    return pl.pallas_call(
        kernel,
        out_shape=outs,
        in_specs=[pl.BlockSpec(memory_space=pltpu.SMEM)] + [vmem] * (len(args) - 1),
        out_specs=[vmem] * len(outs),
        scratch_shapes=[pltpu.VMEM(s, t) for s, t in scratch],
        compiler_params=pltpu.CompilerParams(vmem_limit_bytes=mib * 1024 * 1024),
        cost_estimate=pl.CostEstimate(flops=flops, bytes_accessed=0, transcendentals=0),
    )(*args)


def body(
    inputs,
    segment_ids,
    cotangent,
    attn_proj,
    out_proj,
    up_proj,
    down_proj,
    pos_table,
    norm_params,
    first_attn,
    second_attn,
    first_out,
    second_out,
    first_up,
    second_up,
    first_down,
    second_down,
    first_pos,
    second_pos,
    first_norm,
    second_norm,
):
    n_dp, n_t = lax.axis_size("dp"), lax.axis_size("tensor")
    me_dp, me_t = lax.axis_index("dp"), lax.axis_index("tensor")
    scal = jnp.stack([me_dp, me_t]).astype(jnp.int32)
    windows, block, width = inputs.shape
    win = block * n_t
    inner = up_proj.shape[1]
    group = attn_proj.shape[2]
    per, out_per, pos_per = attn_proj.shape[1], out_proj.shape[0], pos_table.shape[0]
    fast = out_per % 16 == 0 and pos_per % 16 == 0 and 2 * per == LANES
    sds = jax.ShapeDtypeStruct

    seg_row = lax.dynamic_slice_in_dim(segment_ids, me_t, 1, 0)
    if fast:
        norm_tile = jnp.concatenate([norm_params, norm_params], axis=1)
        norm_high = norm_tile.astype(BF16)
        norm_low = (norm_tile - norm_high.astype(F32)).astype(BF16)
        none = jnp.zeros_like(norm_high)
        ga = jnp.concatenate(
            [
                attn_proj.astype(BF16).reshape(3 * per, group),
                pos_table.astype(BF16).reshape(pos_per, width // LANES, LANES).transpose(1, 0, 2).reshape(-1, LANES),
                jnp.concatenate([norm_high, none, norm_low, none]),
            ]
        )
        gb = jnp.concatenate([up_proj.astype(BF16), down_proj.astype(BF16), out_proj.astype(BF16)])
        found_a = gather(ga, True)
        x_parts = to_windows(inputs, me_t)
        found_b = gather(gb, False)
        a_args, a_places = [f[0] for f in found_a], tuple(f[1] for f in found_a)
        b_args, b_places = [f[0] for f in found_b], tuple(f[1] for f in found_b)
    else:
        x_parts = to_windows(inputs, me_t)
        relative = me_t ^ jnp.arange(n_t)
        whole = [lax.all_gather(lax.all_gather(v.astype(BF16), "dp"), "tensor") for v in (attn_proj, out_proj, up_proj, down_proj)]
        attn_w, out_w, up_w, down_w = [jnp.take(v, relative, axis=0) for v in whole]
        attn_w = attn_w.transpose(0, 1, 3, 2, 4).reshape(n_t, width, 3 * group)
        pos_w = lax.all_gather(lax.all_gather(pos_table.astype(BF16), "dp", axis=0, tiled=True), "tensor", axis=0, tiled=True)
        norm_w = lax.all_gather(norm_params, "dp", axis=1, tiled=True)
        norm_w = jnp.concatenate([norm_w, jnp.zeros_like(norm_w)])
        a_args, a_places = [attn_w, pos_w, norm_w], None
        b_args, b_places = [up_w.reshape(n_t, width, inner), down_w.reshape(n_t, inner, width), out_w.reshape(n_t * group, width)], None

    hid, qkv, pt, mixt, attn_all, norm_all = call(
        functools.partial(attention_kernel, a_places, len(a_args)),
        [
            sds((win, width), F32),
            sds((n_t, win, 3 * group), BF16),
            sds((n_t * group // HD, win, win), BF16),
            sds((n_t * group, win), BF16),
            sds((n_t, width, 3 * group), BF16),
            sds((8, width), F32),
        ],
        [((win, width), BF16), ((win, width), BF16), ((win, win), F32), ((n_dp, 16, LANES), F32)],
        [scal, *x_parts, seg_row, *a_args],
        32,
        2 * win * width * 3 * width,
    )
    cot_parts = to_windows(cotangent, me_t)

    blocks = [sds((block, width), BF16), sds((1, block, width), BF16), sds((2, block, width), BF16)]
    if fast:
        rows_b = 2 * per + out_per
        grads_b = [sds((4, n_dp // 2, rows_b, width), BF16)] * 2
    else:
        grads_b = [sds((n_t, width, inner), BF16), sds((n_t, inner, width), BF16), sds((n_t * group, width), BF16)]
    res_k, res_1, res_x, gone, gm, gnorm, *got_b = call(
        functools.partial(ffn_kernel, b_places, len(b_args)),
        [*blocks, sds((win, width), F32), sds((n_t, win, group), BF16), sds((8, width), F32), *grads_b],
        [
            ((win, width), BF16),
            ((n_t * group, width), BF16),
            ((n_t, width, inner), BF16),
            ((n_t, inner, width), BF16),
            ((win, width), F32),
            ((win, width), F32),
            ((win, width), F32),
            ((win, LANES), F32),
            ((win, width), F32),
            ((win, width), BF16),
            ((n_t, win, inner), BF16),
            ((n_t, win, inner), F32),
            ((win, width), BF16),
            ((width, win), BF16),
        ],
        [scal, *cot_parts, hid, mixt, norm_all, *b_args],
        50,
        12 * win * width * n_t * inner,
    )
    if fast:
        sum_b = scatter_sum(*got_b, False)
    outputs = from_windows(res_k, res_1, res_x, me_t)

    blocks = [sds((block, width), F32), *blocks[1:]]
    if fast:
        rows_a = 3 * per + width // LANES * pos_per + 16
        grads_a = [sds((4, n_dp // 2, rows_a, LANES), BF16)] * 2
    else:
        grads_a = [sds((n_t, width, 3 * group), BF16), sds((win, width), BF16)]
    gi_k, gi_1, gi_x, *got_a = call(
        functools.partial(attention_back_kernel, fast),
        [*blocks, *grads_a],
        [
            ((width, win), BF16),
            ((LANES // HD, win, win), BF16),
            ((n_t, win, 3 * group), BF16),
            ((win, width), F32),
            ((LANES, win), F32),
        ],
        [scal, hid, qkv, pt, gm, attn_all, gone, gnorm],
        40,
        4 * win * width * 3 * width,
    )
    gi_1, gi_x = gi_1.astype(F32), gi_x
    grad_input = from_windows(gi_k.astype(F32), gi_1.astype(BF16), gi_x, me_t)

    if fast:
        sum_a = scatter_sum(*got_a, True)
        g_attn = sum_a[: 3 * per].reshape(3, per, group)
        at = 3 * per
        n_pos = width // LANES * pos_per
        g_pos = sum_a[at : at + n_pos].reshape(width // LANES, pos_per, LANES).transpose(1, 0, 2).reshape(pos_per, width)
        tile = sum_a[at + n_pos : at + n_pos + 4]
        g_norm = jnp.where((me_dp & 1) == 1, tile[:, LANES // 2 :], tile[:, : LANES // 2])
        g_up, g_down, g_out = sum_b[:per], sum_b[per : 2 * per], sum_b[2 * per :]
    else:

        def reduced(value, own_axis):
            arrived = lax.all_to_all(value, "dp", split_axis=0, concat_axis=0, tiled=True)
            part = arrived.astype(F32).sum(axis=0).astype(BF16)
            arrived = lax.all_to_all(part, "tensor", split_axis=0, concat_axis=0, tiled=True)
            return arrived.astype(F32).sum(axis=0)

        gup, gdown, gout = got_b
        gattn, gpos = got_a
        gup, gdown, gout, gattn = [jnp.take(v, relative, axis=0) for v in (gup, gdown, gout.reshape(n_t, group, width), gattn)]
        g_up = reduced(gup.reshape(n_t, n_dp, per, inner).swapaxes(0, 1), 0)
        g_down = reduced(gdown.reshape(n_t, n_dp, inner // n_dp, width).swapaxes(0, 1), 0)
        g_out = reduced(gout.reshape(n_t, n_dp, out_per, width).swapaxes(0, 1), 0)
        g_pos = reduced(gpos.reshape(n_t, n_dp, pos_per, width).swapaxes(0, 1), 0)
        g_attn = reduced(gattn.reshape(n_t, n_dp, per, 3, group).swapaxes(0, 1), 0).swapaxes(0, 1)
        cut = gnorm[:4].reshape(4, n_dp, width // n_dp).swapaxes(0, 1).astype(BF16)
        g_norm = reduced(jnp.broadcast_to(cut[:, None], (n_dp, n_t, *cut.shape[1:])), 0)

    masters = (attn_proj, out_proj, up_proj, down_proj, pos_table, norm_params)
    gradients = (g_attn, g_out, g_up, g_down, g_pos, g_norm)
    firsts = (first_attn, first_out, first_up, first_down, first_pos, first_norm)
    seconds = (second_attn, second_out, second_up, second_down, second_pos, second_norm)
    updated = []
    for index in range(6):
        updated += adam_step(masters[index], gradients[index], firsts[index], seconds[index], RATES[index], DECAYS[index])
    return (outputs, grad_input, *updated)


def solution(mesh):
    acts = P("dp", "tensor", None)
    attn = P(None, "dp", "tensor")
    both = P(("tensor", "dp"), None)
    up = P("dp", "tensor")
    norm = P(None, "dp")
    return jax.shard_map(
        body,
        mesh=mesh,
        in_specs=(acts, P("dp", None), acts, attn, both, up, both, both, norm, *(attn,) * 2, *(both,) * 2, *(up,) * 2, *(both,) * 4, *(norm,) * 2),
        out_specs=(acts, acts, *(attn,) * 3, *(both,) * 3, *(up,) * 3, *(both,) * 6, *(norm,) * 3),
        check_vma=False,
    )
```

time: 494 us -> 205 us (0.41)
  blocking collectives: 189 us -> 0 us
  waiting for transfers between devices: 149 us -> 80.9 us
  matrix products: 62.7 us -> 0 us
  Pallas kernels: 0 us -> 44 us
  starting transfers between devices: 21.1 us -> 39.9 us
  other arithmetic: 33.9 us -> 16.4 us
  between operations: 14.9 us -> 1.36 us
    all_gather x6 -> x0, blocking collectives: 183 us -> none  [the longest x1 32.7 us: body(): lax.all_gather(pos_table, 'dp', axis=0, tiled=True)]
    ppermute x0 -> x49, waiting for transfers between devices: none -> 80.9 us  [swap(): lax.ppermute(value, AXES, [(i, i ^ mask) for i in range(lax.axis_size('dp...]
    reduce_scatter x4 -> x0, waiting for transfers between devices: 69.2 us -> none  [the longest x1 31.8 us: body(): lax.psum_scatter(ffn_part.astype(jnp.bfloat16), 'tensor', scatter_dimensi...]
    dot_general x40 -> x0, matrix products: 62.7 us -> none  [the longest x8 6.18 us: window_scores(): jnp.einsum('qhd,khd->hqk', query_rows, key_rows, preferred_element_type=j...]
    pallas_call x0 -> x3, Pallas kernels: none -> 44 us  [call(): pl.pallas_call(kernel, out_shape=outs, in_specs=[pl.BlockSpec(memory_spac...]
    all_to_all x5 -> x0, waiting for transfers between devices: 40.1 us -> none  [sent_and_summed(): lax.all_to_all(tiles, axis, split_axis=0, concat_axis=0, tiled=True)]
    ppermute x0 -> x49, starting transfers between devices: none -> 39.9 us  [swap(): lax.ppermute(value, AXES, [(i, i ^ mask) for i in range(lax.axis_size('dp...]
    all_gather x4 -> x0, waiting for transfers between devices: 39.5 us -> none  [the longest x1 22.5 us: body(): lax.all_gather(grad_two.astype(jnp.bfloat16), 'tensor', axis=1, tiled=True)]
  transfers between devices with their start and end apart: 13 -> 49, of which waited for: 10 -> 17; matrix products, arithmetic and copies ran while one was open for 5% -> 8% of each run, Pallas kernels for 0% -> 4%
where the time goes in v1:
time: 205 us; the launch traced here: 204 us
  waiting for transfers between devices  80.9 us (39%)
  Pallas kernels  44 us (21%)
  starting transfers between devices  39.9 us (19%)
  local copies, waits for them, and re-layouts  21.9 us (11%)
  other arithmetic  16.4 us (8%)
    ppermute x49, waiting for transfers between devices, swap(): lax.ppermute(value, AXES, [(i, i ^ mask) for i in range(lax.axis_size('dp...  80.9 us
    pallas_call x3, Pallas kernels, call(): pl.pallas_call(kernel, out_shape=outs, in_specs=[pl.BlockSpec(memory_spac...  44 us
    ppermute x49, starting transfers between devices, swap(): lax.ppermute(value, AXES, [(i, i ^ mask) for i in range(lax.axis_size('dp...  39.9 us
    unnamed x100, local copies, waits for them, and re-layouts  16.1 us
  transfers between devices with their start and end apart: 49, of which 17 were waited for; matrix products, arithmetic and copies ran while one was open for 8% of the time, Pallas kernels for 4%

profile of v1, /device:TPU:0, one launch (start us, length us, event | category | flops | bytes accessed | tf_op | source)
XLA Modules:
  0.0 204.4 jit_solution(16879096313877345341)
XLA Ops:
  4.1 5.1 %collective-permute-start.8 = (bf16[272,128]{1,0:T(8,128)(2,1)S(1)}, bf16[272,128]{1,0:T(8,128)(2,1)S(1)}, u32[]{:S(2)}, u32[]{:S(2)}) collective-permute-start(bf16[272,128]{1,0:T(8,128)(2,1)S(1)} %concatenate.10), channel_id=1, source_target_pairs={{0,24},{1,25},{2,26},{3,27},{4,28},{5,29},{6,30},{7,31},{8,16},{9,... | collective-permute-start | bytes 208904 | tf_op jit(solution)/shard_map/ppermute | solution.py:39
  12.5 2.4 %collective-permute-start.17 = (bf16[144,512]{1,0:T(8,128)(2,1)S(1)}, bf16[144,512]{1,0:T(8,128)(2,1)S(1)}, u32[]{:S(2)}, u32[]{:S(2)}) collective-permute-start(bf16[144,512]{1,0:T(8,128)(2,1)S(1)} %get-tuple-element.96), channel_id=1, source_target_pairs={{0,16},{1,17},{2,18},{3,19},{4,20},{5,21},{6,22},{7,23},{8,24},{9,... | collective-permute-start | bytes 442376 | tf_op jit(solution)/shard_map/ppermute | solution.py:39
  14.9 2.0 collective-permute-start.16
  20.2 5.6 %collective-permute-done.17 = bf16[144,512]{1,0:T(8,128)(2,1)S(1)} collective-permute-done((bf16[144,512]{1,0:T(8,128)(2,1)S(1)}, bf16[144,512]{1,0:T(8,128)(2,1)S(1)}, u32[]{:S(2)}, u32[]{:S(2)}) %collective-permute-start.17) | collective-permute-done | bytes 147488 | tf_op jit(solution)/shard_map/ppermute | solution.py:39
  25.8 2.4 %collective-permute-start.14 = (bf16[4,272,128]{2,1,0:T(8,128)(2,1)S(1)}, bf16[4,272,128]{2,1,0:T(8,128)(2,1)S(1)}, u32[]{:S(2)}, u32[]{:S(2)}) collective-permute-start(bf16[4,272,128]{2,1,0:T(8,128)(2,1)S(1)} %pad_maximum_fusion.3.refs_5_), channel_id=1, source_target_pairs={{0,6},{1,7},{2,4},{3,5},{4,2},{5,3},{6,0},{7,1},{8,14},{9,15},{10,... | collective-permute-start | bytes 835592 | tf_op jit(solution)/shard_map/ppermute | solution.py:39
  35.1 4.5 %collective-permute-done.14.refs_11_ = bf16[4,272,128]{2,1,0:T(8,128)(2,1)S(1)} collective-permute-done((bf16[4,272,128]{2,1,0:T(8,128)(2,1)S(1)}, bf16[4,272,128]{2,1,0:T(8,128)(2,1)S(1)}, u32[]{:S(2)}, u32[]{:S(2)}) %collective-permute-start.14) | collective-permute-done | bytes 278560 | tf_op jit(solution)/shard_map/ppermute | solution.py:39
  39.6 15.8 %collective-permute-done.12.refs_9_ = bf16[4,272,128]{2,1,0:T(8,128)(2,1)S(1)} collective-permute-done((bf16[4,272,128]{2,1,0:T(8,128)(2,1)S(1)}, bf16[4,272,128]{2,1,0:T(8,128)(2,1)S(1)}, u32[]{:S(2)}, u32[]{:S(2)}) %collective-permute-start.12) | collective-permute-done | bytes 278560 | tf_op jit(solution)/shard_map/ppermute | solution.py:39
  67.4 3.9 %collective-permute-done.26.refs_15_ = bf16[2,144,512]{2,1,0:T(8,128)(2,1)} collective-permute-done((bf16[2,144,512]{2,1,0:T(8,128)(2,1)}, bf16[2,144,512]{2,1,0:T(8,128)(2,1)}, u32[]{:S(2)}, u32[]{:S(2)}) %collective-permute-start.26) | collective-permute-done | bytes 294944 | tf_op jit(solution)/shard_map/ppermute | solution.py:39
  80.4 9.0 %shard_map.356 = (f32[512,512]{1,0:T(8,128)S(1)}, bf16[4,512,384]{2,1,0:T(8,128)(2,1)S(1)}, bf16[8,512,512]{2,1,0:T(8,128)(2,1)S(1)}, bf16[512,512]{1,0:T(8,128)...) custom-call(s32[2]{0:T(128)S(1)} %pad_add_fusion.scal, bf16[4,128,512]{2,1,0:T(8,128)(2,1)S(1)} %copy-done.1, ...), custom_call_target="tpu_custom_call" | custom-call | flops 805306368 | tf_op jit(solution)/shard_map/pallas_call | solution.py:422
  90.4 23.0 %shard_map.357 = (bf16[128,512]{1,0:T(8,128)(2,1)S(1)}, bf16[1,128,512]{2,1,0:T(8,128)(2,1)S(1)}, bf16[2,128,512]{2,1,0:T(8,128)(2,1)S(1)}, f32[512,512]{1,0:T(8...) custom-call(s32[2]{0:T(128)S(1)} %pad_add_fusion.scal, ...), custom_call_target="tpu_custom_call" | custom-call | flops 6442450944 | tf_op jit(solution)/shard_map/pallas_call | solution.py:422
  114.6 12.1 %shard_map.358 = (f32[128,512]{1,0:T(8,128)S(1)}, bf16[1,128,512]{2,1,0:T(8,128)(2,1)}, bf16[2,128,512]{2,1,0:T(8,128)(2,1)S(1)}, bf16[4,4,272,128]{3,2,1,0:T(8,128)(2,1)S(1)}, bf16[4,4,272,128]{3,2,1,0:T(8,128)(2,1)}) custom-call(s32[2]{0:T(128)S(1)} %pad_add_fusion.scal, f32[512,512]{1,0:T(8,128)S(1)} %copy-done.3, ...), custom_call_target="tpu_custom_call" | custom-call | flops 1610612736 | tf_op jit(solution)/shard_map/pallas_call | solution.py:422
  129.2 7.1 %collective-permute-done.31 = bf16[2,128,512]{2,1,0:T(8,128)(2,1)S(1)} collective-permute-done((bf16[2,128,512]{2,1,0:T(8,128)(2,1)S(1)}, bf16[2,128,512]{2,1,0:T(8,128)(2,1)S(1)}, u32[]{:S(2)}, u32[]{:S(2)}) %collective-permute-start.31) | collective-permute-done | bytes 262176 | tf_op jit(solution)/shard_map/ppermute | solution.py:39
  137.0 4.4 %collective-permute-done.28 = bf16[2,128,512]{2,1,0:T(8,128)(2,1)S(1)} collective-permute-done((bf16[2,128,512]{2,1,0:T(8,128)(2,1)S(1)}, bf16[2,128,512]{2,1,0:T(8,128)(2,1)S(1)}, u32[]{:S(2)}, u32[]{:S(2)}) %collective-permute-start.28) | collective-permute-done | bytes 262176 | tf_op jit(solution)/shard_map/ppermute | solution.py:39
  149.9 4.0 %collective-permute-done.35 = bf16[4,272,128]{2,1,0:T(8,128)(2,1)S(1)} collective-permute-done((bf16[4,272,128]{2,1,0:T(8,128)(2,1)S(1)}, bf16[4,272,128]{2,1,0:T(8,128)(2,1)S(1)}, u32[]{:S(2)}, u32[]{:S(2)}) %collective-permute-start.35) | collective-permute-done | bytes 278560 | tf_op jit(solution)/shard_map/ppermute | solution.py:39
  153.9 5.6 %collective-permute-done.37 = bf16[4,272,128]{2,1,0:T(8,128)(2,1)S(1)} collective-permute-done((bf16[4,272,128]{2,1,0:T(8,128)(2,1)S(1)}, bf16[4,272,128]{2,1,0:T(8,128)(2,1)S(1)}, u32[]{:S(2)}, u32[]{:S(2)}) %collective-permute-start.37) | collective-permute-done | bytes 278560 | tf_op jit(solution)/shard_map/ppermute | solution.py:39
  161.7 3.0 %collective-permute-start.40 = (bf16[272,128]{1,0:T(8,128)(2,1)S(1)}, bf16[272,128]{1,0:T(8,128)(2,1)S(1)}, u32[]{:S(2)}, u32[]{:S(2)}) collective-permute-start(bf16[272,128]{1,0:T(8,128)(2,1)S(1)} %get-tuple-element.93), channel_id=1, source_target_pairs={{0,24},{1,25},{2,26},{3,27},{4,28},{5,29},{6,30},{7,31},{8,16},{9,... | collective-permute-start | bytes 208904 | tf_op jit(solution)/shard_map/ppermute | solution.py:39
  165.2 2.4 %add_convert_fusion = bf16[4,4,144,512]{3,2,1,0:T(8,128)(2,1)S(1)} fusion(bf16[4,4,144,512]{3,2,1,0:T(8,128)(2,1)} %collective-permute-done.41, bf16[4,4,144,512]{3,2,1,0:T(8,128)(2,1)S(1)} %copy-done.26), kind=kLoop, calls=%fused_computation | loop fusion | flops 4718592 | bytes 7077888 | tf_op jit(solution)/shard_map/convert_element_type | solution.py:390
  168.3 2.3 %collective-permute-done.39 = bf16[272,128]{1,0:T(8,128)(2,1)S(1)} collective-permute-done((bf16[272,128]{1,0:T(8,128)(2,1)S(1)}, bf16[272,128]{1,0:T(8,128)(2,1)S(1)}, u32[]{:S(2)}, u32[]{:S(2)}) %collective-permute-start.39) | collective-permute-done | bytes 69664 | tf_op jit(solution)/shard_map/ppermute | solution.py:39
  173.0 7.1 %collective-permute-done.42 = bf16[2,2,144,512]{3,2,1,0:T(8,128)(2,1)S(1)} collective-permute-done((bf16[2,2,144,512]{3,2,1,0:T(8,128)(2,1)S(1)}, bf16[2,2,144,512]{3,2,1,0:T(8,128)(2,1)S(1)}, u32[]{:S(2)}, u32[]{:S(2)}) %collective-permute-start.42) | collective-permute-done | bytes 589856 | tf_op jit(solution)/shard_map/ppermute | solution.py:39
  180.8 5.7 %collective-permute-done.45 = bf16[2,2,144,512]{3,2,1,0:T(8,128)(2,1)S(1)} collective-permute-done((bf16[2,2,144,512]{3,2,1,0:T(8,128)(2,1)S(1)}, bf16[2,2,144,512]{3,2,1,0:T(8,128)(2,1)S(1)}, u32[]{:S(2)}, u32[]{:S(2)}) %collective-permute-start.45) | collective-permute-done | bytes 589856 | tf_op jit(solution)/shard_map/ppermute | solution.py:39
  187.4 2.3 %collective-permute-done.43 = bf16[2,144,512]{2,1,0:T(8,128)(2,1)S(1)} collective-permute-done((bf16[2,144,512]{2,1,0:T(8,128)(2,1)S(1)}, bf16[2,144,512]{2,1,0:T(8,128)(2,1)S(1)}, u32[]{:S(2)}, u32[]{:S(2)}) %collective-permute-start.43) | collective-permute-done | bytes 294944 | tf_op jit(solution)/shard_map/ppermute | solution.py:39
  190.2 3.4 %collective-permute-done.46 = bf16[2,144,512]{2,1,0:T(8,128)(2,1)S(1)} collective-permute-done((bf16[2,144,512]{2,1,0:T(8,128)(2,1)S(1)}, bf16[2,144,512]{2,1,0:T(8,128)(2,1)S(1)}, u32[]{:S(2)}, u32[]{:S(2)}) %collective-permute-start.46) | collective-permute-done | bytes 294944 | tf_op jit(solution)/shard_map/ppermute | solution.py:39
  194.2 2.1 %collective-permute-start.48 = (bf16[144,512]{1,0:T(8,128)(2,1)S(1)}, bf16[144,512]{1,0:T(8,128)(2,1)S(1)}, u32[]{:S(2)}, u32[]{:S(2)}) collective-permute-start(bf16[144,512]{1,0:T(8,128)(2,1)S(1)} %get-tuple-element.91), channel_id=1, source_target_pairs={{0,24},{1,25},{2,26},{3,27},{4,28},{5,29},{6,30},{7,31},{8,16},{9,... | collective-permute-start | bytes 442376 | tf_op jit(solution)/shard_map/ppermute | solution.py:39
  197.0 5.6 %collective-permute-done.47 = bf16[144,512]{1,0:T(8,128)(2,1)S(1)} collective-permute-done((bf16[144,512]{1,0:T(8,128)(2,1)S(1)}, bf16[144,512]{1,0:T(8,128)(2,1)S(1)}, u32[]{:S(2)}, u32[]{:S(2)}) %collective-permute-start.47) | collective-permute-done | bytes 147488 | tf_op jit(solution)/shard_map/ppermute | solution.py:39
  (230 shorter events, 62.4 us)
Async XLA Ops:
  4.1 13.8 %collective-permute-start.8 = (bf16[272,128]{1,0:T(8,128)(2,1)S(1)}, bf16[272,128]{1,0:T(8,128)(2,1)S(1)}, u32[]{:S(2)}, u32[]{:S(2)}) collective-permute-start(bf16[272,128]{1,0:T(8,128)(2,1)S(1)} %concatenate.10), channel_id=1, source_target_pairs={{0,24},{1,25},{2,26},{3,27},{4,28},{5,29},{6,30},{7,31},{8,16},{9,... | collective-permute-start | bytes 208904 | tf_op jit(solution)/shard_map/ppermute | solution.py:39
  12.5 13.3 %collective-permute-start.17 = (bf16[144,512]{1,0:T(8,128)(2,1)S(1)}, bf16[144,512]{1,0:T(8,128)(2,1)S(1)}, u32[]{:S(2)}, u32[]{:S(2)}) collective-permute-start(bf16[144,512]{1,0:T(8,128)(2,1)S(1)} %get-tuple-element.96), channel_id=1, source_target_pairs={{0,16},{1,17},{2,18},{3,19},{4,20},{5,21},{6,22},{7,23},{8,24},{9,... | collective-permute-start | bytes 442376 | tf_op jit(solution)/shard_map/ppermute | solution.py:39
  14.9 13.4 %collective-permute-start.16 = (bf16[144,512]{1,0:T(8,128)(2,1)S(1)}, bf16[144,512]{1,0:T(8,128)(2,1)S(1)}, u32[]{:S(2)}, u32[]{:S(2)}) collective-permute-start(bf16[144,512]{1,0:T(8,128)(2,1)S(1)} %get-tuple-element.96), channel_id=1, source_target_pairs={{0,8},{1,9},{2,10},{3,11},{4,12},{5,13},{6,14},{7,15},{8,0},{9,1},... | collective-permute-start | bytes 442376 | tf_op jit(solution)/shard_map/ppermute | solution.py:39
  18.1 14.0 %collective-permute-start = (bf16[2,128,512]{2,1,0:T(8,128)(2,1)S(1)}, bf16[2,128,512]{2,1,0:T(8,128)(2,1)}, u32[]{:S(2)}, u32[]{:S(2)}) collective-permute-start(bf16[2,128,512]{2,1,0:T(8,128)(2,1)S(1)} %constant_dynamic-slice_fusion.6), channel_id=1, source_target_pairs={{0,2},{1,3},{2,0},{3,1},{4,6},{5,7},{6,4},{7,5},{8,10},{9,11},{10,... | collective-permute-start | bytes 786440 | tf_op jit(solution)/shard_map/ppermute | solution.py:39
  19.7 13.8 %collective-permute-start.3 = (bf16[2,128,512]{2,1,0:T(8,128)(2,1)S(1)}, bf16[2,128,512]{2,1,0:T(8,128)(2,1)S(1)}, u32[]{:S(2)}, u32[]{:S(2)}) collective-permute-start(bf16[2,128,512]{2,1,0:T(8,128)(2,1)S(1)} %constant_dynamic-slice_fusion.3), channel_id=1, source_target_pairs={{0,2},{1,3},{2,0},{3,1},{4,6},{5,7},{6,4},{7,5},{8,10},{9,11},{10,... | collective-permute-start | bytes 786440 | tf_op jit(solution)/shard_map/ppermute | solution.py:39
  25.8 13.8 %collective-permute-start.14 = (bf16[4,272,128]{2,1,0:T(8,128)(2,1)S(1)}, bf16[4,272,128]{2,1,0:T(8,128)(2,1)S(1)}, u32[]{:S(2)}, u32[]{:S(2)}) collective-permute-start(bf16[4,272,128]{2,1,0:T(8,128)(2,1)S(1)} %pad_maximum_fusion.3.refs_5_), channel_id=1, source_target_pairs={{0,6},{1,7},{2,4},{3,5},{4,2},{5,3},{6,0},{7,1},{8,14},{9,15},{10,... | collective-permute-start | bytes 835592 | tf_op jit(solution)/shard_map/ppermute | solution.py:39
  30.4 26.6 %collective-permute-start.22 = (bf16[4,144,512]{2,1,0:T(8,128)(2,1)S(1)}, bf16[4,144,512]{2,1,0:T(8,128)(2,1)}, u32[]{:S(2)}, u32[]{:S(2)}) collective-permute-start(bf16[4,144,512]{2,1,0:T(8,128)(2,1)S(1)} %pad_maximum_fusion.1.refs_7_), channel_id=1, source_target_pairs={{0,4},{1,5},{2,6},{3,7},{4,0},{5,1},{6,2},{7,3},{8,12},{9,13},{10,... | collective-permute-start | bytes 1769480 | tf_op jit(solution)/shard_map/ppermute | solution.py:39
  31.5 26.0 %collective-permute-start.20 = (bf16[4,144,512]{2,1,0:T(8,128)(2,1)S(1)}, bf16[4,144,512]{2,1,0:T(8,128)(2,1)}, u32[]{:S(2)}, u32[]{:S(2)}) collective-permute-start(bf16[4,144,512]{2,1,0:T(8,128)(2,1)S(1)} %pad_maximum_fusion.1.refs_7_), channel_id=1, source_target_pairs={{0,2},{1,3},{2,0},{3,1},{4,6},{5,7},{6,4},{7,5},{8,10},{9,11},{10,... | collective-permute-start | bytes 1769480 | tf_op jit(solution)/shard_map/ppermute | solution.py:39
  32.1 23.4 %collective-permute-start.12 = (bf16[4,272,128]{2,1,0:T(8,128)(2,1)S(1)}, bf16[4,272,128]{2,1,0:T(8,128)(2,1)S(1)}, u32[]{:S(2)}, u32[]{:S(2)}) collective-permute-start(bf16[4,272,128]{2,1,0:T(8,128)(2,1)S(1)} %pad_maximum_fusion.3.refs_5_), channel_id=1, source_target_pairs={{0,4},{1,5},{2,6},{3,7},{4,0},{5,1},{6,2},{7,3},{8,12},{9,13},{10,... | collective-permute-start | bytes 835592 | tf_op jit(solution)/shard_map/ppermute | solution.py:39
  33.6 21.8 %collective-permute-start.10 = (bf16[4,272,128]{2,1,0:T(8,128)(2,1)S(1)}, bf16[4,272,128]{2,1,0:T(8,128)(2,1)S(1)}, u32[]{:S(2)}, u32[]{:S(2)}) collective-permute-start(bf16[4,272,128]{2,1,0:T(8,128)(2,1)S(1)} %pad_maximum_fusion.3.refs_5_), channel_id=1, source_target_pairs={{0,2},{1,3},{2,0},{3,1},{4,6},{5,7},{6,4},{7,5},{8,10},{9,11},{10,... | collective-permute-start | bytes 835592 | tf_op jit(solution)/shard_map/ppermute | solution.py:39
  39.6 16.3 %collective-permute-start.9 = (bf16[4,272,128]{2,1,0:T(8,128)(2,1)S(1)}, bf16[4,272,128]{2,1,0:T(8,128)(2,1)S(1)}, u32[]{:S(2)}, u32[]{:S(2)}) collective-permute-start(bf16[4,272,128]{2,1,0:T(8,128)(2,1)S(1)} %pad_maximum_fusion.3.refs_5_), channel_id=1, source_target_pairs={{0,1},{1,0},{2,3},{3,2},{4,5},{5,4},{6,7},{7,6},{8,9},{9,8},{10,11... | collective-permute-start | bytes 835592 | tf_op jit(solution)/shard_map/ppermute | solution.py:39
  65.4 24.9 %collective-permute-start.19 = (bf16[4,144,512]{2,1,0:T(8,128)(2,1)S(1)}, bf16[4,144,512]{2,1,0:T(8,128)(2,1)}, u32[]{:S(2)}, u32[]{:S(2)}) collective-permute-start(bf16[4,144,512]{2,1,0:T(8,128)(2,1)S(1)} %pad_maximum_fusion.1.refs_7_), channel_id=1, source_target_pairs={{0,1},{1,0},{2,3},{3,2},{4,5},{5,4},{6,7},{7,6},{8,9},{9,8},{10,11... | collective-permute-start | bytes 1769480 | tf_op jit(solution)/shard_map/ppermute | solution.py:39
  66.2 24.1 %collective-permute-start.23 = (bf16[4,144,512]{2,1,0:T(8,128)(2,1)}, bf16[4,144,512]{2,1,0:T(8,128)(2,1)}, u32[]{:S(2)}, u32[]{:S(2)}) collective-permute-start(bf16[4,144,512]{2,1,0:T(8,128)(2,1)} %collective-permute-done.22.refs_11_), channel_id=1, source_target_pairs={{0,1},{1,0},{2,3},{3,2},{4,5},{5,4},{6,7},{7,6},{8,9},{9,8},{10,11... | collective-permute-start | bytes 1769480 | tf_op jit(solution)/shard_map/ppermute | solution.py:39
  67.4 22.9 %collective-permute-start.21 = (bf16[4,144,512]{2,1,0:T(8,128)(2,1)}, bf16[4,144,512]{2,1,0:T(8,128)(2,1)}, u32[]{:S(2)}, u32[]{:S(2)}) collective-permute-start(bf16[4,144,512]{2,1,0:T(8,128)(2,1)} %collective-permute-done.20.refs_9_), channel_id=1, source_target_pairs={{0,1},{1,0},{2,3},{3,2},{4,5},{5,4},{6,7},{7,6},{8,9},{9,8},{10,11... | collective-permute-start | bytes 1769480 | tf_op jit(solution)/shard_map/ppermute | solution.py:39
  71.3 19.0 %collective-permute-start.27 = (bf16[2,144,512]{2,1,0:T(8,128)(2,1)}, bf16[2,144,512]{2,1,0:T(8,128)(2,1)S(1)}, u32[]{:S(2)}, u32[]{:S(2)}) collective-permute-start(bf16[2,144,512]{2,1,0:T(8,128)(2,1)} %collective-permute-done.26.refs_15_), channel_id=1, source_target_pairs={{0,1},{1,0},{2,3},{3,2},{4,5},{5,4},{6,7},{7,6},{8,9},{9,8},{10,11... | collective-permute-start | bytes 884744 | tf_op jit(solution)/shard_map/ppermute | solution.py:39
  72.7 17.6 %collective-permute-start.25 = (bf16[2,144,512]{2,1,0:T(8,128)(2,1)}, bf16[2,144,512]{2,1,0:T(8,128)(2,1)S(1)}, u32[]{:S(2)}, u32[]{:S(2)}) collective-permute-start(bf16[2,144,512]{2,1,0:T(8,128)(2,1)} %collective-permute-done.24.refs_13_), channel_id=1, source_target_pairs={{0,1},{1,0},{2,3},{3,2},{4,5},{5,4},{6,7},{7,6},{8,9},{9,8},{10,11... | collective-permute-start | bytes 884744 | tf_op jit(solution)/shard_map/ppermute | solution.py:39
  126.6 17.4 %collective-permute-start.34 = (bf16[4,4,272,128]{3,2,1,0:T(8,128)(2,1)}, bf16[4,4,272,128]{3,2,1,0:T(8,128)(2,1)S(1)}, u32[]{:S(2)}, u32[]{:S(2)}) collective-permute-start(bf16[4,4,272,128]{3,2,1,0:T(8,128)(2,1)} %get-tuple-element.55), channel_id=1, source_target_pairs={{0,1},{1,0},{2,3},{3,2},{4,5},{5,4},{6,7},{7,6},{8,9},{9,8},{10,11... | collective-permute-start | bytes 3342344 | tf_op jit(solution)/shard_map/ppermute | solution.py:39
  127.1 38.0 %collective-permute-start.41 = (bf16[4,4,144,512]{3,2,1,0:T(8,128)(2,1)}, bf16[4,4,144,512]{3,2,1,0:T(8,128)(2,1)}, u32[]{:S(2)}, u32[]{:S(2)}) collective-permute-start(bf16[4,4,144,512]{3,2,1,0:T(8,128)(2,1)} %get-tuple-element.57), channel_id=1, source_target_pairs={{0,1},{1,0},{2,3},{3,2},{4,5},{5,4},{6,7},{7,6},{8,9},{9,8},{10,11... | collective-permute-start | bytes 7077896 | tf_op jit(solution)/shard_map/ppermute | solution.py:39
  128.1 13.3 %collective-permute-start.28 = (bf16[2,128,512]{2,1,0:T(8,128)(2,1)S(1)}, bf16[2,128,512]{2,1,0:T(8,128)(2,1)S(1)}, u32[]{:S(2)}, u32[]{:S(2)}) collective-permute-start(bf16[2,128,512]{2,1,0:T(8,128)(2,1)S(1)} %get-tuple-element.42), channel_id=1, source_target_pairs={{0,2},{1,3},{2,0},{3,1},{4,6},{5,7},{6,4},{7,5},{8,10},{9,11},{10,... | collective-permute-start | bytes 786440 | tf_op jit(solution)/shard_map/ppermute | solution.py:39
  129.2 12.3 %collective-permute-start.33 = (bf16[1,128,512]{2,1,0:T(8,128)(2,1)}, bf16[1,128,512]{2,1,0:T(8,128)(2,1)}, u32[]{:S(2)}, u32[]{:S(2)}) collective-permute-start(bf16[1,128,512]{2,1,0:T(8,128)(2,1)} %get-tuple-element.52), channel_id=1, source_target_pairs={{0,1},{1,0},{2,3},{3,2},{4,5},{5,4},{6,7},{7,6},{8,9},{9,8},{10,11... | collective-permute-start | bytes 393224 | tf_op jit(solution)/shard_map/ppermute | solution.py:39
  145.4 14.1 %collective-permute-start.37 = (bf16[4,272,128]{2,1,0:T(8,128)(2,1)S(1)}, bf16[4,272,128]{2,1,0:T(8,128)(2,1)S(1)}, u32[]{:S(2)}, u32[]{:S(2)}) collective-permute-start(bf16[4,272,128]{2,1,0:T(8,128)(2,1)S(1)} %get-tuple-element.77), channel_id=1, source_target_pairs={{0,6},{1,7},{2,4},{3,5},{4,2},{5,3},{6,0},{7,1},{8,14},{9,15},{10,... | collective-permute-start | bytes 835592 | tf_op jit(solution)/shard_map/ppermute | solution.py:39
  147.0 13.9 %collective-permute-start.36 = (bf16[4,272,128]{2,1,0:T(8,128)(2,1)S(1)}, bf16[4,272,128]{2,1,0:T(8,128)(2,1)S(1)}, u32[]{:S(2)}, u32[]{:S(2)}) collective-permute-start(bf16[4,272,128]{2,1,0:T(8,128)(2,1)S(1)} %get-tuple-element.78), channel_id=1, source_target_pairs={{0,4},{1,5},{2,6},{3,7},{4,0},{5,1},{6,2},{7,3},{8,12},{9,13},{10,... | collective-permute-start | bytes 835592 | tf_op jit(solution)/shard_map/ppermute | solution.py:39
  167.7 12.4 %collective-permute-start.42 = (bf16[2,2,144,512]{3,2,1,0:T(8,128)(2,1)S(1)}, bf16[2,2,144,512]{3,2,1,0:T(8,128)(2,1)S(1)}, u32[]{:S(2)}, u32[]{:S(2)}) collective-permute-start(bf16[2,2,144,512]{3,2,1,0:T(8,128)(2,1)S(1)} %slice.160), channel_id=1, source_target_pairs={{0,2},{1,3},{2,0},{3,1},{4,6},{5,7},{6,4},{7,5},{8,10},{9,11},{10,... | collective-permute-start | bytes 1769480 | tf_op jit(solution)/shard_map/ppermute | solution.py:39
  171.6 14.9 %collective-permute-start.45 = (bf16[2,2,144,512]{3,2,1,0:T(8,128)(2,1)S(1)}, bf16[2,2,144,512]{3,2,1,0:T(8,128)(2,1)S(1)}, u32[]{:S(2)}, u32[]{:S(2)}) collective-permute-start(bf16[2,2,144,512]{3,2,1,0:T(8,128)(2,1)S(1)} %slice.133), channel_id=1, source_target_pairs={{0,4},{1,5},{2,6},{3,7},{4,0},{5,1},{6,2},{7,3},{8,12},{9,13},{10,... | collective-permute-start | bytes 1769480 | tf_op jit(solution)/shard_map/ppermute | solution.py:39
  (75 other events, 657.8 us)

commit v2 on v1

--- a/solution.py
+++ b/solution.py
@@ -43,23 +43,58 @@
     return pl.ds(pl.multiple_of(start, step), size)
 
 
-def fill_window(me_t, parts, out_ref):
+def fill_window(me_t, which, parts, out_ref, sems):
     own, rx, c1, c3 = parts
     n = own.shape[1]
-    out_ref[rows_at(me_t * n, n, n), :] = own[me_t]
-    out_ref[rows_at((me_t ^ 1) * n, n, n), :] = c1[0]
-    out_ref[rows_at((me_t ^ 2) * n, n, n), :] = rx[me_t & 1]
-    out_ref[rows_at((me_t ^ 3) * n, n, n), :] = c3[0]
+    sources = (own.at[me_t], c1.at[which], rx.at[which], c3.at[which])
+    copies = [pltpu.make_async_copy(src, out_ref.at[rows_at((me_t ^ r) * n, n, n), :], sems.at[r]) for r, src in enumerate(sources)]
+    for copy in copies:
+        copy.start()
+    return copies
+
+
+def prepare_kernel(scal, inputs, cot, attn, out, up, down, pos, norm, ga, gb, xs, c1, attn_s, out_s, up_s, down_s, pos_s, norm_s, sems):
+    me_t = scal[1]
+    moves = [(attn, attn_s), (pos, pos_s), (norm, norm_s), (up, up_s), (down, down_s), (out, out_s)]
+    for r, (rel, ref, at) in enumerate(((2, xs, 0), (3, xs, 2), (1, c1, 0))):
+        moves += [(inputs.at[me_t ^ rel], ref.at[at]), (cot.at[me_t ^ rel], ref.at[at + 1])]
+    copies = [pltpu.make_async_copy(src, dst, sems.at[i]) for i, (src, dst) in enumerate(moves)]
+    for copy in copies:
+        copy.start()
+    for copy in copies[:3]:
+        copy.wait()
+    per = attn.shape[1]
+    pos_per = pos.shape[0]
+    tiles = pos.shape[1] // LANES
+    for t in range(3):
+        ga[t * per : (t + 1) * per, :] = attn_s[t].astype(BF16)
+    for k in range(tiles):
+        at = 3 * per + k * pos_per
+        ga[at : at + pos_per, :] = pos_s[:, k * LANES : (k + 1) * LANES].astype(BF16)
+    at = 3 * per + tiles * pos_per
+    both = norm_s[...]
+    both = jnp.concatenate([both, both], axis=1)
+    both = jnp.concatenate([both, jnp.zeros_like(both)], axis=0)
+    high = both.astype(BF16)
+    low = (both - high.astype(F32)).astype(BF16)
+    ga[at : at + 16, :] = jnp.concatenate([high, low], axis=0)
+    for copy in copies[3:6]:
+        copy.wait()
+    gb[0:per, :] = up_s[...].astype(BF16)
+    gb[per : 2 * per, :] = down_s[...].astype(BF16)
+    gb[2 * per :, :] = out_s[...].astype(BF16)
+    for copy in copies[6:]:
+        copy.wait()
 
 
 def attention_kernel(places, n_pieces, scal, *refs):
-    own, rx, c1, c3, seg_row = refs[:5]
+    own, rx, c1, c3, segs = refs[:5]
     pieces = refs[5 : 5 + n_pieces]
-    hid_o, qkv_o, pt_o, mixt_o, w_o, nrm_o, x_s, pos_s, bias_s, nrm_s = refs[5 + n_pieces :]
+    hid_o, qkv_o, pt_o, mixt_o, w_o, nrm_o, x_s, pos_s, bias_s, nrm_s, sems = refs[5 + n_pieces :]
     me_dp, me_t = scal[0], scal[1]
     win, width = x_s.shape
     groups = w_o.shape[0]
-    fill_window(me_t, (own, rx, c1, c3), x_s)
+    filling = fill_window(me_t, 0, (own, rx, c1, c3), x_s, sems)
     if places is None:
         w_o[...] = pieces[0][...]
         pos_s[...] = pieces[1][...]
@@ -68,10 +103,10 @@
         n_dp = nrm_s.shape[0]
         per = width // n_dp
         pos_per = win // (n_dp * groups)
-        for ref, (xr, yr, z0, c) in zip(pieces, places, strict=True):
+        for ref, (xr, yr, zs, c) in zip(pieces, places, strict=True):
             tr = xr * 2 + c
-            for i in range(ref.shape[0]):
-                src = me_dp ^ ((z0 + i) * 2 + yr)
+            for i, zr in enumerate(zs):
+                src = me_dp ^ (zr * 2 + yr)
                 for t in range(3):
                     w_o[tr, rows_at(src * per, per, per), t * LANES : (t + 1) * LANES] = ref[i, t * per : (t + 1) * per]
                 where = (me_t ^ tr) * (win // groups) + src * pos_per
@@ -88,7 +123,7 @@
             both = jnp.where(low_lane, left[0:8] + left[8:16], right[0:8] + right[8:16])
             nrm_o[:, j * LANES : (j + 1) * LANES] = both
 
-    seg = seg_row[...].astype(F32)
+    seg = segs[pl.ds(me_t, 1), :].astype(F32)
     seg_col = jnp.transpose(jnp.broadcast_to(seg, (LANES, win)))
     for i in range(win // LANES):
         key_seg = seg_col[i * LANES : (i + 1) * LANES, 0:1]
@@ -97,6 +132,8 @@
         counts = (key_seg == seg) & (query_at >= key_at)
         bias_s[i * LANES : (i + 1) * LANES, :] = jnp.where(counts, 0.0, NEG_FILL)
 
+    for copy in filling:
+        copy.wait()
     hidden = x_s[...].astype(F32) + pos_s[...].astype(F32)
     hid_o[...] = hidden
     x_s[...] = hidden.astype(BF16)
@@ -144,6 +181,16 @@
 CHUNK = 64
 
 
+def chunk_of(refs, tr, r):
+    c, xr, yr, zr = tr & 1, tr >> 1, r & 1, r >> 1
+    half = refs[0].shape[0] // 4
+    if zr < half:
+        first, slot = xr == 1, yr * half + zr
+    else:
+        first, slot = yr == 1, 2 * half + xr * half + zr - half
+    return refs[2 * c + (0 if first else 1)], slot
+
+
 def ffn_kernel(places, n_pieces, scal, *refs):
     own, rx, c1, c3, hid, mixt, nrm = refs[:7]
     pieces = refs[7 : 7 + n_pieces]
@@ -153,26 +200,25 @@
         gup_o, gdown_o, gout_o = rest[6:9]
         rest = rest[9:]
     else:
-        keep_o, send_o = rest[6:8]
-        rest = rest[8:]
-    cot_s, out_s, up_s, down_s, a_s, b_s, xh1_s, r1_s, n1_s, sent_s, act_s, dg_s, low_s, xt_s = rest
+        chunks_o = rest[6:10]
+        rest = rest[10:]
+    cot_s, out_s, up_s, down_s, a_s, b_s, g_s, xh1_s, r1_s, n1_s, sent_s, act_s, dg_s, low_s, xt_s, sems = rest
     me_dp, me_t = scal[0], scal[1]
     win, width = hid.shape
     groups = up_s.shape[0]
-    fill_window(me_t, (own, rx, c1, c3), cot_s)
+    filling = fill_window(me_t, 1, (own, rx, c1, c3), cot_s, sems)
     if places is None:
-        up_s[...] = pieces[0][...]
-        down_s[...] = pieces[1][...]
-        out_s[...] = pieces[2][...]
         n_dp = 1
-    else:
-        n_dp = 2 * max(z0 + ref.shape[0] for ref, (_, _, z0, _) in zip(pieces, places, strict=True))
+        for src, dst in zip(pieces, (out_s, up_s, down_s), strict=True):
+            dst[...] = src[...]
+    else:
+        n_dp = 2 * sum(len(zs) for _, yr, zs, c in places if yr == 0 and c == 0) // 2
         per = width // n_dp
         out_per = LANES // n_dp
-        for ref, (xr, yr, z0, c) in zip(pieces, places, strict=True):
+        for ref, (xr, yr, zs, c) in zip(pieces, places, strict=True):
             tr = xr * 2 + c
-            for i in range(ref.shape[0]):
-                src = me_dp ^ ((z0 + i) * 2 + yr)
+            for i, zr in enumerate(zs):
+                src = me_dp ^ (zr * 2 + yr)
                 up_s[tr, rows_at(src * per, per, per), :] = ref[i, 0:per]
                 down_s[tr, rows_at(src * per, per, per), :] = ref[i, per : 2 * per]
                 out_s[rows_at(tr * LANES + src * out_per, out_per, out_per), :] = ref[i, 2 * per : 2 * per + out_per]
@@ -206,6 +252,9 @@
 
         chunks(gelu)
         n1_s[...] += mm(act_s[g], down_s[g])
+
+    for copy in filling:
+        copy.wait()
 
     def norm_two(i, sums):
         at = rows_at(i * CHUNK, CHUNK, CHUNK)
@@ -221,28 +270,28 @@
     gain_two, shift_two = lax.fori_loop(0, win // CHUNK, norm_two, (zero, zero))
     put_blocks(me_t, n1_s, res_k, res_1, res_x)
 
-    def put(c, xr, first, height, value):
-        ref = keep_o if c == 0 else send_o
-        each = value.shape[0] // n_dp
-        for d in range(n_dp):
-            rel = d ^ me_dp
-            ref[xr * 2 + (rel & 1), rel >> 1, first : first + height, :] = value[d * each : (d + 1) * each].astype(BF16)
+    def put(g, first, height, source, base):
+        for r in range(n_dp):
+            ref, slot = chunk_of(chunks_o, g, r)
+            ref[slot, first : first + height, :] = source[rows_at(base + (r ^ me_dp) * height, height, height), :].astype(BF16)
 
     xt_s[...] = jnp.transpose(sent_s[...])
-    for xr in range(groups // 2):
-        for c in range(2):
-            g = xr * 2 + c
-            gdown = mm(jnp.transpose(act_s[g]), low_s[...])
-            a_s[...] = mm(low_s[...], down_s[g], NT)
-            act_s[g] = (a_s[...] * dg_s[g]).astype(BF16)
-            gup = mm(xt_s[...], act_s[g])
-            if places is None:
-                gdown_o[g] = gdown.astype(BF16)
-                gup_o[g] = gup.astype(BF16)
-            else:
-                put(c, xr, 0, per, gup)
-                put(c, xr, per, per, gdown)
-            b_s[...] += mm(act_s[g], up_s[g], NT)
+    for g in range(groups):
+        gdown = mm(jnp.transpose(act_s[g]), low_s[...])
+        if places is None:
+            gdown_o[g] = gdown.astype(BF16)
+        else:
+            g_s[...] = gdown
+            put(g, per, per, g_s, 0)
+        a_s[...] = mm(low_s[...], down_s[g], NT)
+        act_s[g] = (a_s[...] * dg_s[g]).astype(BF16)
+        gup = mm(xt_s[...], act_s[g])
+        if places is None:
+            gup_o[g] = gup.astype(BF16)
+        else:
+            g_s[...] = gup
+            put(g, 0, per, g_s, 0)
+        b_s[...] += mm(act_s[g], up_s[g], NT)
 
     def norm_one_back(i, sums):
         at = rows_at(i * CHUNK, CHUNK, CHUNK)
@@ -262,10 +311,9 @@
     if places is None:
         gout_o[...] = gout.astype(BF16)
     else:
-        for xr in range(groups // 2):
-            for c in range(2):
-                g = xr * 2 + c
-                put(c, xr, 2 * per, out_per, gout[g * LANES : (g + 1) * LANES])
+        g_s[...] = gout
+        for g in range(groups):
+            put(g, 2 * per, out_per, g_s, g * LANES)
     gm = mm(low_s[...], out_s[...], NT).astype(BF16)
     for g in range(groups):
         gm_o[g] = gm[:, g * LANES : (g + 1) * LANES]
@@ -277,7 +325,7 @@
         keep_o, send_o = rest[3:5]
     else:
         gattn_o, gpos_o = rest[3:5]
-    ht_s, ds_s, dqkv_s, acc_s, dqt_s = rest[5:]
+    ht_s, ds_s, dqkv_s, acc_s, dqt_s, g_s = rest[5:]
     me_dp, me_t = scal[0], scal[1]
     win, width = hid.shape
     groups = w.shape[0]
@@ -329,83 +377,121 @@
     n_dp = 2 * keep_o.shape[1]
     per = width // n_dp
     pos_per = win // (n_dp * groups)
-    for xr in range(groups // 2):
-        for c in range(2):
-            g = xr * 2 + c
-            ref = keep_o if c == 0 else send_o
-            grad = mm(ht_s[...], dqkv_s[g])
-            for d in range(n_dp):
-                rel = d ^ me_dp
-                a, b = xr * 2 + (rel & 1), rel >> 1
-                for t in range(3):
-                    ref[a, b, t * per : (t + 1) * per, :] = grad[d * per : (d + 1) * per, t * LANES : (t + 1) * LANES].astype(BF16)
-                where = (me_t ^ g) * (win // groups) + d * pos_per
-                for k in range(width // LANES):
-                    at = 3 * per + k * pos_per
-                    ref[a, b, at : at + pos_per, :] = acc_s[rows_at(where, pos_per, pos_per), k * LANES : (k + 1) * LANES].astype(BF16)
-                at = 3 * per + width // LANES * pos_per
-                pair = d // 2 * LANES
-                tile = gnorm[0:8, pair : pair + LANES]
-                ref[a, b, at : at + 16, :] = jnp.concatenate([tile, tile], axis=0).astype(BF16)
-
-
-def to_windows(value, me_t):
-    x, c = me_t >> 1, me_t & 1
-    rx = swap(lax.dynamic_slice_in_dim(value, 2 * (1 - x), 2, 0), 0, 2)
-    c1 = swap(lax.dynamic_slice_in_dim(value, me_t ^ 1, 1, 0), 0, 1)
-    c3 = swap(lax.dynamic_slice_in_dim(rx, 1 - c, 1, 0), 0, 1)
-    return value, rx, c1, c3
-
-
-def from_windows(keep, s1, sx, me_t):
-    rx = swap(sx, 0, 2)
-    r1 = swap(s1, 0, 1)[0]
-    r3 = swap(rx[1:2], 0, 1)[0]
+    for g in range(groups):
+        g_s[...] = mm(ht_s[...], dqkv_s[g])
+        for r in range(n_dp):
+            d = r ^ me_dp
+            ref, slot = (send_o if g & 1 else keep_o), ((g >> 1) * 2 + (r & 1), r >> 1)
+            for t in range(3):
+                ref[*slot, t * per : (t + 1) * per, :] = g_s[rows_at(d * per, per, per), t * LANES : (t + 1) * LANES].astype(BF16)
+            where = (me_t ^ g) * (win // groups) + d * pos_per
+            for k in range(width // LANES):
+                at = 3 * per + k * pos_per
+                ref[*slot, at : at + pos_per, :] = acc_s[rows_at(where, pos_per, pos_per), k * LANES : (k + 1) * LANES].astype(BF16)
+            at = 3 * per + width // LANES * pos_per
+            tile = gnorm[0:8, rows_at((d >> 1) * LANES, LANES, LANES)]
+            ref[*slot, at : at + 16, :] = jnp.concatenate([tile, tile], axis=0).astype(BF16)
+
+
+def after(value, *others):
+    return lax.optimization_barrier((value, *others))[0]
+
+
+def in_order(keep, r1, r2, r3, me_t):
     flip = (me_t & 1) == 1
     low = [jnp.where(flip, r1, keep), jnp.where(flip, keep, r1)]
-    high = [jnp.where(flip, r3, rx[0]), jnp.where(flip, rx[0], r3)]
+    high = [jnp.where(flip, r3, r2), jnp.where(flip, r2, r3)]
     cross = (me_t >> 1) == 1
     return jnp.stack([jnp.where(cross, high[0], low[0]), jnp.where(cross, high[1], low[1]), jnp.where(cross, low[0], high[0]), jnp.where(cross, low[1], high[1])])
 
 
-def gather(value, direct):
+def gather_z(value, *others):
     nz = lax.axis_size("dp") // 2
-    q = jnp.stack([value] + [swap(value, 2 * k, 0) for k in range(1, nz)])
-    qx, qy = swap(q, 0, 2), swap(q, 1, 0)
-    found = [(q, (0, 0, 0)), (qx, (1, 0, 0)), (qy, (0, 1, 0))]
-    if direct:
-        found.append((swap(q, 1, 2), (1, 1, 0)))
-    else:
-        half = nz // 2
-        found.append((swap(qx[:half], 1, 0), (1, 1, 0)))
-        found.append((swap(qy[half:], 0, 2), (1, 1, half)))
+    q, order = value[None], [0]
+    step = nz // 2
+    while step:
+        if step == 1:
+            q = after(q, *others)
+        q = jnp.concatenate([q, swap(q, step * 2, 0)])
+        order = order + [z ^ step for z in order]
+        step //= 2
+    return q, tuple(order)
+
+
+def both_cores(found):
     out = []
     for array, place in found:
         out.append((array, (*place, 0)))
         out.append((swap(array, 0, 1), (*place, 1)))
-    return out
-
-
-def add(a, b):
-    return (a.astype(F32) + b.astype(F32)).astype(BF16)
-
-
-def scatter_sum(keep, send, direct):
-    total = add(keep, swap(send, 0, 1))
-    nz = total.shape[1]
-    if direct:
-        parts = [total[0], swap(total[2], 0, 2), swap(total[1], 1, 0), swap(total[3], 1, 2)]
-        total = sum(p.astype(F32) for p in parts).astype(BF16)
-    else:
-        half = nz // 2
-        a, b = total[:, :half], total[:, half:]
-        a = add(a[:2], swap(a[2:], 0, 2))
-        b = add(b[0::2], swap(b[1::2], 1, 0))
-        a = add(a[0], swap(a[1], 1, 0))
-        b = add(b[0], swap(b[1], 0, 2))
-        total = jnp.concatenate([a, b])
-    arrived = [total[0]] + [swap(total[k], 2 * k, 0) for k in range(1, nz)]
-    return sum(p.astype(F32) for p in arrived)
+    return [f[0] for f in out], tuple(f[1] for f in out)
+
+
+def total(*parts):
+    return sum(p.astype(F32) for p in parts)
+
+
+def low(*parts):
+    return total(*parts).astype(BF16)
+
+
+class Reduction:
+    def __init__(self, keep_first, keep_rest, send_first, send_rest):
+        self.half = keep_first.shape[0] // 4
+        self.n = keep_first.shape[0] // 2
+        self.sums = [(keep_rest,)]
+        self.send_rest = send_rest
+        got = swap(send_first, 0, 1)
+        self.a = low(keep_first[: self.n], got[: self.n])
+        self.b = low(keep_first[self.n :], got[self.n :])
+
+    def terms(self, a, start, stop):
+        at = 0 if a else self.n
+        found = [k[at + start : at + stop] for k in self.rest]
+        for pair in self.got:
+            g = pair[0 if a else 1]
+            if g.shape[0] >= stop:
+                found.append(g[start:stop])
+        return found
+
+    def first(self):
+        self.rest = [self.sums[0][0], swap(self.send_rest, 0, 1)]
+        self.got = [(swap(self.a, 0, 2), swap(self.b, 1, 0))]
+        return self.got[0]
+
+    def second(self):
+        h = self.half
+        a, b = low(*self.terms(True, h, 2 * h)), low(*self.terms(False, h, 2 * h))
+        self.got.append((swap(a, 1, 0), swap(b, 0, 2)))
+        return self.got[1]
+
+    def over_z(self, *others):
+        h = self.half
+        arrived = []
+        for z in range(1, 2 * h):
+            chunk = low(*self.terms(z < h, z % h, z % h + 1))
+            arrived.append(swap(after(chunk, *others), 2 * z, 0))
+        return arrived
+
+    def result(self, arrived):
+        return total(*self.terms(True, 0, 1), *arrived)[0]
+
+
+class DirectReduction:
+    def __init__(self, keep, send):
+        got = swap(send, 0, 1)
+        self.sums = [low(k, got[i]) for i, k in enumerate(keep)]
+
+    def over_xy(self):
+        s = self.sums
+        self.parts = [s[0], swap(s[2], 0, 2), swap(s[1], 1, 0), swap(s[3], 1, 2)]
+        return self.parts[1:]
+
+    def over_z(self, *others):
+        nz = self.parts[0].shape[0]
+        return [swap(after(low(*[p[z] for p in self.parts]), *others), 2 * z, 0) for z in range(1, nz)]
+
+    def result(self, arrived):
+        return total(*[p[0] for p in self.parts], *arrived)
 
 
 def adam_step(weight, gradient, moment_one, second, step_rate, decay_rate):
@@ -417,14 +503,15 @@
     return (weight_new, first_new, second_new)
 
 
-def call(kernel, outs, scratch, args, mib, flops):
+def call(kernel, outs, scratch, args, spaces, mib, flops):
     vmem = pl.BlockSpec(memory_space=pltpu.VMEM)
+    kinds = {"s": pl.BlockSpec(memory_space=pltpu.SMEM), "v": vmem, "a": pl.BlockSpec(memory_space=pl.ANY), "h": pl.BlockSpec(memory_space=pltpu.HBM)}
     return pl.pallas_call(
         kernel,
         out_shape=outs,
-        in_specs=[pl.BlockSpec(memory_space=pltpu.SMEM)] + [vmem] * (len(args) - 1),
+        in_specs=[kinds[k] for k in spaces],
         out_specs=[vmem] * len(outs),
-        scratch_shapes=[pltpu.VMEM(s, t) for s, t in scratch],
+        scratch_shapes=[pltpu.VMEM(*s) if isinstance(s, tuple) else pltpu.SemaphoreType.DMA(tuple(s)) for s in scratch],
         compiler_params=pltpu.CompilerParams(vmem_limit_bytes=mib * 1024 * 1024),
         cost_estimate=pl.CostEstimate(flops=flops, bytes_accessed=0, transcendentals=0),
     )(*args)
@@ -464,27 +551,32 @@
     fast = out_per % 16 == 0 and pos_per % 16 == 0 and 2 * per == LANES
     sds = jax.ShapeDtypeStruct
 
-    seg_row = lax.dynamic_slice_in_dim(segment_ids, me_t, 1, 0)
     if fast:
-        norm_tile = jnp.concatenate([norm_params, norm_params], axis=1)
-        norm_high = norm_tile.astype(BF16)
-        norm_low = (norm_tile - norm_high.astype(F32)).astype(BF16)
-        none = jnp.zeros_like(norm_high)
-        ga = jnp.concatenate(
-            [
-                attn_proj.astype(BF16).reshape(3 * per, group),
-                pos_table.astype(BF16).reshape(pos_per, width // LANES, LANES).transpose(1, 0, 2).reshape(-1, LANES),
-                jnp.concatenate([norm_high, none, norm_low, none]),
-            ]
+        ga, gb, xs, c1 = call(
+            prepare_kernel,
+            [sds((3 * per + width // LANES * pos_per + 16, LANES), BF16), sds((2 * per + out_per, width), BF16), sds((4, block, width), BF16), sds((2, block, width), BF16)],
+            [(v.shape, F32) for v in (attn_proj, out_proj, up_proj, down_proj, pos_table, norm_params)] + [[12]],
+            [scal, inputs, cotangent, attn_proj, out_proj, up_proj, down_proj, pos_table, norm_params],
+            "s" + "h" * 8,
+            60,
+            1_000_000,
         )
-        gb = jnp.concatenate([up_proj.astype(BF16), down_proj.astype(BF16), out_proj.astype(BF16)])
-        found_a = gather(ga, True)
-        x_parts = to_windows(inputs, me_t)
-        found_b = gather(gb, False)
-        a_args, a_places = [f[0] for f in found_a], tuple(f[1] for f in found_a)
-        b_args, b_places = [f[0] for f in found_b], tuple(f[1] for f in found_b)
-    else:
-        x_parts = to_windows(inputs, me_t)
+        qa, za = gather_z(ga)
+        rx = swap(xs, 0, 2)
+        qb, zb = gather_z(gb, qa, rx)
+        c1 = swap(c1, 0, 1)
+        c3 = swap(rx[2:], 0, 1)
+        found_a = [(qa, (0, 0, za)), (swap(qa, 0, 2), (1, 0, za)), (swap(qa, 1, 0), (0, 1, za)), (after(swap(qa, 1, 2), qb), (1, 1, za))]
+        a_args, a_places = both_cores(found_a)
+        qbx, qby, qbxy = swap(qb, 0, 2), swap(qb, 1, 0), swap(qb, 1, 2)
+    else:
+
+        def pair(rel):
+            return jnp.concatenate([lax.dynamic_slice_in_dim(v, me_t ^ rel, 1, 0) for v in (inputs, cotangent)])
+
+        rx = swap(jnp.concatenate([pair(2), pair(3)]), 0, 2)
+        c1 = swap(pair(1), 0, 1)
+        c3 = swap(rx[2:], 0, 1)
         relative = me_t ^ jnp.arange(n_t)
         whole = [lax.all_gather(lax.all_gather(v.astype(BF16), "dp"), "tensor") for v in (attn_proj, out_proj, up_proj, down_proj)]
         attn_w, out_w, up_w, down_w = [jnp.take(v, relative, axis=0) for v in whole]
@@ -493,7 +585,7 @@
         norm_w = lax.all_gather(norm_params, "dp", axis=1, tiled=True)
         norm_w = jnp.concatenate([norm_w, jnp.zeros_like(norm_w)])
         a_args, a_places = [attn_w, pos_w, norm_w], None
-        b_args, b_places = [up_w.reshape(n_t, width, inner), down_w.reshape(n_t, inner, width), out_w.reshape(n_t * group, width)], None
+        b_args, b_places = [out_w.reshape(n_t * group, width), up_w.reshape(n_t, width, inner), down_w.reshape(n_t, inner, width)], None
 
     hid, qkv, pt, mixt, attn_all, norm_all = call(
         functools.partial(attention_kernel, a_places, len(a_args)),
@@ -505,17 +597,20 @@
             sds((n_t, width, 3 * group), BF16),
             sds((8, width), F32),
         ],
-        [((win, width), BF16), ((win, width), BF16), ((win, win), F32), ((n_dp, 16, LANES), F32)],
-        [scal, *x_parts, seg_row, *a_args],
-        32,
-        2 * win * width * 3 * width,
+        [((win, width), BF16), ((win, width), BF16), ((win, win), F32), ((n_dp, 16, LANES), F32), [4]],
+        [scal, inputs, rx, c1, c3, segment_ids, *a_args],
+        "shaaav" + "v" * len(a_args),
+        12,
+        1_000_000,
     )
-    cot_parts = to_windows(cotangent, me_t)
+    if fast:
+        qbxy = after(qbxy, hid)
+        b_args, b_places = both_cores([(qb, (0, 0, zb)), (qbx, (1, 0, zb)), (qby, (0, 1, zb)), (qbxy, (1, 1, zb))])
 
     blocks = [sds((block, width), BF16), sds((1, block, width), BF16), sds((2, block, width), BF16)]
     if fast:
         rows_b = 2 * per + out_per
-        grads_b = [sds((4, n_dp // 2, rows_b, width), BF16)] * 2
+        grads_b = [sds((n_dp, rows_b, width), BF16)] * 4
     else:
         grads_b = [sds((n_t, width, inner), BF16), sds((n_t, inner, width), BF16), sds((n_t * group, width), BF16)]
     res_k, res_1, res_x, gone, gm, gnorm, *got_b = call(
@@ -529,6 +624,7 @@
             ((win, width), F32),
             ((win, width), F32),
             ((win, width), F32),
+            ((win, width), F32),
             ((win, LANES), F32),
             ((win, width), F32),
             ((win, width), BF16),
@@ -536,14 +632,17 @@
             ((n_t, win, inner), F32),
             ((win, width), BF16),
             ((width, win), BF16),
+            [4],
         ],
-        [scal, *cot_parts, hid, mixt, norm_all, *b_args],
-        50,
-        12 * win * width * n_t * inner,
+        [scal, cotangent, rx, c1, c3, hid, mixt, norm_all, *b_args],
+        "shaaavvv" + "v" * len(b_args),
+        24,
+        1_000_000,
     )
     if fast:
-        sum_b = scatter_sum(*got_b, False)
-    outputs = from_windows(res_k, res_1, res_x, me_t)
+        red_b = Reduction(*got_b)
+        gone = after(gone, red_b.a, red_b.b)
+        first_b = red_b.first()
 
     blocks = [sds((block, width), F32), *blocks[1:]]
     if fast:
@@ -560,16 +659,31 @@
             ((n_t, win, 3 * group), BF16),
             ((win, width), F32),
             ((LANES, win), F32),
+            ((width, 3 * group), F32),
         ],
         [scal, hid, qkv, pt, gm, attn_all, gone, gnorm],
-        40,
-        4 * win * width * 3 * width,
+        "s" + "v" * 7,
+        14,
+        1_000_000,
     )
-    gi_1, gi_x = gi_1.astype(F32), gi_x
-    grad_input = from_windows(gi_k.astype(F32), gi_1.astype(BF16), gi_x, me_t)
-
+    leaving = jnp.concatenate([res_x[:1], gi_x[:1], res_x[1:], gi_x[1:]])
     if fast:
-        sum_a = scatter_sum(*got_a, True)
+        red_a = DirectReduction(got_a[0], after(got_a[1], *first_b))
+        red_b.second()
+        xy_a = red_a.over_xy()
+        z_b = red_b.over_z()
+        z_a = red_a.over_z(*z_b)
+        leaving = after(leaving, *xy_a)
+        r2 = swap(leaving, 0, 2)
+        sum_b = red_b.result(z_b)
+        sum_a = red_a.result(z_a)
+    else:
+        r2 = swap(leaving, 0, 2)
+    r3 = swap(r2[2:], 0, 1)
+    outputs = in_order(res_k, swap(res_1, 0, 1)[0], r2[0], r3[0], me_t)
+    grad_input = in_order(gi_k, swap(gi_1, 0, 1)[0].astype(F32), r2[1].astype(F32), r3[1].astype(F32), me_t)
+
+    if fast:
         g_attn = sum_a[: 3 * per].reshape(3, per, group)
         at = 3 * per
         n_pos = width // LANES * pos_per

time: 205 us -> 166 us (0.81)
  waiting for transfers between devices: 80.9 us -> 62.1 us
  local copies, waits for them, and re-layouts: 21.9 us -> 8.95 us
  starting transfers between devices: 39.9 us -> 35.2 us
  other arithmetic: 16.4 us -> 14.3 us
    ppermute x49 -> x41, waiting for transfers between devices: 80.9 us -> 62.1 us  [swap(): lax.ppermute(value, AXES, [(i, i ^ mask) for i in range(lax.axis_size('dp...]
    unnamed x100 -> x67, local copies, waits for them, and re-layouts: 16.1 us -> 8.84 us
    ppermute x49 -> x41, starting transfers between devices: 39.9 us -> 35.2 us  [swap(): lax.ppermute(value, AXES, [(i, i ^ mask) for i in range(lax.axis_size('dp...]
    convert_element_type x13 -> x4, other arithmetic: 8.52 us -> 4.69 us  [low(): return total(*parts).astype(BF16)]
    slice x7 -> x4, local copies, waits for them, and re-layouts: 3.56 us -> 0.07 us  [the longest x2 0.04 us: body(): leaving = jnp.concatenate([res_x[:1], gi_x[:1], res_x[1:], gi_x[1:]])]
    pallas_call x3 -> x4, Pallas kernels: 44 us -> 43.7 us  [call(): pl.pallas_call(kernel, out_shape=outs, in_specs=[kinds[k] for k in spaces...]
  transfers between devices with their start and end apart: 49 -> 41, of which waited for: 17 -> 21; matrix products, arithmetic and copies ran while one was open for 8% -> 8% of each run, Pallas kernels for 4% -> 12%
where the time goes in v2:
time: 166 us
  waiting for transfers between devices  62.1 us (37%)
  Pallas kernels  43.7 us (26%)
  starting transfers between devices  35.2 us (21%)
  other arithmetic  14.3 us (9%)
  local copies, waits for them, and re-layouts  8.95 us (5%)
    ppermute x41, waiting for transfers between devices, swap(): lax.ppermute(value, AXES, [(i, i ^ mask) for i in range(lax.axis_size('dp...  62.1 us
    pallas_call x4, Pallas kernels, call(): pl.pallas_call(kernel, out_shape=outs, in_specs=[kinds[k] for k in spaces...  43.7 us
    ppermute x41, starting transfers between devices, swap(): lax.ppermute(value, AXES, [(i, i ^ mask) for i in range(lax.axis_size('dp...  35.2 us
    unnamed x67, local copies, waits for them, and re-layouts  8.84 us
    convert_element_type x4, other arithmetic, low(): return total(*parts).astype(BF16)  4.69 us
    sub x5, other arithmetic, adam_step(): weight - step_rate * (fixed_first / (jnp.sqrt(fixed_second) + ADAM_EPS) +...  3.74 us
  transfers between devices with their start and end apart: 41, of which 21 were waited for; matrix products, arithmetic and copies ran while one was open for 8% of the time, Pallas kernels for 12%

profile of v2, /device:TPU:0, one launch (start us, length us, event | category | flops | bytes accessed | tf_op | source)
XLA Modules:
  0.0 165.6 jit_solution(6811364242327095607)
XLA Ops:
  1.2 3.1 %shard_map.356 = (bf16[272,128]{1,0:T(8,128)(2,1)}, bf16[144,512]{1,0:T(8,128)(2,1)}, bf16[4,128,512]{2,1,0:T(8,128)(2,1)}, bf16[2,128,512]{2,1,0:T(8,128)(2,1)}) custom-call(s32[2]{0:T(128)} %pad_add_fusion.scal, bf16[4,128,512]{2,1,0:T(8,128)(2,1)} %refs_0_.2, bf16[4,128,512]{2,1,0:T(8,128)(2,1)} %refs_0_.3, f32[3,64,128]{2,1,0:T(8,128)} %attn.1, ...), custom_call_target="tpu_custom_call" | custom-call | flops 1000000 | tf_op jit(solution)/shard_map/pallas_call | solution.py:509
  4.3 3.0 %collective-permute-start = (bf16[4,128,512]{2,1,0:T(8,128)(2,1)}, bf16[4,128,512]{2,1,0:T(8,128)(2,1)S(1)}, u32[]{:S(2)}, u32[]{:S(2)}) collective-permute-start(bf16[4,128,512]{2,1,0:T(8,128)(2,1)} %get-tuple-element.54), channel_id=1, source_target_pairs={{0,2},{1,3},{2,0},{3,1},{4,6},{5,7},{6,4},{7,5},{8,10},{9,11},{10,... | collective-permute-start | bytes 1572872 | tf_op jit(solution)/shard_map/ppermute | solution.py:39
  7.3 2.6 %collective-permute-start.3 = (bf16[1,272,128]{2,1,0:T(8,128)(2,1)}, bf16[1,272,128]{2,1,0:T(8,128)(2,1)S(1)}, u32[]{:S(2)}, u32[]{:S(2)}) collective-permute-start(bf16[1,272,128]{2,1,0:T(8,128)(2,1)} %bitcast.143), channel_id=1, source_target_pairs={{0,16},{1,17},{2,18},{3,19},{4,20},{5,21},{6,22},{7,23},{8,24},{9,... | collective-permute-start | bytes 208904 | tf_op jit(solution)/shard_map/ppermute | solution.py:39
  10.3 7.0 %collective-permute-done.3 = bf16[1,272,128]{2,1,0:T(8,128)(2,1)S(1)} collective-permute-done((bf16[1,272,128]{2,1,0:T(8,128)(2,1)}, bf16[1,272,128]{2,1,0:T(8,128)(2,1)S(1)}, u32[]{:S(2)}, u32[]{:S(2)}) %collective-permute-start.3) | collective-permute-done | bytes 69664 | tf_op jit(solution)/shard_map/ppermute | solution.py:39
  21.2 2.0 %collective-permute-done.4 = bf16[2,272,128]{2,1,0:T(8,128)(2,1)S(1)} collective-permute-done((bf16[2,272,128]{2,1,0:T(8,128)(2,1)S(1)}, bf16[2,272,128]{2,1,0:T(8,128)(2,1)S(1)}, u32[]{:S(2)}, u32[]{:S(2)}) %collective-permute-start.4) | collective-permute-done | bytes 139296 | tf_op jit(solution)/shard_map/ppermute | solution.py:39
  27.7 2.8 %collective-permute-done.12 = bf16[2,144,512]{2,1,0:T(8,128)(2,1)S(1)} collective-permute-done((bf16[2,144,512]{2,1,0:T(8,128)(2,1)S(1)}, bf16[2,144,512]{2,1,0:T(8,128)(2,1)S(1)}, u32[]{:S(2)}, u32[]{:S(2)}) %collective-permute-start.12) | collective-permute-done | bytes 294944 | tf_op jit(solution)/shard_map/ppermute | solution.py:39
  32.1 2.6 %collective-permute-done.10.refs_11_ = bf16[4,272,128]{2,1,0:T(8,128)(2,1)S(1)} collective-permute-done((bf16[4,272,128]{2,1,0:T(8,128)(2,1)S(1)}, bf16[4,272,128]{2,1,0:T(8,128)(2,1)S(1)}, u32[]{:S(2)}, u32[]{:S(2)}) %collective-permute-start.10) | collective-permute-done | bytes 278560 | tf_op jit(solution)/shard_map/ppermute | solution.py:39
  35.2 5.5 %collective-permute-done.6.refs_7_ = bf16[4,272,128]{2,1,0:T(8,128)(2,1)S(1)} collective-permute-done((bf16[4,272,128]{2,1,0:T(8,128)(2,1)S(1)}, bf16[4,272,128]{2,1,0:T(8,128)(2,1)S(1)}, u32[]{:S(2)}, u32[]{:S(2)}) %collective-permute-start.6) | collective-permute-done | bytes 278560 | tf_op jit(solution)/shard_map/ppermute | solution.py:39
  41.2 8.1 %collective-permute-done.8.refs_9_ = bf16[4,272,128]{2,1,0:T(8,128)(2,1)S(1)} collective-permute-done((bf16[4,272,128]{2,1,0:T(8,128)(2,1)S(1)}, bf16[4,272,128]{2,1,0:T(8,128)(2,1)S(1)}, u32[]{:S(2)}, u32[]{:S(2)}) %collective-permute-start.8) | collective-permute-done | bytes 278560 | tf_op jit(solution)/shard_map/ppermute | solution.py:39
  53.0 9.4 %shard_map.357 = (f32[512,512]{1,0:T(8,128)S(1)}, bf16[4,512,384]{2,1,0:T(8,128)(2,1)S(1)}, bf16[8,512,512]{2,1,0:T(8,128)(2,1)S(1)}, bf16[512,512]{1,0:T(8,128)...) custom-call(s32[2]{0:T(128)S(1)} %copy-done.11, bf16[4,128,512]{2,1,0:T(8,128)(2,1)S(1)} %copy-done.3, ...), custom_call_target="tpu_custom_call" | custom-call | flops 1000000 | tf_op jit(solution)/shard_map/pallas_call | solution.py:509
  62.5 2.0 %copy-done = bf16[8,512,512]{2,1,0:T(8,128)(2,1)} copy-done((bf16[8,512,512]{2,1,0:T(8,128)(2,1)}, bf16[8,512,512]{2,1,0:T(8,128)(2,1)S(1)}, u32[]{:S(2)}) %copy-start) | copy-done | bytes 4194328
  69.3 20.2 %shard_map.358 = (bf16[128,512]{1,0:T(8,128)(2,1)S(1)}, bf16[1,128,512]{2,1,0:T(8,128)(2,1)S(1)}, bf16[2,128,512]{2,1,0:T(8,128)(2,1)S(1)}, f32[512,512]{1,0:T(8...) custom-call(s32[2]{0:T(128)S(1)} %copy-done.11, ...), custom_call_target="tpu_custom_call" | custom-call | flops 1000000 | tf_op jit(solution)/shard_map/pallas_call | solution.py:509
  90.2 2.3 %collective-permute-done.21 = bf16[8,144,512]{2,1,0:T(8,128)(2,1)S(1)} collective-permute-done((bf16[8,144,512]{2,1,0:T(8,128)(2,1)S(1)}, bf16[8,144,512]{2,1,0:T(8,128)(2,1)S(1)}, u32[]{:S(2)}, u32[]{:S(2)}) %collective-permute-start.21) | collective-permute-done | bytes 1179680 | tf_op jit(solution)/shard_map/ppermute | solution.py:39
  94.5 2.2 %copy-done.1 = bf16[8,512,512]{2,1,0:T(8,128)(2,1)S(1)} copy-done((bf16[8,512,512]{2,1,0:T(8,128)(2,1)S(1)}, bf16[8,512,512]{2,1,0:T(8,128)(2,1)}, u32[]{:S(2)}) %copy-start.1) | copy-done | bytes 4194328
  100.0 11.1 %shard_map.359 = (f32[128,512]{1,0:T(8,128)S(1)}, bf16[1,128,512]{2,1,0:T(8,128)(2,1)S(1)}, bf16[2,128,512]{2,1,0:T(8,128)(2,1)S(1)}, bf16[4,4,272,128]{3,2,1,0:T(8,128)(2,1)S(1)}, bf16[4,4,272,128]{3,2,1,0:T(8,128)(2,1)S(1)}) custom-call(s32[2]{0:T(128)S(1)} %copy-done.12, f32[512,512]{1,0:T(8,128)S(1)} %get-tuple-element.60.refs_4_.hid, ...), custom_call_target="tpu_custom_call" | custom-call | flops 1000000 | tf_op jit(solution)/shard_map/pallas_call | solution.py:509
  112.8 2.0 %collective-permute-start.33 = (bf16[2,144,512]{2,1,0:T(8,128)(2,1)S(1)}, bf16[2,144,512]{2,1,0:T(8,128)(2,1)S(1)}, u32[]{:S(2)}, u32[]{:S(2)}) collective-permute-start(bf16[2,144,512]{2,1,0:T(8,128)(2,1)S(1)} %get-tuple-element.110), channel_id=1, source_target_pairs={{0,4},{1,5},{2,6},{3,7},{4,0},{5,1},{6,2},{7,3},{8,12},{9,13},{10,... | collective-permute-start | bytes 884744 | tf_op jit(solution)/shard_map/ppermute | solution.py:39
  114.8 1.9 %collective-permute-start.35 = (bf16[2,144,512]{2,1,0:T(8,128)(2,1)S(1)}, bf16[2,144,512]{2,1,0:T(8,128)(2,1)S(1)}, u32[]{:S(2)}, u32[]{:S(2)}) collective-permute-start(bf16[2,144,512]{2,1,0:T(8,128)(2,1)S(1)} %get-tuple-element.109), channel_id=1, source_target_pairs={{0,2},{1,3},{2,0},{3,1},{4,6},{5,7},{6,4},{7,5},{8,10},{9,11},{10,... | collective-permute-start | bytes 884744 | tf_op jit(solution)/shard_map/ppermute | solution.py:39
  116.9 5.2 %collective-permute-done.33 = bf16[2,144,512]{2,1,0:T(8,128)(2,1)S(1)} collective-permute-done((bf16[2,144,512]{2,1,0:T(8,128)(2,1)S(1)}, bf16[2,144,512]{2,1,0:T(8,128)(2,1)S(1)}, u32[]{:S(2)}, u32[]{:S(2)}) %collective-permute-start.33) | collective-permute-done | bytes 294944 | tf_op jit(solution)/shard_map/ppermute | solution.py:39
  125.2 1.9 %collective-permute-start.34 = (bf16[1,144,512]{2,1,0:T(8,128)(2,1)S(1)}, bf16[1,144,512]{2,1,0:T(8,128)(2,1)S(1)}, u32[]{:S(2)}, u32[]{:S(2)}) collective-permute-start(bf16[1,144,512]{2,1,0:T(8,128)(2,1)S(1)} %get-tuple-element.108), channel_id=1, source_target_pairs={{0,8},{1,9},{2,10},{3,11},{4,12},{5,13},{6,14},{7,15},{8,0},{9,1},... | collective-permute-start | bytes 442376 | tf_op jit(solution)/shard_map/ppermute | solution.py:39
  132.5 8.1 %collective-permute-done.36 = bf16[1,144,512]{2,1,0:T(8,128)(2,1)S(1)} collective-permute-done((bf16[1,144,512]{2,1,0:T(8,128)(2,1)S(1)}, bf16[1,144,512]{2,1,0:T(8,128)(2,1)S(1)}, u32[]{:S(2)}, u32[]{:S(2)}) %collective-permute-start.36) | collective-permute-done | bytes 147488 | tf_op jit(solution)/shard_map/ppermute | solution.py:39
  144.4 3.6 %collective-permute-done.27 = bf16[4,272,128]{2,1,0:T(8,128)(2,1)S(1)} collective-permute-done((bf16[4,272,128]{2,1,0:T(8,128)(2,1)S(1)}, bf16[4,272,128]{2,1,0:T(8,128)(2,1)S(1)}, u32[]{:S(2)}, u32[]{:S(2)}) %collective-permute-start.27) | collective-permute-done | bytes 278560 | tf_op jit(solution)/shard_map/ppermute | solution.py:39
  148.3 2.7 %collective-permute-start.39 = (bf16[272,128]{1,0:T(8,128)(2,1)S(1)}, bf16[272,128]{1,0:T(8,128)(2,1)S(1)}, u32[]{:S(2)}, u32[]{:S(2)}) collective-permute-start(bf16[272,128]{1,0:T(8,128)(2,1)S(1)} %get-tuple-element.86), channel_id=1, source_target_pairs={{0,16},{1,17},{2,18},{3,19},{4,20},{5,21},{6,22},{7,23},{8,24},{9,... | collective-permute-start | bytes 208904 | tf_op jit(solution)/shard_map/ppermute | solution.py:39
  154.9 2.2 %collective-permute-done.40 = bf16[272,128]{1,0:T(8,128)(2,1)S(1)} collective-permute-done((bf16[272,128]{1,0:T(8,128)(2,1)S(1)}, bf16[272,128]{1,0:T(8,128)(2,1)S(1)}, u32[]{:S(2)}, u32[]{:S(2)}) %collective-permute-start.40) | collective-permute-done | bytes 69664 | tf_op jit(solution)/shard_map/ppermute | solution.py:39
  158.0 3.8 %collective-permute-done.28 = bf16[4,128,512]{2,1,0:T(8,128)(2,1)S(1)} collective-permute-done((bf16[4,128,512]{2,1,0:T(8,128)(2,1)S(1)}, bf16[4,128,512]{2,1,0:T(8,128)(2,1)S(1)}, u32[]{:S(2)}, u32[]{:S(2)}) %collective-permute-start.28) | collective-permute-done | bytes 524320 | tf_op jit(solution)/shard_map/ppermute | solution.py:39
  (157 shorter events, 49.0 us)
Async XLA Ops:
  4.3 18.9 %collective-permute-start = (bf16[4,128,512]{2,1,0:T(8,128)(2,1)}, bf16[4,128,512]{2,1,0:T(8,128)(2,1)S(1)}, u32[]{:S(2)}, u32[]{:S(2)}) collective-permute-start(bf16[4,128,512]{2,1,0:T(8,128)(2,1)} %get-tuple-element.54), channel_id=1, source_target_pairs={{0,2},{1,3},{2,0},{3,1},{4,6},{5,7},{6,4},{7,5},{8,10},{9,11},{10,... | collective-permute-start | bytes 1572872 | tf_op jit(solution)/shard_map/ppermute | solution.py:39
  7.3 9.9 %collective-permute-start.3 = (bf16[1,272,128]{2,1,0:T(8,128)(2,1)}, bf16[1,272,128]{2,1,0:T(8,128)(2,1)S(1)}, u32[]{:S(2)}, u32[]{:S(2)}) collective-permute-start(bf16[1,272,128]{2,1,0:T(8,128)(2,1)} %bitcast.143), channel_id=1, source_target_pairs={{0,16},{1,17},{2,18},{3,19},{4,20},{5,21},{6,22},{7,23},{8,24},{9,... | collective-permute-start | bytes 208904 | tf_op jit(solution)/shard_map/ppermute | solution.py:39
  9.9 10.3 %collective-permute-start.11 = (bf16[1,144,512]{2,1,0:T(8,128)(2,1)}, bf16[1,144,512]{2,1,0:T(8,128)(2,1)S(1)}, u32[]{:S(2)}, u32[]{:S(2)}) collective-permute-start(bf16[1,144,512]{2,1,0:T(8,128)(2,1)} %bitcast.140), channel_id=1, source_target_pairs={{0,16},{1,17},{2,18},{3,19},{4,20},{5,21},{6,22},{7,23},{8,24},{9,... | collective-permute-start | bytes 442376 | tf_op jit(solution)/shard_map/ppermute | solution.py:39
  24.2 10.5 %collective-permute-start.10 = (bf16[4,272,128]{2,1,0:T(8,128)(2,1)S(1)}, bf16[4,272,128]{2,1,0:T(8,128)(2,1)S(1)}, u32[]{:S(2)}, u32[]{:S(2)}) collective-permute-start(bf16[4,272,128]{2,1,0:T(8,128)(2,1)S(1)} %pad_maximum_fusion.4.refs_5_), channel_id=1, source_target_pairs={{0,6},{1,7},{2,4},{3,5},{4,2},{5,3},{6,0},{7,1},{8,14},{9,15},{10,... | collective-permute-start | bytes 835592 | tf_op jit(solution)/shard_map/ppermute | solution.py:39
  25.7 15.0 %collective-permute-start.6 = (bf16[4,272,128]{2,1,0:T(8,128)(2,1)S(1)}, bf16[4,272,128]{2,1,0:T(8,128)(2,1)S(1)}, u32[]{:S(2)}, u32[]{:S(2)}) collective-permute-start(bf16[4,272,128]{2,1,0:T(8,128)(2,1)S(1)} %pad_maximum_fusion.4.refs_5_), channel_id=1, source_target_pairs={{0,2},{1,3},{2,0},{3,1},{4,6},{5,7},{6,4},{7,5},{8,10},{9,11},{10,... | collective-permute-start | bytes 835592 | tf_op jit(solution)/shard_map/ppermute | solution.py:39
  27.2 22.1 %collective-permute-start.8 = (bf16[4,272,128]{2,1,0:T(8,128)(2,1)S(1)}, bf16[4,272,128]{2,1,0:T(8,128)(2,1)S(1)}, u32[]{:S(2)}, u32[]{:S(2)}) collective-permute-start(bf16[4,272,128]{2,1,0:T(8,128)(2,1)S(1)} %pad_maximum_fusion.4.refs_5_), channel_id=1, source_target_pairs={{0,4},{1,5},{2,6},{3,7},{4,0},{5,1},{6,2},{7,3},{8,12},{9,13},{10,... | collective-permute-start | bytes 835592 | tf_op jit(solution)/shard_map/ppermute | solution.py:39
  30.5 18.8 %collective-permute-start.5 = (bf16[4,272,128]{2,1,0:T(8,128)(2,1)S(1)}, bf16[4,272,128]{2,1,0:T(8,128)(2,1)S(1)}, u32[]{:S(2)}, u32[]{:S(2)}) collective-permute-start(bf16[4,272,128]{2,1,0:T(8,128)(2,1)S(1)} %pad_maximum_fusion.4.refs_5_), channel_id=1, source_target_pairs={{0,1},{1,0},{2,3},{3,2},{4,5},{5,4},{6,7},{7,6},{8,9},{9,8},{10,11... | collective-permute-start | bytes 835592 | tf_op jit(solution)/shard_map/ppermute | solution.py:39
  30.6 35.1 %collective-permute-start.19 = (bf16[4,144,512]{2,1,0:T(8,128)(2,1)S(1)}, bf16[4,144,512]{2,1,0:T(8,128)(2,1)S(1)}, u32[]{:S(2)}, u32[]{:S(2)}) collective-permute-start(bf16[4,144,512]{2,1,0:T(8,128)(2,1)S(1)} %constant_dynamic-update-slice_fusion.refs_7_), channel_id=1, source_target_pairs={{0,6},{1,7},{2,4},{3,5},{4,2},{5,3},{6,0},{7,1},{8,14},{9,15},{10,... | collective-permute-start | bytes 1769480 | tf_op jit(solution)/shard_map/ppermute | solution.py:39
  34.7 31.3 %collective-permute-start.15 = (bf16[4,144,512]{2,1,0:T(8,128)(2,1)S(1)}, bf16[4,144,512]{2,1,0:T(8,128)(2,1)S(1)}, u32[]{:S(2)}, u32[]{:S(2)}) collective-permute-start(bf16[4,144,512]{2,1,0:T(8,128)(2,1)S(1)} %constant_dynamic-update-slice_fusion.refs_7_), channel_id=1, source_target_pairs={{0,2},{1,3},{2,0},{3,1},{4,6},{5,7},{6,4},{7,5},{8,10},{9,11},{10,... | collective-permute-start | bytes 1769480 | tf_op jit(solution)/shard_map/ppermute | solution.py:39
  40.7 25.5 %collective-permute-start.17 = (bf16[4,144,512]{2,1,0:T(8,128)(2,1)S(1)}, bf16[4,144,512]{2,1,0:T(8,128)(2,1)S(1)}, u32[]{:S(2)}, u32[]{:S(2)}) collective-permute-start(bf16[4,144,512]{2,1,0:T(8,128)(2,1)S(1)} %constant_dynamic-update-slice_fusion.refs_7_), channel_id=1, source_target_pairs={{0,4},{1,5},{2,6},{3,7},{4,0},{5,1},{6,2},{7,3},{8,12},{9,13},{10,... | collective-permute-start | bytes 1769480 | tf_op jit(solution)/shard_map/ppermute | solution.py:39
  52.8 13.7 %collective-permute-start.14 = (bf16[4,144,512]{2,1,0:T(8,128)(2,1)S(1)}, bf16[4,144,512]{2,1,0:T(8,128)(2,1)S(1)}, u32[]{:S(2)}, u32[]{:S(2)}) collective-permute-start(bf16[4,144,512]{2,1,0:T(8,128)(2,1)S(1)} %constant_dynamic-update-slice_fusion.refs_7_), channel_id=1, source_target_pairs={{0,1},{1,0},{2,3},{3,2},{4,5},{5,4},{6,7},{7,6},{8,9},{9,8},{10,11... | collective-permute-start | bytes 1769480 | tf_op jit(solution)/shard_map/ppermute | solution.py:39
  89.9 21.4 %collective-permute-start.32 = (bf16[8,144,512]{2,1,0:T(8,128)(2,1)}, bf16[8,144,512]{2,1,0:T(8,128)(2,1)}, u32[]{:S(2)}, u32[]{:S(2)}) collective-permute-start(bf16[8,144,512]{2,1,0:T(8,128)(2,1)} %get-tuple-element.84), channel_id=1, source_target_pairs={{0,1},{1,0},{2,3},{3,2},{4,5},{5,4},{6,7},{7,6},{8,9},{9,8},{10,11... | collective-permute-start | bytes 3538952 | tf_op jit(solution)/shard_map/ppermute | solution.py:39
  93.9 17.1 %collective-permute-start.22 = (bf16[4,144,512]{2,1,0:T(8,128)(2,1)}, bf16[4,144,512]{2,1,0:T(8,128)(2,1)}, u32[]{:S(2)}, u32[]{:S(2)}) collective-permute-start(bf16[4,144,512]{2,1,0:T(8,128)(2,1)} %get-tuple-element.112), channel_id=1, source_target_pairs={{0,2},{1,3},{2,0},{3,1},{4,6},{5,7},{6,4},{7,5},{8,10},{9,11},{10,... | collective-permute-start | bytes 1769480 | tf_op jit(solution)/shard_map/ppermute | solution.py:39
  94.0 17.0 %collective-permute-start.23 = (bf16[4,144,512]{2,1,0:T(8,128)(2,1)}, bf16[4,144,512]{2,1,0:T(8,128)(2,1)}, u32[]{:S(2)}, u32[]{:S(2)}) collective-permute-start(bf16[4,144,512]{2,1,0:T(8,128)(2,1)} %get-tuple-element.111), channel_id=1, source_target_pairs={{0,4},{1,5},{2,6},{3,7},{4,0},{5,1},{6,2},{7,3},{8,12},{9,13},{10,... | collective-permute-start | bytes 1769480 | tf_op jit(solution)/shard_map/ppermute | solution.py:39
  94.1 70.5 %collective-permute-start.30 = (bf16[1,128,512]{2,1,0:T(8,128)(2,1)}, bf16[1,128,512]{2,1,0:T(8,128)(2,1)S(1)}, u32[]{:S(2)}, u32[]{:S(2)}) collective-permute-start(bf16[1,128,512]{2,1,0:T(8,128)(2,1)} %copy-done.13), channel_id=1, source_target_pairs={{0,1},{1,0},{2,3},{3,2},{4,5},{5,4},{6,7},{7,6},{8,9},{9,8},{10,11... | collective-permute-start | bytes 393224 | tf_op jit(solution)/shard_map/ppermute | solution.py:39
  111.0 19.2 %collective-permute-start.24 = (bf16[4,4,272,128]{3,2,1,0:T(8,128)(2,1)S(1)}, bf16[4,4,272,128]{3,2,1,0:T(8,128)(2,1)S(1)}, u32[]{:S(2)}, u32[]{:S(2)}) collective-permute-start(bf16[4,4,272,128]{3,2,1,0:T(8,128)(2,1)S(1)} %get-tuple-element.77), channel_id=1, source_target_pairs={{0,1},{1,0},{2,3},{3,2},{4,5},{5,4},{6,7},{7,6},{8,9},{9,8},{10,11... | collective-permute-start | bytes 3342344 | tf_op jit(solution)/shard_map/ppermute | solution.py:39
  112.8 9.3 %collective-permute-start.33 = (bf16[2,144,512]{2,1,0:T(8,128)(2,1)S(1)}, bf16[2,144,512]{2,1,0:T(8,128)(2,1)S(1)}, u32[]{:S(2)}, u32[]{:S(2)}) collective-permute-start(bf16[2,144,512]{2,1,0:T(8,128)(2,1)S(1)} %get-tuple-element.110), channel_id=1, source_target_pairs={{0,4},{1,5},{2,6},{3,7},{4,0},{5,1},{6,2},{7,3},{8,12},{9,13},{10,... | collective-permute-start | bytes 884744 | tf_op jit(solution)/shard_map/ppermute | solution.py:39
  114.8 8.9 %collective-permute-start.35 = (bf16[2,144,512]{2,1,0:T(8,128)(2,1)S(1)}, bf16[2,144,512]{2,1,0:T(8,128)(2,1)S(1)}, u32[]{:S(2)}, u32[]{:S(2)}) collective-permute-start(bf16[2,144,512]{2,1,0:T(8,128)(2,1)S(1)} %get-tuple-element.109), channel_id=1, source_target_pairs={{0,2},{1,3},{2,0},{3,1},{4,6},{5,7},{6,4},{7,5},{8,10},{9,11},{10,... | collective-permute-start | bytes 884744 | tf_op jit(solution)/shard_map/ppermute | solution.py:39
  127.1 13.5 %collective-permute-start.36 = (bf16[1,144,512]{2,1,0:T(8,128)(2,1)S(1)}, bf16[1,144,512]{2,1,0:T(8,128)(2,1)S(1)}, u32[]{:S(2)}, u32[]{:S(2)}) collective-permute-start(bf16[1,144,512]{2,1,0:T(8,128)(2,1)S(1)} %get-tuple-element.107), channel_id=1, source_target_pairs={{0,16},{1,17},{2,18},{3,19},{4,20},{5,21},{6,22},{7,23},{8,24},{9,... | collective-permute-start | bytes 442376 | tf_op jit(solution)/shard_map/ppermute | solution.py:39
  128.8 13.4 %collective-permute-start.37 = (bf16[1,144,512]{2,1,0:T(8,128)(2,1)S(1)}, bf16[1,144,512]{2,1,0:T(8,128)(2,1)S(1)}, u32[]{:S(2)}, u32[]{:S(2)}) collective-permute-start(bf16[1,144,512]{2,1,0:T(8,128)(2,1)S(1)} %get-tuple-element.106), channel_id=1, source_target_pairs={{0,24},{1,25},{2,26},{3,27},{4,28},{5,29},{6,30},{7,31},{8,16},{9,... | collective-permute-start | bytes 442376 | tf_op jit(solution)/shard_map/ppermute | solution.py:39
  130.6 13.8 %collective-permute-start.25 = (bf16[4,272,128]{2,1,0:T(8,128)(2,1)S(1)}, bf16[4,272,128]{2,1,0:T(8,128)(2,1)S(1)}, u32[]{:S(2)}, u32[]{:S(2)}) collective-permute-start(bf16[4,272,128]{2,1,0:T(8,128)(2,1)S(1)} %get-tuple-element.116), channel_id=1, source_target_pairs={{0,2},{1,3},{2,0},{3,1},{4,6},{5,7},{6,4},{7,5},{8,10},{9,11},{10,... | collective-permute-start | bytes 835592 | tf_op jit(solution)/shard_map/ppermute | solution.py:39
  132.2 12.2 %collective-permute-start.26 = (bf16[4,272,128]{2,1,0:T(8,128)(2,1)S(1)}, bf16[4,272,128]{2,1,0:T(8,128)(2,1)S(1)}, u32[]{:S(2)}, u32[]{:S(2)}) collective-permute-start(bf16[4,272,128]{2,1,0:T(8,128)(2,1)S(1)} %get-tuple-element.115), channel_id=1, source_target_pairs={{0,4},{1,5},{2,6},{3,7},{4,0},{5,1},{6,2},{7,3},{8,12},{9,13},{10,... | collective-permute-start | bytes 835592 | tf_op jit(solution)/shard_map/ppermute | solution.py:39
  152.7 9.2 %collective-permute-start.28 = (bf16[4,128,512]{2,1,0:T(8,128)(2,1)S(1)}, bf16[4,128,512]{2,1,0:T(8,128)(2,1)S(1)}, u32[]{:S(2)}, u32[]{:S(2)}) collective-permute-start(bf16[4,128,512]{2,1,0:T(8,128)(2,1)S(1)} %pad_maximum_fusion.1), channel_id=1, source_target_pairs={{0,2},{1,3},{2,0},{3,1},{4,6},{5,7},{6,4},{7,5},{8,10},{9,11},{10,... | collective-permute-start | bytes 1572872 | tf_op jit(solution)/shard_map/ppermute | solution.py:39
  154.8 8.5 %collective-permute-start.31 = (bf16[1,128,512]{2,1,0:T(8,128)(2,1)S(1)}, bf16[1,128,512]{2,1,0:T(8,128)(2,1)S(1)}, u32[]{:S(2)}, u32[]{:S(2)}) collective-permute-start(bf16[1,128,512]{2,1,0:T(8,128)(2,1)S(1)} %get-tuple-element.81), channel_id=1, source_target_pairs={{0,1},{1,0},{2,3},{3,2},{4,5},{5,4},{6,7},{7,6},{8,9},{9,8},{10,11... | collective-permute-start | bytes 393224 | tf_op jit(solution)/shard_map/ppermute | solution.py:39
  (50 other events, 450.9 us)

commit v3 on v2

v3 whole, which is shorter than its diff:
```python
import functools

import jax
import jax.numpy as jnp
from jax import lax
from jax.experimental import pallas as pl
from jax.experimental.pallas import tpu as pltpu
from jax.sharding import PartitionSpec as P

HD = 64
STEP = 10
LANES = 128

NORM_EPS = 1e-05
NEG_FILL = -1e30
BETA_ONE = 0.9
BETA_TWO = 0.95
ADAM_EPS = 1e-08
RATES = (0.03, 0.2, 0.03, 0.02, 0.3, 0.3)
DECAYS = (0.1, 0.1, 0.1, 0.1, 0.1, 0.0)
GELU_A = 0.7978845608028654
GELU_B = 0.044715

F32 = jnp.float32
BF16 = jnp.bfloat16
AXES = ("dp", "tensor")

NN = (((1,), (0,)), ((), ()))
NT = (((1,), (1,)), ((), ()))
TN = (((0,), (0,)), ((), ()))
QUERIES = 256


def total(*parts):
    return sum(p.astype(F32) for p in parts)


def low(*parts):
    return total(*parts).astype(BF16)


def adam_step(weight, gradient, moment_one, second, step_rate, decay_rate):
    first_new = BETA_ONE * moment_one + (1.0 - BETA_ONE) * gradient
    second_new = BETA_TWO * second + (1.0 - BETA_TWO) * gradient * gradient
    fixed_first = first_new / (1.0 - BETA_ONE**STEP)
    fixed_second = second_new / (1.0 - BETA_TWO**STEP)
    weight_new = weight - step_rate * (fixed_first / (jnp.sqrt(fixed_second) + ADAM_EPS) + decay_rate * weight)
    return (weight_new, first_new, second_new)


def mm(a, b, dims=NN):
    return lax.dot_general(a, b, dims, preferred_element_type=F32)


def swap(value, rd, rt):
    n_t = lax.axis_size("tensor")
    mask = rd * n_t + rt
    return lax.ppermute(value, AXES, [(i, i ^ mask) for i in range(lax.axis_size("dp") * n_t)])


def rows_at(start, size, step):
    return pl.ds(pl.multiple_of(start, step), size)


def by_head(rows):
    lane = lax.broadcasted_iota(jnp.int32, (rows, LANES), 1)

    def keep(h):
        here = (lane >= h * HD) & (lane < (h + 1) * HD)
        return lambda v: jnp.where(here, v, jnp.zeros_like(v))

    return [keep(h) for h in range(LANES // HD)]


def fill_window(me_t, which, parts, out_ref, sems):
    own, rx, c1, c3 = parts
    n = own.shape[1]
    sources = (own.at[me_t], c1.at[which], rx.at[which], c3.at[which])
    copies = [pltpu.make_async_copy(src, out_ref.at[rows_at((me_t ^ r) * n, n, n), :], sems.at[r]) for r, src in enumerate(sources)]
    for copy in copies:
        copy.start()
    return copies


def copies_in(moves, sems):
    copies = [pltpu.make_async_copy(src, dst, sems.at[i]) for i, (src, dst) in enumerate(moves)]
    for copy in copies:
        copy.start()
    return copies


def prepare_kernel(scal, inputs, cot, attn, pos, norm, out, up, down, ga, gb, xs, c1, attn_s, pos_s, norm_s, out_s, up_s, down_s, sems):
    me_t = scal[1]
    moves = [(attn, attn_s), (pos, pos_s), (norm, norm_s), (up, up_s), (down, down_s), (out, out_s)]
    for rel, ref, at in ((2, xs, 0), (3, xs, 2), (1, c1, 0)):
        moves += [(inputs.at[me_t ^ rel], ref.at[at]), (cot.at[me_t ^ rel], ref.at[at + 1])]
    copies = copies_in(moves, sems)
    for copy in copies[:3]:
        copy.wait()
    per = attn.shape[1]
    pos_per = pos.shape[0]
    tiles = pos.shape[1] // LANES
    for t in range(3):
        ga[0, t * per : (t + 1) * per, :] = attn_s[t].astype(BF16)
    for k in range(tiles):
        at = 3 * per + k * pos_per
        ga[0, at : at + pos_per, :] = pos_s[:, k * LANES : (k + 1) * LANES].astype(BF16)
    at = 3 * per + tiles * pos_per
    both = norm_s[...]
    both = jnp.concatenate([both, both], axis=1)
    both = jnp.concatenate([both, jnp.zeros_like(both)], axis=0)
    high = both.astype(BF16)
    rest = (both - high.astype(F32)).astype(BF16)
    ga[0, at : at + 16, :] = jnp.concatenate([high, rest], axis=0)
    for copy in copies[3:6]:
        copy.wait()
    gb[0, 0:per, :] = up_s[...].astype(BF16)
    gb[0, per : 2 * per, :] = down_s[...].astype(BF16)
    gb[0, 2 * per :, :] = out_s[...].astype(BF16)
    for copy in copies[6:]:
        copy.wait()


def stack_kernel(own, got, both):
    n = own.shape[0]
    both[:n] = own[...]
    both[n:] = got[...]


def attention_kernel(places, n_pieces, scal, *refs):
    own, rx, c1, c3, segs = refs[:5]
    pieces = refs[5 : 5 + n_pieces]
    hid_o, qkv_h, pt_h, mix_o, w_h, nrm_o, x_s, pos_s, bias_s, nrm_s, w_o, qkv_o, pt_o, sems, out_sems = refs[5 + n_pieces :]
    leaving = []

    def leave(src, dst):
        leaving.append(pltpu.make_async_copy(src, dst, out_sems.at[len(leaving)]))
        leaving[-1].start()

    me_dp, me_t = scal[0], scal[1]
    win, width = x_s.shape
    groups = w_o.shape[1] // (3 * LANES)
    filling = fill_window(me_t, 0, (own, rx, c1, c3), x_s, sems)
    if places is None:
        w_o[...] = pieces[0][...]
        pos_s[...] = pieces[1][...]
        nrm_o[...] = pieces[2][...]
    else:
        n_dp = nrm_s.shape[0]
        per = width // n_dp
        pos_per = win // (n_dp * groups)
        for ref, (xr, yr, zs, c) in zip(pieces, places, strict=True):
            tr = xr * 2 + c
            for i, zr in enumerate(zs):
                src = me_dp ^ (zr * 2 + yr)
                for t in range(3):
                    at = (tr * 3 + t) * LANES
                    w_o[rows_at(src * per, per, per), at : at + LANES] = ref[i, t * per : (t + 1) * per]
                where = (me_t ^ tr) * (win // groups) + src * pos_per
                for k in range(width // LANES):
                    at = 3 * per + k * pos_per
                    pos_s[rows_at(where, pos_per, pos_per), k * LANES : (k + 1) * LANES] = ref[i, at : at + pos_per]
                if tr == 0:
                    at = 3 * per + width // LANES * pos_per
                    nrm_s[src] = ref[i, at : at + 16].astype(F32)
        low_lane = lax.broadcasted_iota(jnp.int32, (8, LANES), 1) < per
        for j in range(n_dp // 2):
            left = nrm_s[2 * j]
            right = nrm_s[2 * j + 1]
            both = jnp.where(low_lane, left[0:8] + left[8:16], right[0:8] + right[8:16])
            nrm_o[:, j * LANES : (j + 1) * LANES] = both

    leave(w_o, w_h)

    seg = segs[pl.ds(me_t, 1), :].astype(F32)
    seg_col = jnp.transpose(jnp.broadcast_to(seg, (LANES, win)))
    for i in range(win // LANES):
        key_seg = seg_col[i * LANES : (i + 1) * LANES, 0:1]
        key_at = lax.broadcasted_iota(jnp.int32, (LANES, win), 0) + i * LANES
        query_at = lax.broadcasted_iota(jnp.int32, (LANES, win), 1)
        counts = (key_seg == seg) & (query_at >= key_at)
        bias_s[i * LANES : (i + 1) * LANES, :] = jnp.where(counts, 0.0, NEG_FILL)

    for copy in filling:
        copy.wait()
    hidden = x_s[...].astype(F32) + pos_s[...].astype(F32)
    hid_o[...] = hidden
    x_s[...] = hidden.astype(BF16)
    heads = by_head(win)
    for g in range(groups):
        at = g * 3 * LANES
        qkv = mm(x_s[...], w_o[:, at : at + 3 * LANES]).astype(BF16)
        q = qkv[:, :LANES] * jnp.asarray(HD**-0.5, BF16)
        k = qkv[:, LANES : 2 * LANES]
        v = qkv[:, 2 * LANES :]
        qkv_o[:, at : at + LANES] = q
        qkv_o[:, at + LANES : at + 3 * LANES] = qkv[:, LANES:]
        for j in range(win // QUERIES):
            ext = (j + 1) * QUERIES
            cols = slice(j * QUERIES, ext)
            mixed = jnp.zeros((QUERIES, LANES), F32)
            for h, only in enumerate(heads):
                s = mm(only(k)[:ext], q[cols], NT) + bias_s[:ext, cols]
                e = jnp.exp(s - jnp.max(s, axis=0, keepdims=True))
                p = (e * (1.0 / jnp.sum(e, axis=0, keepdims=True))).astype(BF16)
                pt_o[len(heads) * g + h, :ext, cols] = p
                mixed += mm(p, only(v)[:ext], TN)
            mix_o[cols, g * LANES : (g + 1) * LANES] = mixed.astype(BF16)
            for h in range(len(heads)):
                leave(pt_o.at[len(heads) * g + h, :ext, cols], pt_h.at[len(heads) * g + h, :ext, cols])
    leave(qkv_o, qkv_h)
    for copy in leaving:
        copy.wait()


def norm_forward(v):
    center = v - jnp.mean(v, axis=-1, keepdims=True)
    rs = lax.rsqrt(jnp.mean(center * center, axis=-1, keepdims=True) + NORM_EPS)
    return center * rs, rs


def norm_backward(g, xhat, rs, gain):
    e = g * gain
    return rs * (e - jnp.mean(e, axis=-1, keepdims=True) - xhat * jnp.mean(e * xhat, axis=-1, keepdims=True))


def put_blocks(me_t, value, keep, s1, sx):
    n = keep.shape[0]
    for r, ref in ((0, keep), (1, s1.at[0]), (2, sx.at[0]), (3, sx.at[1])):
        ref[...] = value[rows_at((me_t ^ r) * n, n, n), :].astype(ref.dtype)


CHUNK = 128


def chunk_of(refs, tr, r):
    c, xr, yr, zr = tr & 1, tr >> 1, r & 1, r >> 1
    half = refs[0].shape[0] // 4
    if zr < half:
        first, slot = xr == 1, yr * half + zr
    else:
        first, slot = yr == 1, 2 * half + xr * half + zr - half
    return refs[2 * c + (0 if first else 1)], slot


def ffn_kernel(places, n_pieces, scal, *refs):
    own, rx, c1, c3, hid, mixed, nrm = refs[:7]
    pieces = refs[7 : 7 + n_pieces]
    rest = refs[7 + n_pieces :]
    res_k, res_1, res_x, gone_o, gm_o, gnorm_o = rest[:6]
    if places is None:
        gup_o, gdown_o, gout_o = rest[6:9]
        rest = rest[9:]
    else:
        chunks_o = rest[6:10]
        rest = rest[10:]
    cot_s, out_s, up_s, down_s, a_s, b_s, g_s, xh1_s, r1_s, n1_s, sent_s, act_s, dg_s, low_s, xt_s, sems = rest
    me_dp, me_t = scal[0], scal[1]
    win, width = hid.shape
    groups = up_s.shape[0]
    filling = fill_window(me_t, 1, (own, rx, c1, c3), cot_s, sems)
    if places is None:
        n_dp = 1
        for src, dst in zip(pieces, (out_s, up_s, down_s), strict=True):
            dst[...] = src[...]
    else:
        n_dp = 2 * sum(len(zs) for _, yr, zs, c in places if yr == 0 and c == 0) // 2
        per = width // n_dp
        out_per = LANES // n_dp
        for ref, (xr, yr, zs, c) in zip(pieces, places, strict=True):
            tr = xr * 2 + c
            for i, zr in enumerate(zs):
                src = me_dp ^ (zr * 2 + yr)
                up_s[tr, rows_at(src * per, per, per), :] = ref[i, 0:per]
                down_s[tr, rows_at(src * per, per, per), :] = ref[i, per : 2 * per]
                out_s[rows_at(tr * LANES + src * out_per, out_per, out_per), :] = ref[i, 2 * per : 2 * per + out_per]

    def chunks(fn):
        for i in range(win // CHUNK):
            fn(slice(i * CHUNK, (i + 1) * CHUNK))

    a_s[0] = mm(mixed[...], out_s[...])

    def norm_one(at):
        xhat, rs = norm_forward(hid[at, :] + a_s[0, at, :])
        xh1_s[at, :] = xhat
        r1_s[at, :] = jnp.broadcast_to(rs, (CHUNK, LANES))
        normed = xhat * nrm[0:1, :] + nrm[1:2, :]
        n1_s[at, :] = normed
        sent_s[at, :] = normed.astype(BF16)

    chunks(norm_one)

    for g in range(groups):
        a_s[g % 2] = mm(sent_s[...], up_s[g])

        def gelu(at, g=g):
            v = a_s[g % 2, at, :]
            t = jnp.tanh(GELU_A * (v + GELU_B * v * v * v))
            act_s[g, at, :] = (0.5 * v * (1.0 + t)).astype(BF16)
            dg_s[g, at, :] = 0.5 * (1.0 + t) + 0.5 * v * (1.0 - t * t) * (GELU_A * (1.0 + 3.0 * GELU_B * v * v))

        chunks(gelu)
        n1_s[...] += mm(act_s[g], down_s[g])

    for copy in filling:
        copy.wait()

    def norm_two(i, sums):
        at = slice(i * CHUNK, (i + 1) * CHUNK)
        xhat, rs = norm_forward(n1_s[at, :])
        n1_s[at, :] = xhat * nrm[2:3, :] + nrm[3:4, :]
        g = cot_s[at, :].astype(F32)
        grad = norm_backward(g, xhat, rs, nrm[2:3, :])
        b_s[at, :] = grad
        low_s[at, :] = grad.astype(BF16)
        return (sums[0] + jnp.sum((g * xhat).reshape(-1, 8, width), axis=0), sums[1] + jnp.sum(g.reshape(-1, 8, width), axis=0))

    def every(step):
        sums = (jnp.zeros((8, width), F32),) * 2
        for i in range(win // CHUNK):
            sums = step(i, sums)
        return sums

    gain_two, shift_two = every(norm_two)
    put_blocks(me_t, n1_s, res_k, res_1, res_x)

    def put(g, first, height, source, base):
        for r in range(n_dp):
            ref, slot = chunk_of(chunks_o, g, r)
            ref[slot, first : first + height, :] = source[rows_at(base + (r ^ me_dp) * height, height, height), :]

    xt_s[...] = jnp.transpose(sent_s[...])
    for g in range(groups):
        gdown = mm(jnp.transpose(act_s[g]), low_s[...])
        if places is None:
            gdown_o[g] = gdown.astype(BF16)
        else:
            g_s[0] = gdown.astype(BF16)
            put(g, per, per, g_s.at[0], 0)
        act_s[g] = (mm(low_s[...], down_s[g], NT) * dg_s[g]).astype(BF16)
        gup = mm(xt_s[...], act_s[g])
        if places is None:
            gup_o[g] = gup.astype(BF16)
        else:
            g_s[1] = gup.astype(BF16)
            put(g, 0, per, g_s.at[1], 0)
        b_s[...] += mm(act_s[g], up_s[g], NT)

    def norm_one_back(i, sums):
        at = slice(i * CHUNK, (i + 1) * CHUNK)
        g = b_s[at, :]
        xhat = xh1_s[at, :]
        grad = norm_backward(g, xhat, r1_s[at, 0:1], nrm[0:1, :])
        gone_o[at, :] = grad
        low_s[at, :] = grad.astype(BF16)
        return (sums[0] + jnp.sum((g * xhat).reshape(-1, 8, width), axis=0), sums[1] + jnp.sum(g.reshape(-1, 8, width), axis=0))

    gain_one, shift_one = every(norm_one_back)
    for k, total in enumerate((gain_one, shift_one, gain_two, shift_two)):
        gnorm_o[k : k + 1, :] = jnp.sum(total, axis=0, keepdims=True)
    gnorm_o[4:8, :] = jnp.zeros((4, width), F32)

    gout = mm(jnp.transpose(mixed[...]), low_s[...])
    if places is None:
        gout_o[...] = gout.astype(BF16)
    else:
        g_s[0] = gout.astype(BF16)
        for g in range(groups):
            put(g, 2 * per, out_per, g_s.at[0], g * LANES)
    gm = mm(low_s[...], out_s[...], NT).astype(BF16)
    for g in range(groups):
        gm_o[g] = gm[:, g * LANES : (g + 1) * LANES]


def attention_back_kernel(fast, scal, hid, qkv_h, pt_h, gm, w_h, gone, gnorm, *rest):
    gi_k, gi_1, gi_x = rest[:3]
    if fast:
        chunks_o = rest[3:7]
        rest = rest[7:]
    else:
        gattn_o, gpos_o = rest[3:5]
        rest = rest[5:]
    ht_s, ds_s, dqkv_s, acc_s, g_s, qkv, pt, w, sems = rest
    me_dp, me_t = scal[0], scal[1]
    win, width = hid.shape
    groups = w.shape[1] // (3 * LANES)
    heads = by_head(win)
    arriving = [pltpu.make_async_copy(qkv_h, qkv, sems.at[0])]
    for n in range(pt.shape[0]):
        for j in range(win // QUERIES):
            ext = (j + 1) * QUERIES
            cols = slice(j * QUERIES, ext)
            arriving.append(pltpu.make_async_copy(pt_h.at[n, :ext, cols], pt.at[n, :ext, cols], sems.at[len(arriving)]))
    arriving.append(pltpu.make_async_copy(w_h, w, sems.at[len(arriving)]))
    for copy in arriving:
        copy.start()
    ht_s[...] = jnp.transpose(hid[...].astype(BF16))
    for g in range(groups):
        at = g * 3 * LANES
        if g == 0:
            arriving[0].wait()
        per_group = len(heads) * (win // QUERIES)
        for copy in arriving[1 + g * per_group : 1 + (g + 1) * per_group]:
            copy.wait()
        q = qkv[:, at : at + LANES]
        k = qkv[:, at + LANES : at + 2 * LANES]
        v = qkv[:, at + 2 * LANES : at + 3 * LANES]
        d_mixed = gm[g]
        for j in range(win // QUERIES):
            ext = (j + 1) * QUERIES
            cols = slice(j * QUERIES, ext)
            dq = jnp.zeros((QUERIES, LANES), F32)
            for h, only in enumerate(heads):
                p = pt[len(heads) * g + h, :ext, cols].astype(F32)
                dp = mm(v[:ext], only(d_mixed)[cols], NT)
                ds = (p * (dp - jnp.sum(p * dp, axis=0, keepdims=True))).astype(BF16)
                ds_s[len(heads) * g + h, :ext, cols] = ds
                dq += mm(ds, only(k)[:ext], TN)
            dqkv_s[cols, at : at + LANES] = (dq * HD**-0.5).astype(BF16)
        for i in range(win // QUERIES):
            rows = slice(i * QUERIES, (i + 1) * QUERIES)
            dk = jnp.zeros((QUERIES, LANES), F32)
            dv = jnp.zeros((QUERIES, LANES), F32)
            for h, only in enumerate(heads):
                dk += mm(ds_s[len(heads) * g + h, rows, i * QUERIES :], only(q)[i * QUERIES :])
                dv += mm(pt[len(heads) * g + h, rows, i * QUERIES :], only(d_mixed)[i * QUERIES :])
            dqkv_s[rows, at + LANES : at + 2 * LANES] = dk.astype(BF16)
            dqkv_s[rows, at + 2 * LANES : at + 3 * LANES] = dv.astype(BF16)
    arriving[-1].wait()
    acc_s[...] = gone[...] + mm(dqkv_s[...], w[...], NT)

    put_blocks(me_t, acc_s, gi_k, gi_1, gi_x)
    if not fast:
        for g in range(groups):
            gattn_o[g] = mm(ht_s[...], dqkv_s[:, g * 3 * LANES : (g + 1) * 3 * LANES]).astype(BF16)
        gpos_o[...] = acc_s[...].astype(BF16)
        return
    n_dp = chunks_o[0].shape[0]
    per = width // n_dp
    pos_per = win // (n_dp * groups)
    for g in range(groups):
        g_s[g % 2] = mm(ht_s[...], dqkv_s[:, g * 3 * LANES : (g + 1) * 3 * LANES]).astype(BF16)
        for r in range(n_dp):
            d = r ^ me_dp
            ref, slot = chunk_of(chunks_o, g, r)
            for t in range(3):
                ref[slot, t * per : (t + 1) * per, :] = g_s[g % 2, rows_at(d * per, per, per), t * LANES : (t + 1) * LANES]
            where = (me_t ^ g) * (win // groups) + d * pos_per
            for k in range(width // LANES):
                at = 3 * per + k * pos_per
                ref[slot, at : at + pos_per, :] = acc_s[rows_at(where, pos_per, pos_per), k * LANES : (k + 1) * LANES].astype(BF16)
            at = 3 * per + width // LANES * pos_per
            tile = gnorm[0:8, rows_at((d >> 1) * LANES, LANES, LANES)]
            ref[slot, at : at + 16, :] = jnp.concatenate([tile, tile], axis=0).astype(BF16)


def near_kernel(rest, got, x, y, x2, y2, own, far, odd):
    own[...] = total(rest[0], got[0], x[0], x2[0])
    far[...] = total(rest[4], got[4], y[0], y2[0])
    odd[0] = low(rest[1], got[1], x[1], x2[1])
    odd[1] = low(rest[5], got[5], y[1], y2[1])


def second_kernel(done, rest, got, x, y, a, b):
    del done
    for i in range(2):
        a[i] = low(rest[2 + i], got[2 + i], x[2 + i])
        b[i] = low(rest[6 + i], got[6 + i], y[2 + i])


def far_kernel(own, far, near, own_o, far_o):
    own_o[...] = total(own[...], near[0])
    far_o[0] = low(far[...], near[1])


def far_near_kernel(own, far, near, rest, got, x, y, x2, y2, own_o, far_o, *others):
    far_kernel(own, far, near, own_o, far_o)
    near_kernel(rest, got, x, y, x2, y2, *others)


def update(refs, gradient, rate, decay):
    weight, one, two, new_weight, new_one, new_two = refs
    new_weight[...], new_one[...], new_two[...] = adam_step(weight[...], gradient, one[...], two[...], rate, decay)


def rows_update_kernel(which, own, far, *refs):
    n = len(which)
    *refs, token = refs
    token[...] = jnp.zeros_like(token)
    grad = total(own[...], far[0])
    at = 0
    for i, index in enumerate(which):
        height = refs[i].shape[0]
        update(refs[i :: n], grad[at : at + height], RATES[index], DECAYS[index])
        at += height


def tiles_update_kernel(scal, done, own, far, *refs):
    del done
    attn, pos, norm = refs[0::3], refs[1::3], refs[2::3]
    grad = total(own[...], far[0])
    per = attn[0].shape[1]
    pos_per, width = pos[0].shape
    update(attn, grad[: 3 * per].reshape(attn[0].shape), RATES[0], DECAYS[0])
    at = 3 * per
    rows = [grad[at + k * pos_per : at + (k + 1) * pos_per] for k in range(width // LANES)]
    update(pos, jnp.concatenate(rows, axis=1), RATES[4], DECAYS[4])
    at += width // LANES * pos_per
    tile = grad[at : at + 8]
    half = jnp.where((scal[0] & 1) == 1, tile[:4, LANES // 2 :], tile[:4, : LANES // 2])
    update(norm, half, RATES[5], DECAYS[5])


def finish_kernel(scal, done, res_k, gi_k, res_1, gi_1, r2, r3, res_o, gi_o, token):
    token[...] = done[...]
    me_t = scal[1]
    for r, (res, gi) in enumerate(((res_k[...], gi_k[...]), (res_1[0], gi_1[0]), (r2[0], r2[1]), (r3[0], r3[1]))):
        res_o[me_t ^ r] = res
        gi_o[me_t ^ r] = gi.astype(F32)


def after(value, *others):
    return lax.optimization_barrier((value, *others))[0]


def gather_z(value, *others):
    nz = lax.axis_size("dp") // 2
    q, order = value, [0]
    step = nz // 2
    while step:
        if step == 1:
            q = after(q, *others)
        out = jax.ShapeDtypeStruct((2 * q.shape[0], *q.shape[1:]), q.dtype)
        q = call(stack_kernel, [out], [], [q, swap(q, step * 2, 0)], "vv", 6, 1_000)[0]
        order = order + [z ^ step for z in order]
        step //= 2
    return q, tuple(order)


def gather_xy(q, order, qx=None, qy=None, *others):
    half = len(order) // 2
    if qx is None:
        qx, qy = swap(q, 0, 2), swap(q, 1, 0)
    a, b = after(qx[:half], *others), after(qy[half:], *others)
    return [(q, (0, 0, order)), (qx, (1, 0, order)), (qy, (0, 1, order)), (swap(a, 1, 0), (1, 1, order[:half])), (swap(b, 0, 2), (1, 1, order[half:]))]


def both_cores(found):
    out = []
    for array, place in found:
        out.append((array, (*place, 0)))
        out.append((swap(array, 0, 1), (*place, 1)))
    return [f[0] for f in out], tuple(f[1] for f in out)


class Reduction:
    def __init__(self, keep_first, keep_rest, send_first, send_rest):
        self.half = keep_first.shape[0] // 4
        self.n = keep_first.shape[0] // 2
        self.sums = [(keep_rest,)]
        self.send_rest = send_rest
        got = swap(send_first, 0, 1)
        self.a = low(keep_first[: self.n], got[: self.n])
        self.b = low(keep_first[self.n :], got[self.n :])

    def terms(self, a, start, stop):
        at = 0 if a else self.n
        found = [k[at + start : at + stop] for k in self.rest]
        for pair in self.got:
            g = pair[0 if a else 1]
            if g.shape[0] >= stop:
                found.append(g[start:stop])
        return found

    def first(self):
        self.rest = [self.sums[0][0], swap(self.send_rest, 0, 1)]
        self.got = [(swap(self.a, 0, 2), swap(self.b, 1, 0))]
        return self.got[0]

    def second(self, *others):
        h = self.half
        a, b = [after(low(*self.terms(part, h, 2 * h)), *others) for part in (True, False)]
        self.got.append((swap(a, 1, 0), swap(b, 0, 2)))
        return self.got[1]

    def over_z(self, *others):
        h = self.half
        arrived = []
        for z in range(1, 2 * h):
            chunk = low(*self.terms(z < h, z % h, z % h + 1))
            arrived.append(swap(after(chunk, *others), 2 * z, 0))
        return arrived

    def result(self, arrived):
        return total(*self.terms(True, 0, 1), *arrived)[0]


def call(kernel, outs, scratch, args, spaces, mib, flops):
    vmem = pl.BlockSpec(memory_space=pltpu.VMEM)
    args = [pltpu.with_memory_space_constraint(v, pltpu.HBM) if k == "h" else v for v, k in zip(args, spaces, strict=True)]
    kinds = {"s": pl.BlockSpec(memory_space=pltpu.SMEM), "v": vmem, "a": pl.BlockSpec(memory_space=pl.ANY), "h": pl.BlockSpec(memory_space=pltpu.HBM)}
    return pl.pallas_call(
        kernel,
        out_shape=outs,
        in_specs=[kinds[k] for k in spaces],
        out_specs=[vmem if isinstance(v, jax.ShapeDtypeStruct) else kinds["h"] for v in outs],
        scratch_shapes=[pltpu.VMEM(*s) if isinstance(s, tuple) else pltpu.SemaphoreType.DMA(tuple(s)) for s in scratch],
        compiler_params=pltpu.CompilerParams(vmem_limit_bytes=mib * 1024 * 1024),
        cost_estimate=pl.CostEstimate(flops=flops, bytes_accessed=0, transcendentals=0),
    )(*args)


def body(
    inputs,
    segment_ids,
    cotangent,
    attn_proj,
    out_proj,
    up_proj,
    down_proj,
    pos_table,
    norm_params,
    first_attn,
    second_attn,
    first_out,
    second_out,
    first_up,
    second_up,
    first_down,
    second_down,
    first_pos,
    second_pos,
    first_norm,
    second_norm,
):
    n_dp, n_t = lax.axis_size("dp"), lax.axis_size("tensor")
    me_dp, me_t = lax.axis_index("dp"), lax.axis_index("tensor")
    scal = jnp.stack([me_dp, me_t]).astype(jnp.int32)
    windows, block, width = inputs.shape
    win = block * n_t
    inner = up_proj.shape[1]
    group = attn_proj.shape[2]
    per, out_per, pos_per = attn_proj.shape[1], out_proj.shape[0], pos_table.shape[0]
    fast = out_per % 16 == 0 and pos_per % 16 == 0 and 2 * per == LANES
    sds = jax.ShapeDtypeStruct

    if fast:
        ga, gb, xs, c1 = call(
            prepare_kernel,
            [
                sds((1, 3 * per + width // LANES * pos_per + 16, LANES), BF16),
                sds((1, 2 * per + out_per, width), BF16),
                sds((4, block, width), BF16),
                sds((2, block, width), BF16),
            ],
            [(v.shape, F32) for v in (attn_proj, pos_table, norm_params, out_proj, up_proj, down_proj)] + [[12]],
            [scal, inputs, cotangent, attn_proj, pos_table, norm_params, out_proj, up_proj, down_proj],
            "s" + "h" * 8,
            8,
            1_000,
        )
        qa, za = gather_z(ga)
        rx = swap(xs, 0, 2)
        qb, zb = gather_z(gb, qa)
        c1 = swap(c1, 0, 1)
        c3 = swap(rx[2:], 0, 1)
        qax, qay, qaxy = swap(qa, 0, 2), swap(qa, 1, 0), swap(qa, 1, 2)
        a_args, a_places = both_cores([(qa, (0, 0, za)), (qax, (1, 0, za)), (qay, (0, 1, za)), (qaxy, (1, 1, za))])
        qb = after(qb, rx, qax, qay)
        qbx, qby = swap(qb, 0, 2), swap(qb, 1, 0)
    else:

        def pair(rel):
            return jnp.concatenate([lax.dynamic_slice_in_dim(v, me_t ^ rel, 1, 0) for v in (inputs, cotangent)])

        rx = swap(jnp.concatenate([pair(2), pair(3)]), 0, 2)
        c1 = swap(pair(1), 0, 1)
        c3 = swap(rx[2:], 0, 1)
        relative = me_t ^ jnp.arange(n_t)
        whole = [lax.all_gather(lax.all_gather(v.astype(BF16), "dp"), "tensor") for v in (attn_proj, out_proj, up_proj, down_proj)]
        attn_w, out_w, up_w, down_w = [jnp.take(v, relative, axis=0) for v in whole]
        attn_w = attn_w.transpose(1, 3, 0, 2, 4).reshape(width, n_t * 3 * group)
        pos_w = lax.all_gather(lax.all_gather(pos_table.astype(BF16), "dp", axis=0, tiled=True), "tensor", axis=0, tiled=True)
        norm_w = lax.all_gather(norm_params, "dp", axis=1, tiled=True)
        norm_w = jnp.concatenate([norm_w, jnp.zeros_like(norm_w)])
        a_args, a_places = [attn_w, pos_w, norm_w], None
        b_args, b_places = [out_w.reshape(n_t * group, width), up_w.reshape(n_t, width, inner), down_w.reshape(n_t, inner, width)], None

    hid, qkv, pt, mixed, attn_all, norm_all = call(
        functools.partial(attention_kernel, a_places, len(a_args)),
        [
            sds((win, width), F32),
            pltpu.HBM((win, n_t * 3 * group), BF16),
            pltpu.HBM((n_t * group // HD, win, win), BF16),
            sds((win, n_t * group), BF16),
            pltpu.HBM((width, n_t * 3 * group), BF16),
            sds((8, width), F32),
        ],
        [((win, width), BF16), ((win, width), BF16), ((win, win), F32), ((n_dp, 16, LANES), F32), ((width, n_t * 3 * group), BF16), ((win, n_t * 3 * group), BF16), ((n_t * group // HD, win, win), BF16), [4], [32]],
        [scal, inputs, rx, c1, c3, segment_ids, *a_args],
        "shaaav" + "v" * len(a_args),
        14,
        1_000_000,
    )
    if fast:
        b_args, b_places = both_cores(gather_xy(qb, zb, qbx, qby, hid))

    blocks = [sds((block, width), BF16), sds((1, block, width), BF16), sds((2, block, width), BF16)]
    if fast:
        rows_b = 2 * per + out_per
        grads_b = [sds((n_dp, rows_b, width), BF16)] * 4
    else:
        grads_b = [sds((n_t, width, inner), BF16), sds((n_t, inner, width), BF16), sds((n_t * group, width), BF16)]
    res_k, res_1, res_x, gone, gm, gnorm, *got_b = call(
        functools.partial(ffn_kernel, b_places, len(b_args)),
        [*blocks, sds((win, width), F32), sds((n_t, win, group), BF16), sds((8, width), F32), *grads_b],
        [
            ((win, width), BF16),
            ((n_t * group, width), BF16),
            ((n_t, width, inner), BF16),
            ((n_t, inner, width), BF16),
            ((2, win, width), F32),
            ((win, width), F32),
            ((2, win, width), BF16),
            ((win, width), F32),
            ((win, LANES), F32),
            ((win, width), F32),
            ((win, width), BF16),
            ((n_t, win, inner), BF16),
            ((n_t, win, inner), F32),
            ((win, width), BF16),
            ((width, win), BF16),
            [4],
        ],
        [scal, cotangent, rx, c1, c3, hid, mixed, norm_all, *b_args],
        "shaaavvv" + "v" * len(b_args),
        22,
        1_000_000,
    )
    if fast:
        red_b = Reduction(*got_b)
        gone = after(gone, red_b.a, red_b.b)
        first_b = red_b.first()

    blocks = [sds((block, width), F32), *blocks[1:]]
    if fast:
        rows_a = 3 * per + width // LANES * pos_per + 16
        grads_a = [sds((n_dp, rows_a, LANES), BF16)] * 4
    else:
        grads_a = [sds((n_t, width, 3 * group), BF16), sds((win, width), BF16)]
    gi_k, gi_1, gi_x, *got_a = call(
        functools.partial(attention_back_kernel, fast),
        [*blocks, *grads_a],
        [
            ((width, win), BF16),
            ((n_t * group // HD, win, win), BF16),
            ((win, n_t * 3 * group), BF16),
            ((win, width), F32),
            ((2, width, 3 * group), BF16),
            ((win, n_t * 3 * group), BF16),
            ((n_t * group // HD, win, win), BF16),
            ((width, n_t * 3 * group), BF16),
            [2 + 2 * n_t * group // HD],
        ],
        [scal, hid, qkv, pt, gm, attn_all, gone, gnorm],
        "svhhvhvv",
        18,
        1_000_000,
    )
    leaving = jnp.concatenate([res_x[:1], gi_x[:1], res_x[1:], gi_x[1:]])
    if fast:
        keep_first, keep_rest, send_first, send_rest = got_a
        red_a = Reduction(keep_first, keep_rest, after(send_first, *first_b), send_rest)
        first_a, second_b = red_a.first(), red_b.second()
        chunk_b, chunk_a = got_b[0].shape[1:], got_a[0].shape[1:]
        before_z = [[sds(chunk, F32), sds(chunk, F32), sds((2, *chunk), BF16)] for chunk in (chunk_b, chunk_a)]
        last = [[sds(chunk, F32), sds((1, *chunk), BF16)] for chunk in (chunk_b, chunk_a)]
        own_b, far_b, odd_b = call(near_kernel, before_z[0], [], [*red_b.rest, *first_b, *second_b], "v" * 6, 8, 1_000)
        a_y, a_x = call(second_kernel, [sds((2, *chunk_a), BF16)] * 2, [], [own_b, *red_a.rest, *first_a], "avvvv", 8, 1_000)
        second_a = swap(a_y, 1, 0), swap(a_x, 0, 2)
        near_b = swap(odd_b, 2, 0)
        own_b, far_b, own_a, far_a, odd_a = call(
            far_near_kernel,
            last[0] + before_z[1],
            [],
            [own_b, far_b, near_b, *red_a.rest, *first_a, *second_a],
            "v" * 9,
            8,
            1_000,
        )
        far_b = swap(far_b, 4, 0)
        r2 = swap(after(leaving, own_a), 0, 2)
        own_a, far_a = call(far_kernel, last[1], [], [own_a, far_a, swap(odd_a, 2, 0)], "vvv", 4, 1_000)
        r2 = after(r2, far_a)
        far_a = swap(far_a, 4, 0)
    else:
        r2 = swap(leaving, 0, 2)
    r3 = swap(r2[2:], 0, 1)
    r1 = [swap(res_1, 0, 1), swap(gi_1, 0, 1)]
    masters = (attn_proj, out_proj, up_proj, down_proj, pos_table, norm_params)
    firsts = (first_attn, first_out, first_up, first_down, first_pos, first_norm)
    seconds = (second_attn, second_out, second_up, second_down, second_pos, second_norm)
    updated = [None] * 6
    token = sds((8, LANES), F32)
    done = jnp.zeros(token.shape, F32)
    if fast:
        which = (2, 3, 1)
        state = [group[i] for group in (masters, firsts, seconds) for i in which]
        new = call(
            functools.partial(rows_update_kernel, which),
            [sds(v.shape, F32) for v in state] + [token],
            [],
            [own_b, far_b, *state],
            "v" * 11,
            8,
            2_000_000_000,
        )
        for i, index in enumerate(which):
            updated[index] = new[i:9:3]
        done = new[9]
    outputs, grad_input, done = call(
        finish_kernel,
        [sds(inputs.shape, BF16), sds(inputs.shape, F32), token],
        [],
        [scal, done, res_k, gi_k, *r1, r2, r3],
        "sv" + "v" * 6,
        8,
        2_000_000_000,
    )
    if fast:
        which = (0, 4, 5)
        state = [group[i] for group in (masters, firsts, seconds) for i in which]
        new = call(
            tiles_update_kernel,
            [sds(v.shape, F32) for v in state],
            [],
            [scal, done, own_a, far_a, *state],
            "sv" + "v" * 11,
            8,
            1_000_000,
        )
        for i, index in enumerate(which):
            updated[index] = new[i::3]
    else:

        def reduced(value, own_axis):
            arrived = lax.all_to_all(value, "dp", split_axis=0, concat_axis=0, tiled=True)
            part = arrived.astype(F32).sum(axis=0).astype(BF16)
            arrived = lax.all_to_all(part, "tensor", split_axis=0, concat_axis=0, tiled=True)
            return arrived.astype(F32).sum(axis=0)

        gup, gdown, gout = got_b
        gattn, gpos = got_a
        gup, gdown, gout, gattn = [jnp.take(v, relative, axis=0) for v in (gup, gdown, gout.reshape(n_t, group, width), gattn)]
        g_up = reduced(gup.reshape(n_t, n_dp, per, inner).swapaxes(0, 1), 0)
        g_down = reduced(gdown.reshape(n_t, n_dp, inner // n_dp, width).swapaxes(0, 1), 0)
        g_out = reduced(gout.reshape(n_t, n_dp, out_per, width).swapaxes(0, 1), 0)
        g_pos = reduced(gpos.reshape(n_t, n_dp, pos_per, width).swapaxes(0, 1), 0)
        g_attn = reduced(gattn.reshape(n_t, n_dp, per, 3, group).swapaxes(0, 1), 0).swapaxes(0, 1)
        cut = gnorm[:4].reshape(4, n_dp, width // n_dp).swapaxes(0, 1).astype(BF16)
        g_norm = reduced(jnp.broadcast_to(cut[:, None], (n_dp, n_t, *cut.shape[1:])), 0)

        gradients = (g_attn, g_out, g_up, g_down, g_pos, g_norm)
        for index in range(6):
            updated[index] = adam_step(masters[index], gradients[index], firsts[index], seconds[index], RATES[index], DECAYS[index])
    return (outputs, grad_input, *[v for new in updated for v in new])


def solution(mesh):
    acts = P("dp", "tensor", None)
    attn = P(None, "dp", "tensor")
    both = P(("tensor", "dp"), None)
    up = P("dp", "tensor")
    norm = P(None, "dp")
    return jax.shard_map(
        body,
        mesh=mesh,
        in_specs=(acts, P("dp", None), acts, attn, both, up, both, both, norm, *(attn,) * 2, *(both,) * 2, *(up,) * 2, *(both,) * 4, *(norm,) * 2),
        out_specs=(acts, acts, *(attn,) * 3, *(both,) * 3, *(up,) * 3, *(both,) * 6, *(norm,) * 3),
        check_vma=False,
    )
```

time: 166 us -> 140 us (0.84)
  other arithmetic: 14.3 us -> 0.91 us
  local copies, waits for them, and re-layouts: 8.95 us -> 0.22 us
  Pallas kernels: 43.7 us -> 39.6 us
  waiting for transfers between devices: 62.1 us -> 64.8 us
  starting transfers between devices: 35.2 us -> 33.1 us
    unnamed x67 -> x38, local copies, waits for them, and re-layouts: 8.84 us -> 0.11 us
    pallas_call x4 -> x15, Pallas kernels: 43.7 us -> 39.6 us  [call(): pl.pallas_call(kernel, out_shape=outs, in_specs=[kinds[k] for k in spaces...]
    convert_element_type x4 -> x3, other arithmetic: 4.69 us -> 0.76 us  [low(): return total(*parts).astype(BF16)]
    sub x5 -> x0, other arithmetic: 3.74 us -> none  [adam_step(): weight - step_rate * (fixed_first / (jnp.sqrt(fixed_second) + ADAM_EPS) +...]
    ppermute x41 -> x43, waiting for transfers between devices: 62.1 us -> 64.8 us  [swap(): lax.ppermute(value, AXES, [(i, i ^ mask) for i in range(lax.axis_size('dp...]
    another operation x4 -> x0, other arithmetic: 2.1 us -> none  [in_order(): jnp.stack([jnp.where(cross, high[0], low[0]), jnp.where(cross, high[1], l...]
    ppermute x41 -> x43, starting transfers between devices: 35.2 us -> 33.1 us  [swap(): lax.ppermute(value, AXES, [(i, i ^ mask) for i in range(lax.axis_size('dp...]
    concatenate x3 -> x0, other arithmetic: 1.86 us -> none  [gather_z(): q = jnp.concatenate([q, swap(q, step * 2, 0)])]
  transfers between devices with their start and end apart: 41 -> 43, of which waited for: 21 -> 27; matrix products, arithmetic and copies ran while one was open for 8% -> 1% of each run, Pallas kernels for 12% -> 16%
where the time goes in v3:
time: 140 us
  waiting for transfers between devices  64.8 us (46%)
  Pallas kernels  39.6 us (28%)
  starting transfers between devices  33.1 us (24%)
    ppermute x43, waiting for transfers between devices, swap(): lax.ppermute(value, AXES, [(i, i ^ mask) for i in range(lax.axis_size('dp...  64.8 us
    pallas_call x15, Pallas kernels, call(): pl.pallas_call(kernel, out_shape=outs, in_specs=[kinds[k] for k in spaces...  39.6 us
    ppermute x43, starting transfers between devices, swap(): lax.ppermute(value, AXES, [(i, i ^ mask) for i in range(lax.axis_size('dp...  33.1 us
  transfers between devices with their start and end apart: 43, of which 27 were waited for; matrix products, arithmetic and copies ran while one was open for 1% of the time, Pallas kernels for 16%

profile of v3, /device:TPU:0, one launch (start us, length us, event | category | flops | bytes accessed | tf_op | source)
XLA Modules:
  0.0 139.8 jit_solution(5069790770750634527)
XLA Ops:
  0.7 2.0 %shard_map.356 = (bf16[1,272,128]{2,1,0:T(8,128)(2,1)S(1)}, bf16[1,144,512]{2,1,0:T(8,128)(2,1)S(1)}, bf16[4,128,512]{2,1,0:T(8,128)(2,1)S(1)}, bf16[2,128,512]{2,1,0:T(8,128)(2,1)S(1)}) custom-call(s32[2]{0:T(128)S(1)} %pad_add_fusion.scal, bf16[4,128,512]{2,1,0:T(8,128)(2,1)} %refs_0_.4, bf16[4,128,512]{2,1,0:T(8,128)(2,1)} %refs_0_.5, ...), custom_call_target="tpu_custom_call" | custom-call | flops 1000 | tf_op jit(solution)/shard_map/pallas_call | solution.py:603
  2.7 3.0 %collective-permute-start = (bf16[4,128,512]{2,1,0:T(8,128)(2,1)S(1)}, bf16[4,128,512]{2,1,0:T(8,128)(2,1)S(1)}, u32[]{:S(2)}, u32[]{:S(2)}) collective-permute-start(bf16[4,128,512]{2,1,0:T(8,128)(2,1)S(1)} %get-tuple-element.89), channel_id=1, source_target_pairs={{0,2},{1,3},{2,0},{3,1},{4,6},{5,7},{6,4},{7,5},{8,10},{9,11},{10,... | collective-permute-start | bytes 1572872 | tf_op jit(solution)/shard_map/ppermute | solution.py:58
  5.7 2.6 %collective-permute-start.3 = (bf16[1,272,128]{2,1,0:T(8,128)(2,1)S(1)}, bf16[1,272,128]{2,1,0:T(8,128)(2,1)S(1)}, u32[]{:S(2)}, u32[]{:S(2)}) collective-permute-start(bf16[1,272,128]{2,1,0:T(8,128)(2,1)S(1)} %get-tuple-element.91.own), channel_id=1, source_target_pairs={{0,16},{1,17},{2,18},{3,19},{4,20},{5,21},{6,22},{7,23},{8,24},{9,... | collective-permute-start | bytes 208904 | tf_op jit(solution)/shard_map/ppermute | solution.py:58
  8.7 6.7 %collective-permute-done.3.got = bf16[1,272,128]{2,1,0:T(8,128)(2,1)S(1)} collective-permute-done((bf16[1,272,128]{2,1,0:T(8,128)(2,1)S(1)}, bf16[1,272,128]{2,1,0:T(8,128)(2,1)S(1)}, u32[]{:S(2)}, u32[]{:S(2)}) %collective-permute-start.3) | collective-permute-done | bytes 69664 | tf_op jit(solution)/shard_map/ppermute | solution.py:58
  15.8 2.7 %collective-permute-done.12.got = bf16[1,144,512]{2,1,0:T(8,128)(2,1)S(1)} collective-permute-done((bf16[1,144,512]{2,1,0:T(8,128)(2,1)S(1)}, bf16[1,144,512]{2,1,0:T(8,128)(2,1)S(1)}, u32[]{:S(2)}, u32[]{:S(2)}) %collective-permute-start.12) | collective-permute-done | bytes 147488 | tf_op jit(solution)/shard_map/ppermute | solution.py:58
  18.5 2.8 %collective-permute-done.4.got = bf16[2,272,128]{2,1,0:T(8,128)(2,1)S(1)} collective-permute-done((bf16[2,272,128]{2,1,0:T(8,128)(2,1)S(1)}, bf16[2,272,128]{2,1,0:T(8,128)(2,1)S(1)}, u32[]{:S(2)}, u32[]{:S(2)}) %collective-permute-start.4) | collective-permute-done | bytes 139296 | tf_op jit(solution)/shard_map/ppermute | solution.py:58
  25.0 4.7 %collective-permute-done.13.got = bf16[2,144,512]{2,1,0:T(8,128)(2,1)S(1)} collective-permute-done((bf16[2,144,512]{2,1,0:T(8,128)(2,1)S(1)}, bf16[2,144,512]{2,1,0:T(8,128)(2,1)S(1)}, u32[]{:S(2)}, u32[]{:S(2)}) %collective-permute-start.13) | collective-permute-done | bytes 294944 | tf_op jit(solution)/shard_map/ppermute | solution.py:58
  30.2 2.4 %collective-permute-done.6.refs_7_ = bf16[4,272,128]{2,1,0:T(8,128)(2,1)S(1)} collective-permute-done((bf16[4,272,128]{2,1,0:T(8,128)(2,1)S(1)}, bf16[4,272,128]{2,1,0:T(8,128)(2,1)S(1)}, u32[]{:S(2)}, u32[]{:S(2)}) %collective-permute-start.6) | collective-permute-done | bytes 278560 | tf_op jit(solution)/shard_map/ppermute | solution.py:58
  34.2 4.4 %collective-permute-done.10.refs_11_ = bf16[4,272,128]{2,1,0:T(8,128)(2,1)S(1)} collective-permute-done((bf16[4,272,128]{2,1,0:T(8,128)(2,1)S(1)}, bf16[4,272,128]{2,1,0:T(8,128)(2,1)S(1)}, u32[]{:S(2)}, u32[]{:S(2)}) %collective-permute-start.10) | collective-permute-done | bytes 278560 | tf_op jit(solution)/shard_map/ppermute | solution.py:58
  41.7 8.9 %shard_map.359 = (f32[512,512]{1,0:T(8,128)S(1)}, bf16[512,1536]{1,0:T(8,128)(2,1)}, bf16[8,512,512]{2,1,0:T(8,128)(2,1)}, bf16[512,512]{1,0:T(8,128)(2,1)S(1)},...) custom-call(s32[2]{0:T(128)S(1)} %pad_add_fusion.scal, bf16[4,128,512]{2,1,0:T(8,128)(2,1)} %refs_0_.4, ...), custom_call_target="tpu_custom_call" | custom-call | flops 1000000 | tf_op jit(solution)/shard_map/pallas_call | solution.py:603
  53.3 6.5 %collective-permute-done.19.refs_13_ = bf16[2,144,512]{2,1,0:T(8,128)(2,1)S(1)} collective-permute-done((bf16[2,144,512]{2,1,0:T(8,128)(2,1)S(1)}, bf16[2,144,512]{2,1,0:T(8,128)(2,1)S(1)}, u32[]{:S(2)}, u32[]{:S(2)}) %collective-permute-start.19) | collective-permute-done | bytes 294944 | tf_op jit(solution)/shard_map/ppermute | solution.py:58
  59.8 1.9 %collective-permute-done.21.refs_15_ = bf16[2,144,512]{2,1,0:T(8,128)(2,1)S(1)} collective-permute-done((bf16[2,144,512]{2,1,0:T(8,128)(2,1)S(1)}, bf16[2,144,512]{2,1,0:T(8,128)(2,1)S(1)}, u32[]{:S(2)}, u32[]{:S(2)}) %collective-permute-start.21) | collective-permute-done | bytes 294944 | tf_op jit(solution)/shard_map/ppermute | solution.py:58
  63.2 13.0 %shard_map.362 = (bf16[128,512]{1,0:T(8,128)(2,1)S(1)}, bf16[1,128,512]{2,1,0:T(8,128)(2,1)S(1)}, bf16[2,128,512]{2,1,0:T(8,128)(2,1)S(1)}, f32[512,512]{1,0:T(8...) custom-call(s32[2]{0:T(128)S(1)} %pad_add_fusion.scal, ...), custom_call_target="tpu_custom_call" | custom-call | flops 1000000 | tf_op jit(solution)/shard_map/pallas_call | solution.py:603
  76.9 2.3 %collective-permute-done.24 = bf16[8,144,512]{2,1,0:T(8,128)(2,1)S(1)} collective-permute-done((bf16[8,144,512]{2,1,0:T(8,128)(2,1)S(1)}, bf16[8,144,512]{2,1,0:T(8,128)(2,1)S(1)}, u32[]{:S(2)}, u32[]{:S(2)}) %collective-permute-start.24) | collective-permute-done | bytes 1179680 | tf_op jit(solution)/shard_map/ppermute | solution.py:58
  80.7 10.7 %shard_map.364 = (f32[128,512]{1,0:T(8,128)S(1)}, bf16[1,128,512]{2,1,0:T(8,128)(2,1)S(1)}, bf16[2,128,512]{2,1,0:T(8,128)(2,1)S(1)}, bf16[8,272,128]{2,1,0:T(8,...) custom-call(s32[2]{0:T(128)S(1)} %pad_add_fusion.scal, ...), custom_call_target="tpu_custom_call" | custom-call | flops 1000000 | tf_op jit(solution)/shard_map/pallas_call | solution.py:603
  91.4 3.6 %collective-permute-done.26.y = bf16[4,144,512]{2,1,0:T(8,128)(2,1)S(1)} collective-permute-done((bf16[4,144,512]{2,1,0:T(8,128)(2,1)S(1)}, bf16[4,144,512]{2,1,0:T(8,128)(2,1)S(1)}, u32[]{:S(2)}, u32[]{:S(2)}) %collective-permute-start.26) | collective-permute-done | bytes 589856 | tf_op jit(solution)/shard_map/ppermute | solution.py:58
  100.4 5.6 %collective-permute-done.27.x2 = bf16[2,144,512]{2,1,0:T(8,128)(2,1)S(1)} collective-permute-done((bf16[2,144,512]{2,1,0:T(8,128)(2,1)S(1)}, bf16[2,144,512]{2,1,0:T(8,128)(2,1)S(1)}, u32[]{:S(2)}, u32[]{:S(2)}) %collective-permute-start.27) | collective-permute-done | bytes 294944 | tf_op jit(solution)/shard_map/ppermute | solution.py:58
  107.8 2.0 %collective-permute-start.29 = (bf16[2,144,512]{2,1,0:T(8,128)(2,1)S(1)}, bf16[2,144,512]{2,1,0:T(8,128)(2,1)S(1)}, u32[]{:S(2)}, u32[]{:S(2)}) collective-permute-start(bf16[2,144,512]{2,1,0:T(8,128)(2,1)S(1)} %get-tuple-element.106), channel_id=1, source_target_pairs={{0,8},{1,9},{2,10},{3,11},{4,12},{5,13},{6,14},{7,15},{8,0},{9,1},... | collective-permute-start | bytes 884744 | tf_op jit(solution)/shard_map/ppermute | solution.py:58
  114.6 2.8 %collective-permute-done.34.x2 = bf16[2,272,128]{2,1,0:T(8,128)(2,1)S(1)} collective-permute-done((bf16[2,272,128]{2,1,0:T(8,128)(2,1)S(1)}, bf16[2,272,128]{2,1,0:T(8,128)(2,1)S(1)}, u32[]{:S(2)}, u32[]{:S(2)}) %collective-permute-start.34) | collective-permute-done | bytes 139296 | tf_op jit(solution)/shard_map/ppermute | solution.py:58
  118.8 2.0 %collective-permute-start.40 = (bf16[2,272,128]{2,1,0:T(8,128)(2,1)S(1)}, bf16[2,272,128]{2,1,0:T(8,128)(2,1)S(1)}, u32[]{:S(2)}, u32[]{:S(2)}) collective-permute-start(bf16[2,272,128]{2,1,0:T(8,128)(2,1)S(1)} %get-tuple-element.133), channel_id=1, source_target_pairs={{0,8},{1,9},{2,10},{3,11},{4,12},{5,13},{6,14},{7,15},{8,0},{9,1},... | collective-permute-start | bytes 417800 | tf_op jit(solution)/shard_map/ppermute | solution.py:58
  120.8 1.8 %collective-permute-start.36 = (bf16[1,144,512]{2,1,0:T(8,128)(2,1)S(1)}, bf16[1,144,512]{2,1,0:T(8,128)(2,1)S(1)}, u32[]{:S(2)}, u32[]{:S(2)}) collective-permute-start(bf16[1,144,512]{2,1,0:T(8,128)(2,1)S(1)} %get-tuple-element.122), channel_id=1, source_target_pairs={{0,16},{1,17},{2,18},{3,19},{4,20},{5,21},{6,22},{7,23},{8,24},{9,... | collective-permute-start | bytes 442376 | tf_op jit(solution)/shard_map/ppermute | solution.py:58
  124.3 5.3 %collective-permute-done.39.r2 = bf16[4,128,512]{2,1,0:T(8,128)(2,1)S(1)} collective-permute-done((bf16[4,128,512]{2,1,0:T(8,128)(2,1)S(1)}, bf16[4,128,512]{2,1,0:T(8,128)(2,1)S(1)}, u32[]{:S(2)}, u32[]{:S(2)}) %collective-permute-start.39) | collective-permute-done | bytes 524320 | tf_op jit(solution)/shard_map/ppermute | solution.py:58
  130.3 3.7 %collective-permute-start.42 = (bf16[1,272,128]{2,1,0:T(8,128)(2,1)S(1)}, bf16[1,272,128]{2,1,0:T(8,128)(2,1)S(1)}, u32[]{:S(2)}, u32[]{:S(2)}) collective-permute-start(bf16[1,272,128]{2,1,0:T(8,128)(2,1)S(1)} %get-tuple-element.134), channel_id=1, source_target_pairs={{0,16},{1,17},{2,18},{3,19},{4,20},{5,21},{6,22},{7,23},{8,24},{9,... | collective-permute-start | bytes 208904 | tf_op jit(solution)/shard_map/ppermute | solution.py:58
  135.3 1.8 %shard_map.369 = (bf16[4,128,512]{2,1,0:T(8,128)(2,1)}, f32[4,128,512]{2,1,0:T(8,128)}, f32[8,128]{1,0:T(8,128)S(1)}) custom-call(s32[2]{0:T(128)S(1)} %pad_add_fusion.scal, f32[8,128]{1,0:T(8,128)S(1)} %get-tuple-element.123.done, bf16[128,512]{1,0:T(8,128)(2,1)S(1)} %get-tuple-element.124.res_k, f32[128,512]{1,0:T(8,128)S(1)} %get-tuple-element.125.gi_k, ...), custom_call_target="tpu_custom_call" | custom-call | flops 2000000000 | tf_op jit(solution)/shard_map/pallas_call | solution.py:603
  (126 shorter events, 35.2 us)
Async XLA Ops:
  2.7 29.9 %collective-permute-start = (bf16[4,128,512]{2,1,0:T(8,128)(2,1)S(1)}, bf16[4,128,512]{2,1,0:T(8,128)(2,1)S(1)}, u32[]{:S(2)}, u32[]{:S(2)}) collective-permute-start(bf16[4,128,512]{2,1,0:T(8,128)(2,1)S(1)} %get-tuple-element.89), channel_id=1, source_target_pairs={{0,2},{1,3},{2,0},{3,1},{4,6},{5,7},{6,4},{7,5},{8,10},{9,11},{10,... | collective-permute-start | bytes 1572872 | tf_op jit(solution)/shard_map/ppermute | solution.py:58
  5.7 9.7 %collective-permute-start.3 = (bf16[1,272,128]{2,1,0:T(8,128)(2,1)S(1)}, bf16[1,272,128]{2,1,0:T(8,128)(2,1)S(1)}, u32[]{:S(2)}, u32[]{:S(2)}) collective-permute-start(bf16[1,272,128]{2,1,0:T(8,128)(2,1)S(1)} %get-tuple-element.91.own), channel_id=1, source_target_pairs={{0,16},{1,17},{2,18},{3,19},{4,20},{5,21},{6,22},{7,23},{8,24},{9,... | collective-permute-start | bytes 208904 | tf_op jit(solution)/shard_map/ppermute | solution.py:58
  8.3 10.1 %collective-permute-start.12 = (bf16[1,144,512]{2,1,0:T(8,128)(2,1)S(1)}, bf16[1,144,512]{2,1,0:T(8,128)(2,1)S(1)}, u32[]{:S(2)}, u32[]{:S(2)}) collective-permute-start(bf16[1,144,512]{2,1,0:T(8,128)(2,1)S(1)} %get-tuple-element.95.own), channel_id=1, source_target_pairs={{0,16},{1,17},{2,18},{3,19},{4,20},{5,21},{6,22},{7,23},{8,24},{9,... | collective-permute-start | bytes 442376 | tf_op jit(solution)/shard_map/ppermute | solution.py:58
  21.4 8.3 %collective-permute-start.13 = (bf16[2,144,512]{2,1,0:T(8,128)(2,1)S(1)}, bf16[2,144,512]{2,1,0:T(8,128)(2,1)S(1)}, u32[]{:S(2)}, u32[]{:S(2)}) collective-permute-start(bf16[2,144,512]{2,1,0:T(8,128)(2,1)S(1)} %shard_map.360.own), channel_id=1, source_target_pairs={{0,8},{1,9},{2,10},{3,11},{4,12},{5,13},{6,14},{7,15},{8,0},{9,1},... | collective-permute-start | bytes 884744 | tf_op jit(solution)/shard_map/ppermute | solution.py:58
  21.5 8.8 %collective-permute-start.8 = (bf16[4,272,128]{2,1,0:T(8,128)(2,1)S(1)}, bf16[4,272,128]{2,1,0:T(8,128)(2,1)S(1)}, u32[]{:S(2)}, u32[]{:S(2)}) collective-permute-start(bf16[4,272,128]{2,1,0:T(8,128)(2,1)S(1)} %shard_map.358.refs_5_), channel_id=1, source_target_pairs={{0,4},{1,5},{2,6},{3,7},{4,0},{5,1},{6,2},{7,3},{8,12},{9,13},{10,... | collective-permute-start | bytes 835592 | tf_op jit(solution)/shard_map/ppermute | solution.py:58
  23.0 9.6 %collective-permute-start.6 = (bf16[4,272,128]{2,1,0:T(8,128)(2,1)S(1)}, bf16[4,272,128]{2,1,0:T(8,128)(2,1)S(1)}, u32[]{:S(2)}, u32[]{:S(2)}) collective-permute-start(bf16[4,272,128]{2,1,0:T(8,128)(2,1)S(1)} %shard_map.358.refs_5_), channel_id=1, source_target_pairs={{0,2},{1,3},{2,0},{3,1},{4,6},{5,7},{6,4},{7,5},{8,10},{9,11},{10,... | collective-permute-start | bytes 835592 | tf_op jit(solution)/shard_map/ppermute | solution.py:58
  23.6 15.0 %collective-permute-start.10 = (bf16[4,272,128]{2,1,0:T(8,128)(2,1)S(1)}, bf16[4,272,128]{2,1,0:T(8,128)(2,1)S(1)}, u32[]{:S(2)}, u32[]{:S(2)}) collective-permute-start(bf16[4,272,128]{2,1,0:T(8,128)(2,1)S(1)} %shard_map.358.refs_5_), channel_id=1, source_target_pairs={{0,6},{1,7},{2,4},{3,5},{4,2},{5,3},{6,0},{7,1},{8,14},{9,15},{10,... | collective-permute-start | bytes 835592 | tf_op jit(solution)/shard_map/ppermute | solution.py:58
  32.6 17.9 %collective-permute-start.17 = (bf16[4,144,512]{2,1,0:T(8,128)(2,1)S(1)}, bf16[4,144,512]{2,1,0:T(8,128)(2,1)S(1)}, u32[]{:S(2)}, u32[]{:S(2)}) collective-permute-start(bf16[4,144,512]{2,1,0:T(8,128)(2,1)S(1)} %shard_map.361.refs_7_), channel_id=1, source_target_pairs={{0,4},{1,5},{2,6},{3,7},{4,0},{5,1},{6,2},{7,3},{8,12},{9,13},{10,... | collective-permute-start | bytes 1769480 | tf_op jit(solution)/shard_map/ppermute | solution.py:58
  33.1 17.5 %collective-permute-start.15 = (bf16[4,144,512]{2,1,0:T(8,128)(2,1)S(1)}, bf16[4,144,512]{2,1,0:T(8,128)(2,1)S(1)}, u32[]{:S(2)}, u32[]{:S(2)}) collective-permute-start(bf16[4,144,512]{2,1,0:T(8,128)(2,1)S(1)} %shard_map.361.refs_7_), channel_id=1, source_target_pairs={{0,2},{1,3},{2,0},{3,1},{4,6},{5,7},{6,4},{7,5},{8,10},{9,11},{10,... | collective-permute-start | bytes 1769480 | tf_op jit(solution)/shard_map/ppermute | solution.py:58
  40.5 21.1 %collective-permute-start.14 = (bf16[4,144,512]{2,1,0:T(8,128)(2,1)S(1)}, bf16[4,144,512]{2,1,0:T(8,128)(2,1)S(1)}, u32[]{:S(2)}, u32[]{:S(2)}) collective-permute-start(bf16[4,144,512]{2,1,0:T(8,128)(2,1)S(1)} %shard_map.361.refs_7_), channel_id=1, source_target_pairs={{0,1},{1,0},{2,3},{3,2},{4,5},{5,4},{6,7},{7,6},{8,9},{9,8},{10,11... | collective-permute-start | bytes 1769480 | tf_op jit(solution)/shard_map/ppermute | solution.py:58
  50.6 9.1 %collective-permute-start.19 = (bf16[2,144,512]{2,1,0:T(8,128)(2,1)S(1)}, bf16[2,144,512]{2,1,0:T(8,128)(2,1)S(1)}, u32[]{:S(2)}, u32[]{:S(2)}) collective-permute-start(bf16[2,144,512]{2,1,0:T(8,128)(2,1)S(1)} %slice.89), channel_id=1, source_target_pairs={{0,4},{1,5},{2,6},{3,7},{4,0},{5,1},{6,2},{7,3},{8,12},{9,13},{10,... | collective-permute-start | bytes 884744 | tf_op jit(solution)/shard_map/ppermute | solution.py:58
  52.2 9.4 %collective-permute-start.18 = (bf16[4,144,512]{2,1,0:T(8,128)(2,1)S(1)}, bf16[4,144,512]{2,1,0:T(8,128)(2,1)S(1)}, u32[]{:S(2)}, u32[]{:S(2)}) collective-permute-start(bf16[4,144,512]{2,1,0:T(8,128)(2,1)S(1)} %collective-permute-done.17.refs_11_), channel_id=1, source_target_pairs={{0,1},{1,0},{2,3},{3,2},{4,5},{5,4},{6,7},{7,6},{8,9},{9,8},{10,11... | collective-permute-start | bytes 1769480 | tf_op jit(solution)/shard_map/ppermute | solution.py:58
  52.2 9.4 %collective-permute-start.16 = (bf16[4,144,512]{2,1,0:T(8,128)(2,1)S(1)}, bf16[4,144,512]{2,1,0:T(8,128)(2,1)S(1)}, u32[]{:S(2)}, u32[]{:S(2)}) collective-permute-start(bf16[4,144,512]{2,1,0:T(8,128)(2,1)S(1)} %collective-permute-done.15.refs_9_), channel_id=1, source_target_pairs={{0,1},{1,0},{2,3},{3,2},{4,5},{5,4},{6,7},{7,6},{8,9},{9,8},{10,11... | collective-permute-start | bytes 1769480 | tf_op jit(solution)/shard_map/ppermute | solution.py:58
  52.7 8.9 %collective-permute-start.21 = (bf16[2,144,512]{2,1,0:T(8,128)(2,1)S(1)}, bf16[2,144,512]{2,1,0:T(8,128)(2,1)S(1)}, u32[]{:S(2)}, u32[]{:S(2)}) collective-permute-start(bf16[2,144,512]{2,1,0:T(8,128)(2,1)S(1)} %slice.90), channel_id=1, source_target_pairs={{0,2},{1,3},{2,0},{3,1},{4,6},{5,7},{6,4},{7,5},{8,10},{9,11},{10,... | collective-permute-start | bytes 884744 | tf_op jit(solution)/shard_map/ppermute | solution.py:58
  76.5 19.3 %collective-permute-start.23 = (bf16[8,144,512]{2,1,0:T(8,128)(2,1)S(1)}, bf16[8,144,512]{2,1,0:T(8,128)(2,1)S(1)}, u32[]{:S(2)}, u32[]{:S(2)}) collective-permute-start(bf16[8,144,512]{2,1,0:T(8,128)(2,1)S(1)} %get-tuple-element.101), channel_id=1, source_target_pairs={{0,1},{1,0},{2,3},{3,2},{4,5},{5,4},{6,7},{7,6},{8,9},{9,8},{10,11... | collective-permute-start | bytes 3538952 | tf_op jit(solution)/shard_map/ppermute | solution.py:58
  79.6 15.4 %collective-permute-start.26 = (bf16[4,144,512]{2,1,0:T(8,128)(2,1)S(1)}, bf16[4,144,512]{2,1,0:T(8,128)(2,1)S(1)}, u32[]{:S(2)}, u32[]{:S(2)}) collective-permute-start(bf16[4,144,512]{2,1,0:T(8,128)(2,1)S(1)} %get-tuple-element.160), channel_id=1, source_target_pairs={{0,4},{1,5},{2,6},{3,7},{4,0},{5,1},{6,2},{7,3},{8,12},{9,13},{10,... | collective-permute-start | bytes 1769480 | tf_op jit(solution)/shard_map/ppermute | solution.py:58
  80.2 15.1 %collective-permute-start.25 = (bf16[4,144,512]{2,1,0:T(8,128)(2,1)S(1)}, bf16[4,144,512]{2,1,0:T(8,128)(2,1)S(1)}, u32[]{:S(2)}, u32[]{:S(2)}) collective-permute-start(bf16[4,144,512]{2,1,0:T(8,128)(2,1)S(1)} %get-tuple-element.161), channel_id=1, source_target_pairs={{0,2},{1,3},{2,0},{3,1},{4,6},{5,7},{6,4},{7,5},{8,10},{9,11},{10,... | collective-permute-start | bytes 1769480 | tf_op jit(solution)/shard_map/ppermute | solution.py:58
  95.3 14.5 %collective-permute-start.30 = (bf16[8,272,128]{2,1,0:T(8,128)(2,1)S(1)}, bf16[8,272,128]{2,1,0:T(8,128)(2,1)S(1)}, u32[]{:S(2)}, u32[]{:S(2)}) collective-permute-start(bf16[8,272,128]{2,1,0:T(8,128)(2,1)S(1)} %get-tuple-element.115), channel_id=1, source_target_pairs={{0,1},{1,0},{2,3},{3,2},{4,5},{5,4},{6,7},{7,6},{8,9},{9,8},{10,11... | collective-permute-start | bytes 1671176 | tf_op jit(solution)/shard_map/ppermute | solution.py:58
  96.0 9.9 %collective-permute-start.27 = (bf16[2,144,512]{2,1,0:T(8,128)(2,1)S(1)}, bf16[2,144,512]{2,1,0:T(8,128)(2,1)S(1)}, u32[]{:S(2)}, u32[]{:S(2)}) collective-permute-start(bf16[2,144,512]{2,1,0:T(8,128)(2,1)S(1)} %get-tuple-element.159), channel_id=1, source_target_pairs={{0,4},{1,5},{2,6},{3,7},{4,0},{5,1},{6,2},{7,3},{8,12},{9,13},{10,... | collective-permute-start | bytes 884744 | tf_op jit(solution)/shard_map/ppermute | solution.py:58
  97.6 9.9 %collective-permute-start.28 = (bf16[2,144,512]{2,1,0:T(8,128)(2,1)S(1)}, bf16[2,144,512]{2,1,0:T(8,128)(2,1)S(1)}, u32[]{:S(2)}, u32[]{:S(2)}) collective-permute-start(bf16[2,144,512]{2,1,0:T(8,128)(2,1)S(1)} %get-tuple-element.158), channel_id=1, source_target_pairs={{0,2},{1,3},{2,0},{3,1},{4,6},{5,7},{6,4},{7,5},{8,10},{9,11},{10,... | collective-permute-start | bytes 884744 | tf_op jit(solution)/shard_map/ppermute | solution.py:58
  98.3 12.7 %collective-permute-start.33 = (bf16[4,272,128]{2,1,0:T(8,128)(2,1)S(1)}, bf16[4,272,128]{2,1,0:T(8,128)(2,1)S(1)}, u32[]{:S(2)}, u32[]{:S(2)}) collective-permute-start(bf16[4,272,128]{2,1,0:T(8,128)(2,1)S(1)} %get-tuple-element.162), channel_id=1, source_target_pairs={{0,4},{1,5},{2,6},{3,7},{4,0},{5,1},{6,2},{7,3},{8,12},{9,13},{10,... | collective-permute-start | bytes 835592 | tf_op jit(solution)/shard_map/ppermute | solution.py:58
  98.9 13.3 %collective-permute-start.32 = (bf16[4,272,128]{2,1,0:T(8,128)(2,1)S(1)}, bf16[4,272,128]{2,1,0:T(8,128)(2,1)S(1)}, u32[]{:S(2)}, u32[]{:S(2)}) collective-permute-start(bf16[4,272,128]{2,1,0:T(8,128)(2,1)S(1)} %get-tuple-element.163), channel_id=1, source_target_pairs={{0,2},{1,3},{2,0},{3,1},{4,6},{5,7},{6,4},{7,5},{8,10},{9,11},{10,... | collective-permute-start | bytes 835592 | tf_op jit(solution)/shard_map/ppermute | solution.py:58
  118.2 11.4 %collective-permute-start.39 = (bf16[4,128,512]{2,1,0:T(8,128)(2,1)S(1)}, bf16[4,128,512]{2,1,0:T(8,128)(2,1)S(1)}, u32[]{:S(2)}, u32[]{:S(2)}) collective-permute-start(bf16[4,128,512]{2,1,0:T(8,128)(2,1)S(1)} %pad_maximum_fusion), channel_id=1, source_target_pairs={{0,2},{1,3},{2,0},{3,1},{4,6},{5,7},{6,4},{7,5},{8,10},{9,11},{10,... | collective-permute-start | bytes 1572872 | tf_op jit(solution)/shard_map/ppermute | solution.py:58
  120.8 13.2 %collective-permute-start.36 = (bf16[1,144,512]{2,1,0:T(8,128)(2,1)S(1)}, bf16[1,144,512]{2,1,0:T(8,128)(2,1)S(1)}, u32[]{:S(2)}, u32[]{:S(2)}) collective-permute-start(bf16[1,144,512]{2,1,0:T(8,128)(2,1)S(1)} %get-tuple-element.122), channel_id=1, source_target_pairs={{0,16},{1,17},{2,18},{3,19},{4,20},{5,21},{6,22},{7,23},{8,24},{9,... | collective-permute-start | bytes 442376 | tf_op jit(solution)/shard_map/ppermute | solution.py:58
  (38 other events, 274.5 us)

commit v4 on v3

--- a/solution.py
+++ b/solution.py
@@ -296,9 +296,10 @@
 
         def gelu(at, g=g):
             v = a_s[g % 2, at, :]
-            t = jnp.tanh(GELU_A * (v + GELU_B * v * v * v))
-            act_s[g, at, :] = (0.5 * v * (1.0 + t)).astype(BF16)
-            dg_s[g, at, :] = 0.5 * (1.0 + t) + 0.5 * v * (1.0 - t * t) * (GELU_A * (1.0 + 3.0 * GELU_B * v * v))
+            square = v * v
+            half = 0.5 + 0.5 * jnp.tanh(v * (GELU_A + GELU_A * GELU_B * square))
+            act_s[g, at, :] = (v * half).astype(BF16)
+            dg_s[g, at, :] = half + (half - half * half) * (v * (2.0 * GELU_A + 6.0 * GELU_A * GELU_B * square))
 
         chunks(gelu)
         n1_s[...] += mm(act_s[g], down_s[g])
@@ -497,7 +498,8 @@
 
 
 def tiles_update_kernel(scal, done, own, far, *refs):
-    del done
+    *refs, token = refs
+    token[...] = done[...]
     attn, pos, norm = refs[0::3], refs[1::3], refs[2::3]
     grad = total(own[...], far[0])
     per = attn[0].shape[1]
@@ -512,8 +514,8 @@
     update(norm, half, RATES[5], DECAYS[5])
 
 
-def finish_kernel(scal, done, res_k, gi_k, res_1, gi_1, r2, r3, res_o, gi_o, token):
-    token[...] = done[...]
+def finish_kernel(scal, done, res_k, gi_k, res_1, gi_1, r2, r3, res_o, gi_o):
+    del done
     me_t = scal[1]
     for r, (res, gi) in enumerate(((res_k[...], gi_k[...]), (res_1[0], gi_1[0]), (r2[0], r2[1]), (r3[0], r3[1]))):
         res_o[me_t ^ r] = res
@@ -768,7 +770,7 @@
         18,
         1_000_000,
     )
-    leaving = jnp.concatenate([res_x[:1], gi_x[:1], res_x[1:], gi_x[1:]])
+    leaving = [jnp.concatenate([res_x[i : i + 1], gi_x[i : i + 1]]) for i in range(2)]
     if fast:
         keep_first, keep_rest, send_first, send_rest = got_a
         red_a = Reduction(keep_first, keep_rest, after(send_first, *first_b), send_rest)
@@ -790,13 +792,11 @@
             1_000,
         )
         far_b = swap(far_b, 4, 0)
-        r2 = swap(after(leaving, own_a), 0, 2)
+        r2, r3 = [swap(after(v, own_a), 0, m) for v, m in zip(leaving, (2, 3), strict=True)]
         own_a, far_a = call(far_kernel, last[1], [], [own_a, far_a, swap(odd_a, 2, 0)], "vvv", 4, 1_000)
-        r2 = after(r2, far_a)
         far_a = swap(far_a, 4, 0)
     else:
-        r2 = swap(leaving, 0, 2)
-    r3 = swap(r2[2:], 0, 1)
+        r2, r3 = [swap(v, 0, m) for v, m in zip(leaving, (2, 3), strict=True)]
     r1 = [swap(res_1, 0, 1), swap(gi_1, 0, 1)]
     masters = (attn_proj, out_proj, up_proj, down_proj, pos_table, norm_params)
     firsts = (first_attn, first_out, first_up, first_down, first_pos, first_norm)
@@ -819,21 +819,12 @@
         for i, index in enumerate(which):
             updated[index] = new[i:9:3]
         done = new[9]
-    outputs, grad_input, done = call(
-        finish_kernel,
-        [sds(inputs.shape, BF16), sds(inputs.shape, F32), token],
-        [],
-        [scal, done, res_k, gi_k, *r1, r2, r3],
-        "sv" + "v" * 6,
-        8,
-        2_000_000_000,
-    )
     if fast:
         which = (0, 4, 5)
         state = [group[i] for group in (masters, firsts, seconds) for i in which]
         new = call(
             tiles_update_kernel,
-            [sds(v.shape, F32) for v in state],
+            [sds(v.shape, F32) for v in state] + [token],
             [],
             [scal, done, own_a, far_a, *state],
             "sv" + "v" * 11,
@@ -841,8 +832,18 @@
             1_000_000,
         )
         for i, index in enumerate(which):
-            updated[index] = new[i::3]
-    else:
+            updated[index] = new[i:9:3]
+        done = new[9]
+    outputs, grad_input = call(
+        finish_kernel,
+        [sds(inputs.shape, BF16), sds(inputs.shape, F32)],
+        [],
+        [scal, done, res_k, gi_k, *r1, r2, r3],
+        "sv" + "v" * 6,
+        8,
+        1_000,
+    )
+    if not fast:
 
         def reduced(value, own_axis):
             arrived = lax.all_to_all(value, "dp", split_axis=0, concat_axis=0, tiled=True)

time: 140 us -> 135 us (0.964)
  waiting for transfers between devices: 64.8 us -> 60.6 us
    ppermute x43, waiting for transfers between devices: 64.8 us -> 60.6 us  [swap(): lax.ppermute(value, AXES, [(i, i ^ mask) for i in range(lax.axis_size('dp...]
  transfers between devices with their start and end apart: 43 -> 43, of which waited for: 27 -> 26; matrix products, arithmetic and copies ran while one was open for 1% -> 1% of each run, Pallas kernels for 16% -> 17%
where the time goes in v4:
time: 135 us
  waiting for transfers between devices  60.6 us (45%)
  Pallas kernels  39.4 us (29%)
  starting transfers between devices  32.3 us (24%)
    ppermute x43, waiting for transfers between devices, swap(): lax.ppermute(value, AXES, [(i, i ^ mask) for i in range(lax.axis_size('dp...  60.6 us
    pallas_call x15, Pallas kernels, call(): pl.pallas_call(kernel, out_shape=outs, in_specs=[kinds[k] for k in spaces...  39.4 us
    ppermute x43, starting transfers between devices, swap(): lax.ppermute(value, AXES, [(i, i ^ mask) for i in range(lax.axis_size('dp...  32.3 us
  transfers between devices with their start and end apart: 43, of which 26 were waited for; matrix products, arithmetic and copies ran while one was open for 1% of the time, Pallas kernels for 17%

profile of v4, /device:TPU:0, one launch (start us, length us, event | category | flops | bytes accessed | tf_op | source)
XLA Modules:
  0.0 134.6 jit_solution(9784318099220519707)
XLA Ops:
  0.7 2.0 %shard_map.356 = (bf16[1,272,128]{2,1,0:T(8,128)(2,1)S(1)}, bf16[1,144,512]{2,1,0:T(8,128)(2,1)S(1)}, bf16[4,128,512]{2,1,0:T(8,128)(2,1)S(1)}, bf16[2,128,512]{2,1,0:T(8,128)(2,1)S(1)}) custom-call(s32[2]{0:T(128)S(1)} %pad_add_fusion.scal, bf16[4,128,512]{2,1,0:T(8,128)(2,1)} %refs_0_.4, bf16[4,128,512]{2,1,0:T(8,128)(2,1)} %refs_0_.5, ...), custom_call_target="tpu_custom_call" | custom-call | flops 1000 | tf_op jit(solution)/shard_map/pallas_call | solution.py:605
  2.7 3.0 %collective-permute-start = (bf16[4,128,512]{2,1,0:T(8,128)(2,1)S(1)}, bf16[4,128,512]{2,1,0:T(8,128)(2,1)S(1)}, u32[]{:S(2)}, u32[]{:S(2)}) collective-permute-start(bf16[4,128,512]{2,1,0:T(8,128)(2,1)S(1)} %get-tuple-element.89), channel_id=1, source_target_pairs={{0,2},{1,3},{2,0},{3,1},{4,6},{5,7},{6,4},{7,5},{8,10},{9,11},{10,... | collective-permute-start | bytes 1572872 | tf_op jit(solution)/shard_map/ppermute | solution.py:58
  5.7 2.6 %collective-permute-start.3 = (bf16[1,272,128]{2,1,0:T(8,128)(2,1)S(1)}, bf16[1,272,128]{2,1,0:T(8,128)(2,1)S(1)}, u32[]{:S(2)}, u32[]{:S(2)}) collective-permute-start(bf16[1,272,128]{2,1,0:T(8,128)(2,1)S(1)} %get-tuple-element.91.own), channel_id=1, source_target_pairs={{0,16},{1,17},{2,18},{3,19},{4,20},{5,21},{6,22},{7,23},{8,24},{9,... | collective-permute-start | bytes 208904 | tf_op jit(solution)/shard_map/ppermute | solution.py:58
  8.7 6.7 %collective-permute-done.3.got = bf16[1,272,128]{2,1,0:T(8,128)(2,1)S(1)} collective-permute-done((bf16[1,272,128]{2,1,0:T(8,128)(2,1)S(1)}, bf16[1,272,128]{2,1,0:T(8,128)(2,1)S(1)}, u32[]{:S(2)}, u32[]{:S(2)}) %collective-permute-start.3) | collective-permute-done | bytes 69664 | tf_op jit(solution)/shard_map/ppermute | solution.py:58
  15.8 2.7 %collective-permute-done.12.got = bf16[1,144,512]{2,1,0:T(8,128)(2,1)S(1)} collective-permute-done((bf16[1,144,512]{2,1,0:T(8,128)(2,1)S(1)}, bf16[1,144,512]{2,1,0:T(8,128)(2,1)S(1)}, u32[]{:S(2)}, u32[]{:S(2)}) %collective-permute-start.12) | collective-permute-done | bytes 147488 | tf_op jit(solution)/shard_map/ppermute | solution.py:58
  18.5 2.8 %collective-permute-done.4.got = bf16[2,272,128]{2,1,0:T(8,128)(2,1)S(1)} collective-permute-done((bf16[2,272,128]{2,1,0:T(8,128)(2,1)S(1)}, bf16[2,272,128]{2,1,0:T(8,128)(2,1)S(1)}, u32[]{:S(2)}, u32[]{:S(2)}) %collective-permute-start.4) | collective-permute-done | bytes 139296 | tf_op jit(solution)/shard_map/ppermute | solution.py:58
  25.0 4.7 %collective-permute-done.13.got = bf16[2,144,512]{2,1,0:T(8,128)(2,1)S(1)} collective-permute-done((bf16[2,144,512]{2,1,0:T(8,128)(2,1)S(1)}, bf16[2,144,512]{2,1,0:T(8,128)(2,1)S(1)}, u32[]{:S(2)}, u32[]{:S(2)}) %collective-permute-start.13) | collective-permute-done | bytes 294944 | tf_op jit(solution)/shard_map/ppermute | solution.py:58
  30.2 2.4 %collective-permute-done.6.refs_7_ = bf16[4,272,128]{2,1,0:T(8,128)(2,1)S(1)} collective-permute-done((bf16[4,272,128]{2,1,0:T(8,128)(2,1)S(1)}, bf16[4,272,128]{2,1,0:T(8,128)(2,1)S(1)}, u32[]{:S(2)}, u32[]{:S(2)}) %collective-permute-start.6) | collective-permute-done | bytes 278560 | tf_op jit(solution)/shard_map/ppermute | solution.py:58
  34.2 4.4 %collective-permute-done.10.refs_11_ = bf16[4,272,128]{2,1,0:T(8,128)(2,1)S(1)} collective-permute-done((bf16[4,272,128]{2,1,0:T(8,128)(2,1)S(1)}, bf16[4,272,128]{2,1,0:T(8,128)(2,1)S(1)}, u32[]{:S(2)}, u32[]{:S(2)}) %collective-permute-start.10) | collective-permute-done | bytes 278560 | tf_op jit(solution)/shard_map/ppermute | solution.py:58
  41.7 8.9 %shard_map.359 = (f32[512,512]{1,0:T(8,128)S(1)}, bf16[512,1536]{1,0:T(8,128)(2,1)}, bf16[8,512,512]{2,1,0:T(8,128)(2,1)}, bf16[512,512]{1,0:T(8,128)(2,1)S(1)},...) custom-call(s32[2]{0:T(128)S(1)} %pad_add_fusion.scal, bf16[4,128,512]{2,1,0:T(8,128)(2,1)} %refs_0_.4, ...), custom_call_target="tpu_custom_call" | custom-call | flops 1000000 | tf_op jit(solution)/shard_map/pallas_call | solution.py:605
  53.3 6.5 %collective-permute-done.19.refs_13_ = bf16[2,144,512]{2,1,0:T(8,128)(2,1)S(1)} collective-permute-done((bf16[2,144,512]{2,1,0:T(8,128)(2,1)S(1)}, bf16[2,144,512]{2,1,0:T(8,128)(2,1)S(1)}, u32[]{:S(2)}, u32[]{:S(2)}) %collective-permute-start.19) | collective-permute-done | bytes 294944 | tf_op jit(solution)/shard_map/ppermute | solution.py:58
  59.8 1.9 %collective-permute-done.21.refs_15_ = bf16[2,144,512]{2,1,0:T(8,128)(2,1)S(1)} collective-permute-done((bf16[2,144,512]{2,1,0:T(8,128)(2,1)S(1)}, bf16[2,144,512]{2,1,0:T(8,128)(2,1)S(1)}, u32[]{:S(2)}, u32[]{:S(2)}) %collective-permute-start.21) | collective-permute-done | bytes 294944 | tf_op jit(solution)/shard_map/ppermute | solution.py:58
  63.2 12.8 %shard_map.362 = (bf16[128,512]{1,0:T(8,128)(2,1)S(1)}, bf16[1,128,512]{2,1,0:T(8,128)(2,1)S(1)}, bf16[2,128,512]{2,1,0:T(8,128)(2,1)S(1)}, f32[512,512]{1,0:T(8...) custom-call(s32[2]{0:T(128)S(1)} %pad_add_fusion.scal, ...), custom_call_target="tpu_custom_call" | custom-call | flops 1000000 | tf_op jit(solution)/shard_map/pallas_call | solution.py:605
  76.6 2.3 %collective-permute-done.24 = bf16[8,144,512]{2,1,0:T(8,128)(2,1)S(1)} collective-permute-done((bf16[8,144,512]{2,1,0:T(8,128)(2,1)S(1)}, bf16[8,144,512]{2,1,0:T(8,128)(2,1)S(1)}, u32[]{:S(2)}, u32[]{:S(2)}) %collective-permute-start.24) | collective-permute-done | bytes 1179680 | tf_op jit(solution)/shard_map/ppermute | solution.py:58
  80.4 10.8 %shard_map.364 = (f32[128,512]{1,0:T(8,128)S(1)}, bf16[1,128,512]{2,1,0:T(8,128)(2,1)S(1)}, bf16[2,128,512]{2,1,0:T(8,128)(2,1)S(1)}, bf16[8,272,128]{2,1,0:T(8,...) custom-call(s32[2]{0:T(128)S(1)} %pad_add_fusion.scal, ...), custom_call_target="tpu_custom_call" | custom-call | flops 1000000 | tf_op jit(solution)/shard_map/pallas_call | solution.py:605
  91.2 3.6 %collective-permute-done.26.y = bf16[4,144,512]{2,1,0:T(8,128)(2,1)S(1)} collective-permute-done((bf16[4,144,512]{2,1,0:T(8,128)(2,1)S(1)}, bf16[4,144,512]{2,1,0:T(8,128)(2,1)S(1)}, u32[]{:S(2)}, u32[]{:S(2)}) %collective-permute-start.26) | collective-permute-done | bytes 589856 | tf_op jit(solution)/shard_map/ppermute | solution.py:58
  100.1 5.6 %collective-permute-done.27.x2 = bf16[2,144,512]{2,1,0:T(8,128)(2,1)S(1)} collective-permute-done((bf16[2,144,512]{2,1,0:T(8,128)(2,1)S(1)}, bf16[2,144,512]{2,1,0:T(8,128)(2,1)S(1)}, u32[]{:S(2)}, u32[]{:S(2)}) %collective-permute-start.27) | collective-permute-done | bytes 294944 | tf_op jit(solution)/shard_map/ppermute | solution.py:58
  107.5 2.0 %collective-permute-start.29 = (bf16[2,144,512]{2,1,0:T(8,128)(2,1)S(1)}, bf16[2,144,512]{2,1,0:T(8,128)(2,1)S(1)}, u32[]{:S(2)}, u32[]{:S(2)}) collective-permute-start(bf16[2,144,512]{2,1,0:T(8,128)(2,1)S(1)} %get-tuple-element.106), channel_id=1, source_target_pairs={{0,8},{1,9},{2,10},{3,11},{4,12},{5,13},{6,14},{7,15},{8,0},{9,1},... | collective-permute-start | bytes 884744 | tf_op jit(solution)/shard_map/ppermute | solution.py:58
  114.3 2.8 %collective-permute-done.34.x2 = bf16[2,272,128]{2,1,0:T(8,128)(2,1)S(1)} collective-permute-done((bf16[2,272,128]{2,1,0:T(8,128)(2,1)S(1)}, bf16[2,272,128]{2,1,0:T(8,128)(2,1)S(1)}, u32[]{:S(2)}, u32[]{:S(2)}) %collective-permute-start.34) | collective-permute-done | bytes 139296 | tf_op jit(solution)/shard_map/ppermute | solution.py:58
  118.0 2.0 %collective-permute-start.37 = (bf16[2,272,128]{2,1,0:T(8,128)(2,1)S(1)}, bf16[2,272,128]{2,1,0:T(8,128)(2,1)S(1)}, u32[]{:S(2)}, u32[]{:S(2)}) collective-permute-start(bf16[2,272,128]{2,1,0:T(8,128)(2,1)S(1)} %get-tuple-element.126), channel_id=1, source_target_pairs={{0,8},{1,9},{2,10},{3,11},{4,12},{5,13},{6,14},{7,15},{8,0},{9,1},... | collective-permute-start | bytes 417800 | tf_op jit(solution)/shard_map/ppermute | solution.py:58
  120.0 1.8 %collective-permute-start.36 = (bf16[1,144,512]{2,1,0:T(8,128)(2,1)S(1)}, bf16[1,144,512]{2,1,0:T(8,128)(2,1)S(1)}, u32[]{:S(2)}, u32[]{:S(2)}) collective-permute-start(bf16[1,144,512]{2,1,0:T(8,128)(2,1)S(1)} %get-tuple-element.122), channel_id=1, source_target_pairs={{0,16},{1,17},{2,18},{3,19},{4,20},{5,21},{6,22},{7,23},{8,24},{9,... | collective-permute-start | bytes 442376 | tf_op jit(solution)/shard_map/ppermute | solution.py:58
  124.2 1.9 %collective-permute-done.36.far = bf16[1,144,512]{2,1,0:T(8,128)(2,1)S(1)} collective-permute-done((bf16[1,144,512]{2,1,0:T(8,128)(2,1)S(1)}, bf16[1,144,512]{2,1,0:T(8,128)(2,1)S(1)}, u32[]{:S(2)}, u32[]{:S(2)}) %collective-permute-start.36) | collective-permute-done | bytes 147488 | tf_op jit(solution)/shard_map/ppermute | solution.py:58
  126.1 1.9 %collective-permute-start.38 = (bf16[1,272,128]{2,1,0:T(8,128)(2,1)S(1)}, bf16[1,272,128]{2,1,0:T(8,128)(2,1)S(1)}, u32[]{:S(2)}, u32[]{:S(2)}) collective-permute-start(bf16[1,272,128]{2,1,0:T(8,128)(2,1)S(1)} %get-tuple-element.128), channel_id=1, source_target_pairs={{0,16},{1,17},{2,18},{3,19},{4,20},{5,21},{6,22},{7,23},{8,24},{9,... | collective-permute-start | bytes 208904 | tf_op jit(solution)/shard_map/ppermute | solution.py:58
  129.2 2.0 %collective-permute-done.38.far = bf16[1,272,128]{2,1,0:T(8,128)(2,1)S(1)} collective-permute-done((bf16[1,272,128]{2,1,0:T(8,128)(2,1)S(1)}, bf16[1,272,128]{2,1,0:T(8,128)(2,1)S(1)}, u32[]{:S(2)}, u32[]{:S(2)}) %collective-permute-start.38) | collective-permute-done | bytes 69664 | tf_op jit(solution)/shard_map/ppermute | solution.py:58
  (125 shorter events, 35.1 us)
Async XLA Ops:
  2.7 29.9 %collective-permute-start = (bf16[4,128,512]{2,1,0:T(8,128)(2,1)S(1)}, bf16[4,128,512]{2,1,0:T(8,128)(2,1)S(1)}, u32[]{:S(2)}, u32[]{:S(2)}) collective-permute-start(bf16[4,128,512]{2,1,0:T(8,128)(2,1)S(1)} %get-tuple-element.89), channel_id=1, source_target_pairs={{0,2},{1,3},{2,0},{3,1},{4,6},{5,7},{6,4},{7,5},{8,10},{9,11},{10,... | collective-permute-start | bytes 1572872 | tf_op jit(solution)/shard_map/ppermute | solution.py:58
  5.7 9.7 %collective-permute-start.3 = (bf16[1,272,128]{2,1,0:T(8,128)(2,1)S(1)}, bf16[1,272,128]{2,1,0:T(8,128)(2,1)S(1)}, u32[]{:S(2)}, u32[]{:S(2)}) collective-permute-start(bf16[1,272,128]{2,1,0:T(8,128)(2,1)S(1)} %get-tuple-element.91.own), channel_id=1, source_target_pairs={{0,16},{1,17},{2,18},{3,19},{4,20},{5,21},{6,22},{7,23},{8,24},{9,... | collective-permute-start | bytes 208904 | tf_op jit(solution)/shard_map/ppermute | solution.py:58
  8.3 10.1 %collective-permute-start.12 = (bf16[1,144,512]{2,1,0:T(8,128)(2,1)S(1)}, bf16[1,144,512]{2,1,0:T(8,128)(2,1)S(1)}, u32[]{:S(2)}, u32[]{:S(2)}) collective-permute-start(bf16[1,144,512]{2,1,0:T(8,128)(2,1)S(1)} %get-tuple-element.95.own), channel_id=1, source_target_pairs={{0,16},{1,17},{2,18},{3,19},{4,20},{5,21},{6,22},{7,23},{8,24},{9,... | collective-permute-start | bytes 442376 | tf_op jit(solution)/shard_map/ppermute | solution.py:58
  21.5 8.8 %collective-permute-start.8 = (bf16[4,272,128]{2,1,0:T(8,128)(2,1)S(1)}, bf16[4,272,128]{2,1,0:T(8,128)(2,1)S(1)}, u32[]{:S(2)}, u32[]{:S(2)}) collective-permute-start(bf16[4,272,128]{2,1,0:T(8,128)(2,1)S(1)} %shard_map.358.refs_5_), channel_id=1, source_target_pairs={{0,4},{1,5},{2,6},{3,7},{4,0},{5,1},{6,2},{7,3},{8,12},{9,13},{10,... | collective-permute-start | bytes 835592 | tf_op jit(solution)/shard_map/ppermute | solution.py:58
  23.0 9.6 %collective-permute-start.6 = (bf16[4,272,128]{2,1,0:T(8,128)(2,1)S(1)}, bf16[4,272,128]{2,1,0:T(8,128)(2,1)S(1)}, u32[]{:S(2)}, u32[]{:S(2)}) collective-permute-start(bf16[4,272,128]{2,1,0:T(8,128)(2,1)S(1)} %shard_map.358.refs_5_), channel_id=1, source_target_pairs={{0,2},{1,3},{2,0},{3,1},{4,6},{5,7},{6,4},{7,5},{8,10},{9,11},{10,... | collective-permute-start | bytes 835592 | tf_op jit(solution)/shard_map/ppermute | solution.py:58
  23.6 15.0 %collective-permute-start.10 = (bf16[4,272,128]{2,1,0:T(8,128)(2,1)S(1)}, bf16[4,272,128]{2,1,0:T(8,128)(2,1)S(1)}, u32[]{:S(2)}, u32[]{:S(2)}) collective-permute-start(bf16[4,272,128]{2,1,0:T(8,128)(2,1)S(1)} %shard_map.358.refs_5_), channel_id=1, source_target_pairs={{0,6},{1,7},{2,4},{3,5},{4,2},{5,3},{6,0},{7,1},{8,14},{9,15},{10,... | collective-permute-start | bytes 835592 | tf_op jit(solution)/shard_map/ppermute | solution.py:58
  32.6 17.9 %collective-permute-start.17 = (bf16[4,144,512]{2,1,0:T(8,128)(2,1)S(1)}, bf16[4,144,512]{2,1,0:T(8,128)(2,1)S(1)}, u32[]{:S(2)}, u32[]{:S(2)}) collective-permute-start(bf16[4,144,512]{2,1,0:T(8,128)(2,1)S(1)} %shard_map.361.refs_7_), channel_id=1, source_target_pairs={{0,4},{1,5},{2,6},{3,7},{4,0},{5,1},{6,2},{7,3},{8,12},{9,13},{10,... | collective-permute-start | bytes 1769480 | tf_op jit(solution)/shard_map/ppermute | solution.py:58
  33.1 17.5 %collective-permute-start.15 = (bf16[4,144,512]{2,1,0:T(8,128)(2,1)S(1)}, bf16[4,144,512]{2,1,0:T(8,128)(2,1)S(1)}, u32[]{:S(2)}, u32[]{:S(2)}) collective-permute-start(bf16[4,144,512]{2,1,0:T(8,128)(2,1)S(1)} %shard_map.361.refs_7_), channel_id=1, source_target_pairs={{0,2},{1,3},{2,0},{3,1},{4,6},{5,7},{6,4},{7,5},{8,10},{9,11},{10,... | collective-permute-start | bytes 1769480 | tf_op jit(solution)/shard_map/ppermute | solution.py:58
  40.5 21.1 %collective-permute-start.14 = (bf16[4,144,512]{2,1,0:T(8,128)(2,1)S(1)}, bf16[4,144,512]{2,1,0:T(8,128)(2,1)S(1)}, u32[]{:S(2)}, u32[]{:S(2)}) collective-permute-start(bf16[4,144,512]{2,1,0:T(8,128)(2,1)S(1)} %shard_map.361.refs_7_), channel_id=1, source_target_pairs={{0,1},{1,0},{2,3},{3,2},{4,5},{5,4},{6,7},{7,6},{8,9},{9,8},{10,11... | collective-permute-start | bytes 1769480 | tf_op jit(solution)/shard_map/ppermute | solution.py:58
  50.6 9.1 %collective-permute-start.19 = (bf16[2,144,512]{2,1,0:T(8,128)(2,1)S(1)}, bf16[2,144,512]{2,1,0:T(8,128)(2,1)S(1)}, u32[]{:S(2)}, u32[]{:S(2)}) collective-permute-start(bf16[2,144,512]{2,1,0:T(8,128)(2,1)S(1)} %slice.85), channel_id=1, source_target_pairs={{0,4},{1,5},{2,6},{3,7},{4,0},{5,1},{6,2},{7,3},{8,12},{9,13},{10,... | collective-permute-start | bytes 884744 | tf_op jit(solution)/shard_map/ppermute | solution.py:58
  52.2 9.4 %collective-permute-start.18 = (bf16[4,144,512]{2,1,0:T(8,128)(2,1)S(1)}, bf16[4,144,512]{2,1,0:T(8,128)(2,1)S(1)}, u32[]{:S(2)}, u32[]{:S(2)}) collective-permute-start(bf16[4,144,512]{2,1,0:T(8,128)(2,1)S(1)} %collective-permute-done.17.refs_11_), channel_id=1, source_target_pairs={{0,1},{1,0},{2,3},{3,2},{4,5},{5,4},{6,7},{7,6},{8,9},{9,8},{10,11... | collective-permute-start | bytes 1769480 | tf_op jit(solution)/shard_map/ppermute | solution.py:58
  52.2 9.4 %collective-permute-start.16 = (bf16[4,144,512]{2,1,0:T(8,128)(2,1)S(1)}, bf16[4,144,512]{2,1,0:T(8,128)(2,1)S(1)}, u32[]{:S(2)}, u32[]{:S(2)}) collective-permute-start(bf16[4,144,512]{2,1,0:T(8,128)(2,1)S(1)} %collective-permute-done.15.refs_9_), channel_id=1, source_target_pairs={{0,1},{1,0},{2,3},{3,2},{4,5},{5,4},{6,7},{7,6},{8,9},{9,8},{10,11... | collective-permute-start | bytes 1769480 | tf_op jit(solution)/shard_map/ppermute | solution.py:58
  52.7 8.9 %collective-permute-start.21 = (bf16[2,144,512]{2,1,0:T(8,128)(2,1)S(1)}, bf16[2,144,512]{2,1,0:T(8,128)(2,1)S(1)}, u32[]{:S(2)}, u32[]{:S(2)}) collective-permute-start(bf16[2,144,512]{2,1,0:T(8,128)(2,1)S(1)} %slice.86), channel_id=1, source_target_pairs={{0,2},{1,3},{2,0},{3,1},{4,6},{5,7},{6,4},{7,5},{8,10},{9,11},{10,... | collective-permute-start | bytes 884744 | tf_op jit(solution)/shard_map/ppermute | solution.py:58
  76.3 19.3 %collective-permute-start.23 = (bf16[8,144,512]{2,1,0:T(8,128)(2,1)S(1)}, bf16[8,144,512]{2,1,0:T(8,128)(2,1)S(1)}, u32[]{:S(2)}, u32[]{:S(2)}) collective-permute-start(bf16[8,144,512]{2,1,0:T(8,128)(2,1)S(1)} %get-tuple-element.101), channel_id=1, source_target_pairs={{0,1},{1,0},{2,3},{3,2},{4,5},{5,4},{6,7},{7,6},{8,9},{9,8},{10,11... | collective-permute-start | bytes 3538952 | tf_op jit(solution)/shard_map/ppermute | solution.py:58
  79.3 15.4 %collective-permute-start.26 = (bf16[4,144,512]{2,1,0:T(8,128)(2,1)S(1)}, bf16[4,144,512]{2,1,0:T(8,128)(2,1)S(1)}, u32[]{:S(2)}, u32[]{:S(2)}) collective-permute-start(bf16[4,144,512]{2,1,0:T(8,128)(2,1)S(1)} %get-tuple-element.160), channel_id=1, source_target_pairs={{0,4},{1,5},{2,6},{3,7},{4,0},{5,1},{6,2},{7,3},{8,12},{9,13},{10,... | collective-permute-start | bytes 1769480 | tf_op jit(solution)/shard_map/ppermute | solution.py:58
  79.9 15.1 %collective-permute-start.25 = (bf16[4,144,512]{2,1,0:T(8,128)(2,1)S(1)}, bf16[4,144,512]{2,1,0:T(8,128)(2,1)S(1)}, u32[]{:S(2)}, u32[]{:S(2)}) collective-permute-start(bf16[4,144,512]{2,1,0:T(8,128)(2,1)S(1)} %get-tuple-element.161), channel_id=1, source_target_pairs={{0,2},{1,3},{2,0},{3,1},{4,6},{5,7},{6,4},{7,5},{8,10},{9,11},{10,... | collective-permute-start | bytes 1769480 | tf_op jit(solution)/shard_map/ppermute | solution.py:58
  95.0 14.6 %collective-permute-start.30 = (bf16[8,272,128]{2,1,0:T(8,128)(2,1)S(1)}, bf16[8,272,128]{2,1,0:T(8,128)(2,1)S(1)}, u32[]{:S(2)}, u32[]{:S(2)}) collective-permute-start(bf16[8,272,128]{2,1,0:T(8,128)(2,1)S(1)} %get-tuple-element.115), channel_id=1, source_target_pairs={{0,1},{1,0},{2,3},{3,2},{4,5},{5,4},{6,7},{7,6},{8,9},{9,8},{10,11... | collective-permute-start | bytes 1671176 | tf_op jit(solution)/shard_map/ppermute | solution.py:58
  95.8 9.9 %collective-permute-start.27 = (bf16[2,144,512]{2,1,0:T(8,128)(2,1)S(1)}, bf16[2,144,512]{2,1,0:T(8,128)(2,1)S(1)}, u32[]{:S(2)}, u32[]{:S(2)}) collective-permute-start(bf16[2,144,512]{2,1,0:T(8,128)(2,1)S(1)} %get-tuple-element.159), channel_id=1, source_target_pairs={{0,4},{1,5},{2,6},{3,7},{4,0},{5,1},{6,2},{7,3},{8,12},{9,13},{10,... | collective-permute-start | bytes 884744 | tf_op jit(solution)/shard_map/ppermute | solution.py:58
  97.4 9.9 %collective-permute-start.28 = (bf16[2,144,512]{2,1,0:T(8,128)(2,1)S(1)}, bf16[2,144,512]{2,1,0:T(8,128)(2,1)S(1)}, u32[]{:S(2)}, u32[]{:S(2)}) collective-permute-start(bf16[2,144,512]{2,1,0:T(8,128)(2,1)S(1)} %get-tuple-element.158), channel_id=1, source_target_pairs={{0,2},{1,3},{2,0},{3,1},{4,6},{5,7},{6,4},{7,5},{8,10},{9,11},{10,... | collective-permute-start | bytes 884744 | tf_op jit(solution)/shard_map/ppermute | solution.py:58
  98.0 12.7 %collective-permute-start.33 = (bf16[4,272,128]{2,1,0:T(8,128)(2,1)S(1)}, bf16[4,272,128]{2,1,0:T(8,128)(2,1)S(1)}, u32[]{:S(2)}, u32[]{:S(2)}) collective-permute-start(bf16[4,272,128]{2,1,0:T(8,128)(2,1)S(1)} %get-tuple-element.162), channel_id=1, source_target_pairs={{0,4},{1,5},{2,6},{3,7},{4,0},{5,1},{6,2},{7,3},{8,12},{9,13},{10,... | collective-permute-start | bytes 835592 | tf_op jit(solution)/shard_map/ppermute | solution.py:58
  98.7 13.3 %collective-permute-start.32 = (bf16[4,272,128]{2,1,0:T(8,128)(2,1)S(1)}, bf16[4,272,128]{2,1,0:T(8,128)(2,1)S(1)}, u32[]{:S(2)}, u32[]{:S(2)}) collective-permute-start(bf16[4,272,128]{2,1,0:T(8,128)(2,1)S(1)} %get-tuple-element.163), channel_id=1, source_target_pairs={{0,2},{1,3},{2,0},{3,1},{4,6},{5,7},{6,4},{7,5},{8,10},{9,11},{10,... | collective-permute-start | bytes 835592 | tf_op jit(solution)/shard_map/ppermute | solution.py:58
  121.9 10.9 %collective-permute-start.41 = (bf16[2,128,512]{2,1,0:T(8,128)(2,1)S(1)}, bf16[2,128,512]{2,1,0:T(8,128)(2,1)S(1)}, u32[]{:S(2)}, u32[]{:S(2)}) collective-permute-start(bf16[2,128,512]{2,1,0:T(8,128)(2,1)S(1)} %get-tuple-element.136), channel_id=1, source_target_pairs={{0,2},{1,3},{2,0},{3,1},{4,6},{5,7},{6,4},{7,5},{8,10},{9,11},{10,... | collective-permute-start | bytes 786440 | tf_op jit(solution)/shard_map/ppermute | solution.py:58
  122.5 10.3 %collective-permute-start.42 = (bf16[2,128,512]{2,1,0:T(8,128)(2,1)S(1)}, bf16[2,128,512]{2,1,0:T(8,128)(2,1)S(1)}, u32[]{:S(2)}, u32[]{:S(2)}) collective-permute-start(bf16[2,128,512]{2,1,0:T(8,128)(2,1)S(1)} %get-tuple-element.137), channel_id=1, source_target_pairs={{0,3},{1,2},{2,1},{3,0},{4,7},{5,6},{6,5},{7,4},{8,11},{9,10},{10,... | collective-permute-start | bytes 786440 | tf_op jit(solution)/shard_map/ppermute | solution.py:58
  122.5 10.2 %collective-permute-start.39 = (bf16[1,128,512]{2,1,0:T(8,128)(2,1)S(1)}, bf16[1,128,512]{2,1,0:T(8,128)(2,1)S(1)}, u32[]{:S(2)}, u32[]{:S(2)}) collective-permute-start(bf16[1,128,512]{2,1,0:T(8,128)(2,1)S(1)} %get-tuple-element.132), channel_id=1, source_target_pairs={{0,1},{1,0},{2,3},{3,2},{4,5},{5,4},{6,7},{7,6},{8,9},{9,8},{10,11... | collective-permute-start | bytes 393224 | tf_op jit(solution)/shard_map/ppermute | solution.py:58
  (38 other events, 226.4 us)

commit v5 on v4

--- a/solution.py
+++ b/solution.py
@@ -526,6 +526,11 @@
     return lax.optimization_barrier((value, *others))[0]
 
 
+def stacked(q, got):
+    out = jax.ShapeDtypeStruct((2 * q.shape[0], *q.shape[1:]), q.dtype)
+    return call(stack_kernel, [out], [], [q, got], "vv", 6, 1_000)[0]
+
+
 def gather_z(value, *others):
     nz = lax.axis_size("dp") // 2
     q, order = value, [0]
@@ -533,8 +538,7 @@
     while step:
         if step == 1:
             q = after(q, *others)
-        out = jax.ShapeDtypeStruct((2 * q.shape[0], *q.shape[1:]), q.dtype)
-        q = call(stack_kernel, [out], [], [q, swap(q, step * 2, 0)], "vv", 6, 1_000)[0]
+        q = stacked(q, swap(q, step * 2, 0))
         order = order + [z ^ step for z in order]
         step //= 2
     return q, tuple(order)
@@ -644,7 +648,7 @@
     inner = up_proj.shape[1]
     group = attn_proj.shape[2]
     per, out_per, pos_per = attn_proj.shape[1], out_proj.shape[0], pos_table.shape[0]
-    fast = out_per % 16 == 0 and pos_per % 16 == 0 and 2 * per == LANES
+    fast = out_per % 16 == 0 and pos_per % 16 == 0 and 2 * per == LANES and n_dp == 8 and n_t == 4
     sds = jax.ShapeDtypeStruct
 
     if fast:
@@ -662,7 +666,9 @@
             8,
             1_000,
         )
-        qa, za = gather_z(ga)
+        a2 = stacked(ga, swap(ga, 4, 0))
+        qa, za = stacked(a2, swap(a2, 2, 0)), (0, 2, 1, 3)
+        gb = after(gb, a2)
         rx = swap(xs, 0, 2)
         qb, zb = gather_z(gb, qa)
         c1 = swap(c1, 0, 1)
@@ -773,7 +779,7 @@
     leaving = [jnp.concatenate([res_x[i : i + 1], gi_x[i : i + 1]]) for i in range(2)]
     if fast:
         keep_first, keep_rest, send_first, send_rest = got_a
-        red_a = Reduction(keep_first, keep_rest, after(send_first, *first_b), send_rest)
+        red_a = Reduction(keep_first, keep_rest, send_first, send_rest)
         first_a, second_b = red_a.first(), red_b.second()
         chunk_b, chunk_a = got_b[0].shape[1:], got_a[0].shape[1:]
         before_z = [[sds(chunk, F32), sds(chunk, F32), sds((2, *chunk), BF16)] for chunk in (chunk_b, chunk_a)]

time: 135 us -> 132 us (0.978)
  waiting for transfers between devices: 60.6 us -> 54.3 us
  starting transfers between devices: 32.3 us -> 36 us
    ppermute x43, waiting for transfers between devices: 60.6 us -> 54.3 us  [swap(): lax.ppermute(value, AXES, [(i, i ^ mask) for i in range(lax.axis_size('dp...]
    ppermute x43, starting transfers between devices: 32.3 us -> 36 us  [swap(): lax.ppermute(value, AXES, [(i, i ^ mask) for i in range(lax.axis_size('dp...]
  transfers between devices with their start and end apart: 43 -> 43, of which waited for: 26 -> 24; matrix products, arithmetic and copies ran while one was open for 1% -> 1% of each run, Pallas kernels for 17% -> 17%
where the time goes in v5:
time: 132 us
  waiting for transfers between devices  54.3 us (41%)
  Pallas kernels  39.4 us (30%)
  starting transfers between devices  36 us (27%)
    ppermute x43, waiting for transfers between devices, swap(): lax.ppermute(value, AXES, [(i, i ^ mask) for i in range(lax.axis_size('dp...  54.3 us
    pallas_call x15, Pallas kernels, call(): pl.pallas_call(kernel, out_shape=outs, in_specs=[kinds[k] for k in spaces...  39.4 us
    ppermute x43, starting transfers between devices, swap(): lax.ppermute(value, AXES, [(i, i ^ mask) for i in range(lax.axis_size('dp...  36 us
  transfers between devices with their start and end apart: 43, of which 24 were waited for; matrix products, arithmetic and copies ran while one was open for 1% of the time, Pallas kernels for 17%

profile of v5, /device:TPU:0, one launch (start us, length us, event | category | flops | bytes accessed | tf_op | source)
XLA Modules:
  0.0 131.9 jit_solution(8231290625669624775)
XLA Ops:
  0.7 2.0 %shard_map.356 = (bf16[1,272,128]{2,1,0:T(8,128)(2,1)S(1)}, bf16[1,144,512]{2,1,0:T(8,128)(2,1)S(1)}, bf16[4,128,512]{2,1,0:T(8,128)(2,1)S(1)}, bf16[2,128,512]{2,1,0:T(8,128)(2,1)S(1)}) custom-call(s32[2]{0:T(128)S(1)} %pad_add_fusion.scal, bf16[4,128,512]{2,1,0:T(8,128)(2,1)} %refs_0_.4, bf16[4,128,512]{2,1,0:T(8,128)(2,1)} %refs_0_.5, ...), custom_call_target="tpu_custom_call" | custom-call | flops 1000 | tf_op jit(solution)/shard_map/pallas_call | solution.py:609
  2.7 3.0 %collective-permute-start = (bf16[4,128,512]{2,1,0:T(8,128)(2,1)S(1)}, bf16[4,128,512]{2,1,0:T(8,128)(2,1)S(1)}, u32[]{:S(2)}, u32[]{:S(2)}) collective-permute-start(bf16[4,128,512]{2,1,0:T(8,128)(2,1)S(1)} %get-tuple-element.89), channel_id=1, source_target_pairs={{0,2},{1,3},{2,0},{3,1},{4,6},{5,7},{6,4},{7,5},{8,10},{9,11},{10,... | collective-permute-start | bytes 1572872 | tf_op jit(solution)/shard_map/ppermute | solution.py:58
  5.7 2.6 %collective-permute-start.3 = (bf16[1,272,128]{2,1,0:T(8,128)(2,1)S(1)}, bf16[1,272,128]{2,1,0:T(8,128)(2,1)S(1)}, u32[]{:S(2)}, u32[]{:S(2)}) collective-permute-start(bf16[1,272,128]{2,1,0:T(8,128)(2,1)S(1)} %get-tuple-element.91.own), channel_id=1, source_target_pairs={{0,16},{1,17},{2,18},{3,19},{4,20},{5,21},{6,22},{7,23},{8,24},{9,... | collective-permute-start | bytes 208904 | tf_op jit(solution)/shard_map/ppermute | solution.py:58
  8.3 3.0 %collective-permute-done.3.got = bf16[1,272,128]{2,1,0:T(8,128)(2,1)S(1)} collective-permute-done((bf16[1,272,128]{2,1,0:T(8,128)(2,1)S(1)}, bf16[1,272,128]{2,1,0:T(8,128)(2,1)S(1)}, u32[]{:S(2)}, u32[]{:S(2)}) %collective-permute-start.3) | collective-permute-done | bytes 69664 | tf_op jit(solution)/shard_map/ppermute | solution.py:58
  11.3 2.4 %collective-permute-start.12 = (bf16[1,144,512]{2,1,0:T(8,128)(2,1)S(1)}, bf16[1,144,512]{2,1,0:T(8,128)(2,1)S(1)}, u32[]{:S(2)}, u32[]{:S(2)}) collective-permute-start(bf16[1,144,512]{2,1,0:T(8,128)(2,1)S(1)} %get-tuple-element.96.own), channel_id=1, source_target_pairs={{0,16},{1,17},{2,18},{3,19},{4,20},{5,21},{6,22},{7,23},{8,24},{9,... | collective-permute-start | bytes 442376 | tf_op jit(solution)/shard_map/ppermute | solution.py:58
  13.7 2.2 %collective-permute-start.4 = (bf16[2,272,128]{2,1,0:T(8,128)(2,1)S(1)}, bf16[2,272,128]{2,1,0:T(8,128)(2,1)S(1)}, u32[]{:S(2)}, u32[]{:S(2)}) collective-permute-start(bf16[2,272,128]{2,1,0:T(8,128)(2,1)S(1)} %shard_map.357.own), channel_id=1, source_target_pairs={{0,8},{1,9},{2,10},{3,11},{4,12},{5,13},{6,14},{7,15},{8,0},{9,1},... | collective-permute-start | bytes 417800 | tf_op jit(solution)/shard_map/ppermute | solution.py:58
  15.9 3.5 %collective-permute-done.4.got = bf16[2,272,128]{2,1,0:T(8,128)(2,1)S(1)} collective-permute-done((bf16[2,272,128]{2,1,0:T(8,128)(2,1)S(1)}, bf16[2,272,128]{2,1,0:T(8,128)(2,1)S(1)}, u32[]{:S(2)}, u32[]{:S(2)}) %collective-permute-start.4) | collective-permute-done | bytes 139296 | tf_op jit(solution)/shard_map/ppermute | solution.py:58
  19.5 1.8 %collective-permute-start.13 = (bf16[2,144,512]{2,1,0:T(8,128)(2,1)S(1)}, bf16[2,144,512]{2,1,0:T(8,128)(2,1)S(1)}, u32[]{:S(2)}, u32[]{:S(2)}) collective-permute-start(bf16[2,144,512]{2,1,0:T(8,128)(2,1)S(1)} %shard_map.360.own), channel_id=1, source_target_pairs={{0,8},{1,9},{2,10},{3,11},{4,12},{5,13},{6,14},{7,15},{8,0},{9,1},... | collective-permute-start | bytes 884744 | tf_op jit(solution)/shard_map/ppermute | solution.py:58
  26.6 5.4 %collective-permute-done.8.refs_9_ = bf16[4,272,128]{2,1,0:T(8,128)(2,1)S(1)} collective-permute-done((bf16[4,272,128]{2,1,0:T(8,128)(2,1)S(1)}, bf16[4,272,128]{2,1,0:T(8,128)(2,1)S(1)}, u32[]{:S(2)}, u32[]{:S(2)}) %collective-permute-start.8) | collective-permute-done | bytes 278560 | tf_op jit(solution)/shard_map/ppermute | solution.py:58
  35.1 3.1 %collective-permute-done.10.refs_11_ = bf16[4,272,128]{2,1,0:T(8,128)(2,1)S(1)} collective-permute-done((bf16[4,272,128]{2,1,0:T(8,128)(2,1)S(1)}, bf16[4,272,128]{2,1,0:T(8,128)(2,1)S(1)}, u32[]{:S(2)}, u32[]{:S(2)}) %collective-permute-start.10) | collective-permute-done | bytes 278560 | tf_op jit(solution)/shard_map/ppermute | solution.py:58
  41.4 8.9 %shard_map.359 = (f32[512,512]{1,0:T(8,128)S(1)}, bf16[512,1536]{1,0:T(8,128)(2,1)}, bf16[8,512,512]{2,1,0:T(8,128)(2,1)}, bf16[512,512]{1,0:T(8,128)(2,1)S(1)},...) custom-call(s32[2]{0:T(128)S(1)} %pad_add_fusion.scal, bf16[4,128,512]{2,1,0:T(8,128)(2,1)} %refs_0_.4, ...), custom_call_target="tpu_custom_call" | custom-call | flops 1000000 | tf_op jit(solution)/shard_map/pallas_call | solution.py:609
  53.0 6.5 %collective-permute-done.19.refs_13_ = bf16[2,144,512]{2,1,0:T(8,128)(2,1)S(1)} collective-permute-done((bf16[2,144,512]{2,1,0:T(8,128)(2,1)S(1)}, bf16[2,144,512]{2,1,0:T(8,128)(2,1)S(1)}, u32[]{:S(2)}, u32[]{:S(2)}) %collective-permute-start.19) | collective-permute-done | bytes 294944 | tf_op jit(solution)/shard_map/ppermute | solution.py:58
  59.5 1.9 %collective-permute-done.21.refs_15_ = bf16[2,144,512]{2,1,0:T(8,128)(2,1)S(1)} collective-permute-done((bf16[2,144,512]{2,1,0:T(8,128)(2,1)S(1)}, bf16[2,144,512]{2,1,0:T(8,128)(2,1)S(1)}, u32[]{:S(2)}, u32[]{:S(2)}) %collective-permute-start.21) | collective-permute-done | bytes 294944 | tf_op jit(solution)/shard_map/ppermute | solution.py:58
  62.9 12.8 %shard_map.362 = (bf16[128,512]{1,0:T(8,128)(2,1)S(1)}, bf16[1,128,512]{2,1,0:T(8,128)(2,1)S(1)}, bf16[2,128,512]{2,1,0:T(8,128)(2,1)S(1)}, f32[512,512]{1,0:T(8...) custom-call(s32[2]{0:T(128)S(1)} %pad_add_fusion.scal, ...), custom_call_target="tpu_custom_call" | custom-call | flops 1000000 | tf_op jit(solution)/shard_map/pallas_call | solution.py:609
  76.3 2.3 %collective-permute-done.24 = bf16[8,144,512]{2,1,0:T(8,128)(2,1)S(1)} collective-permute-done((bf16[8,144,512]{2,1,0:T(8,128)(2,1)S(1)}, bf16[8,144,512]{2,1,0:T(8,128)(2,1)S(1)}, u32[]{:S(2)}, u32[]{:S(2)}) %collective-permute-start.24) | collective-permute-done | bytes 1179680 | tf_op jit(solution)/shard_map/ppermute | solution.py:58
  80.2 10.8 %shard_map.364 = (f32[128,512]{1,0:T(8,128)S(1)}, bf16[1,128,512]{2,1,0:T(8,128)(2,1)S(1)}, bf16[2,128,512]{2,1,0:T(8,128)(2,1)S(1)}, bf16[8,272,128]{2,1,0:T(8,...) custom-call(s32[2]{0:T(128)S(1)} %pad_add_fusion.scal, ...), custom_call_target="tpu_custom_call" | custom-call | flops 1000000 | tf_op jit(solution)/shard_map/pallas_call | solution.py:609
  91.5 3.0 %collective-permute-done.26.y = bf16[4,144,512]{2,1,0:T(8,128)(2,1)S(1)} collective-permute-done((bf16[4,144,512]{2,1,0:T(8,128)(2,1)S(1)}, bf16[4,144,512]{2,1,0:T(8,128)(2,1)S(1)}, u32[]{:S(2)}, u32[]{:S(2)}) %collective-permute-start.26) | collective-permute-done | bytes 589856 | tf_op jit(solution)/shard_map/ppermute | solution.py:58
  99.3 5.7 %collective-permute-done.27.x2 = bf16[2,144,512]{2,1,0:T(8,128)(2,1)S(1)} collective-permute-done((bf16[2,144,512]{2,1,0:T(8,128)(2,1)S(1)}, bf16[2,144,512]{2,1,0:T(8,128)(2,1)S(1)}, u32[]{:S(2)}, u32[]{:S(2)}) %collective-permute-start.27) | collective-permute-done | bytes 294944 | tf_op jit(solution)/shard_map/ppermute | solution.py:58
  107.2 1.8 %collective-permute-done.33.y = bf16[4,272,128]{2,1,0:T(8,128)(2,1)S(1)} collective-permute-done((bf16[4,272,128]{2,1,0:T(8,128)(2,1)S(1)}, bf16[4,272,128]{2,1,0:T(8,128)(2,1)S(1)}, u32[]{:S(2)}, u32[]{:S(2)}) %collective-permute-start.33) | collective-permute-done | bytes 278560 | tf_op jit(solution)/shard_map/ppermute | solution.py:58
  111.5 3.9 %collective-permute-done.34.x2 = bf16[2,272,128]{2,1,0:T(8,128)(2,1)S(1)} collective-permute-done((bf16[2,272,128]{2,1,0:T(8,128)(2,1)S(1)}, bf16[2,272,128]{2,1,0:T(8,128)(2,1)S(1)}, u32[]{:S(2)}, u32[]{:S(2)}) %collective-permute-start.34) | collective-permute-done | bytes 139296 | tf_op jit(solution)/shard_map/ppermute | solution.py:58
  116.7 1.9 %collective-permute-start.36 = (bf16[1,144,512]{2,1,0:T(8,128)(2,1)S(1)}, bf16[1,144,512]{2,1,0:T(8,128)(2,1)S(1)}, u32[]{:S(2)}, u32[]{:S(2)}) collective-permute-start(bf16[1,144,512]{2,1,0:T(8,128)(2,1)S(1)} %get-tuple-element.122), channel_id=1, source_target_pairs={{0,16},{1,17},{2,18},{3,19},{4,20},{5,21},{6,22},{7,23},{8,24},{9,... | collective-permute-start | bytes 442376 | tf_op jit(solution)/shard_map/ppermute | solution.py:58
  120.9 2.1 %collective-permute-done.37.near = bf16[2,272,128]{2,1,0:T(8,128)(2,1)S(1)} collective-permute-done((bf16[2,272,128]{2,1,0:T(8,128)(2,1)S(1)}, bf16[2,272,128]{2,1,0:T(8,128)(2,1)S(1)}, u32[]{:S(2)}, u32[]{:S(2)}) %collective-permute-start.37) | collective-permute-done | bytes 139296 | tf_op jit(solution)/shard_map/ppermute | solution.py:58
  126.0 2.6 %collective-permute-done.38.far = bf16[1,272,128]{2,1,0:T(8,128)(2,1)S(1)} collective-permute-done((bf16[1,272,128]{2,1,0:T(8,128)(2,1)S(1)}, bf16[1,272,128]{2,1,0:T(8,128)(2,1)S(1)}, u32[]{:S(2)}, u32[]{:S(2)}) %collective-permute-start.38) | collective-permute-done | bytes 69664 | tf_op jit(solution)/shard_map/ppermute | solution.py:58
  130.2 1.8 %shard_map.370 = (bf16[4,128,512]{2,1,0:T(8,128)(2,1)}, f32[4,128,512]{2,1,0:T(8,128)}) custom-call(s32[2]{0:T(128)S(1)} %pad_add_fusion.scal, f32[8,128]{1,0:T(8,128)S(1)} %get-tuple-element.129.done, bf16[128,512]{1,0:T(8,128)(2,1)S(1)} %get-tuple-element.130.res_k, f32[128,512]{1,0:T(8,128)S(1)} %get-tuple-element.131.gi_k, ...), custom_call_target="tpu_custom_call" | custom-call | flops 1000 | tf_op jit(solution)/shard_map/pallas_call | solution.py:609
  (125 shorter events, 35.9 us)
Async XLA Ops:
  2.7 29.6 %collective-permute-start = (bf16[4,128,512]{2,1,0:T(8,128)(2,1)S(1)}, bf16[4,128,512]{2,1,0:T(8,128)(2,1)S(1)}, u32[]{:S(2)}, u32[]{:S(2)}) collective-permute-start(bf16[4,128,512]{2,1,0:T(8,128)(2,1)S(1)} %get-tuple-element.89), channel_id=1, source_target_pairs={{0,2},{1,3},{2,0},{3,1},{4,6},{5,7},{6,4},{7,5},{8,10},{9,11},{10,... | collective-permute-start | bytes 1572872 | tf_op jit(solution)/shard_map/ppermute | solution.py:58
  11.3 8.2 %collective-permute-start.12 = (bf16[1,144,512]{2,1,0:T(8,128)(2,1)S(1)}, bf16[1,144,512]{2,1,0:T(8,128)(2,1)S(1)}, u32[]{:S(2)}, u32[]{:S(2)}) collective-permute-start(bf16[1,144,512]{2,1,0:T(8,128)(2,1)S(1)} %get-tuple-element.96.own), channel_id=1, source_target_pairs={{0,16},{1,17},{2,18},{3,19},{4,20},{5,21},{6,22},{7,23},{8,24},{9,... | collective-permute-start | bytes 442376 | tf_op jit(solution)/shard_map/ppermute | solution.py:58
  21.3 10.7 %collective-permute-start.8 = (bf16[4,272,128]{2,1,0:T(8,128)(2,1)S(1)}, bf16[4,272,128]{2,1,0:T(8,128)(2,1)S(1)}, u32[]{:S(2)}, u32[]{:S(2)}) collective-permute-start(bf16[4,272,128]{2,1,0:T(8,128)(2,1)S(1)} %shard_map.358.refs_5_), channel_id=1, source_target_pairs={{0,4},{1,5},{2,6},{3,7},{4,0},{5,1},{6,2},{7,3},{8,12},{9,13},{10,... | collective-permute-start | bytes 835592 | tf_op jit(solution)/shard_map/ppermute | solution.py:58
  22.8 9.6 %collective-permute-start.6 = (bf16[4,272,128]{2,1,0:T(8,128)(2,1)S(1)}, bf16[4,272,128]{2,1,0:T(8,128)(2,1)S(1)}, u32[]{:S(2)}, u32[]{:S(2)}) collective-permute-start(bf16[4,272,128]{2,1,0:T(8,128)(2,1)S(1)} %shard_map.358.refs_5_), channel_id=1, source_target_pairs={{0,2},{1,3},{2,0},{3,1},{4,6},{5,7},{6,4},{7,5},{8,10},{9,11},{10,... | collective-permute-start | bytes 835592 | tf_op jit(solution)/shard_map/ppermute | solution.py:58
  23.3 15.0 %collective-permute-start.10 = (bf16[4,272,128]{2,1,0:T(8,128)(2,1)S(1)}, bf16[4,272,128]{2,1,0:T(8,128)(2,1)S(1)}, u32[]{:S(2)}, u32[]{:S(2)}) collective-permute-start(bf16[4,272,128]{2,1,0:T(8,128)(2,1)S(1)} %shard_map.358.refs_5_), channel_id=1, source_target_pairs={{0,6},{1,7},{2,4},{3,5},{4,2},{5,3},{6,0},{7,1},{8,14},{9,15},{10,... | collective-permute-start | bytes 835592 | tf_op jit(solution)/shard_map/ppermute | solution.py:58
  32.4 17.9 %collective-permute-start.17 = (bf16[4,144,512]{2,1,0:T(8,128)(2,1)S(1)}, bf16[4,144,512]{2,1,0:T(8,128)(2,1)S(1)}, u32[]{:S(2)}, u32[]{:S(2)}) collective-permute-start(bf16[4,144,512]{2,1,0:T(8,128)(2,1)S(1)} %shard_map.361.refs_7_), channel_id=1, source_target_pairs={{0,4},{1,5},{2,6},{3,7},{4,0},{5,1},{6,2},{7,3},{8,12},{9,13},{10,... | collective-permute-start | bytes 1769480 | tf_op jit(solution)/shard_map/ppermute | solution.py:58
  34.1 16.2 %collective-permute-start.15 = (bf16[4,144,512]{2,1,0:T(8,128)(2,1)S(1)}, bf16[4,144,512]{2,1,0:T(8,128)(2,1)S(1)}, u32[]{:S(2)}, u32[]{:S(2)}) collective-permute-start(bf16[4,144,512]{2,1,0:T(8,128)(2,1)S(1)} %shard_map.361.refs_7_), channel_id=1, source_target_pairs={{0,2},{1,3},{2,0},{3,1},{4,6},{5,7},{6,4},{7,5},{8,10},{9,11},{10,... | collective-permute-start | bytes 1769480 | tf_op jit(solution)/shard_map/ppermute | solution.py:58
  40.3 21.1 %collective-permute-start.14 = (bf16[4,144,512]{2,1,0:T(8,128)(2,1)S(1)}, bf16[4,144,512]{2,1,0:T(8,128)(2,1)S(1)}, u32[]{:S(2)}, u32[]{:S(2)}) collective-permute-start(bf16[4,144,512]{2,1,0:T(8,128)(2,1)S(1)} %shard_map.361.refs_7_), channel_id=1, source_target_pairs={{0,1},{1,0},{2,3},{3,2},{4,5},{5,4},{6,7},{7,6},{8,9},{9,8},{10,11... | collective-permute-start | bytes 1769480 | tf_op jit(solution)/shard_map/ppermute | solution.py:58
  50.4 9.1 %collective-permute-start.19 = (bf16[2,144,512]{2,1,0:T(8,128)(2,1)S(1)}, bf16[2,144,512]{2,1,0:T(8,128)(2,1)S(1)}, u32[]{:S(2)}, u32[]{:S(2)}) collective-permute-start(bf16[2,144,512]{2,1,0:T(8,128)(2,1)S(1)} %slice.85), channel_id=1, source_target_pairs={{0,4},{1,5},{2,6},{3,7},{4,0},{5,1},{6,2},{7,3},{8,12},{9,13},{10,... | collective-permute-start | bytes 884744 | tf_op jit(solution)/shard_map/ppermute | solution.py:58
  51.9 9.4 %collective-permute-start.18 = (bf16[4,144,512]{2,1,0:T(8,128)(2,1)S(1)}, bf16[4,144,512]{2,1,0:T(8,128)(2,1)S(1)}, u32[]{:S(2)}, u32[]{:S(2)}) collective-permute-start(bf16[4,144,512]{2,1,0:T(8,128)(2,1)S(1)} %collective-permute-done.17.refs_11_), channel_id=1, source_target_pairs={{0,1},{1,0},{2,3},{3,2},{4,5},{5,4},{6,7},{7,6},{8,9},{9,8},{10,11... | collective-permute-start | bytes 1769480 | tf_op jit(solution)/shard_map/ppermute | solution.py:58
  51.9 9.4 %collective-permute-start.16 = (bf16[4,144,512]{2,1,0:T(8,128)(2,1)S(1)}, bf16[4,144,512]{2,1,0:T(8,128)(2,1)S(1)}, u32[]{:S(2)}, u32[]{:S(2)}) collective-permute-start(bf16[4,144,512]{2,1,0:T(8,128)(2,1)S(1)} %collective-permute-done.15.refs_9_), channel_id=1, source_target_pairs={{0,1},{1,0},{2,3},{3,2},{4,5},{5,4},{6,7},{7,6},{8,9},{9,8},{10,11... | collective-permute-start | bytes 1769480 | tf_op jit(solution)/shard_map/ppermute | solution.py:58
  52.4 8.9 %collective-permute-start.21 = (bf16[2,144,512]{2,1,0:T(8,128)(2,1)S(1)}, bf16[2,144,512]{2,1,0:T(8,128)(2,1)S(1)}, u32[]{:S(2)}, u32[]{:S(2)}) collective-permute-start(bf16[2,144,512]{2,1,0:T(8,128)(2,1)S(1)} %slice.86), channel_id=1, source_target_pairs={{0,2},{1,3},{2,0},{3,1},{4,6},{5,7},{6,4},{7,5},{8,10},{9,11},{10,... | collective-permute-start | bytes 884744 | tf_op jit(solution)/shard_map/ppermute | solution.py:58
  76.0 15.6 %collective-permute-start.23 = (bf16[8,144,512]{2,1,0:T(8,128)(2,1)S(1)}, bf16[8,144,512]{2,1,0:T(8,128)(2,1)S(1)}, u32[]{:S(2)}, u32[]{:S(2)}) collective-permute-start(bf16[8,144,512]{2,1,0:T(8,128)(2,1)S(1)} %get-tuple-element.102), channel_id=1, source_target_pairs={{0,1},{1,0},{2,3},{3,2},{4,5},{5,4},{6,7},{7,6},{8,9},{9,8},{10,11... | collective-permute-start | bytes 3538952 | tf_op jit(solution)/shard_map/ppermute | solution.py:58
  79.0 15.4 %collective-permute-start.26 = (bf16[4,144,512]{2,1,0:T(8,128)(2,1)S(1)}, bf16[4,144,512]{2,1,0:T(8,128)(2,1)S(1)}, u32[]{:S(2)}, u32[]{:S(2)}) collective-permute-start(bf16[4,144,512]{2,1,0:T(8,128)(2,1)S(1)} %get-tuple-element.160), channel_id=1, source_target_pairs={{0,4},{1,5},{2,6},{3,7},{4,0},{5,1},{6,2},{7,3},{8,12},{9,13},{10,... | collective-permute-start | bytes 1769480 | tf_op jit(solution)/shard_map/ppermute | solution.py:58
  79.6 15.1 %collective-permute-start.25 = (bf16[4,144,512]{2,1,0:T(8,128)(2,1)S(1)}, bf16[4,144,512]{2,1,0:T(8,128)(2,1)S(1)}, u32[]{:S(2)}, u32[]{:S(2)}) collective-permute-start(bf16[4,144,512]{2,1,0:T(8,128)(2,1)S(1)} %get-tuple-element.161), channel_id=1, source_target_pairs={{0,2},{1,3},{2,0},{3,1},{4,6},{5,7},{6,4},{7,5},{8,10},{9,11},{10,... | collective-permute-start | bytes 1769480 | tf_op jit(solution)/shard_map/ppermute | solution.py:58
  91.0 16.2 %collective-permute-start.30 = (bf16[8,272,128]{2,1,0:T(8,128)(2,1)S(1)}, bf16[8,272,128]{2,1,0:T(8,128)(2,1)S(1)}, u32[]{:S(2)}, u32[]{:S(2)}) collective-permute-start(bf16[8,272,128]{2,1,0:T(8,128)(2,1)S(1)} %get-tuple-element.116), channel_id=1, source_target_pairs={{0,1},{1,0},{2,3},{3,2},{4,5},{5,4},{6,7},{7,6},{8,9},{9,8},{10,11... | collective-permute-start | bytes 1671176 | tf_op jit(solution)/shard_map/ppermute | solution.py:58
  95.0 10.0 %collective-permute-start.27 = (bf16[2,144,512]{2,1,0:T(8,128)(2,1)S(1)}, bf16[2,144,512]{2,1,0:T(8,128)(2,1)S(1)}, u32[]{:S(2)}, u32[]{:S(2)}) collective-permute-start(bf16[2,144,512]{2,1,0:T(8,128)(2,1)S(1)} %get-tuple-element.159), channel_id=1, source_target_pairs={{0,4},{1,5},{2,6},{3,7},{4,0},{5,1},{6,2},{7,3},{8,12},{9,13},{10,... | collective-permute-start | bytes 884744 | tf_op jit(solution)/shard_map/ppermute | solution.py:58
  96.5 9.9 %collective-permute-start.28 = (bf16[2,144,512]{2,1,0:T(8,128)(2,1)S(1)}, bf16[2,144,512]{2,1,0:T(8,128)(2,1)S(1)}, u32[]{:S(2)}, u32[]{:S(2)}) collective-permute-start(bf16[2,144,512]{2,1,0:T(8,128)(2,1)S(1)} %get-tuple-element.158), channel_id=1, source_target_pairs={{0,2},{1,3},{2,0},{3,1},{4,6},{5,7},{6,4},{7,5},{8,10},{9,11},{10,... | collective-permute-start | bytes 884744 | tf_op jit(solution)/shard_map/ppermute | solution.py:58
  97.2 11.8 %collective-permute-start.33 = (bf16[4,272,128]{2,1,0:T(8,128)(2,1)S(1)}, bf16[4,272,128]{2,1,0:T(8,128)(2,1)S(1)}, u32[]{:S(2)}, u32[]{:S(2)}) collective-permute-start(bf16[4,272,128]{2,1,0:T(8,128)(2,1)S(1)} %get-tuple-element.162), channel_id=1, source_target_pairs={{0,4},{1,5},{2,6},{3,7},{4,0},{5,1},{6,2},{7,3},{8,12},{9,13},{10,... | collective-permute-start | bytes 835592 | tf_op jit(solution)/shard_map/ppermute | solution.py:58
  97.8 12.3 %collective-permute-start.32 = (bf16[4,272,128]{2,1,0:T(8,128)(2,1)S(1)}, bf16[4,272,128]{2,1,0:T(8,128)(2,1)S(1)}, u32[]{:S(2)}, u32[]{:S(2)}) collective-permute-start(bf16[4,272,128]{2,1,0:T(8,128)(2,1)S(1)} %get-tuple-element.163), channel_id=1, source_target_pairs={{0,2},{1,3},{2,0},{3,1},{4,6},{5,7},{6,4},{7,5},{8,10},{9,11},{10,... | collective-permute-start | bytes 835592 | tf_op jit(solution)/shard_map/ppermute | solution.py:58
  106.8 9.2 %collective-permute-start.29 = (bf16[2,144,512]{2,1,0:T(8,128)(2,1)S(1)}, bf16[2,144,512]{2,1,0:T(8,128)(2,1)S(1)}, u32[]{:S(2)}, u32[]{:S(2)}) collective-permute-start(bf16[2,144,512]{2,1,0:T(8,128)(2,1)S(1)} %get-tuple-element.107), channel_id=1, source_target_pairs={{0,8},{1,9},{2,10},{3,11},{4,12},{5,13},{6,14},{7,15},{8,0},{9,1},... | collective-permute-start | bytes 884744 | tf_op jit(solution)/shard_map/ppermute | solution.py:58
  118.7 11.4 %collective-permute-start.41 = (bf16[2,128,512]{2,1,0:T(8,128)(2,1)S(1)}, bf16[2,128,512]{2,1,0:T(8,128)(2,1)S(1)}, u32[]{:S(2)}, u32[]{:S(2)}) collective-permute-start(bf16[2,128,512]{2,1,0:T(8,128)(2,1)S(1)} %get-tuple-element.136), channel_id=1, source_target_pairs={{0,2},{1,3},{2,0},{3,1},{4,6},{5,7},{6,4},{7,5},{8,10},{9,11},{10,... | collective-permute-start | bytes 786440 | tf_op jit(solution)/shard_map/ppermute | solution.py:58
  119.3 10.9 %collective-permute-start.42 = (bf16[2,128,512]{2,1,0:T(8,128)(2,1)S(1)}, bf16[2,128,512]{2,1,0:T(8,128)(2,1)S(1)}, u32[]{:S(2)}, u32[]{:S(2)}) collective-permute-start(bf16[2,128,512]{2,1,0:T(8,128)(2,1)S(1)} %get-tuple-element.137), channel_id=1, source_target_pairs={{0,3},{1,2},{2,1},{3,0},{4,7},{5,6},{6,5},{7,4},{8,11},{9,10},{10,... | collective-permute-start | bytes 786440 | tf_op jit(solution)/shard_map/ppermute | solution.py:58
  119.3 10.8 %collective-permute-start.39 = (bf16[1,128,512]{2,1,0:T(8,128)(2,1)S(1)}, bf16[1,128,512]{2,1,0:T(8,128)(2,1)S(1)}, u32[]{:S(2)}, u32[]{:S(2)}) collective-permute-start(bf16[1,128,512]{2,1,0:T(8,128)(2,1)S(1)} %get-tuple-element.132), channel_id=1, source_target_pairs={{0,1},{1,0},{2,3},{3,2},{4,5},{5,4},{6,7},{7,6},{8,9},{9,8},{10,11... | collective-permute-start | bytes 393224 | tf_op jit(solution)/shard_map/ppermute | solution.py:58
  (38 other events, 214.4 us)

commit v6 on v5

--- a/solution.py
+++ b/solution.py
@@ -72,14 +72,11 @@
     return [keep(h) for h in range(LANES // HD)]
 
 
-def fill_window(me_t, which, parts, out_ref, sems):
+def fill_window(me_t, which, parts, out_ref):
     own, rx, c1, c3 = parts
     n = own.shape[1]
-    sources = (own.at[me_t], c1.at[which], rx.at[which], c3.at[which])
-    copies = [pltpu.make_async_copy(src, out_ref.at[rows_at((me_t ^ r) * n, n, n), :], sems.at[r]) for r, src in enumerate(sources)]
-    for copy in copies:
-        copy.start()
-    return copies
+    for r, ref in enumerate((own, c1, rx, c3)):
+        out_ref[rows_at((me_t ^ r) * n, n, n), :] = ref[which]
 
 
 def copies_in(moves, sems):
@@ -89,10 +86,10 @@
     return copies
 
 
-def prepare_kernel(scal, inputs, cot, attn, pos, norm, out, up, down, ga, gb, xs, c1, attn_s, pos_s, norm_s, out_s, up_s, down_s, sems):
+def prepare_kernel(scal, inputs, cot, attn, pos, norm, out, up, down, ga, gb, xs, c1, own, attn_s, pos_s, norm_s, out_s, up_s, down_s, sems):
     me_t = scal[1]
     moves = [(attn, attn_s), (pos, pos_s), (norm, norm_s), (up, up_s), (down, down_s), (out, out_s)]
-    for rel, ref, at in ((2, xs, 0), (3, xs, 2), (1, c1, 0)):
+    for rel, ref, at in ((2, xs, 0), (3, xs, 2), (1, c1, 0), (0, own, 0)):
         moves += [(inputs.at[me_t ^ rel], ref.at[at]), (cot.at[me_t ^ rel], ref.at[at + 1])]
     copies = copies_in(moves, sems)
     for copy in copies[:3]:
@@ -130,7 +127,7 @@
 def attention_kernel(places, n_pieces, scal, *refs):
     own, rx, c1, c3, segs = refs[:5]
     pieces = refs[5 : 5 + n_pieces]
-    hid_o, qkv_h, pt_h, mix_o, w_h, nrm_o, x_s, pos_s, bias_s, nrm_s, w_o, qkv_o, pt_o, sems, out_sems = refs[5 + n_pieces :]
+    hid_o, qkv_h, pt_h, mix_o, w_h, nrm_o, x_s, pos_s, bias_s, nrm_s, w_o, qkv_o, pt_o, out_sems = refs[5 + n_pieces :]
     leaving = []
 
     def leave(src, dst):
@@ -140,7 +137,7 @@
     me_dp, me_t = scal[0], scal[1]
     win, width = x_s.shape
     groups = w_o.shape[1] // (3 * LANES)
-    filling = fill_window(me_t, 0, (own, rx, c1, c3), x_s, sems)
+    fill_window(me_t, 0, (own, rx, c1, c3), x_s)
     if places is None:
         w_o[...] = pieces[0][...]
         pos_s[...] = pieces[1][...]
@@ -181,8 +178,6 @@
         counts = (key_seg == seg) & (query_at >= key_at)
         bias_s[i * LANES : (i + 1) * LANES, :] = jnp.where(counts, 0.0, NEG_FILL)
 
-    for copy in filling:
-        copy.wait()
     hidden = x_s[...].astype(F32) + pos_s[...].astype(F32)
     hid_o[...] = hidden
     x_s[...] = hidden.astype(BF16)
@@ -195,6 +190,7 @@
         v = qkv[:, 2 * LANES :]
         qkv_o[:, at : at + LANES] = q
         qkv_o[:, at + LANES : at + 3 * LANES] = qkv[:, LANES:]
+        leave(qkv_o.at[:, at : at + 3 * LANES], qkv_h.at[:, at : at + 3 * LANES])
         for j in range(win // QUERIES):
             ext = (j + 1) * QUERIES
             cols = slice(j * QUERIES, ext)
@@ -208,7 +204,6 @@
             mix_o[cols, g * LANES : (g + 1) * LANES] = mixed.astype(BF16)
             for h in range(len(heads)):
                 leave(pt_o.at[len(heads) * g + h, :ext, cols], pt_h.at[len(heads) * g + h, :ext, cols])
-    leave(qkv_o, qkv_h)
     for copy in leaving:
         copy.wait()
 
@@ -254,11 +249,11 @@
     else:
         chunks_o = rest[6:10]
         rest = rest[10:]
-    cot_s, out_s, up_s, down_s, a_s, b_s, g_s, xh1_s, r1_s, n1_s, sent_s, act_s, dg_s, low_s, xt_s, sems = rest
+    cot_s, out_s, up_s, down_s, a_s, b_s, g_s, xh1_s, r1_s, n1_s, sent_s, act_s, dg_s, low_s, xt_s = rest
     me_dp, me_t = scal[0], scal[1]
     win, width = hid.shape
     groups = up_s.shape[0]
-    filling = fill_window(me_t, 1, (own, rx, c1, c3), cot_s, sems)
+    fill_window(me_t, 1, (own, rx, c1, c3), cot_s)
     if places is None:
         n_dp = 1
         for src, dst in zip(pieces, (out_s, up_s, down_s), strict=True):
@@ -303,9 +298,6 @@
 
         chunks(gelu)
         n1_s[...] += mm(act_s[g], down_s[g])
-
-    for copy in filling:
-        copy.wait()
 
     def norm_two(i, sums):
         at = slice(i * CHUNK, (i + 1) * CHUNK)
@@ -387,22 +379,23 @@
     win, width = hid.shape
     groups = w.shape[1] // (3 * LANES)
     heads = by_head(win)
-    arriving = [pltpu.make_async_copy(qkv_h, qkv, sems.at[0])]
-    for n in range(pt.shape[0]):
-        for j in range(win // QUERIES):
-            ext = (j + 1) * QUERIES
-            cols = slice(j * QUERIES, ext)
-            arriving.append(pltpu.make_async_copy(pt_h.at[n, :ext, cols], pt.at[n, :ext, cols], sems.at[len(arriving)]))
+    arriving = []
+    for g in range(groups):
+        lanes = slice(g * 3 * LANES, (g + 1) * 3 * LANES)
+        arriving.append(pltpu.make_async_copy(qkv_h.at[:, lanes], qkv.at[:, lanes], sems.at[len(arriving)]))
+        for n in range(g * len(heads), (g + 1) * len(heads)):
+            for j in range(win // QUERIES):
+                ext = (j + 1) * QUERIES
+                cols = slice(j * QUERIES, ext)
+                arriving.append(pltpu.make_async_copy(pt_h.at[n, :ext, cols], pt.at[n, :ext, cols], sems.at[len(arriving)]))
     arriving.append(pltpu.make_async_copy(w_h, w, sems.at[len(arriving)]))
     for copy in arriving:
         copy.start()
     ht_s[...] = jnp.transpose(hid[...].astype(BF16))
     for g in range(groups):
         at = g * 3 * LANES
-        if g == 0:
-            arriving[0].wait()
-        per_group = len(heads) * (win // QUERIES)
-        for copy in arriving[1 + g * per_group : 1 + (g + 1) * per_group]:
+        per_group = 1 + len(heads) * (win // QUERIES)
+        for copy in arriving[g * per_group : (g + 1) * per_group]:
             copy.wait()
         q = qkv[:, at : at + LANES]
         k = qkv[:, at + LANES : at + 2 * LANES]
@@ -514,12 +507,18 @@
     update(norm, half, RATES[5], DECAYS[5])
 
 
-def finish_kernel(scal, done, res_k, gi_k, res_1, gi_1, r2, r3, res_o, gi_o):
+def finish_kernel(scal, done, res_k, gi_k, res_1, gi_1, r2, r3, res_o, gi_o, gi_s, sems):
     del done
     me_t = scal[1]
-    for r, (res, gi) in enumerate(((res_k[...], gi_k[...]), (res_1[0], gi_1[0]), (r2[0], r2[1]), (r3[0], r3[1]))):
-        res_o[me_t ^ r] = res
-        gi_o[me_t ^ r] = gi.astype(F32)
+    moves = [(gi_k, gi_o.at[me_t])]
+    moves += [(res, res_o.at[me_t ^ r]) for r, res in enumerate((res_k, res_1.at[0], r2.at[0], r3.at[0]))]
+    copies = copies_in(moves, sems)
+    for r, gi in ((1, gi_1.at[0]), (2, r2.at[1]), (3, r3.at[1])):
+        gi_s[r - 1] = gi[...].astype(F32)
+        copies.append(pltpu.make_async_copy(gi_s.at[r - 1], gi_o.at[me_t ^ r], sems.at[4 + r]))
+        copies[-1].start()
+    for copy in copies:
+        copy.wait()
 
 
 def after(value, *others):
@@ -652,15 +651,16 @@
     sds = jax.ShapeDtypeStruct
 
     if fast:
-        ga, gb, xs, c1 = call(
+        ga, gb, xs, c1, own = call(
             prepare_kernel,
             [
                 sds((1, 3 * per + width // LANES * pos_per + 16, LANES), BF16),
                 sds((1, 2 * per + out_per, width), BF16),
                 sds((4, block, width), BF16),
                 sds((2, block, width), BF16),
+                sds((2, block, width), BF16),
             ],
-            [(v.shape, F32) for v in (attn_proj, pos_table, norm_params, out_proj, up_proj, down_proj)] + [[12]],
+            [(v.shape, F32) for v in (attn_proj, pos_table, norm_params, out_proj, up_proj, down_proj)] + [[14]],
             [scal, inputs, cotangent, attn_proj, pos_table, norm_params, out_proj, up_proj, down_proj],
             "s" + "h" * 8,
             8,
@@ -683,7 +683,7 @@
             return jnp.concatenate([lax.dynamic_slice_in_dim(v, me_t ^ rel, 1, 0) for v in (inputs, cotangent)])
 
         rx = swap(jnp.concatenate([pair(2), pair(3)]), 0, 2)
-        c1 = swap(pair(1), 0, 1)
+        own, c1 = pair(0), swap(pair(1), 0, 1)
         c3 = swap(rx[2:], 0, 1)
         relative = me_t ^ jnp.arange(n_t)
         whole = [lax.all_gather(lax.all_gather(v.astype(BF16), "dp"), "tensor") for v in (attn_proj, out_proj, up_proj, down_proj)]
@@ -705,9 +705,9 @@
             pltpu.HBM((width, n_t * 3 * group), BF16),
             sds((8, width), F32),
         ],
-        [((win, width), BF16), ((win, width), BF16), ((win, win), F32), ((n_dp, 16, LANES), F32), ((width, n_t * 3 * group), BF16), ((win, n_t * 3 * group), BF16), ((n_t * group // HD, win, win), BF16), [4], [32]],
-        [scal, inputs, rx, c1, c3, segment_ids, *a_args],
-        "shaaav" + "v" * len(a_args),
+        [((win, width), BF16), ((win, width), BF16), ((win, win), F32), ((n_dp, 16, LANES), F32), ((width, n_t * 3 * group), BF16), ((win, n_t * 3 * group), BF16), ((n_t * group // HD, win, win), BF16), [32]],
+        [scal, own, rx, c1, c3, segment_ids, *a_args],
+        "svvvvv" + "v" * len(a_args),
         14,
         1_000_000,
     )
@@ -739,11 +739,10 @@
             ((n_t, win, inner), F32),
             ((win, width), BF16),
             ((width, win), BF16),
-            [4],
         ],
-        [scal, cotangent, rx, c1, c3, hid, mixed, norm_all, *b_args],
-        "shaaavvv" + "v" * len(b_args),
-        22,
+        [scal, own, rx, c1, c3, hid, mixed, norm_all, *b_args],
+        "svvvvvvv" + "v" * len(b_args),
+        26,
         1_000_000,
     )
     if fast:
@@ -769,7 +768,7 @@
             ((win, n_t * 3 * group), BF16),
             ((n_t * group // HD, win, win), BF16),
             ((width, n_t * 3 * group), BF16),
-            [2 + 2 * n_t * group // HD],
+            [1 + n_t + 2 * n_t * group // HD],
         ],
         [scal, hid, qkv, pt, gm, attn_all, gone, gnorm],
         "svhhvhvv",
@@ -842,8 +841,8 @@
         done = new[9]
     outputs, grad_input = call(
         finish_kernel,
-        [sds(inputs.shape, BF16), sds(inputs.shape, F32)],
-        [],
+        [pltpu.HBM(inputs.shape, BF16), pltpu.HBM(inputs.shape, F32)],
+        [((3, block, width), F32), [8]],
         [scal, done, res_k, gi_k, *r1, r2, r3],
         "sv" + "v" * 6,
         8,

time: 132 us -> 130 us (0.985)
  Pallas kernels: 39.4 us -> 36.3 us
    pallas_call x15, Pallas kernels: 39.4 us -> 36.3 us  [call(): pl.pallas_call(kernel, out_shape=outs, in_specs=[kinds[k] for k in spaces...]
  transfers between devices with their start and end apart: 43 -> 43, of which waited for: 24 -> 24; matrix products, arithmetic and copies ran while one was open for 1% -> 1% of each run, Pallas kernels for 17% -> 16%
where the time goes in v6:
time: 130 us; the launch traced here: 129 us
  waiting for transfers between devices  54.7 us (42%)
  Pallas kernels  36.3 us (28%)
  starting transfers between devices  36 us (28%)
  between operations  1.32 us (1%)
    ppermute x43, waiting for transfers between devices, swap(): lax.ppermute(value, AXES, [(i, i ^ mask) for i in range(lax.axis_size('dp...  54.7 us
    pallas_call x15, Pallas kernels, call(): pl.pallas_call(kernel, out_shape=outs, in_specs=[kinds[k] for k in spaces...  36.3 us
    ppermute x43, starting transfers between devices, swap(): lax.ppermute(value, AXES, [(i, i ^ mask) for i in range(lax.axis_size('dp...  36 us
  transfers between devices with their start and end apart: 43, of which 24 were waited for; matrix products, arithmetic and copies ran while one was open for 1% of the time, Pallas kernels for 16%

profile of v6, /device:TPU:0, one launch (start us, length us, event | category | flops | bytes accessed | tf_op | source)
XLA Modules:
  0.0 129.4 jit_solution(9666959545084736496)
XLA Ops:
  0.7 2.1 %shard_map.356 = (bf16[1,272,128]{2,1,0:T(8,128)(2,1)S(1)}, bf16[1,144,512]{2,1,0:T(8,128)(2,1)S(1)}, bf16[4,128,512]{2,1,0:T(8,128)(2,1)S(1)}, bf16[2,128,512]{2,1,0:T(8,128)(2,1)S(1)}, bf16[2,128,512]{2,1,0:T(8,128)(2,1)S(1)}) custom-call(s32[2]{0:T(128)S(1)} %pad_add_fusion.scal, bf16[4,128,512]{2,1,0:T(8,128)(2,1)} %inputs.1, bf16[4,128,512]{2,1,0:T(8,128)(2,1)} %cot.1, ...), custom_call_target="tpu_custom_call" | custom-call | flops 1000 | tf_op jit(solution)/shard_map/pallas_call | solution.py:608
  2.8 3.0 %collective-permute-start = (bf16[4,128,512]{2,1,0:T(8,128)(2,1)S(1)}, bf16[4,128,512]{2,1,0:T(8,128)(2,1)S(1)}, u32[]{:S(2)}, u32[]{:S(2)}) collective-permute-start(bf16[4,128,512]{2,1,0:T(8,128)(2,1)S(1)} %get-tuple-element.91), channel_id=1, source_target_pairs={{0,2},{1,3},{2,0},{3,1},{4,6},{5,7},{6,4},{7,5},{8,10},{9,11},{10,... | collective-permute-start | bytes 1572872 | tf_op jit(solution)/shard_map/ppermute | solution.py:58
  5.8 2.6 %collective-permute-start.3 = (bf16[1,272,128]{2,1,0:T(8,128)(2,1)S(1)}, bf16[1,272,128]{2,1,0:T(8,128)(2,1)S(1)}, u32[]{:S(2)}, u32[]{:S(2)}) collective-permute-start(bf16[1,272,128]{2,1,0:T(8,128)(2,1)S(1)} %get-tuple-element.93.own), channel_id=1, source_target_pairs={{0,16},{1,17},{2,18},{3,19},{4,20},{5,21},{6,22},{7,23},{8,24},{9,... | collective-permute-start | bytes 208904 | tf_op jit(solution)/shard_map/ppermute | solution.py:58
  8.4 3.0 %collective-permute-done.3.got = bf16[1,272,128]{2,1,0:T(8,128)(2,1)S(1)} collective-permute-done((bf16[1,272,128]{2,1,0:T(8,128)(2,1)S(1)}, bf16[1,272,128]{2,1,0:T(8,128)(2,1)S(1)}, u32[]{:S(2)}, u32[]{:S(2)}) %collective-permute-start.3) | collective-permute-done | bytes 69664 | tf_op jit(solution)/shard_map/ppermute | solution.py:58
  11.4 2.4 %collective-permute-start.12 = (bf16[1,144,512]{2,1,0:T(8,128)(2,1)S(1)}, bf16[1,144,512]{2,1,0:T(8,128)(2,1)S(1)}, u32[]{:S(2)}, u32[]{:S(2)}) collective-permute-start(bf16[1,144,512]{2,1,0:T(8,128)(2,1)S(1)} %get-tuple-element.98.own), channel_id=1, source_target_pairs={{0,16},{1,17},{2,18},{3,19},{4,20},{5,21},{6,22},{7,23},{8,24},{9,... | collective-permute-start | bytes 442376 | tf_op jit(solution)/shard_map/ppermute | solution.py:58
  13.8 2.2 %collective-permute-start.4 = (bf16[2,272,128]{2,1,0:T(8,128)(2,1)S(1)}, bf16[2,272,128]{2,1,0:T(8,128)(2,1)S(1)}, u32[]{:S(2)}, u32[]{:S(2)}) collective-permute-start(bf16[2,272,128]{2,1,0:T(8,128)(2,1)S(1)} %shard_map.357.own), channel_id=1, source_target_pairs={{0,8},{1,9},{2,10},{3,11},{4,12},{5,13},{6,14},{7,15},{8,0},{9,1},... | collective-permute-start | bytes 417800 | tf_op jit(solution)/shard_map/ppermute | solution.py:58
  16.0 3.5 %collective-permute-done.4.got = bf16[2,272,128]{2,1,0:T(8,128)(2,1)S(1)} collective-permute-done((bf16[2,272,128]{2,1,0:T(8,128)(2,1)S(1)}, bf16[2,272,128]{2,1,0:T(8,128)(2,1)S(1)}, u32[]{:S(2)}, u32[]{:S(2)}) %collective-permute-start.4) | collective-permute-done | bytes 139296 | tf_op jit(solution)/shard_map/ppermute | solution.py:58
  19.6 1.8 %collective-permute-start.13 = (bf16[2,144,512]{2,1,0:T(8,128)(2,1)S(1)}, bf16[2,144,512]{2,1,0:T(8,128)(2,1)S(1)}, u32[]{:S(2)}, u32[]{:S(2)}) collective-permute-start(bf16[2,144,512]{2,1,0:T(8,128)(2,1)S(1)} %shard_map.360.own), channel_id=1, source_target_pairs={{0,8},{1,9},{2,10},{3,11},{4,12},{5,13},{6,14},{7,15},{8,0},{9,1},... | collective-permute-start | bytes 884744 | tf_op jit(solution)/shard_map/ppermute | solution.py:58
  24.9 1.7 %collective-permute-done.13.got = bf16[2,144,512]{2,1,0:T(8,128)(2,1)S(1)} collective-permute-done((bf16[2,144,512]{2,1,0:T(8,128)(2,1)S(1)}, bf16[2,144,512]{2,1,0:T(8,128)(2,1)S(1)}, u32[]{:S(2)}, u32[]{:S(2)}) %collective-permute-start.13) | collective-permute-done | bytes 294944 | tf_op jit(solution)/shard_map/ppermute | solution.py:58
  26.6 5.4 %collective-permute-done.8.refs_9_ = bf16[4,272,128]{2,1,0:T(8,128)(2,1)S(1)} collective-permute-done((bf16[4,272,128]{2,1,0:T(8,128)(2,1)S(1)}, bf16[4,272,128]{2,1,0:T(8,128)(2,1)S(1)}, u32[]{:S(2)}, u32[]{:S(2)}) %collective-permute-start.8) | collective-permute-done | bytes 278560 | tf_op jit(solution)/shard_map/ppermute | solution.py:58
  35.2 3.1 %collective-permute-done.10.refs_11_ = bf16[4,272,128]{2,1,0:T(8,128)(2,1)S(1)} collective-permute-done((bf16[4,272,128]{2,1,0:T(8,128)(2,1)S(1)}, bf16[4,272,128]{2,1,0:T(8,128)(2,1)S(1)}, u32[]{:S(2)}, u32[]{:S(2)}) %collective-permute-start.10) | collective-permute-done | bytes 278560 | tf_op jit(solution)/shard_map/ppermute | solution.py:58
  41.5 7.5 %shard_map.359 = (f32[512,512]{1,0:T(8,128)S(1)}, bf16[512,1536]{1,0:T(8,128)(2,1)}, bf16[8,512,512]{2,1,0:T(8,128)(2,1)}, bf16[512,512]{1,0:T(8,128)(2,1)S(1)},...) custom-call(s32[2]{0:T(128)S(1)} %pad_add_fusion.scal, bf16[2,128,512]{2,1,0:T(8,128)(2,1)S(1)} %get-tuple-element.90.refs_0_, ...), custom_call_target="tpu_custom_call" | custom-call | flops 1000000 | tf_op jit(solution)/shard_map/pallas_call | solution.py:608
  51.7 6.5 %collective-permute-done.19.refs_13_ = bf16[2,144,512]{2,1,0:T(8,128)(2,1)S(1)} collective-permute-done((bf16[2,144,512]{2,1,0:T(8,128)(2,1)S(1)}, bf16[2,144,512]{2,1,0:T(8,128)(2,1)S(1)}, u32[]{:S(2)}, u32[]{:S(2)}) %collective-permute-start.19) | collective-permute-done | bytes 294944 | tf_op jit(solution)/shard_map/ppermute | solution.py:58
  58.2 1.9 %collective-permute-done.21.refs_15_ = bf16[2,144,512]{2,1,0:T(8,128)(2,1)S(1)} collective-permute-done((bf16[2,144,512]{2,1,0:T(8,128)(2,1)S(1)}, bf16[2,144,512]{2,1,0:T(8,128)(2,1)S(1)}, u32[]{:S(2)}, u32[]{:S(2)}) %collective-permute-start.21) | collective-permute-done | bytes 294944 | tf_op jit(solution)/shard_map/ppermute | solution.py:58
  61.7 11.4 %shard_map.362 = (bf16[128,512]{1,0:T(8,128)(2,1)S(1)}, bf16[1,128,512]{2,1,0:T(8,128)(2,1)S(1)}, bf16[2,128,512]{2,1,0:T(8,128)(2,1)S(1)}, f32[512,512]{1,0:T(8...) custom-call(s32[2]{0:T(128)S(1)} %pad_add_fusion.scal, ...), custom_call_target="tpu_custom_call" | custom-call | flops 1000000 | tf_op jit(solution)/shard_map/pallas_call | solution.py:608
  73.6 2.3 %collective-permute-done.24 = bf16[8,144,512]{2,1,0:T(8,128)(2,1)S(1)} collective-permute-done((bf16[8,144,512]{2,1,0:T(8,128)(2,1)S(1)}, bf16[8,144,512]{2,1,0:T(8,128)(2,1)S(1)}, u32[]{:S(2)}, u32[]{:S(2)}) %collective-permute-start.24) | collective-permute-done | bytes 1179680 | tf_op jit(solution)/shard_map/ppermute | solution.py:58
  77.4 10.4 %shard_map.364 = (f32[128,512]{1,0:T(8,128)S(1)}, bf16[1,128,512]{2,1,0:T(8,128)(2,1)S(1)}, bf16[2,128,512]{2,1,0:T(8,128)(2,1)S(1)}, bf16[8,272,128]{2,1,0:T(8,...) custom-call(s32[2]{0:T(128)S(1)} %pad_add_fusion.scal, ...), custom_call_target="tpu_custom_call" | custom-call | flops 1000000 | tf_op jit(solution)/shard_map/pallas_call | solution.py:608
  88.5 3.3 %collective-permute-done.26.y = bf16[4,144,512]{2,1,0:T(8,128)(2,1)S(1)} collective-permute-done((bf16[4,144,512]{2,1,0:T(8,128)(2,1)S(1)}, bf16[4,144,512]{2,1,0:T(8,128)(2,1)S(1)}, u32[]{:S(2)}, u32[]{:S(2)}) %collective-permute-start.26) | collective-permute-done | bytes 589856 | tf_op jit(solution)/shard_map/ppermute | solution.py:58
  96.6 5.7 %collective-permute-done.27.x2 = bf16[2,144,512]{2,1,0:T(8,128)(2,1)S(1)} collective-permute-done((bf16[2,144,512]{2,1,0:T(8,128)(2,1)S(1)}, bf16[2,144,512]{2,1,0:T(8,128)(2,1)S(1)}, u32[]{:S(2)}, u32[]{:S(2)}) %collective-permute-start.27) | collective-permute-done | bytes 294944 | tf_op jit(solution)/shard_map/ppermute | solution.py:58
  104.5 1.8 %collective-permute-done.33.y = bf16[4,272,128]{2,1,0:T(8,128)(2,1)S(1)} collective-permute-done((bf16[4,272,128]{2,1,0:T(8,128)(2,1)S(1)}, bf16[4,272,128]{2,1,0:T(8,128)(2,1)S(1)}, u32[]{:S(2)}, u32[]{:S(2)}) %collective-permute-start.33) | collective-permute-done | bytes 278560 | tf_op jit(solution)/shard_map/ppermute | solution.py:58
  108.7 3.9 %collective-permute-done.34.x2 = bf16[2,272,128]{2,1,0:T(8,128)(2,1)S(1)} collective-permute-done((bf16[2,272,128]{2,1,0:T(8,128)(2,1)S(1)}, bf16[2,272,128]{2,1,0:T(8,128)(2,1)S(1)}, u32[]{:S(2)}, u32[]{:S(2)}) %collective-permute-start.34) | collective-permute-done | bytes 139296 | tf_op jit(solution)/shard_map/ppermute | solution.py:58
  114.0 2.0 %collective-permute-start.36 = (bf16[1,144,512]{2,1,0:T(8,128)(2,1)S(1)}, bf16[1,144,512]{2,1,0:T(8,128)(2,1)S(1)}, u32[]{:S(2)}, u32[]{:S(2)}) collective-permute-start(bf16[1,144,512]{2,1,0:T(8,128)(2,1)S(1)} %get-tuple-element.124), channel_id=1, source_target_pairs={{0,16},{1,17},{2,18},{3,19},{4,20},{5,21},{6,22},{7,23},{8,24},{9,... | collective-permute-start | bytes 442376 | tf_op jit(solution)/shard_map/ppermute | solution.py:58
  118.2 2.1 %collective-permute-done.37.near = bf16[2,272,128]{2,1,0:T(8,128)(2,1)S(1)} collective-permute-done((bf16[2,272,128]{2,1,0:T(8,128)(2,1)S(1)}, bf16[2,272,128]{2,1,0:T(8,128)(2,1)S(1)}, u32[]{:S(2)}, u32[]{:S(2)}) %collective-permute-start.37) | collective-permute-done | bytes 139296 | tf_op jit(solution)/shard_map/ppermute | solution.py:58
  123.3 2.6 %collective-permute-done.38.far = bf16[1,272,128]{2,1,0:T(8,128)(2,1)S(1)} collective-permute-done((bf16[1,272,128]{2,1,0:T(8,128)(2,1)S(1)}, bf16[1,272,128]{2,1,0:T(8,128)(2,1)S(1)}, u32[]{:S(2)}, u32[]{:S(2)}) %collective-permute-start.38) | collective-permute-done | bytes 69664 | tf_op jit(solution)/shard_map/ppermute | solution.py:58
  (125 shorter events, 35.8 us)
Async XLA Ops:
  2.8 29.6 %collective-permute-start = (bf16[4,128,512]{2,1,0:T(8,128)(2,1)S(1)}, bf16[4,128,512]{2,1,0:T(8,128)(2,1)S(1)}, u32[]{:S(2)}, u32[]{:S(2)}) collective-permute-start(bf16[4,128,512]{2,1,0:T(8,128)(2,1)S(1)} %get-tuple-element.91), channel_id=1, source_target_pairs={{0,2},{1,3},{2,0},{3,1},{4,6},{5,7},{6,4},{7,5},{8,10},{9,11},{10,... | collective-permute-start | bytes 1572872 | tf_op jit(solution)/shard_map/ppermute | solution.py:58
  11.4 8.2 %collective-permute-start.12 = (bf16[1,144,512]{2,1,0:T(8,128)(2,1)S(1)}, bf16[1,144,512]{2,1,0:T(8,128)(2,1)S(1)}, u32[]{:S(2)}, u32[]{:S(2)}) collective-permute-start(bf16[1,144,512]{2,1,0:T(8,128)(2,1)S(1)} %get-tuple-element.98.own), channel_id=1, source_target_pairs={{0,16},{1,17},{2,18},{3,19},{4,20},{5,21},{6,22},{7,23},{8,24},{9,... | collective-permute-start | bytes 442376 | tf_op jit(solution)/shard_map/ppermute | solution.py:58
  21.4 10.7 %collective-permute-start.8 = (bf16[4,272,128]{2,1,0:T(8,128)(2,1)S(1)}, bf16[4,272,128]{2,1,0:T(8,128)(2,1)S(1)}, u32[]{:S(2)}, u32[]{:S(2)}) collective-permute-start(bf16[4,272,128]{2,1,0:T(8,128)(2,1)S(1)} %shard_map.358.refs_5_), channel_id=1, source_target_pairs={{0,4},{1,5},{2,6},{3,7},{4,0},{5,1},{6,2},{7,3},{8,12},{9,13},{10,... | collective-permute-start | bytes 835592 | tf_op jit(solution)/shard_map/ppermute | solution.py:58
  22.9 9.6 %collective-permute-start.6 = (bf16[4,272,128]{2,1,0:T(8,128)(2,1)S(1)}, bf16[4,272,128]{2,1,0:T(8,128)(2,1)S(1)}, u32[]{:S(2)}, u32[]{:S(2)}) collective-permute-start(bf16[4,272,128]{2,1,0:T(8,128)(2,1)S(1)} %shard_map.358.refs_5_), channel_id=1, source_target_pairs={{0,2},{1,3},{2,0},{3,1},{4,6},{5,7},{6,4},{7,5},{8,10},{9,11},{10,... | collective-permute-start | bytes 835592 | tf_op jit(solution)/shard_map/ppermute | solution.py:58
  23.4 15.0 %collective-permute-start.10 = (bf16[4,272,128]{2,1,0:T(8,128)(2,1)S(1)}, bf16[4,272,128]{2,1,0:T(8,128)(2,1)S(1)}, u32[]{:S(2)}, u32[]{:S(2)}) collective-permute-start(bf16[4,272,128]{2,1,0:T(8,128)(2,1)S(1)} %shard_map.358.refs_5_), channel_id=1, source_target_pairs={{0,6},{1,7},{2,4},{3,5},{4,2},{5,3},{6,0},{7,1},{8,14},{9,15},{10,... | collective-permute-start | bytes 835592 | tf_op jit(solution)/shard_map/ppermute | solution.py:58
  32.5 16.5 %collective-permute-start.17 = (bf16[4,144,512]{2,1,0:T(8,128)(2,1)S(1)}, bf16[4,144,512]{2,1,0:T(8,128)(2,1)S(1)}, u32[]{:S(2)}, u32[]{:S(2)}) collective-permute-start(bf16[4,144,512]{2,1,0:T(8,128)(2,1)S(1)} %shard_map.361.refs_7_), channel_id=1, source_target_pairs={{0,4},{1,5},{2,6},{3,7},{4,0},{5,1},{6,2},{7,3},{8,12},{9,13},{10,... | collective-permute-start | bytes 1769480 | tf_op jit(solution)/shard_map/ppermute | solution.py:58
  34.2 14.8 %collective-permute-start.15 = (bf16[4,144,512]{2,1,0:T(8,128)(2,1)S(1)}, bf16[4,144,512]{2,1,0:T(8,128)(2,1)S(1)}, u32[]{:S(2)}, u32[]{:S(2)}) collective-permute-start(bf16[4,144,512]{2,1,0:T(8,128)(2,1)S(1)} %shard_map.361.refs_7_), channel_id=1, source_target_pairs={{0,2},{1,3},{2,0},{3,1},{4,6},{5,7},{6,4},{7,5},{8,10},{9,11},{10,... | collective-permute-start | bytes 1769480 | tf_op jit(solution)/shard_map/ppermute | solution.py:58
  40.4 19.7 %collective-permute-start.14 = (bf16[4,144,512]{2,1,0:T(8,128)(2,1)S(1)}, bf16[4,144,512]{2,1,0:T(8,128)(2,1)S(1)}, u32[]{:S(2)}, u32[]{:S(2)}) collective-permute-start(bf16[4,144,512]{2,1,0:T(8,128)(2,1)S(1)} %shard_map.361.refs_7_), channel_id=1, source_target_pairs={{0,1},{1,0},{2,3},{3,2},{4,5},{5,4},{6,7},{7,6},{8,9},{9,8},{10,11... | collective-permute-start | bytes 1769480 | tf_op jit(solution)/shard_map/ppermute | solution.py:58
  49.1 9.1 %collective-permute-start.19 = (bf16[2,144,512]{2,1,0:T(8,128)(2,1)S(1)}, bf16[2,144,512]{2,1,0:T(8,128)(2,1)S(1)}, u32[]{:S(2)}, u32[]{:S(2)}) collective-permute-start(bf16[2,144,512]{2,1,0:T(8,128)(2,1)S(1)} %slice.85), channel_id=1, source_target_pairs={{0,4},{1,5},{2,6},{3,7},{4,0},{5,1},{6,2},{7,3},{8,12},{9,13},{10,... | collective-permute-start | bytes 884744 | tf_op jit(solution)/shard_map/ppermute | solution.py:58
  50.7 9.4 %collective-permute-start.18 = (bf16[4,144,512]{2,1,0:T(8,128)(2,1)S(1)}, bf16[4,144,512]{2,1,0:T(8,128)(2,1)S(1)}, u32[]{:S(2)}, u32[]{:S(2)}) collective-permute-start(bf16[4,144,512]{2,1,0:T(8,128)(2,1)S(1)} %collective-permute-done.17.refs_11_), channel_id=1, source_target_pairs={{0,1},{1,0},{2,3},{3,2},{4,5},{5,4},{6,7},{7,6},{8,9},{9,8},{10,11... | collective-permute-start | bytes 1769480 | tf_op jit(solution)/shard_map/ppermute | solution.py:58
  50.7 9.4 %collective-permute-start.16 = (bf16[4,144,512]{2,1,0:T(8,128)(2,1)S(1)}, bf16[4,144,512]{2,1,0:T(8,128)(2,1)S(1)}, u32[]{:S(2)}, u32[]{:S(2)}) collective-permute-start(bf16[4,144,512]{2,1,0:T(8,128)(2,1)S(1)} %collective-permute-done.15.refs_9_), channel_id=1, source_target_pairs={{0,1},{1,0},{2,3},{3,2},{4,5},{5,4},{6,7},{7,6},{8,9},{9,8},{10,11... | collective-permute-start | bytes 1769480 | tf_op jit(solution)/shard_map/ppermute | solution.py:58
  51.2 8.9 %collective-permute-start.21 = (bf16[2,144,512]{2,1,0:T(8,128)(2,1)S(1)}, bf16[2,144,512]{2,1,0:T(8,128)(2,1)S(1)}, u32[]{:S(2)}, u32[]{:S(2)}) collective-permute-start(bf16[2,144,512]{2,1,0:T(8,128)(2,1)S(1)} %slice.86), channel_id=1, source_target_pairs={{0,2},{1,3},{2,0},{3,1},{4,6},{5,7},{6,4},{7,5},{8,10},{9,11},{10,... | collective-permute-start | bytes 884744 | tf_op jit(solution)/shard_map/ppermute | solution.py:58
  73.2 15.2 %collective-permute-start.23 = (bf16[8,144,512]{2,1,0:T(8,128)(2,1)S(1)}, bf16[8,144,512]{2,1,0:T(8,128)(2,1)S(1)}, u32[]{:S(2)}, u32[]{:S(2)}) collective-permute-start(bf16[8,144,512]{2,1,0:T(8,128)(2,1)S(1)} %get-tuple-element.104), channel_id=1, source_target_pairs={{0,1},{1,0},{2,3},{3,2},{4,5},{5,4},{6,7},{7,6},{8,9},{9,8},{10,11... | collective-permute-start | bytes 3538952 | tf_op jit(solution)/shard_map/ppermute | solution.py:58
  76.3 15.4 %collective-permute-start.26 = (bf16[4,144,512]{2,1,0:T(8,128)(2,1)S(1)}, bf16[4,144,512]{2,1,0:T(8,128)(2,1)S(1)}, u32[]{:S(2)}, u32[]{:S(2)}) collective-permute-start(bf16[4,144,512]{2,1,0:T(8,128)(2,1)S(1)} %get-tuple-element.162), channel_id=1, source_target_pairs={{0,4},{1,5},{2,6},{3,7},{4,0},{5,1},{6,2},{7,3},{8,12},{9,13},{10,... | collective-permute-start | bytes 1769480 | tf_op jit(solution)/shard_map/ppermute | solution.py:58
  76.9 15.1 %collective-permute-start.25 = (bf16[4,144,512]{2,1,0:T(8,128)(2,1)S(1)}, bf16[4,144,512]{2,1,0:T(8,128)(2,1)S(1)}, u32[]{:S(2)}, u32[]{:S(2)}) collective-permute-start(bf16[4,144,512]{2,1,0:T(8,128)(2,1)S(1)} %get-tuple-element.163), channel_id=1, source_target_pairs={{0,2},{1,3},{2,0},{3,1},{4,6},{5,7},{6,4},{7,5},{8,10},{9,11},{10,... | collective-permute-start | bytes 1769480 | tf_op jit(solution)/shard_map/ppermute | solution.py:58
  88.0 16.5 %collective-permute-start.30 = (bf16[8,272,128]{2,1,0:T(8,128)(2,1)S(1)}, bf16[8,272,128]{2,1,0:T(8,128)(2,1)S(1)}, u32[]{:S(2)}, u32[]{:S(2)}) collective-permute-start(bf16[8,272,128]{2,1,0:T(8,128)(2,1)S(1)} %get-tuple-element.118), channel_id=1, source_target_pairs={{0,1},{1,0},{2,3},{3,2},{4,5},{5,4},{6,7},{7,6},{8,9},{9,8},{10,11... | collective-permute-start | bytes 1671176 | tf_op jit(solution)/shard_map/ppermute | solution.py:58
  92.2 10.0 %collective-permute-start.27 = (bf16[2,144,512]{2,1,0:T(8,128)(2,1)S(1)}, bf16[2,144,512]{2,1,0:T(8,128)(2,1)S(1)}, u32[]{:S(2)}, u32[]{:S(2)}) collective-permute-start(bf16[2,144,512]{2,1,0:T(8,128)(2,1)S(1)} %get-tuple-element.161), channel_id=1, source_target_pairs={{0,4},{1,5},{2,6},{3,7},{4,0},{5,1},{6,2},{7,3},{8,12},{9,13},{10,... | collective-permute-start | bytes 884744 | tf_op jit(solution)/shard_map/ppermute | solution.py:58
  93.8 9.9 %collective-permute-start.28 = (bf16[2,144,512]{2,1,0:T(8,128)(2,1)S(1)}, bf16[2,144,512]{2,1,0:T(8,128)(2,1)S(1)}, u32[]{:S(2)}, u32[]{:S(2)}) collective-permute-start(bf16[2,144,512]{2,1,0:T(8,128)(2,1)S(1)} %get-tuple-element.160), channel_id=1, source_target_pairs={{0,2},{1,3},{2,0},{3,1},{4,6},{5,7},{6,4},{7,5},{8,10},{9,11},{10,... | collective-permute-start | bytes 884744 | tf_op jit(solution)/shard_map/ppermute | solution.py:58
  94.5 11.8 %collective-permute-start.33 = (bf16[4,272,128]{2,1,0:T(8,128)(2,1)S(1)}, bf16[4,272,128]{2,1,0:T(8,128)(2,1)S(1)}, u32[]{:S(2)}, u32[]{:S(2)}) collective-permute-start(bf16[4,272,128]{2,1,0:T(8,128)(2,1)S(1)} %get-tuple-element.164), channel_id=1, source_target_pairs={{0,4},{1,5},{2,6},{3,7},{4,0},{5,1},{6,2},{7,3},{8,12},{9,13},{10,... | collective-permute-start | bytes 835592 | tf_op jit(solution)/shard_map/ppermute | solution.py:58
  95.1 12.3 %collective-permute-start.32 = (bf16[4,272,128]{2,1,0:T(8,128)(2,1)S(1)}, bf16[4,272,128]{2,1,0:T(8,128)(2,1)S(1)}, u32[]{:S(2)}, u32[]{:S(2)}) collective-permute-start(bf16[4,272,128]{2,1,0:T(8,128)(2,1)S(1)} %get-tuple-element.165), channel_id=1, source_target_pairs={{0,2},{1,3},{2,0},{3,1},{4,6},{5,7},{6,4},{7,5},{8,10},{9,11},{10,... | collective-permute-start | bytes 835592 | tf_op jit(solution)/shard_map/ppermute | solution.py:58
  104.1 9.2 %collective-permute-start.29 = (bf16[2,144,512]{2,1,0:T(8,128)(2,1)S(1)}, bf16[2,144,512]{2,1,0:T(8,128)(2,1)S(1)}, u32[]{:S(2)}, u32[]{:S(2)}) collective-permute-start(bf16[2,144,512]{2,1,0:T(8,128)(2,1)S(1)} %get-tuple-element.109), channel_id=1, source_target_pairs={{0,8},{1,9},{2,10},{3,11},{4,12},{5,13},{6,14},{7,15},{8,0},{9,1},... | collective-permute-start | bytes 884744 | tf_op jit(solution)/shard_map/ppermute | solution.py:58
  116.0 11.5 %collective-permute-start.41 = (bf16[2,128,512]{2,1,0:T(8,128)(2,1)S(1)}, bf16[2,128,512]{2,1,0:T(8,128)(2,1)S(1)}, u32[]{:S(2)}, u32[]{:S(2)}) collective-permute-start(bf16[2,128,512]{2,1,0:T(8,128)(2,1)S(1)} %get-tuple-element.138), channel_id=1, source_target_pairs={{0,2},{1,3},{2,0},{3,1},{4,6},{5,7},{6,4},{7,5},{8,10},{9,11},{10,... | collective-permute-start | bytes 786440 | tf_op jit(solution)/shard_map/ppermute | solution.py:58
  116.6 10.9 %collective-permute-start.42 = (bf16[2,128,512]{2,1,0:T(8,128)(2,1)S(1)}, bf16[2,128,512]{2,1,0:T(8,128)(2,1)S(1)}, u32[]{:S(2)}, u32[]{:S(2)}) collective-permute-start(bf16[2,128,512]{2,1,0:T(8,128)(2,1)S(1)} %get-tuple-element.139), channel_id=1, source_target_pairs={{0,3},{1,2},{2,1},{3,0},{4,7},{5,6},{6,5},{7,4},{8,11},{9,10},{10,... | collective-permute-start | bytes 786440 | tf_op jit(solution)/shard_map/ppermute | solution.py:58
  116.6 10.8 %collective-permute-start.39 = (bf16[1,128,512]{2,1,0:T(8,128)(2,1)S(1)}, bf16[1,128,512]{2,1,0:T(8,128)(2,1)S(1)}, u32[]{:S(2)}, u32[]{:S(2)}) collective-permute-start(bf16[1,128,512]{2,1,0:T(8,128)(2,1)S(1)} %get-tuple-element.134), channel_id=1, source_target_pairs={{0,1},{1,0},{2,3},{3,2},{4,5},{5,4},{6,7},{7,6},{8,9},{9,8},{10,11... | collective-permute-start | bytes 393224 | tf_op jit(solution)/shard_map/ppermute | solution.py:58
  (38 other events, 214.8 us)

commit v7 on v6

--- a/solution.py
+++ b/solution.py
@@ -124,16 +124,48 @@
     both[n:] = got[...]
 
 
+def leaver(sems):
+    leaving = []
+
+    def leave(src, dst):
+        leaving.append(pltpu.make_async_copy(src, dst, sems.at[len(leaving)]))
+        leaving[-1].start()
+
+    return leaving, leave
+
+
+def attend(x, w, groups, bias, qkv_o, qkv_h, pt_o, pt_h, mix_o, leave):
+    win = x.shape[0]
+    heads = by_head(win)
+    for g in groups:
+        at = g * 3 * LANES
+        qkv = mm(x[...], w[:, at : at + 3 * LANES]).astype(BF16)
+        q = qkv[:, :LANES] * jnp.asarray(HD**-0.5, BF16)
+        k = qkv[:, LANES : 2 * LANES]
+        v = qkv[:, 2 * LANES :]
+        qkv_o[:, at : at + LANES] = q
+        qkv_o[:, at + LANES : at + 3 * LANES] = qkv[:, LANES:]
+        leave(qkv_o.at[:, at : at + 3 * LANES], qkv_h.at[:, at : at + 3 * LANES])
+        for j in range(win // QUERIES):
+            ext = (j + 1) * QUERIES
+            cols = slice(j * QUERIES, ext)
+            mixed = jnp.zeros((QUERIES, LANES), F32)
+            for h, only in enumerate(heads):
+                s = mm(only(k)[:ext], q[cols], NT) + bias[:ext, cols]
+                e = jnp.exp(s - jnp.max(s, axis=0, keepdims=True))
+                p = (e * (1.0 / jnp.sum(e, axis=0, keepdims=True))).astype(BF16)
+                pt_o[len(heads) * g + h, :ext, cols] = p
+                mixed += mm(p, only(v)[:ext], TN)
+            mix_o[cols, g * LANES : (g + 1) * LANES] = mixed.astype(BF16)
+            for h in range(len(heads)):
+                leave(pt_o.at[len(heads) * g + h, :ext, cols], pt_h.at[len(heads) * g + h, :ext, cols])
+
+
 def attention_kernel(places, n_pieces, scal, *refs):
     own, rx, c1, c3, segs = refs[:5]
     pieces = refs[5 : 5 + n_pieces]
-    hid_o, qkv_h, pt_h, mix_o, w_h, nrm_o, x_s, pos_s, bias_s, nrm_s, w_o, qkv_o, pt_o, out_sems = refs[5 + n_pieces :]
-    leaving = []
-
-    def leave(src, dst):
-        leaving.append(pltpu.make_async_copy(src, dst, out_sems.at[len(leaving)]))
-        leaving[-1].start()
-
+    hid_o, qkv_h, pt_h, mix_o, w_h, nrm_o, x_s, wlast_o, bias_s, pos_s, nrm_s, w_o, qkv_o, pt_o, out_sems = refs[5 + n_pieces :]
+    leaving, leave = leaver(out_sems)
     me_dp, me_t = scal[0], scal[1]
     win, width = x_s.shape
     groups = w_o.shape[1] // (3 * LANES)
@@ -181,29 +213,16 @@
     hidden = x_s[...].astype(F32) + pos_s[...].astype(F32)
     hid_o[...] = hidden
     x_s[...] = hidden.astype(BF16)
-    heads = by_head(win)
-    for g in range(groups):
-        at = g * 3 * LANES
-        qkv = mm(x_s[...], w_o[:, at : at + 3 * LANES]).astype(BF16)
-        q = qkv[:, :LANES] * jnp.asarray(HD**-0.5, BF16)
-        k = qkv[:, LANES : 2 * LANES]
-        v = qkv[:, 2 * LANES :]
-        qkv_o[:, at : at + LANES] = q
-        qkv_o[:, at + LANES : at + 3 * LANES] = qkv[:, LANES:]
-        leave(qkv_o.at[:, at : at + 3 * LANES], qkv_h.at[:, at : at + 3 * LANES])
-        for j in range(win // QUERIES):
-            ext = (j + 1) * QUERIES
-            cols = slice(j * QUERIES, ext)
-            mixed = jnp.zeros((QUERIES, LANES), F32)
-            for h, only in enumerate(heads):
-                s = mm(only(k)[:ext], q[cols], NT) + bias_s[:ext, cols]
-                e = jnp.exp(s - jnp.max(s, axis=0, keepdims=True))
-                p = (e * (1.0 / jnp.sum(e, axis=0, keepdims=True))).astype(BF16)
-                pt_o[len(heads) * g + h, :ext, cols] = p
-                mixed += mm(p, only(v)[:ext], TN)
-            mix_o[cols, g * LANES : (g + 1) * LANES] = mixed.astype(BF16)
-            for h in range(len(heads)):
-                leave(pt_o.at[len(heads) * g + h, :ext, cols], pt_h.at[len(heads) * g + h, :ext, cols])
+    first = qkv_o.shape[1] // (3 * LANES)
+    attend(x_s, w_o, range(first), bias_s, qkv_o, qkv_h, pt_o, pt_h, mix_o, leave)
+    wlast_o[...] = w_o[:, first * 3 * LANES :]
+    for copy in leaving:
+        copy.wait()
+
+
+def attention_rest_kernel(x, w, bias, qkv_h, pt_h, mix_o, qkv_o, pt_o, out_sems):
+    leaving, leave = leaver(out_sems)
+    attend(x, w, range(w.shape[1] // (3 * LANES)), bias, qkv_o, qkv_h, pt_o, pt_h, mix_o, leave)
     for copy in leaving:
         copy.wait()
 
@@ -230,26 +249,29 @@
 
 def chunk_of(refs, tr, r):
     c, xr, yr, zr = tr & 1, tr >> 1, r & 1, r >> 1
-    half = refs[0].shape[0] // 4
+    half = refs[0].shape[0] // 2
     if zr < half:
-        first, slot = xr == 1, yr * half + zr
+        kind, slot = (0, yr * half + zr) if xr == 1 else (2, yr * half + zr)
     else:
-        first, slot = yr == 1, 2 * half + xr * half + zr - half
-    return refs[2 * c + (0 if first else 1)], slot
+        kind, slot = (1, xr * half + zr - half) if yr == 1 else (2, 2 * half + xr * half + zr - half)
+    return refs[3 * c + kind], slot
 
 
 def ffn_kernel(places, n_pieces, scal, *refs):
-    own, rx, c1, c3, hid, mixed, nrm = refs[:7]
-    pieces = refs[7 : 7 + n_pieces]
-    rest = refs[7 + n_pieces :]
+    own, rx, c1, c3, hid, mixed_a, mixed_b, nrm = refs[:8]
+    pieces = refs[8 : 8 + n_pieces]
+    rest = refs[8 + n_pieces :]
     res_k, res_1, res_x, gone_o, gm_o, gnorm_o = rest[:6]
     if places is None:
         gup_o, gdown_o, gout_o = rest[6:9]
         rest = rest[9:]
     else:
-        chunks_o = rest[6:10]
-        rest = rest[10:]
-    cot_s, out_s, up_s, down_s, a_s, b_s, g_s, xh1_s, r1_s, n1_s, sent_s, act_s, dg_s, low_s, xt_s = rest
+        chunks_o = rest[6:12]
+        rest = rest[12:]
+    cot_s, out_s, up_s, down_s, a_s, b_s, g_s, xh1_s, r1_s, n1_s, sent_s, act_s, dg_s, low_s, xt_s, mixed = rest
+    split = mixed_a.shape[1]
+    mixed[:, :split] = mixed_a[...]
+    mixed[:, split:] = mixed_b[...]
     me_dp, me_t = scal[0], scal[1]
     win, width = hid.shape
     groups = up_s.shape[0]
@@ -259,7 +281,7 @@
         for src, dst in zip(pieces, (out_s, up_s, down_s), strict=True):
             dst[...] = src[...]
     else:
-        n_dp = 2 * sum(len(zs) for _, yr, zs, c in places if yr == 0 and c == 0) // 2
+        n_dp = chunks_o[2].shape[0]
         per = width // n_dp
         out_per = LANES // n_dp
         for ref, (xr, yr, zs, c) in zip(pieces, places, strict=True):
@@ -366,11 +388,11 @@
         gm_o[g] = gm[:, g * LANES : (g + 1) * LANES]
 
 
-def attention_back_kernel(fast, scal, hid, qkv_h, pt_h, gm, w_h, gone, gnorm, *rest):
+def attention_back_kernel(fast, scal, hid, qkv_a, qkv_b, pt_a, pt_b, gm, w_h, gone, gnorm, *rest):
     gi_k, gi_1, gi_x = rest[:3]
     if fast:
-        chunks_o = rest[3:7]
-        rest = rest[7:]
+        chunks_o = rest[3:9]
+        rest = rest[9:]
     else:
         gattn_o, gpos_o = rest[3:5]
         rest = rest[5:]
@@ -381,13 +403,16 @@
     heads = by_head(win)
     arriving = []
     for g in range(groups):
+        first = qkv_a.shape[1] // (3 * LANES)
+        qkv_h, pt_h, base = (qkv_a, pt_a, 0) if g < first else (qkv_b, pt_b, first)
         lanes = slice(g * 3 * LANES, (g + 1) * 3 * LANES)
-        arriving.append(pltpu.make_async_copy(qkv_h.at[:, lanes], qkv.at[:, lanes], sems.at[len(arriving)]))
+        there = slice((g - base) * 3 * LANES, (g - base + 1) * 3 * LANES)
+        arriving.append(pltpu.make_async_copy(qkv_h.at[:, there], qkv.at[:, lanes], sems.at[len(arriving)]))
         for n in range(g * len(heads), (g + 1) * len(heads)):
             for j in range(win // QUERIES):
                 ext = (j + 1) * QUERIES
                 cols = slice(j * QUERIES, ext)
-                arriving.append(pltpu.make_async_copy(pt_h.at[n, :ext, cols], pt.at[n, :ext, cols], sems.at[len(arriving)]))
+                arriving.append(pltpu.make_async_copy(pt_h.at[n - base * len(heads), :ext, cols], pt.at[n, :ext, cols], sems.at[len(arriving)]))
     arriving.append(pltpu.make_async_copy(w_h, w, sems.at[len(arriving)]))
     for copy in arriving:
         copy.start()
@@ -430,7 +455,7 @@
             gattn_o[g] = mm(ht_s[...], dqkv_s[:, g * 3 * LANES : (g + 1) * 3 * LANES]).astype(BF16)
         gpos_o[...] = acc_s[...].astype(BF16)
         return
-    n_dp = chunks_o[0].shape[0]
+    n_dp = chunks_o[2].shape[0]
     per = width // n_dp
     pos_per = win // (n_dp * groups)
     for g in range(groups):
@@ -560,14 +585,13 @@
 
 
 class Reduction:
-    def __init__(self, keep_first, keep_rest, send_first, send_rest):
-        self.half = keep_first.shape[0] // 4
-        self.n = keep_first.shape[0] // 2
+    def __init__(self, keep_a, keep_b, keep_rest, send_a, send_b, send_rest):
+        self.half = keep_a.shape[0] // 2
+        self.n = keep_a.shape[0]
         self.sums = [(keep_rest,)]
         self.send_rest = send_rest
-        got = swap(send_first, 0, 1)
-        self.a = low(keep_first[: self.n], got[: self.n])
-        self.b = low(keep_first[self.n :], got[self.n :])
+        got_a, got_b = swap(send_a, 0, 1), swap(send_b, 0, 1)
+        self.a, self.b = low(keep_a, got_a), low(keep_b, got_b)
 
     def terms(self, a, start, stop):
         at = 0 if a else self.n
@@ -695,29 +719,43 @@
         a_args, a_places = [attn_w, pos_w, norm_w], None
         b_args, b_places = [out_w.reshape(n_t * group, width), up_w.reshape(n_t, width, inner), down_w.reshape(n_t, inner, width)], None
 
-    hid, qkv, pt, mixed, attn_all, norm_all = call(
+    first = n_t - 1
+    heads_of = group // HD
+
+    def kept(groups):
+        return [pltpu.HBM((win, groups * 3 * group), BF16), pltpu.HBM((groups * heads_of, win, win), BF16), sds((win, groups * group), BF16)]
+
+    def work(groups):
+        return [((win, groups * 3 * group), BF16), ((groups * heads_of, win, win), BF16), [groups * (1 + 2 * heads_of) + 1]]
+
+    hid, qkv_a, pt_a, mixed_a, attn_all, norm_all, x_all, w_last, bias = call(
         functools.partial(attention_kernel, a_places, len(a_args)),
         [
             sds((win, width), F32),
-            pltpu.HBM((win, n_t * 3 * group), BF16),
-            pltpu.HBM((n_t * group // HD, win, win), BF16),
-            sds((win, n_t * group), BF16),
+            *kept(first),
             pltpu.HBM((width, n_t * 3 * group), BF16),
             sds((8, width), F32),
+            sds((win, width), BF16),
+            sds((width, 3 * group), BF16),
+            sds((win, win), F32),
         ],
-        [((win, width), BF16), ((win, width), BF16), ((win, win), F32), ((n_dp, 16, LANES), F32), ((width, n_t * 3 * group), BF16), ((win, n_t * 3 * group), BF16), ((n_t * group // HD, win, win), BF16), [32]],
+        [((win, width), BF16), ((n_dp, 16, LANES), F32), ((width, n_t * 3 * group), BF16), *work(first)],
         [scal, own, rx, c1, c3, segment_ids, *a_args],
         "svvvvv" + "v" * len(a_args),
         14,
         1_000_000,
     )
     if fast:
-        b_args, b_places = both_cores(gather_xy(qb, zb, qbx, qby, hid))
+        found = gather_xy(qb, zb, qbx, qby, x_all)
+    qkv_b, pt_b, mixed_b = call(attention_rest_kernel, kept(1), work(1), [x_all, w_last, bias], "vvv", 6, 1_000_000)
+    if fast:
+        found[3:] = [(after(v, mixed_b), at) for v, at in found[3:]]
+        b_args, b_places = both_cores(found)
 
     blocks = [sds((block, width), BF16), sds((1, block, width), BF16), sds((2, block, width), BF16)]
     if fast:
         rows_b = 2 * per + out_per
-        grads_b = [sds((n_dp, rows_b, width), BF16)] * 4
+        grads_b = [sds((n, rows_b, width), BF16) for n in (n_dp // 2, n_dp // 2, n_dp)] * 2
     else:
         grads_b = [sds((n_t, width, inner), BF16), sds((n_t, inner, width), BF16), sds((n_t * group, width), BF16)]
     res_k, res_1, res_x, gone, gm, gnorm, *got_b = call(
@@ -739,9 +777,10 @@
             ((n_t, win, inner), F32),
             ((win, width), BF16),
             ((width, win), BF16),
+            ((win, n_t * group), BF16),
         ],
-        [scal, own, rx, c1, c3, hid, mixed, norm_all, *b_args],
-        "svvvvvvv" + "v" * len(b_args),
+        [scal, own, rx, c1, c3, hid, mixed_a, mixed_b, norm_all, *b_args],
+        "svvvvvvvv" + "v" * len(b_args),
         26,
         1_000_000,
     )
@@ -753,7 +792,7 @@
     blocks = [sds((block, width), F32), *blocks[1:]]
     if fast:
         rows_a = 3 * per + width // LANES * pos_per + 16
-        grads_a = [sds((n_dp, rows_a, LANES), BF16)] * 4
+        grads_a = [sds((n, rows_a, LANES), BF16) for n in (n_dp // 2, n_dp // 2, n_dp)] * 2
     else:
         grads_a = [sds((n_t, width, 3 * group), BF16), sds((win, width), BF16)]
     gi_k, gi_1, gi_x, *got_a = call(
@@ -770,15 +809,14 @@
             ((width, n_t * 3 * group), BF16),
             [1 + n_t + 2 * n_t * group // HD],
         ],
-        [scal, hid, qkv, pt, gm, attn_all, gone, gnorm],
-        "svhhvhvv",
+        [scal, hid, qkv_a, qkv_b, pt_a, pt_b, gm, attn_all, gone, gnorm],
+        "svhhhhvhvv",
         18,
         1_000_000,
     )
     leaving = [jnp.concatenate([res_x[i : i + 1], gi_x[i : i + 1]]) for i in range(2)]
     if fast:
-        keep_first, keep_rest, send_first, send_rest = got_a
-        red_a = Reduction(keep_first, keep_rest, send_first, send_rest)
+        red_a = Reduction(*got_a)
         first_a, second_b = red_a.first(), red_b.second()
         chunk_b, chunk_a = got_b[0].shape[1:], got_a[0].shape[1:]
         before_z = [[sds(chunk, F32), sds(chunk, F32), sds((2, *chunk), BF16)] for chunk in (chunk_b, chunk_a)]

time: 130 us -> 127 us (0.977)
  waiting for transfers between devices: 54.7 us -> 48 us
  starting transfers between devices: 36 us -> 39.4 us
    ppermute x43 -> x45, waiting for transfers between devices: 54.7 us -> 48 us  [swap(): lax.ppermute(value, AXES, [(i, i ^ mask) for i in range(lax.axis_size('dp...]
    ppermute x43 -> x45, starting transfers between devices: 36 us -> 39.4 us  [swap(): lax.ppermute(value, AXES, [(i, i ^ mask) for i in range(lax.axis_size('dp...]
    pallas_call x15 -> x16, Pallas kernels: 36.3 us -> 37 us  [call(): pl.pallas_call(kernel, out_shape=outs, in_specs=[kinds[k] for k in spaces...]
  transfers between devices with their start and end apart: 43 -> 45, of which waited for: 24 -> 24; matrix products, arithmetic and copies ran while one was open for 1% -> 1% of each run, Pallas kernels for 16% -> 17%
where the time goes in v7:
time: 127 us
  waiting for transfers between devices  48 us (38%)
  starting transfers between devices  39.4 us (31%)
  Pallas kernels  37 us (29%)
  between operations  1.31 us (1%)
    ppermute x45, waiting for transfers between devices, swap(): lax.ppermute(value, AXES, [(i, i ^ mask) for i in range(lax.axis_size('dp...  48 us
    ppermute x45, starting transfers between devices, swap(): lax.ppermute(value, AXES, [(i, i ^ mask) for i in range(lax.axis_size('dp...  39.4 us
    pallas_call x16, Pallas kernels, call(): pl.pallas_call(kernel, out_shape=outs, in_specs=[kinds[k] for k in spaces...  37 us
  transfers between devices with their start and end apart: 45, of which 24 were waited for; matrix products, arithmetic and copies ran while one was open for 1% of the time, Pallas kernels for 17%

profile of v7, /device:TPU:0, one launch (start us, length us, event | category | flops | bytes accessed | tf_op | source)
XLA Modules:
  0.0 126.8 jit_solution(16482817391529300131)
XLA Ops:
  0.7 2.1 %shard_map.356 = (bf16[1,272,128]{2,1,0:T(8,128)(2,1)S(1)}, bf16[1,144,512]{2,1,0:T(8,128)(2,1)S(1)}, bf16[4,128,512]{2,1,0:T(8,128)(2,1)S(1)}, bf16[2,128,512]{2,1,0:T(8,128)(2,1)S(1)}, bf16[2,128,512]{2,1,0:T(8,128)(2,1)S(1)}) custom-call(s32[2]{0:T(128)S(1)} %pad_add_fusion.scal, bf16[4,128,512]{2,1,0:T(8,128)(2,1)} %inputs.1, bf16[4,128,512]{2,1,0:T(8,128)(2,1)} %cot.1, ...), custom_call_target="tpu_custom_call" | custom-call | flops 1000 | tf_op jit(solution)/shard_map/pallas_call | solution.py:632
  2.8 3.0 %collective-permute-start = (bf16[4,128,512]{2,1,0:T(8,128)(2,1)S(1)}, bf16[4,128,512]{2,1,0:T(8,128)(2,1)S(1)}, u32[]{:S(2)}, u32[]{:S(2)}) collective-permute-start(bf16[4,128,512]{2,1,0:T(8,128)(2,1)S(1)} %get-tuple-element.103), channel_id=1, source_target_pairs={{0,2},{1,3},{2,0},{3,1},{4,6},{5,7},{6,4},{7,5},{8,10},{9,11},{10,... | collective-permute-start | bytes 1572872 | tf_op jit(solution)/shard_map/ppermute | solution.py:58
  5.8 2.6 %collective-permute-start.3 = (bf16[1,272,128]{2,1,0:T(8,128)(2,1)S(1)}, bf16[1,272,128]{2,1,0:T(8,128)(2,1)S(1)}, u32[]{:S(2)}, u32[]{:S(2)}) collective-permute-start(bf16[1,272,128]{2,1,0:T(8,128)(2,1)S(1)} %get-tuple-element.105.own), channel_id=1, source_target_pairs={{0,16},{1,17},{2,18},{3,19},{4,20},{5,21},{6,22},{7,23},{8,24},{9,... | collective-permute-start | bytes 208904 | tf_op jit(solution)/shard_map/ppermute | solution.py:58
  8.4 3.0 %collective-permute-done.3.got = bf16[1,272,128]{2,1,0:T(8,128)(2,1)S(1)} collective-permute-done((bf16[1,272,128]{2,1,0:T(8,128)(2,1)S(1)}, bf16[1,272,128]{2,1,0:T(8,128)(2,1)S(1)}, u32[]{:S(2)}, u32[]{:S(2)}) %collective-permute-start.3) | collective-permute-done | bytes 69664 | tf_op jit(solution)/shard_map/ppermute | solution.py:58
  11.4 2.4 %collective-permute-start.12 = (bf16[1,144,512]{2,1,0:T(8,128)(2,1)S(1)}, bf16[1,144,512]{2,1,0:T(8,128)(2,1)S(1)}, u32[]{:S(2)}, u32[]{:S(2)}) collective-permute-start(bf16[1,144,512]{2,1,0:T(8,128)(2,1)S(1)} %get-tuple-element.114.own), channel_id=1, source_target_pairs={{0,16},{1,17},{2,18},{3,19},{4,20},{5,21},{6,22},{7,23},{8,24},{9,... | collective-permute-start | bytes 442376 | tf_op jit(solution)/shard_map/ppermute | solution.py:58
  13.8 2.2 %collective-permute-start.4 = (bf16[2,272,128]{2,1,0:T(8,128)(2,1)S(1)}, bf16[2,272,128]{2,1,0:T(8,128)(2,1)S(1)}, u32[]{:S(2)}, u32[]{:S(2)}) collective-permute-start(bf16[2,272,128]{2,1,0:T(8,128)(2,1)S(1)} %shard_map.357.own), channel_id=1, source_target_pairs={{0,8},{1,9},{2,10},{3,11},{4,12},{5,13},{6,14},{7,15},{8,0},{9,1},... | collective-permute-start | bytes 417800 | tf_op jit(solution)/shard_map/ppermute | solution.py:58
  16.0 3.5 %collective-permute-done.4.got = bf16[2,272,128]{2,1,0:T(8,128)(2,1)S(1)} collective-permute-done((bf16[2,272,128]{2,1,0:T(8,128)(2,1)S(1)}, bf16[2,272,128]{2,1,0:T(8,128)(2,1)S(1)}, u32[]{:S(2)}, u32[]{:S(2)}) %collective-permute-start.4) | collective-permute-done | bytes 139296 | tf_op jit(solution)/shard_map/ppermute | solution.py:58
  19.6 1.8 %collective-permute-start.13 = (bf16[2,144,512]{2,1,0:T(8,128)(2,1)S(1)}, bf16[2,144,512]{2,1,0:T(8,128)(2,1)S(1)}, u32[]{:S(2)}, u32[]{:S(2)}) collective-permute-start(bf16[2,144,512]{2,1,0:T(8,128)(2,1)S(1)} %shard_map.361.own), channel_id=1, source_target_pairs={{0,8},{1,9},{2,10},{3,11},{4,12},{5,13},{6,14},{7,15},{8,0},{9,1},... | collective-permute-start | bytes 884744 | tf_op jit(solution)/shard_map/ppermute | solution.py:58
  24.9 1.7 %collective-permute-done.13.got = bf16[2,144,512]{2,1,0:T(8,128)(2,1)S(1)} collective-permute-done((bf16[2,144,512]{2,1,0:T(8,128)(2,1)S(1)}, bf16[2,144,512]{2,1,0:T(8,128)(2,1)S(1)}, u32[]{:S(2)}, u32[]{:S(2)}) %collective-permute-start.13) | collective-permute-done | bytes 294944 | tf_op jit(solution)/shard_map/ppermute | solution.py:58
  26.6 5.4 %collective-permute-done.8.refs_9_ = bf16[4,272,128]{2,1,0:T(8,128)(2,1)S(1)} collective-permute-done((bf16[4,272,128]{2,1,0:T(8,128)(2,1)S(1)}, bf16[4,272,128]{2,1,0:T(8,128)(2,1)S(1)}, u32[]{:S(2)}, u32[]{:S(2)}) %collective-permute-start.8) | collective-permute-done | bytes 278560 | tf_op jit(solution)/shard_map/ppermute | solution.py:58
  32.5 1.7 %collective-permute-start.17 = (bf16[4,144,512]{2,1,0:T(8,128)(2,1)S(1)}, bf16[4,144,512]{2,1,0:T(8,128)(2,1)S(1)}, u32[]{:S(2)}, u32[]{:S(2)}) collective-permute-start(bf16[4,144,512]{2,1,0:T(8,128)(2,1)S(1)} %shard_map.362.refs_8_), channel_id=1, source_target_pairs={{0,4},{1,5},{2,6},{3,7},{4,0},{5,1},{6,2},{7,3},{8,12},{9,13},{10,... | collective-permute-start | bytes 1769480 | tf_op jit(solution)/shard_map/ppermute | solution.py:58
  35.2 3.1 %collective-permute-done.10.refs_11_ = bf16[4,272,128]{2,1,0:T(8,128)(2,1)S(1)} collective-permute-done((bf16[4,272,128]{2,1,0:T(8,128)(2,1)S(1)}, bf16[4,272,128]{2,1,0:T(8,128)(2,1)S(1)}, u32[]{:S(2)}, u32[]{:S(2)}) %collective-permute-start.10) | collective-permute-done | bytes 278560 | tf_op jit(solution)/shard_map/ppermute | solution.py:58
  41.5 6.0 %shard_map.359 = (f32[512,512]{1,0:T(8,128)S(1)}, bf16[512,1152]{1,0:T(8,128)(2,1)}, bf16[6,512,512]{2,1,0:T(8,128)(2,1)}, bf16[512,384]{1,0:T(8,128)(2,1)S(1)},...) custom-call(s32[2]{0:T(128)S(1)} %pad_add_fusion.scal, ...), custom_call_target="tpu_custom_call" | custom-call | flops 1000000 | tf_op jit(solution)/shard_map/pallas_call | solution.py:632
  50.2 2.2 %shard_map.360 = (bf16[512,384]{1,0:T(8,128)(2,1)}, bf16[2,512,512]{2,1,0:T(8,128)(2,1)}, bf16[512,128]{1,0:T(8,128)(2,1)S(1)}) custom-call(bf16[512,512]{1,0:T(8,128)(2,1)S(1)} %get-tuple-element.108.x, bf16[512,384]{1,0:T(8,128)(2,1)S(1)} %get-tuple-element.109.w, f32[512,512]{1,0:T(8,128)S(1)} %get-tuple-element.110.bias), custom_call_target="tpu_custom_call" | custom-call | flops 1000000 | tf_op jit(solution)/shard_map/pallas_call | solution.py:632
  52.4 4.2 %collective-permute-done.21.refs_16_ = bf16[2,144,512]{2,1,0:T(8,128)(2,1)S(1)} collective-permute-done((bf16[2,144,512]{2,1,0:T(8,128)(2,1)S(1)}, bf16[2,144,512]{2,1,0:T(8,128)(2,1)S(1)}, u32[]{:S(2)}, u32[]{:S(2)}) %collective-permute-start.21) | collective-permute-done | bytes 294944 | tf_op jit(solution)/shard_map/ppermute | solution.py:58
  59.0 11.3 %shard_map.363 = (bf16[128,512]{1,0:T(8,128)(2,1)S(1)}, bf16[1,128,512]{2,1,0:T(8,128)(2,1)S(1)}, bf16[2,128,512]{2,1,0:T(8,128)(2,1)S(1)}, f32[512,512]{1,0:T(8...) custom-call(s32[2]{0:T(128)S(1)} %pad_add_fusion.scal, ...), custom_call_target="tpu_custom_call" | custom-call | flops 1000000 | tf_op jit(solution)/shard_map/pallas_call | solution.py:632
  75.8 10.5 %shard_map.365 = (f32[128,512]{1,0:T(8,128)S(1)}, bf16[1,128,512]{2,1,0:T(8,128)(2,1)S(1)}, bf16[2,128,512]{2,1,0:T(8,128)(2,1)S(1)}, bf16[4,272,128]{2,1,0:T(8,...) custom-call(s32[2]{0:T(128)S(1)} %pad_add_fusion.scal, ...), custom_call_target="tpu_custom_call" | custom-call | flops 1000000 | tf_op jit(solution)/shard_map/pallas_call | solution.py:632
  94.1 5.6 %collective-permute-done.28.x2 = bf16[2,144,512]{2,1,0:T(8,128)(2,1)S(1)} collective-permute-done((bf16[2,144,512]{2,1,0:T(8,128)(2,1)S(1)}, bf16[2,144,512]{2,1,0:T(8,128)(2,1)S(1)}, u32[]{:S(2)}, u32[]{:S(2)}) %collective-permute-start.28) | collective-permute-done | bytes 294944 | tf_op jit(solution)/shard_map/ppermute | solution.py:58
  101.9 3.0 %collective-permute-done.33.x = bf16[4,272,128]{2,1,0:T(8,128)(2,1)S(1)} collective-permute-done((bf16[4,272,128]{2,1,0:T(8,128)(2,1)S(1)}, bf16[4,272,128]{2,1,0:T(8,128)(2,1)S(1)}, u32[]{:S(2)}, u32[]{:S(2)}) %collective-permute-start.33) | collective-permute-done | bytes 278560 | tf_op jit(solution)/shard_map/ppermute | solution.py:58
  107.1 3.1 %collective-permute-done.36.x2 = bf16[2,272,128]{2,1,0:T(8,128)(2,1)S(1)} collective-permute-done((bf16[2,272,128]{2,1,0:T(8,128)(2,1)S(1)}, bf16[2,272,128]{2,1,0:T(8,128)(2,1)S(1)}, u32[]{:S(2)}, u32[]{:S(2)}) %collective-permute-start.36) | collective-permute-done | bytes 139296 | tf_op jit(solution)/shard_map/ppermute | solution.py:58
  111.4 1.9 %collective-permute-start.38 = (bf16[1,144,512]{2,1,0:T(8,128)(2,1)S(1)}, bf16[1,144,512]{2,1,0:T(8,128)(2,1)S(1)}, u32[]{:S(2)}, u32[]{:S(2)}) collective-permute-start(bf16[1,144,512]{2,1,0:T(8,128)(2,1)S(1)} %get-tuple-element.148), channel_id=1, source_target_pairs={{0,16},{1,17},{2,18},{3,19},{4,20},{5,21},{6,22},{7,23},{8,24},{9,... | collective-permute-start | bytes 442376 | tf_op jit(solution)/shard_map/ppermute | solution.py:58
  115.6 2.1 %collective-permute-done.39.near = bf16[2,272,128]{2,1,0:T(8,128)(2,1)S(1)} collective-permute-done((bf16[2,272,128]{2,1,0:T(8,128)(2,1)S(1)}, bf16[2,272,128]{2,1,0:T(8,128)(2,1)S(1)}, u32[]{:S(2)}, u32[]{:S(2)}) %collective-permute-start.39) | collective-permute-done | bytes 139296 | tf_op jit(solution)/shard_map/ppermute | solution.py:58
  120.7 2.6 %collective-permute-done.40.far = bf16[1,272,128]{2,1,0:T(8,128)(2,1)S(1)} collective-permute-done((bf16[1,272,128]{2,1,0:T(8,128)(2,1)S(1)}, bf16[1,272,128]{2,1,0:T(8,128)(2,1)S(1)}, u32[]{:S(2)}, u32[]{:S(2)}) %collective-permute-start.40) | collective-permute-done | bytes 69664 | tf_op jit(solution)/shard_map/ppermute | solution.py:58
  124.9 1.7 %shard_map.371 = (bf16[4,128,512]{2,1,0:T(8,128)(2,1)}, f32[4,128,512]{2,1,0:T(8,128)}) custom-call(s32[2]{0:T(128)S(1)} %pad_add_fusion.scal, f32[8,128]{1,0:T(8,128)S(1)} %get-tuple-element.155.done, bf16[128,512]{1,0:T(8,128)(2,1)S(1)} %get-tuple-element.156.res_k, f32[128,512]{1,0:T(8,128)S(1)} %get-tuple-element.157.gi_k, ...), custom_call_target="tpu_custom_call" | custom-call | flops 1000 | tf_op jit(solution)/shard_map/pallas_call | solution.py:632
  (132 shorter events, 38.7 us)
Async XLA Ops:
  2.8 29.6 %collective-permute-start = (bf16[4,128,512]{2,1,0:T(8,128)(2,1)S(1)}, bf16[4,128,512]{2,1,0:T(8,128)(2,1)S(1)}, u32[]{:S(2)}, u32[]{:S(2)}) collective-permute-start(bf16[4,128,512]{2,1,0:T(8,128)(2,1)S(1)} %get-tuple-element.103), channel_id=1, source_target_pairs={{0,2},{1,3},{2,0},{3,1},{4,6},{5,7},{6,4},{7,5},{8,10},{9,11},{10,... | collective-permute-start | bytes 1572872 | tf_op jit(solution)/shard_map/ppermute | solution.py:58
  11.4 8.2 %collective-permute-start.12 = (bf16[1,144,512]{2,1,0:T(8,128)(2,1)S(1)}, bf16[1,144,512]{2,1,0:T(8,128)(2,1)S(1)}, u32[]{:S(2)}, u32[]{:S(2)}) collective-permute-start(bf16[1,144,512]{2,1,0:T(8,128)(2,1)S(1)} %get-tuple-element.114.own), channel_id=1, source_target_pairs={{0,16},{1,17},{2,18},{3,19},{4,20},{5,21},{6,22},{7,23},{8,24},{9,... | collective-permute-start | bytes 442376 | tf_op jit(solution)/shard_map/ppermute | solution.py:58
  21.4 10.7 %collective-permute-start.8 = (bf16[4,272,128]{2,1,0:T(8,128)(2,1)S(1)}, bf16[4,272,128]{2,1,0:T(8,128)(2,1)S(1)}, u32[]{:S(2)}, u32[]{:S(2)}) collective-permute-start(bf16[4,272,128]{2,1,0:T(8,128)(2,1)S(1)} %shard_map.358.refs_5_), channel_id=1, source_target_pairs={{0,4},{1,5},{2,6},{3,7},{4,0},{5,1},{6,2},{7,3},{8,12},{9,13},{10,... | collective-permute-start | bytes 835592 | tf_op jit(solution)/shard_map/ppermute | solution.py:58
  22.9 9.6 %collective-permute-start.6 = (bf16[4,272,128]{2,1,0:T(8,128)(2,1)S(1)}, bf16[4,272,128]{2,1,0:T(8,128)(2,1)S(1)}, u32[]{:S(2)}, u32[]{:S(2)}) collective-permute-start(bf16[4,272,128]{2,1,0:T(8,128)(2,1)S(1)} %shard_map.358.refs_5_), channel_id=1, source_target_pairs={{0,2},{1,3},{2,0},{3,1},{4,6},{5,7},{6,4},{7,5},{8,10},{9,11},{10,... | collective-permute-start | bytes 835592 | tf_op jit(solution)/shard_map/ppermute | solution.py:58
  23.4 15.0 %collective-permute-start.10 = (bf16[4,272,128]{2,1,0:T(8,128)(2,1)S(1)}, bf16[4,272,128]{2,1,0:T(8,128)(2,1)S(1)}, u32[]{:S(2)}, u32[]{:S(2)}) collective-permute-start(bf16[4,272,128]{2,1,0:T(8,128)(2,1)S(1)} %shard_map.358.refs_5_), channel_id=1, source_target_pairs={{0,6},{1,7},{2,4},{3,5},{4,2},{5,3},{6,0},{7,1},{8,14},{9,15},{10,... | collective-permute-start | bytes 835592 | tf_op jit(solution)/shard_map/ppermute | solution.py:58
  32.5 15.0 %collective-permute-start.17 = (bf16[4,144,512]{2,1,0:T(8,128)(2,1)S(1)}, bf16[4,144,512]{2,1,0:T(8,128)(2,1)S(1)}, u32[]{:S(2)}, u32[]{:S(2)}) collective-permute-start(bf16[4,144,512]{2,1,0:T(8,128)(2,1)S(1)} %shard_map.362.refs_8_), channel_id=1, source_target_pairs={{0,4},{1,5},{2,6},{3,7},{4,0},{5,1},{6,2},{7,3},{8,12},{9,13},{10,... | collective-permute-start | bytes 1769480 | tf_op jit(solution)/shard_map/ppermute | solution.py:58
  34.2 13.9 %collective-permute-start.15 = (bf16[4,144,512]{2,1,0:T(8,128)(2,1)S(1)}, bf16[4,144,512]{2,1,0:T(8,128)(2,1)S(1)}, u32[]{:S(2)}, u32[]{:S(2)}) collective-permute-start(bf16[4,144,512]{2,1,0:T(8,128)(2,1)S(1)} %shard_map.362.refs_8_), channel_id=1, source_target_pairs={{0,2},{1,3},{2,0},{3,1},{4,6},{5,7},{6,4},{7,5},{8,10},{9,11},{10,... | collective-permute-start | bytes 1769480 | tf_op jit(solution)/shard_map/ppermute | solution.py:58
  47.5 9.1 %collective-permute-start.21 = (bf16[2,144,512]{2,1,0:T(8,128)(2,1)S(1)}, bf16[2,144,512]{2,1,0:T(8,128)(2,1)S(1)}, u32[]{:S(2)}, u32[]{:S(2)}) collective-permute-start(bf16[2,144,512]{2,1,0:T(8,128)(2,1)S(1)} %slice.54), channel_id=1, source_target_pairs={{0,2},{1,3},{2,0},{3,1},{4,6},{5,7},{6,4},{7,5},{8,10},{9,11},{10,... | collective-permute-start | bytes 884744 | tf_op jit(solution)/shard_map/ppermute | solution.py:58
  48.1 8.8 %collective-permute-start.19 = (bf16[2,144,512]{2,1,0:T(8,128)(2,1)S(1)}, bf16[2,144,512]{2,1,0:T(8,128)(2,1)S(1)}, u32[]{:S(2)}, u32[]{:S(2)}) collective-permute-start(bf16[2,144,512]{2,1,0:T(8,128)(2,1)S(1)} %slice.53), channel_id=1, source_target_pairs={{0,4},{1,5},{2,6},{3,7},{4,0},{5,1},{6,2},{7,3},{8,12},{9,13},{10,... | collective-permute-start | bytes 884744 | tf_op jit(solution)/shard_map/ppermute | solution.py:58
  49.7 7.8 %collective-permute-start.14 = (bf16[4,144,512]{2,1,0:T(8,128)(2,1)S(1)}, bf16[4,144,512]{2,1,0:T(8,128)(2,1)S(1)}, u32[]{:S(2)}, u32[]{:S(2)}) collective-permute-start(bf16[4,144,512]{2,1,0:T(8,128)(2,1)S(1)} %shard_map.362.refs_8_), channel_id=1, source_target_pairs={{0,1},{1,0},{2,3},{3,2},{4,5},{5,4},{6,7},{7,6},{8,9},{9,8},{10,11... | collective-permute-start | bytes 1769480 | tf_op jit(solution)/shard_map/ppermute | solution.py:58
  49.7 7.8 %collective-permute-start.18 = (bf16[4,144,512]{2,1,0:T(8,128)(2,1)S(1)}, bf16[4,144,512]{2,1,0:T(8,128)(2,1)S(1)}, u32[]{:S(2)}, u32[]{:S(2)}) collective-permute-start(bf16[4,144,512]{2,1,0:T(8,128)(2,1)S(1)} %collective-permute-done.17.refs_12_), channel_id=1, source_target_pairs={{0,1},{1,0},{2,3},{3,2},{4,5},{5,4},{6,7},{7,6},{8,9},{9,8},{10,11... | collective-permute-start | bytes 1769480 | tf_op jit(solution)/shard_map/ppermute | solution.py:58
  50.2 7.3 %collective-permute-start.16 = (bf16[4,144,512]{2,1,0:T(8,128)(2,1)S(1)}, bf16[4,144,512]{2,1,0:T(8,128)(2,1)S(1)}, u32[]{:S(2)}, u32[]{:S(2)}) collective-permute-start(bf16[4,144,512]{2,1,0:T(8,128)(2,1)S(1)} %collective-permute-done.15.refs_10_), channel_id=1, source_target_pairs={{0,1},{1,0},{2,3},{3,2},{4,5},{5,4},{6,7},{7,6},{8,9},{9,8},{10,11... | collective-permute-start | bytes 1769480 | tf_op jit(solution)/shard_map/ppermute | solution.py:58
  70.9 18.5 %collective-permute-start.23 = (bf16[8,144,512]{2,1,0:T(8,128)(2,1)S(1)}, bf16[8,144,512]{2,1,0:T(8,128)(2,1)S(1)}, u32[]{:S(2)}, u32[]{:S(2)}) collective-permute-start(bf16[8,144,512]{2,1,0:T(8,128)(2,1)S(1)} %get-tuple-element.122), channel_id=1, source_target_pairs={{0,1},{1,0},{2,3},{3,2},{4,5},{5,4},{6,7},{7,6},{8,9},{9,8},{10,11... | collective-permute-start | bytes 3538952 | tf_op jit(solution)/shard_map/ppermute | solution.py:58
  72.6 15.4 %collective-permute-start.25 = (bf16[4,144,512]{2,1,0:T(8,128)(2,1)S(1)}, bf16[4,144,512]{2,1,0:T(8,128)(2,1)S(1)}, u32[]{:S(2)}, u32[]{:S(2)}) collective-permute-start(bf16[4,144,512]{2,1,0:T(8,128)(2,1)S(1)} %add_convert_fusion.1), channel_id=1, source_target_pairs={{0,2},{1,3},{2,0},{3,1},{4,6},{5,7},{6,4},{7,5},{8,10},{9,11},{10,... | collective-permute-start | bytes 1769480 | tf_op jit(solution)/shard_map/ppermute | solution.py:58
  74.3 15.2 %collective-permute-start.27 = (bf16[4,144,512]{2,1,0:T(8,128)(2,1)S(1)}, bf16[4,144,512]{2,1,0:T(8,128)(2,1)S(1)}, u32[]{:S(2)}, u32[]{:S(2)}) collective-permute-start(bf16[4,144,512]{2,1,0:T(8,128)(2,1)S(1)} %add_convert_fusion), channel_id=1, source_target_pairs={{0,4},{1,5},{2,6},{3,7},{4,0},{5,1},{6,2},{7,3},{8,12},{9,13},{10,... | collective-permute-start | bytes 1769480 | tf_op jit(solution)/shard_map/ppermute | solution.py:58
  88.0 17.0 %collective-permute-start.31 = (bf16[8,272,128]{2,1,0:T(8,128)(2,1)S(1)}, bf16[8,272,128]{2,1,0:T(8,128)(2,1)S(1)}, u32[]{:S(2)}, u32[]{:S(2)}) collective-permute-start(bf16[8,272,128]{2,1,0:T(8,128)(2,1)S(1)} %get-tuple-element.140), channel_id=1, source_target_pairs={{0,1},{1,0},{2,3},{3,2},{4,5},{5,4},{6,7},{7,6},{8,9},{9,8},{10,11... | collective-permute-start | bytes 1671176 | tf_op jit(solution)/shard_map/ppermute | solution.py:58
  89.7 10.0 %collective-permute-start.28 = (bf16[2,144,512]{2,1,0:T(8,128)(2,1)S(1)}, bf16[2,144,512]{2,1,0:T(8,128)(2,1)S(1)}, u32[]{:S(2)}, u32[]{:S(2)}) collective-permute-start(bf16[2,144,512]{2,1,0:T(8,128)(2,1)S(1)} %get-tuple-element.185), channel_id=1, source_target_pairs={{0,4},{1,5},{2,6},{3,7},{4,0},{5,1},{6,2},{7,3},{8,12},{9,13},{10,... | collective-permute-start | bytes 884744 | tf_op jit(solution)/shard_map/ppermute | solution.py:58
  91.3 9.9 %collective-permute-start.29 = (bf16[2,144,512]{2,1,0:T(8,128)(2,1)S(1)}, bf16[2,144,512]{2,1,0:T(8,128)(2,1)S(1)}, u32[]{:S(2)}, u32[]{:S(2)}) collective-permute-start(bf16[2,144,512]{2,1,0:T(8,128)(2,1)S(1)} %get-tuple-element.184), channel_id=1, source_target_pairs={{0,2},{1,3},{2,0},{3,1},{4,6},{5,7},{6,4},{7,5},{8,10},{9,11},{10,... | collective-permute-start | bytes 884744 | tf_op jit(solution)/shard_map/ppermute | solution.py:58
  92.2 12.7 %collective-permute-start.33 = (bf16[4,272,128]{2,1,0:T(8,128)(2,1)S(1)}, bf16[4,272,128]{2,1,0:T(8,128)(2,1)S(1)}, u32[]{:S(2)}, u32[]{:S(2)}) collective-permute-start(bf16[4,272,128]{2,1,0:T(8,128)(2,1)S(1)} %add_convert_fusion.5), channel_id=1, source_target_pairs={{0,2},{1,3},{2,0},{3,1},{4,6},{5,7},{6,4},{7,5},{8,10},{9,11},{10,... | collective-permute-start | bytes 835592 | tf_op jit(solution)/shard_map/ppermute | solution.py:58
  93.5 11.4 %collective-permute-start.35 = (bf16[4,272,128]{2,1,0:T(8,128)(2,1)S(1)}, bf16[4,272,128]{2,1,0:T(8,128)(2,1)S(1)}, u32[]{:S(2)}, u32[]{:S(2)}) collective-permute-start(bf16[4,272,128]{2,1,0:T(8,128)(2,1)S(1)} %add_convert_fusion.4), channel_id=1, source_target_pairs={{0,4},{1,5},{2,6},{3,7},{4,0},{5,1},{6,2},{7,3},{8,12},{9,13},{10,... | collective-permute-start | bytes 835592 | tf_op jit(solution)/shard_map/ppermute | solution.py:58
  101.5 9.2 %collective-permute-start.30 = (bf16[2,144,512]{2,1,0:T(8,128)(2,1)S(1)}, bf16[2,144,512]{2,1,0:T(8,128)(2,1)S(1)}, u32[]{:S(2)}, u32[]{:S(2)}) collective-permute-start(bf16[2,144,512]{2,1,0:T(8,128)(2,1)S(1)} %get-tuple-element.129), channel_id=1, source_target_pairs={{0,8},{1,9},{2,10},{3,11},{4,12},{5,13},{6,14},{7,15},{8,0},{9,1},... | collective-permute-start | bytes 884744 | tf_op jit(solution)/shard_map/ppermute | solution.py:58
  113.4 11.5 %collective-permute-start.43 = (bf16[2,128,512]{2,1,0:T(8,128)(2,1)S(1)}, bf16[2,128,512]{2,1,0:T(8,128)(2,1)S(1)}, u32[]{:S(2)}, u32[]{:S(2)}) collective-permute-start(bf16[2,128,512]{2,1,0:T(8,128)(2,1)S(1)} %get-tuple-element.162), channel_id=1, source_target_pairs={{0,2},{1,3},{2,0},{3,1},{4,6},{5,7},{6,4},{7,5},{8,10},{9,11},{10,... | collective-permute-start | bytes 786440 | tf_op jit(solution)/shard_map/ppermute | solution.py:58
  115.0 9.9 %collective-permute-start.44 = (bf16[2,128,512]{2,1,0:T(8,128)(2,1)S(1)}, bf16[2,128,512]{2,1,0:T(8,128)(2,1)S(1)}, u32[]{:S(2)}, u32[]{:S(2)}) collective-permute-start(bf16[2,128,512]{2,1,0:T(8,128)(2,1)S(1)} %get-tuple-element.163), channel_id=1, source_target_pairs={{0,3},{1,2},{2,1},{3,0},{4,7},{5,6},{6,5},{7,4},{8,11},{9,10},{10,... | collective-permute-start | bytes 786440 | tf_op jit(solution)/shard_map/ppermute | solution.py:58
  115.0 9.9 %collective-permute-start.41 = (bf16[1,128,512]{2,1,0:T(8,128)(2,1)S(1)}, bf16[1,128,512]{2,1,0:T(8,128)(2,1)S(1)}, u32[]{:S(2)}, u32[]{:S(2)}) collective-permute-start(bf16[1,128,512]{2,1,0:T(8,128)(2,1)S(1)} %get-tuple-element.158), channel_id=1, source_target_pairs={{0,1},{1,0},{2,3},{3,2},{4,5},{5,4},{6,7},{7,6},{8,9},{9,8},{10,11... | collective-permute-start | bytes 393224 | tf_op jit(solution)/shard_map/ppermute | solution.py:58
  (40 other events, 223.6 us)

commit v8 on v7

--- a/solution.py
+++ b/solution.py
@@ -719,7 +719,7 @@
         a_args, a_places = [attn_w, pos_w, norm_w], None
         b_args, b_places = [out_w.reshape(n_t * group, width), up_w.reshape(n_t, width, inner), down_w.reshape(n_t, inner, width)], None
 
-    first = n_t - 1
+    first = n_t // 2
     heads_of = group // HD
 
     def kept(groups):
@@ -736,7 +736,7 @@
             pltpu.HBM((width, n_t * 3 * group), BF16),
             sds((8, width), F32),
             sds((win, width), BF16),
-            sds((width, 3 * group), BF16),
+            sds((width, (n_t - first) * 3 * group), BF16),
             sds((win, win), F32),
         ],
         [((win, width), BF16), ((n_dp, 16, LANES), F32), ((width, n_t * 3 * group), BF16), *work(first)],
@@ -747,7 +747,7 @@
     )
     if fast:
         found = gather_xy(qb, zb, qbx, qby, x_all)
-    qkv_b, pt_b, mixed_b = call(attention_rest_kernel, kept(1), work(1), [x_all, w_last, bias], "vvv", 6, 1_000_000)
+    qkv_b, pt_b, mixed_b = call(attention_rest_kernel, kept(n_t - first), work(n_t - first), [x_all, w_last, bias], "vvv", 6, 1_000_000)
     if fast:
         found[3:] = [(after(v, mixed_b), at) for v, at in found[3:]]
         b_args, b_places = both_cores(found)

time: 127 us -> 126 us (level)
  waiting for transfers between devices: 48 us -> 46.7 us
    ppermute x45, waiting for transfers between devices: 48 us -> 46.7 us  [swap(): lax.ppermute(value, AXES, [(i, i ^ mask) for i in range(lax.axis_size('dp...]
  transfers between devices with their start and end apart: 45 -> 45, of which waited for: 24 -> 26; matrix products, arithmetic and copies ran while one was open for 1% -> 1% of each run, Pallas kernels for 17% -> 17%
where the time goes in v8:
time: 126 us; the launch traced here: 125 us
  waiting for transfers between devices  46.7 us (37%)
  starting transfers between devices  39.3 us (31%)
  Pallas kernels  37 us (29%)
  between operations  1.29 us (1%)
    ppermute x45, waiting for transfers between devices, swap(): lax.ppermute(value, AXES, [(i, i ^ mask) for i in range(lax.axis_size('dp...  46.7 us
    ppermute x45, starting transfers between devices, swap(): lax.ppermute(value, AXES, [(i, i ^ mask) for i in range(lax.axis_size('dp...  39.3 us
    pallas_call x16, Pallas kernels, call(): pl.pallas_call(kernel, out_shape=outs, in_specs=[kinds[k] for k in spaces...  37 us
  transfers between devices with their start and end apart: 45, of which 26 were waited for; matrix products, arithmetic and copies ran while one was open for 1% of the time, Pallas kernels for 17%

profile of v8, /device:TPU:0, one launch (start us, length us, event | category | flops | bytes accessed | tf_op | source)
XLA Modules:
  0.0 125.4 jit_solution(4607130180765312391)
XLA Ops:
  0.7 2.1 %shard_map.356 = (bf16[1,272,128]{2,1,0:T(8,128)(2,1)S(1)}, bf16[1,144,512]{2,1,0:T(8,128)(2,1)S(1)}, bf16[4,128,512]{2,1,0:T(8,128)(2,1)S(1)}, bf16[2,128,512]{2,1,0:T(8,128)(2,1)S(1)}, bf16[2,128,512]{2,1,0:T(8,128)(2,1)S(1)}) custom-call(s32[2]{0:T(128)S(1)} %pad_add_fusion.scal, bf16[4,128,512]{2,1,0:T(8,128)(2,1)} %inputs.1, bf16[4,128,512]{2,1,0:T(8,128)(2,1)} %cot.1, ...), custom_call_target="tpu_custom_call" | custom-call | flops 1000 | tf_op jit(solution)/shard_map/pallas_call | solution.py:632
  2.8 3.0 %collective-permute-start = (bf16[4,128,512]{2,1,0:T(8,128)(2,1)S(1)}, bf16[4,128,512]{2,1,0:T(8,128)(2,1)S(1)}, u32[]{:S(2)}, u32[]{:S(2)}) collective-permute-start(bf16[4,128,512]{2,1,0:T(8,128)(2,1)S(1)} %get-tuple-element.103), channel_id=1, source_target_pairs={{0,2},{1,3},{2,0},{3,1},{4,6},{5,7},{6,4},{7,5},{8,10},{9,11},{10,... | collective-permute-start | bytes 1572872 | tf_op jit(solution)/shard_map/ppermute | solution.py:58
  5.8 2.6 %collective-permute-start.3 = (bf16[1,272,128]{2,1,0:T(8,128)(2,1)S(1)}, bf16[1,272,128]{2,1,0:T(8,128)(2,1)S(1)}, u32[]{:S(2)}, u32[]{:S(2)}) collective-permute-start(bf16[1,272,128]{2,1,0:T(8,128)(2,1)S(1)} %get-tuple-element.105.own), channel_id=1, source_target_pairs={{0,16},{1,17},{2,18},{3,19},{4,20},{5,21},{6,22},{7,23},{8,24},{9,... | collective-permute-start | bytes 208904 | tf_op jit(solution)/shard_map/ppermute | solution.py:58
  8.4 3.0 %collective-permute-done.3.got = bf16[1,272,128]{2,1,0:T(8,128)(2,1)S(1)} collective-permute-done((bf16[1,272,128]{2,1,0:T(8,128)(2,1)S(1)}, bf16[1,272,128]{2,1,0:T(8,128)(2,1)S(1)}, u32[]{:S(2)}, u32[]{:S(2)}) %collective-permute-start.3) | collective-permute-done | bytes 69664 | tf_op jit(solution)/shard_map/ppermute | solution.py:58
  11.4 2.4 %collective-permute-start.12 = (bf16[1,144,512]{2,1,0:T(8,128)(2,1)S(1)}, bf16[1,144,512]{2,1,0:T(8,128)(2,1)S(1)}, u32[]{:S(2)}, u32[]{:S(2)}) collective-permute-start(bf16[1,144,512]{2,1,0:T(8,128)(2,1)S(1)} %get-tuple-element.114.own), channel_id=1, source_target_pairs={{0,16},{1,17},{2,18},{3,19},{4,20},{5,21},{6,22},{7,23},{8,24},{9,... | collective-permute-start | bytes 442376 | tf_op jit(solution)/shard_map/ppermute | solution.py:58
  13.8 2.2 %collective-permute-start.4 = (bf16[2,272,128]{2,1,0:T(8,128)(2,1)S(1)}, bf16[2,272,128]{2,1,0:T(8,128)(2,1)S(1)}, u32[]{:S(2)}, u32[]{:S(2)}) collective-permute-start(bf16[2,272,128]{2,1,0:T(8,128)(2,1)S(1)} %shard_map.357.own), channel_id=1, source_target_pairs={{0,8},{1,9},{2,10},{3,11},{4,12},{5,13},{6,14},{7,15},{8,0},{9,1},... | collective-permute-start | bytes 417800 | tf_op jit(solution)/shard_map/ppermute | solution.py:58
  16.0 3.5 %collective-permute-done.4.got = bf16[2,272,128]{2,1,0:T(8,128)(2,1)S(1)} collective-permute-done((bf16[2,272,128]{2,1,0:T(8,128)(2,1)S(1)}, bf16[2,272,128]{2,1,0:T(8,128)(2,1)S(1)}, u32[]{:S(2)}, u32[]{:S(2)}) %collective-permute-start.4) | collective-permute-done | bytes 139296 | tf_op jit(solution)/shard_map/ppermute | solution.py:58
  19.6 1.8 %collective-permute-start.13 = (bf16[2,144,512]{2,1,0:T(8,128)(2,1)S(1)}, bf16[2,144,512]{2,1,0:T(8,128)(2,1)S(1)}, u32[]{:S(2)}, u32[]{:S(2)}) collective-permute-start(bf16[2,144,512]{2,1,0:T(8,128)(2,1)S(1)} %shard_map.361.own), channel_id=1, source_target_pairs={{0,8},{1,9},{2,10},{3,11},{4,12},{5,13},{6,14},{7,15},{8,0},{9,1},... | collective-permute-start | bytes 884744 | tf_op jit(solution)/shard_map/ppermute | solution.py:58
  24.9 1.7 %collective-permute-done.13.got = bf16[2,144,512]{2,1,0:T(8,128)(2,1)S(1)} collective-permute-done((bf16[2,144,512]{2,1,0:T(8,128)(2,1)S(1)}, bf16[2,144,512]{2,1,0:T(8,128)(2,1)S(1)}, u32[]{:S(2)}, u32[]{:S(2)}) %collective-permute-start.13) | collective-permute-done | bytes 294944 | tf_op jit(solution)/shard_map/ppermute | solution.py:58
  26.6 5.4 %collective-permute-done.8.refs_9_ = bf16[4,272,128]{2,1,0:T(8,128)(2,1)S(1)} collective-permute-done((bf16[4,272,128]{2,1,0:T(8,128)(2,1)S(1)}, bf16[4,272,128]{2,1,0:T(8,128)(2,1)S(1)}, u32[]{:S(2)}, u32[]{:S(2)}) %collective-permute-start.8) | collective-permute-done | bytes 278560 | tf_op jit(solution)/shard_map/ppermute | solution.py:58
  32.5 1.7 %collective-permute-start.17 = (bf16[4,144,512]{2,1,0:T(8,128)(2,1)S(1)}, bf16[4,144,512]{2,1,0:T(8,128)(2,1)S(1)}, u32[]{:S(2)}, u32[]{:S(2)}) collective-permute-start(bf16[4,144,512]{2,1,0:T(8,128)(2,1)S(1)} %shard_map.362.refs_8_), channel_id=1, source_target_pairs={{0,4},{1,5},{2,6},{3,7},{4,0},{5,1},{6,2},{7,3},{8,12},{9,13},{10,... | collective-permute-start | bytes 1769480 | tf_op jit(solution)/shard_map/ppermute | solution.py:58
  35.2 3.1 %collective-permute-done.10.refs_11_ = bf16[4,272,128]{2,1,0:T(8,128)(2,1)S(1)} collective-permute-done((bf16[4,272,128]{2,1,0:T(8,128)(2,1)S(1)}, bf16[4,272,128]{2,1,0:T(8,128)(2,1)S(1)}, u32[]{:S(2)}, u32[]{:S(2)}) %collective-permute-start.10) | collective-permute-done | bytes 278560 | tf_op jit(solution)/shard_map/ppermute | solution.py:58
  41.5 4.6 %shard_map.359 = (f32[512,512]{1,0:T(8,128)S(1)}, bf16[512,768]{1,0:T(8,128)(2,1)}, bf16[4,512,512]{2,1,0:T(8,128)(2,1)}, bf16[512,256]{1,0:T(8,128)(2,1)S(1)}, ...) custom-call(s32[2]{0:T(128)S(1)} %pad_add_fusion.scal, ...), custom_call_target="tpu_custom_call" | custom-call | flops 1000000 | tf_op jit(solution)/shard_map/pallas_call | solution.py:632
  49.3 3.6 %shard_map.360 = (bf16[512,768]{1,0:T(8,128)(2,1)}, bf16[4,512,512]{2,1,0:T(8,128)(2,1)}, bf16[512,256]{1,0:T(8,128)(2,1)S(1)}) custom-call(bf16[512,512]{1,0:T(8,128)(2,1)S(1)} %get-tuple-element.108.x, bf16[512,768]{1,0:T(8,128)(2,1)S(1)} %get-tuple-element.109.w, f32[512,512]{1,0:T(8,128)S(1)} %get-tuple-element.110.bias), custom_call_target="tpu_custom_call" | custom-call | flops 1000000 | tf_op jit(solution)/shard_map/pallas_call | solution.py:632
  52.9 2.3 %collective-permute-done.21.refs_16_ = bf16[2,144,512]{2,1,0:T(8,128)(2,1)S(1)} collective-permute-done((bf16[2,144,512]{2,1,0:T(8,128)(2,1)S(1)}, bf16[2,144,512]{2,1,0:T(8,128)(2,1)S(1)}, u32[]{:S(2)}, u32[]{:S(2)}) %collective-permute-start.21) | collective-permute-done | bytes 294944 | tf_op jit(solution)/shard_map/ppermute | solution.py:58
  57.5 11.3 %shard_map.363 = (bf16[128,512]{1,0:T(8,128)(2,1)S(1)}, bf16[1,128,512]{2,1,0:T(8,128)(2,1)S(1)}, bf16[2,128,512]{2,1,0:T(8,128)(2,1)S(1)}, f32[512,512]{1,0:T(8...) custom-call(s32[2]{0:T(128)S(1)} %pad_add_fusion.scal, ...), custom_call_target="tpu_custom_call" | custom-call | flops 1000000 | tf_op jit(solution)/shard_map/pallas_call | solution.py:632
  74.4 10.5 %shard_map.365 = (f32[128,512]{1,0:T(8,128)S(1)}, bf16[1,128,512]{2,1,0:T(8,128)(2,1)S(1)}, bf16[2,128,512]{2,1,0:T(8,128)(2,1)S(1)}, bf16[4,272,128]{2,1,0:T(8,...) custom-call(s32[2]{0:T(128)S(1)} %pad_add_fusion.scal, ...), custom_call_target="tpu_custom_call" | custom-call | flops 1000000 | tf_op jit(solution)/shard_map/pallas_call | solution.py:632
  92.7 5.6 %collective-permute-done.28.x2 = bf16[2,144,512]{2,1,0:T(8,128)(2,1)S(1)} collective-permute-done((bf16[2,144,512]{2,1,0:T(8,128)(2,1)S(1)}, bf16[2,144,512]{2,1,0:T(8,128)(2,1)S(1)}, u32[]{:S(2)}, u32[]{:S(2)}) %collective-permute-start.28) | collective-permute-done | bytes 294944 | tf_op jit(solution)/shard_map/ppermute | solution.py:58
  100.5 3.0 %collective-permute-done.33.x = bf16[4,272,128]{2,1,0:T(8,128)(2,1)S(1)} collective-permute-done((bf16[4,272,128]{2,1,0:T(8,128)(2,1)S(1)}, bf16[4,272,128]{2,1,0:T(8,128)(2,1)S(1)}, u32[]{:S(2)}, u32[]{:S(2)}) %collective-permute-start.33) | collective-permute-done | bytes 278560 | tf_op jit(solution)/shard_map/ppermute | solution.py:58
  105.7 3.0 %collective-permute-done.36.x2 = bf16[2,272,128]{2,1,0:T(8,128)(2,1)S(1)} collective-permute-done((bf16[2,272,128]{2,1,0:T(8,128)(2,1)S(1)}, bf16[2,272,128]{2,1,0:T(8,128)(2,1)S(1)}, u32[]{:S(2)}, u32[]{:S(2)}) %collective-permute-start.36) | collective-permute-done | bytes 139296 | tf_op jit(solution)/shard_map/ppermute | solution.py:58
  110.0 1.9 %collective-permute-start.38 = (bf16[1,144,512]{2,1,0:T(8,128)(2,1)S(1)}, bf16[1,144,512]{2,1,0:T(8,128)(2,1)S(1)}, u32[]{:S(2)}, u32[]{:S(2)}) collective-permute-start(bf16[1,144,512]{2,1,0:T(8,128)(2,1)S(1)} %get-tuple-element.148), channel_id=1, source_target_pairs={{0,16},{1,17},{2,18},{3,19},{4,20},{5,21},{6,22},{7,23},{8,24},{9,... | collective-permute-start | bytes 442376 | tf_op jit(solution)/shard_map/ppermute | solution.py:58
  114.2 2.1 %collective-permute-done.39.near = bf16[2,272,128]{2,1,0:T(8,128)(2,1)S(1)} collective-permute-done((bf16[2,272,128]{2,1,0:T(8,128)(2,1)S(1)}, bf16[2,272,128]{2,1,0:T(8,128)(2,1)S(1)}, u32[]{:S(2)}, u32[]{:S(2)}) %collective-permute-start.39) | collective-permute-done | bytes 139296 | tf_op jit(solution)/shard_map/ppermute | solution.py:58
  119.3 2.6 %collective-permute-done.40.far = bf16[1,272,128]{2,1,0:T(8,128)(2,1)S(1)} collective-permute-done((bf16[1,272,128]{2,1,0:T(8,128)(2,1)S(1)}, bf16[1,272,128]{2,1,0:T(8,128)(2,1)S(1)}, u32[]{:S(2)}, u32[]{:S(2)}) %collective-permute-start.40) | collective-permute-done | bytes 69664 | tf_op jit(solution)/shard_map/ppermute | solution.py:58
  123.4 1.7 %shard_map.371 = (bf16[4,128,512]{2,1,0:T(8,128)(2,1)}, f32[4,128,512]{2,1,0:T(8,128)}) custom-call(s32[2]{0:T(128)S(1)} %pad_add_fusion.scal, f32[8,128]{1,0:T(8,128)S(1)} %get-tuple-element.155.done, bf16[128,512]{1,0:T(8,128)(2,1)S(1)} %get-tuple-element.156.res_k, f32[128,512]{1,0:T(8,128)S(1)} %get-tuple-element.157.gi_k, ...), custom_call_target="tpu_custom_call" | custom-call | flops 1000 | tf_op jit(solution)/shard_map/pallas_call | solution.py:632
  (132 shorter events, 39.2 us)
Async XLA Ops:
  2.8 29.6 %collective-permute-start = (bf16[4,128,512]{2,1,0:T(8,128)(2,1)S(1)}, bf16[4,128,512]{2,1,0:T(8,128)(2,1)S(1)}, u32[]{:S(2)}, u32[]{:S(2)}) collective-permute-start(bf16[4,128,512]{2,1,0:T(8,128)(2,1)S(1)} %get-tuple-element.103), channel_id=1, source_target_pairs={{0,2},{1,3},{2,0},{3,1},{4,6},{5,7},{6,4},{7,5},{8,10},{9,11},{10,... | collective-permute-start | bytes 1572872 | tf_op jit(solution)/shard_map/ppermute | solution.py:58
  11.4 8.2 %collective-permute-start.12 = (bf16[1,144,512]{2,1,0:T(8,128)(2,1)S(1)}, bf16[1,144,512]{2,1,0:T(8,128)(2,1)S(1)}, u32[]{:S(2)}, u32[]{:S(2)}) collective-permute-start(bf16[1,144,512]{2,1,0:T(8,128)(2,1)S(1)} %get-tuple-element.114.own), channel_id=1, source_target_pairs={{0,16},{1,17},{2,18},{3,19},{4,20},{5,21},{6,22},{7,23},{8,24},{9,... | collective-permute-start | bytes 442376 | tf_op jit(solution)/shard_map/ppermute | solution.py:58
  21.4 10.7 %collective-permute-start.8 = (bf16[4,272,128]{2,1,0:T(8,128)(2,1)S(1)}, bf16[4,272,128]{2,1,0:T(8,128)(2,1)S(1)}, u32[]{:S(2)}, u32[]{:S(2)}) collective-permute-start(bf16[4,272,128]{2,1,0:T(8,128)(2,1)S(1)} %shard_map.358.refs_5_), channel_id=1, source_target_pairs={{0,4},{1,5},{2,6},{3,7},{4,0},{5,1},{6,2},{7,3},{8,12},{9,13},{10,... | collective-permute-start | bytes 835592 | tf_op jit(solution)/shard_map/ppermute | solution.py:58
  22.9 9.6 %collective-permute-start.6 = (bf16[4,272,128]{2,1,0:T(8,128)(2,1)S(1)}, bf16[4,272,128]{2,1,0:T(8,128)(2,1)S(1)}, u32[]{:S(2)}, u32[]{:S(2)}) collective-permute-start(bf16[4,272,128]{2,1,0:T(8,128)(2,1)S(1)} %shard_map.358.refs_5_), channel_id=1, source_target_pairs={{0,2},{1,3},{2,0},{3,1},{4,6},{5,7},{6,4},{7,5},{8,10},{9,11},{10,... | collective-permute-start | bytes 835592 | tf_op jit(solution)/shard_map/ppermute | solution.py:58
  23.4 15.0 %collective-permute-start.10 = (bf16[4,272,128]{2,1,0:T(8,128)(2,1)S(1)}, bf16[4,272,128]{2,1,0:T(8,128)(2,1)S(1)}, u32[]{:S(2)}, u32[]{:S(2)}) collective-permute-start(bf16[4,272,128]{2,1,0:T(8,128)(2,1)S(1)} %shard_map.358.refs_5_), channel_id=1, source_target_pairs={{0,6},{1,7},{2,4},{3,5},{4,2},{5,3},{6,0},{7,1},{8,14},{9,15},{10,... | collective-permute-start | bytes 835592 | tf_op jit(solution)/shard_map/ppermute | solution.py:58
  32.5 14.0 %collective-permute-start.17 = (bf16[4,144,512]{2,1,0:T(8,128)(2,1)S(1)}, bf16[4,144,512]{2,1,0:T(8,128)(2,1)S(1)}, u32[]{:S(2)}, u32[]{:S(2)}) collective-permute-start(bf16[4,144,512]{2,1,0:T(8,128)(2,1)S(1)} %shard_map.362.refs_8_), channel_id=1, source_target_pairs={{0,4},{1,5},{2,6},{3,7},{4,0},{5,1},{6,2},{7,3},{8,12},{9,13},{10,... | collective-permute-start | bytes 1769480 | tf_op jit(solution)/shard_map/ppermute | solution.py:58
  34.2 13.1 %collective-permute-start.15 = (bf16[4,144,512]{2,1,0:T(8,128)(2,1)S(1)}, bf16[4,144,512]{2,1,0:T(8,128)(2,1)S(1)}, u32[]{:S(2)}, u32[]{:S(2)}) collective-permute-start(bf16[4,144,512]{2,1,0:T(8,128)(2,1)S(1)} %shard_map.362.refs_8_), channel_id=1, source_target_pairs={{0,2},{1,3},{2,0},{3,1},{4,6},{5,7},{6,4},{7,5},{8,10},{9,11},{10,... | collective-permute-start | bytes 1769480 | tf_op jit(solution)/shard_map/ppermute | solution.py:58
  46.5 8.6 %collective-permute-start.21 = (bf16[2,144,512]{2,1,0:T(8,128)(2,1)S(1)}, bf16[2,144,512]{2,1,0:T(8,128)(2,1)S(1)}, u32[]{:S(2)}, u32[]{:S(2)}) collective-permute-start(bf16[2,144,512]{2,1,0:T(8,128)(2,1)S(1)} %slice.54), channel_id=1, source_target_pairs={{0,2},{1,3},{2,0},{3,1},{4,6},{5,7},{6,4},{7,5},{8,10},{9,11},{10,... | collective-permute-start | bytes 884744 | tf_op jit(solution)/shard_map/ppermute | solution.py:58
  47.4 8.2 %collective-permute-start.19 = (bf16[2,144,512]{2,1,0:T(8,128)(2,1)S(1)}, bf16[2,144,512]{2,1,0:T(8,128)(2,1)S(1)}, u32[]{:S(2)}, u32[]{:S(2)}) collective-permute-start(bf16[2,144,512]{2,1,0:T(8,128)(2,1)S(1)} %slice.53), channel_id=1, source_target_pairs={{0,4},{1,5},{2,6},{3,7},{4,0},{5,1},{6,2},{7,3},{8,12},{9,13},{10,... | collective-permute-start | bytes 884744 | tf_op jit(solution)/shard_map/ppermute | solution.py:58
  48.8 7.3 %collective-permute-start.14 = (bf16[4,144,512]{2,1,0:T(8,128)(2,1)S(1)}, bf16[4,144,512]{2,1,0:T(8,128)(2,1)S(1)}, u32[]{:S(2)}, u32[]{:S(2)}) collective-permute-start(bf16[4,144,512]{2,1,0:T(8,128)(2,1)S(1)} %shard_map.362.refs_8_), channel_id=1, source_target_pairs={{0,1},{1,0},{2,3},{3,2},{4,5},{5,4},{6,7},{7,6},{8,9},{9,8},{10,11... | collective-permute-start | bytes 1769480 | tf_op jit(solution)/shard_map/ppermute | solution.py:58
  48.8 7.3 %collective-permute-start.18 = (bf16[4,144,512]{2,1,0:T(8,128)(2,1)S(1)}, bf16[4,144,512]{2,1,0:T(8,128)(2,1)S(1)}, u32[]{:S(2)}, u32[]{:S(2)}) collective-permute-start(bf16[4,144,512]{2,1,0:T(8,128)(2,1)S(1)} %collective-permute-done.17.refs_12_), channel_id=1, source_target_pairs={{0,1},{1,0},{2,3},{3,2},{4,5},{5,4},{6,7},{7,6},{8,9},{9,8},{10,11... | collective-permute-start | bytes 1769480 | tf_op jit(solution)/shard_map/ppermute | solution.py:58
  69.5 18.5 %collective-permute-start.23 = (bf16[8,144,512]{2,1,0:T(8,128)(2,1)S(1)}, bf16[8,144,512]{2,1,0:T(8,128)(2,1)S(1)}, u32[]{:S(2)}, u32[]{:S(2)}) collective-permute-start(bf16[8,144,512]{2,1,0:T(8,128)(2,1)S(1)} %get-tuple-element.122), channel_id=1, source_target_pairs={{0,1},{1,0},{2,3},{3,2},{4,5},{5,4},{6,7},{7,6},{8,9},{9,8},{10,11... | collective-permute-start | bytes 3538952 | tf_op jit(solution)/shard_map/ppermute | solution.py:58
  71.1 15.4 %collective-permute-start.25 = (bf16[4,144,512]{2,1,0:T(8,128)(2,1)S(1)}, bf16[4,144,512]{2,1,0:T(8,128)(2,1)S(1)}, u32[]{:S(2)}, u32[]{:S(2)}) collective-permute-start(bf16[4,144,512]{2,1,0:T(8,128)(2,1)S(1)} %add_convert_fusion.1), channel_id=1, source_target_pairs={{0,2},{1,3},{2,0},{3,1},{4,6},{5,7},{6,4},{7,5},{8,10},{9,11},{10,... | collective-permute-start | bytes 1769480 | tf_op jit(solution)/shard_map/ppermute | solution.py:58
  72.8 15.2 %collective-permute-start.27 = (bf16[4,144,512]{2,1,0:T(8,128)(2,1)S(1)}, bf16[4,144,512]{2,1,0:T(8,128)(2,1)S(1)}, u32[]{:S(2)}, u32[]{:S(2)}) collective-permute-start(bf16[4,144,512]{2,1,0:T(8,128)(2,1)S(1)} %add_convert_fusion), channel_id=1, source_target_pairs={{0,4},{1,5},{2,6},{3,7},{4,0},{5,1},{6,2},{7,3},{8,12},{9,13},{10,... | collective-permute-start | bytes 1769480 | tf_op jit(solution)/shard_map/ppermute | solution.py:58
  86.6 17.0 %collective-permute-start.31 = (bf16[8,272,128]{2,1,0:T(8,128)(2,1)S(1)}, bf16[8,272,128]{2,1,0:T(8,128)(2,1)S(1)}, u32[]{:S(2)}, u32[]{:S(2)}) collective-permute-start(bf16[8,272,128]{2,1,0:T(8,128)(2,1)S(1)} %get-tuple-element.140), channel_id=1, source_target_pairs={{0,1},{1,0},{2,3},{3,2},{4,5},{5,4},{6,7},{7,6},{8,9},{9,8},{10,11... | collective-permute-start | bytes 1671176 | tf_op jit(solution)/shard_map/ppermute | solution.py:58
  88.2 10.0 %collective-permute-start.28 = (bf16[2,144,512]{2,1,0:T(8,128)(2,1)S(1)}, bf16[2,144,512]{2,1,0:T(8,128)(2,1)S(1)}, u32[]{:S(2)}, u32[]{:S(2)}) collective-permute-start(bf16[2,144,512]{2,1,0:T(8,128)(2,1)S(1)} %get-tuple-element.185), channel_id=1, source_target_pairs={{0,4},{1,5},{2,6},{3,7},{4,0},{5,1},{6,2},{7,3},{8,12},{9,13},{10,... | collective-permute-start | bytes 884744 | tf_op jit(solution)/shard_map/ppermute | solution.py:58
  89.8 9.9 %collective-permute-start.29 = (bf16[2,144,512]{2,1,0:T(8,128)(2,1)S(1)}, bf16[2,144,512]{2,1,0:T(8,128)(2,1)S(1)}, u32[]{:S(2)}, u32[]{:S(2)}) collective-permute-start(bf16[2,144,512]{2,1,0:T(8,128)(2,1)S(1)} %get-tuple-element.184), channel_id=1, source_target_pairs={{0,2},{1,3},{2,0},{3,1},{4,6},{5,7},{6,4},{7,5},{8,10},{9,11},{10,... | collective-permute-start | bytes 884744 | tf_op jit(solution)/shard_map/ppermute | solution.py:58
  90.8 12.7 %collective-permute-start.33 = (bf16[4,272,128]{2,1,0:T(8,128)(2,1)S(1)}, bf16[4,272,128]{2,1,0:T(8,128)(2,1)S(1)}, u32[]{:S(2)}, u32[]{:S(2)}) collective-permute-start(bf16[4,272,128]{2,1,0:T(8,128)(2,1)S(1)} %add_convert_fusion.5), channel_id=1, source_target_pairs={{0,2},{1,3},{2,0},{3,1},{4,6},{5,7},{6,4},{7,5},{8,10},{9,11},{10,... | collective-permute-start | bytes 835592 | tf_op jit(solution)/shard_map/ppermute | solution.py:58
  92.1 11.4 %collective-permute-start.35 = (bf16[4,272,128]{2,1,0:T(8,128)(2,1)S(1)}, bf16[4,272,128]{2,1,0:T(8,128)(2,1)S(1)}, u32[]{:S(2)}, u32[]{:S(2)}) collective-permute-start(bf16[4,272,128]{2,1,0:T(8,128)(2,1)S(1)} %add_convert_fusion.4), channel_id=1, source_target_pairs={{0,4},{1,5},{2,6},{3,7},{4,0},{5,1},{6,2},{7,3},{8,12},{9,13},{10,... | collective-permute-start | bytes 835592 | tf_op jit(solution)/shard_map/ppermute | solution.py:58
  100.1 9.2 %collective-permute-start.30 = (bf16[2,144,512]{2,1,0:T(8,128)(2,1)S(1)}, bf16[2,144,512]{2,1,0:T(8,128)(2,1)S(1)}, u32[]{:S(2)}, u32[]{:S(2)}) collective-permute-start(bf16[2,144,512]{2,1,0:T(8,128)(2,1)S(1)} %get-tuple-element.129), channel_id=1, source_target_pairs={{0,8},{1,9},{2,10},{3,11},{4,12},{5,13},{6,14},{7,15},{8,0},{9,1},... | collective-permute-start | bytes 884744 | tf_op jit(solution)/shard_map/ppermute | solution.py:58
  112.0 11.5 %collective-permute-start.43 = (bf16[2,128,512]{2,1,0:T(8,128)(2,1)S(1)}, bf16[2,128,512]{2,1,0:T(8,128)(2,1)S(1)}, u32[]{:S(2)}, u32[]{:S(2)}) collective-permute-start(bf16[2,128,512]{2,1,0:T(8,128)(2,1)S(1)} %get-tuple-element.162), channel_id=1, source_target_pairs={{0,2},{1,3},{2,0},{3,1},{4,6},{5,7},{6,4},{7,5},{8,10},{9,11},{10,... | collective-permute-start | bytes 786440 | tf_op jit(solution)/shard_map/ppermute | solution.py:58
  113.5 9.9 %collective-permute-start.44 = (bf16[2,128,512]{2,1,0:T(8,128)(2,1)S(1)}, bf16[2,128,512]{2,1,0:T(8,128)(2,1)S(1)}, u32[]{:S(2)}, u32[]{:S(2)}) collective-permute-start(bf16[2,128,512]{2,1,0:T(8,128)(2,1)S(1)} %get-tuple-element.163), channel_id=1, source_target_pairs={{0,3},{1,2},{2,1},{3,0},{4,7},{5,6},{6,5},{7,4},{8,11},{9,10},{10,... | collective-permute-start | bytes 786440 | tf_op jit(solution)/shard_map/ppermute | solution.py:58
  113.5 9.9 %collective-permute-start.41 = (bf16[1,128,512]{2,1,0:T(8,128)(2,1)S(1)}, bf16[1,128,512]{2,1,0:T(8,128)(2,1)S(1)}, u32[]{:S(2)}, u32[]{:S(2)}) collective-permute-start(bf16[1,128,512]{2,1,0:T(8,128)(2,1)S(1)} %get-tuple-element.158), channel_id=1, source_target_pairs={{0,1},{1,0},{2,3},{3,2},{4,5},{5,4},{6,7},{7,6},{8,9},{9,8},{10,11... | collective-permute-start | bytes 393224 | tf_op jit(solution)/shard_map/ppermute | solution.py:58
  116.3 7.1 %collective-permute-start.42 = (bf16[1,128,512]{2,1,0:T(8,128)(2,1)S(1)}, bf16[1,128,512]{2,1,0:T(8,128)(2,1)S(1)}, u32[]{:S(2)}, u32[]{:S(2)}) collective-permute-start(bf16[1,128,512]{2,1,0:T(8,128)(2,1)S(1)} %get-tuple-element.159), channel_id=1, source_target_pairs={{0,1},{1,0},{2,3},{3,2},{4,5},{5,4},{6,7},{7,6},{8,9},{9,8},{10,11... | collective-permute-start | bytes 393224 | tf_op jit(solution)/shard_map/ppermute | solution.py:58
  (40 other events, 223.4 us)

commit v9 on v8

--- a/solution.py
+++ b/solution.py
@@ -118,6 +118,24 @@
         copy.wait()
 
 
+def mask_kernel(scal, segs, bias):
+    me_t = scal[1]
+    win = bias.shape[0]
+    seg = segs[pl.ds(me_t, 1), :].astype(F32)
+    seg_col = jnp.transpose(jnp.broadcast_to(seg, (LANES, win)))
+    for i in range(win // LANES):
+        key_seg = seg_col[i * LANES : (i + 1) * LANES, 0:1]
+        key_at = lax.broadcasted_iota(jnp.int32, (LANES, win), 0) + i * LANES
+        query_at = lax.broadcasted_iota(jnp.int32, (LANES, win), 1)
+        counts = (key_seg == seg) & (query_at >= key_at)
+        bias[i * LANES : (i + 1) * LANES, :] = jnp.where(counts, 0.0, NEG_FILL)
+
+
+def stack_mask_kernel(scal, segs, own, got, both, bias):
+    stack_kernel(own, got, both)
+    mask_kernel(scal, segs, bias)
+
+
 def stack_kernel(own, got, both):
     n = own.shape[0]
     both[:n] = own[...]
@@ -162,9 +180,9 @@
 
 
 def attention_kernel(places, n_pieces, scal, *refs):
-    own, rx, c1, c3, segs = refs[:5]
+    own, rx, c1, c3, bias = refs[:5]
     pieces = refs[5 : 5 + n_pieces]
-    hid_o, qkv_h, pt_h, mix_o, w_h, nrm_o, x_s, wlast_o, bias_s, pos_s, nrm_s, w_o, qkv_o, pt_o, out_sems = refs[5 + n_pieces :]
+    hid_o, qkv_h, pt_h, mix_o, w_h, nrm_o, x_s, wlast_o, pos_s, nrm_s, w_o, qkv_o, pt_o, out_sems = refs[5 + n_pieces :]
     leaving, leave = leaver(out_sems)
     me_dp, me_t = scal[0], scal[1]
     win, width = x_s.shape
@@ -201,20 +219,11 @@
 
     leave(w_o, w_h)
 
-    seg = segs[pl.ds(me_t, 1), :].astype(F32)
-    seg_col = jnp.transpose(jnp.broadcast_to(seg, (LANES, win)))
-    for i in range(win // LANES):
-        key_seg = seg_col[i * LANES : (i + 1) * LANES, 0:1]
-        key_at = lax.broadcasted_iota(jnp.int32, (LANES, win), 0) + i * LANES
-        query_at = lax.broadcasted_iota(jnp.int32, (LANES, win), 1)
-        counts = (key_seg == seg) & (query_at >= key_at)
-        bias_s[i * LANES : (i + 1) * LANES, :] = jnp.where(counts, 0.0, NEG_FILL)
-
     hidden = x_s[...].astype(F32) + pos_s[...].astype(F32)
     hid_o[...] = hidden
     x_s[...] = hidden.astype(BF16)
     first = qkv_o.shape[1] // (3 * LANES)
-    attend(x_s, w_o, range(first), bias_s, qkv_o, qkv_h, pt_o, pt_h, mix_o, leave)
+    attend(x_s, w_o, range(first), bias, qkv_o, qkv_h, pt_o, pt_h, mix_o, leave)
     wlast_o[...] = w_o[:, first * 3 * LANES :]
     for copy in leaving:
         copy.wait()
@@ -694,7 +703,17 @@
         qa, za = stacked(a2, swap(a2, 2, 0)), (0, 2, 1, 3)
         gb = after(gb, a2)
         rx = swap(xs, 0, 2)
-        qb, zb = gather_z(gb, qa)
+        b2 = after(stacked(gb, swap(gb, 4, 0)), qa)
+        qb, bias = call(
+            stack_mask_kernel,
+            [sds((2 * b2.shape[0], *b2.shape[1:]), BF16), sds((win, win), F32)],
+            [],
+            [scal, segment_ids, b2, swap(b2, 2, 0)],
+            "svvv",
+            10,
+            1_000,
+        )
+        zb = za
         c1 = swap(c1, 0, 1)
         c3 = swap(rx[2:], 0, 1)
         qax, qay, qaxy = swap(qa, 0, 2), swap(qa, 1, 0), swap(qa, 1, 2)
@@ -702,6 +721,8 @@
         qb = after(qb, rx, qax, qay)
         qbx, qby = swap(qb, 0, 2), swap(qb, 1, 0)
     else:
+
+        bias = call(mask_kernel, [sds((win, win), F32)], [], [scal, segment_ids], "sv", 6, 1_000)[0]
 
         def pair(rel):
             return jnp.concatenate([lax.dynamic_slice_in_dim(v, me_t ^ rel, 1, 0) for v in (inputs, cotangent)])
@@ -728,7 +749,7 @@
     def work(groups):
         return [((win, groups * 3 * group), BF16), ((groups * heads_of, win, win), BF16), [groups * (1 + 2 * heads_of) + 1]]
 
-    hid, qkv_a, pt_a, mixed_a, attn_all, norm_all, x_all, w_last, bias = call(
+    hid, qkv_a, pt_a, mixed_a, attn_all, norm_all, x_all, w_last = call(
         functools.partial(attention_kernel, a_places, len(a_args)),
         [
             sds((win, width), F32),
@@ -737,10 +758,9 @@
             sds((8, width), F32),
             sds((win, width), BF16),
             sds((width, (n_t - first) * 3 * group), BF16),
-            sds((win, win), F32),
         ],
         [((win, width), BF16), ((n_dp, 16, LANES), F32), ((width, n_t * 3 * group), BF16), *work(first)],
-        [scal, own, rx, c1, c3, segment_ids, *a_args],
+        [scal, own, rx, c1, c3, bias, *a_args],
         "svvvvv" + "v" * len(a_args),
         14,
         1_000_000,

time: 126 us -> 126 us (level)
  transfers between devices with their start and end apart: 45 -> 45, of which waited for: 26 -> 26; matrix products, arithmetic and copies ran while one was open for 1% -> 1% of each run, Pallas kernels for 17% -> 18%
where the time goes in v9:
time: 126 us; the launch traced here: 125 us
  waiting for transfers between devices  45.9 us (36%)
  starting transfers between devices  39.3 us (31%)
  Pallas kernels  37.8 us (30%)
  between operations  1.29 us (1%)
    ppermute x45, waiting for transfers between devices, swap(): lax.ppermute(value, AXES, [(i, i ^ mask) for i in range(lax.axis_size('dp...  45.9 us
    ppermute x45, starting transfers between devices, swap(): lax.ppermute(value, AXES, [(i, i ^ mask) for i in range(lax.axis_size('dp...  39.3 us
    pallas_call x16, Pallas kernels, call(): pl.pallas_call(kernel, out_shape=outs, in_specs=[kinds[k] for k in spaces...  37.8 us
  transfers between devices with their start and end apart: 45, of which 26 were waited for; matrix products, arithmetic and copies ran while one was open for 1% of the time, Pallas kernels for 18%

profile of v9, /device:TPU:0, one launch (start us, length us, event | category | flops | bytes accessed | tf_op | source)
XLA Modules:
  0.0 125.4 jit_solution(2552549740629852026)
XLA Ops:
  0.7 2.1 %shard_map.356 = (bf16[1,272,128]{2,1,0:T(8,128)(2,1)S(1)}, bf16[1,144,512]{2,1,0:T(8,128)(2,1)S(1)}, bf16[4,128,512]{2,1,0:T(8,128)(2,1)S(1)}, bf16[2,128,512]{2,1,0:T(8,128)(2,1)S(1)}, bf16[2,128,512]{2,1,0:T(8,128)(2,1)S(1)}) custom-call(s32[2]{0:T(128)S(1)} %pad_add_fusion.scal, bf16[4,128,512]{2,1,0:T(8,128)(2,1)} %inputs.1, bf16[4,128,512]{2,1,0:T(8,128)(2,1)} %cot.1, ...), custom_call_target="tpu_custom_call" | custom-call | flops 1000 | tf_op jit(solution)/shard_map/pallas_call | solution.py:641
  2.8 3.0 %collective-permute-start = (bf16[4,128,512]{2,1,0:T(8,128)(2,1)S(1)}, bf16[4,128,512]{2,1,0:T(8,128)(2,1)S(1)}, u32[]{:S(2)}, u32[]{:S(2)}) collective-permute-start(bf16[4,128,512]{2,1,0:T(8,128)(2,1)S(1)} %get-tuple-element.104), channel_id=1, source_target_pairs={{0,2},{1,3},{2,0},{3,1},{4,6},{5,7},{6,4},{7,5},{8,10},{9,11},{10,... | collective-permute-start | bytes 1572872 | tf_op jit(solution)/shard_map/ppermute | solution.py:58
  5.8 2.6 %collective-permute-start.3 = (bf16[1,272,128]{2,1,0:T(8,128)(2,1)S(1)}, bf16[1,272,128]{2,1,0:T(8,128)(2,1)S(1)}, u32[]{:S(2)}, u32[]{:S(2)}) collective-permute-start(bf16[1,272,128]{2,1,0:T(8,128)(2,1)S(1)} %get-tuple-element.107.own), channel_id=1, source_target_pairs={{0,16},{1,17},{2,18},{3,19},{4,20},{5,21},{6,22},{7,23},{8,24},{9,... | collective-permute-start | bytes 208904 | tf_op jit(solution)/shard_map/ppermute | solution.py:58
  8.4 3.0 %collective-permute-done.3.got = bf16[1,272,128]{2,1,0:T(8,128)(2,1)S(1)} collective-permute-done((bf16[1,272,128]{2,1,0:T(8,128)(2,1)S(1)}, bf16[1,272,128]{2,1,0:T(8,128)(2,1)S(1)}, u32[]{:S(2)}, u32[]{:S(2)}) %collective-permute-start.3) | collective-permute-done | bytes 69664 | tf_op jit(solution)/shard_map/ppermute | solution.py:58
  11.4 2.4 %collective-permute-start.4 = (bf16[1,144,512]{2,1,0:T(8,128)(2,1)S(1)}, bf16[1,144,512]{2,1,0:T(8,128)(2,1)S(1)}, u32[]{:S(2)}, u32[]{:S(2)}) collective-permute-start(bf16[1,144,512]{2,1,0:T(8,128)(2,1)S(1)} %get-tuple-element.108.own), channel_id=1, source_target_pairs={{0,16},{1,17},{2,18},{3,19},{4,20},{5,21},{6,22},{7,23},{8,24},{9,... | collective-permute-start | bytes 442376 | tf_op jit(solution)/shard_map/ppermute | solution.py:58
  13.8 2.2 %collective-permute-start.5 = (bf16[2,272,128]{2,1,0:T(8,128)(2,1)S(1)}, bf16[2,272,128]{2,1,0:T(8,128)(2,1)S(1)}, u32[]{:S(2)}, u32[]{:S(2)}) collective-permute-start(bf16[2,272,128]{2,1,0:T(8,128)(2,1)S(1)} %shard_map.357.own), channel_id=1, source_target_pairs={{0,8},{1,9},{2,10},{3,11},{4,12},{5,13},{6,14},{7,15},{8,0},{9,1},... | collective-permute-start | bytes 417800 | tf_op jit(solution)/shard_map/ppermute | solution.py:58
  16.0 3.5 %collective-permute-done.5.got = bf16[2,272,128]{2,1,0:T(8,128)(2,1)S(1)} collective-permute-done((bf16[2,272,128]{2,1,0:T(8,128)(2,1)S(1)}, bf16[2,272,128]{2,1,0:T(8,128)(2,1)S(1)}, u32[]{:S(2)}, u32[]{:S(2)}) %collective-permute-start.5) | collective-permute-done | bytes 139296 | tf_op jit(solution)/shard_map/ppermute | solution.py:58
  19.6 1.8 %collective-permute-start.6 = (bf16[2,144,512]{2,1,0:T(8,128)(2,1)S(1)}, bf16[2,144,512]{2,1,0:T(8,128)(2,1)S(1)}, u32[]{:S(2)}, u32[]{:S(2)}) collective-permute-start(bf16[2,144,512]{2,1,0:T(8,128)(2,1)S(1)} %shard_map.358.own), channel_id=1, source_target_pairs={{0,8},{1,9},{2,10},{3,11},{4,12},{5,13},{6,14},{7,15},{8,0},{9,1},... | collective-permute-start | bytes 884744 | tf_op jit(solution)/shard_map/ppermute | solution.py:58
  24.8 1.7 %collective-permute-done.6.got = bf16[2,144,512]{2,1,0:T(8,128)(2,1)S(1)} collective-permute-done((bf16[2,144,512]{2,1,0:T(8,128)(2,1)S(1)}, bf16[2,144,512]{2,1,0:T(8,128)(2,1)S(1)}, u32[]{:S(2)}, u32[]{:S(2)}) %collective-permute-start.6) | collective-permute-done | bytes 294944 | tf_op jit(solution)/shard_map/ppermute | solution.py:58
  27.4 4.6 %collective-permute-done.10.refs_9_ = bf16[4,272,128]{2,1,0:T(8,128)(2,1)S(1)} collective-permute-done((bf16[4,272,128]{2,1,0:T(8,128)(2,1)S(1)}, bf16[4,272,128]{2,1,0:T(8,128)(2,1)S(1)}, u32[]{:S(2)}, u32[]{:S(2)}) %collective-permute-start.10) | collective-permute-done | bytes 278560 | tf_op jit(solution)/shard_map/ppermute | solution.py:58
  35.2 3.1 %collective-permute-done.12.refs_11_ = bf16[4,272,128]{2,1,0:T(8,128)(2,1)S(1)} collective-permute-done((bf16[4,272,128]{2,1,0:T(8,128)(2,1)S(1)}, bf16[4,272,128]{2,1,0:T(8,128)(2,1)S(1)}, u32[]{:S(2)}, u32[]{:S(2)}) %collective-permute-start.12) | collective-permute-done | bytes 278560 | tf_op jit(solution)/shard_map/ppermute | solution.py:58
  41.5 4.6 %shard_map.361 = (f32[512,512]{1,0:T(8,128)S(1)}, bf16[512,768]{1,0:T(8,128)(2,1)}, bf16[4,512,512]{2,1,0:T(8,128)(2,1)}, bf16[512,256]{1,0:T(8,128)(2,1)S(1)}, ...) custom-call(s32[2]{0:T(128)S(1)} %pad_add_fusion.scal, ...), custom_call_target="tpu_custom_call" | custom-call | flops 1000000 | tf_op jit(solution)/shard_map/pallas_call | solution.py:641
  49.3 3.6 %shard_map.362 = (bf16[512,768]{1,0:T(8,128)(2,1)}, bf16[4,512,512]{2,1,0:T(8,128)(2,1)}, bf16[512,256]{1,0:T(8,128)(2,1)S(1)}) custom-call(bf16[512,512]{1,0:T(8,128)(2,1)S(1)} %get-tuple-element.113.x, bf16[512,768]{1,0:T(8,128)(2,1)S(1)} %get-tuple-element.114.w, f32[512,512]{1,0:T(8,128)S(1)} %get-tuple-element.110.refs_4_.bias), custom_call_target="tpu_custom_call" | custom-call | flops 1000000 | tf_op jit(solution)/shard_map/pallas_call | solution.py:641
  52.9 2.3 %collective-permute-done.21.refs_16_ = bf16[2,144,512]{2,1,0:T(8,128)(2,1)S(1)} collective-permute-done((bf16[2,144,512]{2,1,0:T(8,128)(2,1)S(1)}, bf16[2,144,512]{2,1,0:T(8,128)(2,1)S(1)}, u32[]{:S(2)}, u32[]{:S(2)}) %collective-permute-start.21) | collective-permute-done | bytes 294944 | tf_op jit(solution)/shard_map/ppermute | solution.py:58
  57.6 11.3 %shard_map.363 = (bf16[128,512]{1,0:T(8,128)(2,1)S(1)}, bf16[1,128,512]{2,1,0:T(8,128)(2,1)S(1)}, bf16[2,128,512]{2,1,0:T(8,128)(2,1)S(1)}, f32[512,512]{1,0:T(8...) custom-call(s32[2]{0:T(128)S(1)} %pad_add_fusion.scal, ...), custom_call_target="tpu_custom_call" | custom-call | flops 1000000 | tf_op jit(solution)/shard_map/pallas_call | solution.py:641
  74.4 10.5 %shard_map.365 = (f32[128,512]{1,0:T(8,128)S(1)}, bf16[1,128,512]{2,1,0:T(8,128)(2,1)S(1)}, bf16[2,128,512]{2,1,0:T(8,128)(2,1)S(1)}, bf16[4,272,128]{2,1,0:T(8,...) custom-call(s32[2]{0:T(128)S(1)} %pad_add_fusion.scal, ...), custom_call_target="tpu_custom_call" | custom-call | flops 1000000 | tf_op jit(solution)/shard_map/pallas_call | solution.py:641
  92.7 5.6 %collective-permute-done.28.x2 = bf16[2,144,512]{2,1,0:T(8,128)(2,1)S(1)} collective-permute-done((bf16[2,144,512]{2,1,0:T(8,128)(2,1)S(1)}, bf16[2,144,512]{2,1,0:T(8,128)(2,1)S(1)}, u32[]{:S(2)}, u32[]{:S(2)}) %collective-permute-start.28) | collective-permute-done | bytes 294944 | tf_op jit(solution)/shard_map/ppermute | solution.py:58
  100.5 3.0 %collective-permute-done.33.x = bf16[4,272,128]{2,1,0:T(8,128)(2,1)S(1)} collective-permute-done((bf16[4,272,128]{2,1,0:T(8,128)(2,1)S(1)}, bf16[4,272,128]{2,1,0:T(8,128)(2,1)S(1)}, u32[]{:S(2)}, u32[]{:S(2)}) %collective-permute-start.33) | collective-permute-done | bytes 278560 | tf_op jit(solution)/shard_map/ppermute | solution.py:58
  105.7 3.0 %collective-permute-done.36.x2 = bf16[2,272,128]{2,1,0:T(8,128)(2,1)S(1)} collective-permute-done((bf16[2,272,128]{2,1,0:T(8,128)(2,1)S(1)}, bf16[2,272,128]{2,1,0:T(8,128)(2,1)S(1)}, u32[]{:S(2)}, u32[]{:S(2)}) %collective-permute-start.36) | collective-permute-done | bytes 139296 | tf_op jit(solution)/shard_map/ppermute | solution.py:58
  110.0 1.9 %collective-permute-start.38 = (bf16[1,144,512]{2,1,0:T(8,128)(2,1)S(1)}, bf16[1,144,512]{2,1,0:T(8,128)(2,1)S(1)}, u32[]{:S(2)}, u32[]{:S(2)}) collective-permute-start(bf16[1,144,512]{2,1,0:T(8,128)(2,1)S(1)} %get-tuple-element.150), channel_id=1, source_target_pairs={{0,16},{1,17},{2,18},{3,19},{4,20},{5,21},{6,22},{7,23},{8,24},{9,... | collective-permute-start | bytes 442376 | tf_op jit(solution)/shard_map/ppermute | solution.py:58
  114.2 2.1 %collective-permute-done.39.near = bf16[2,272,128]{2,1,0:T(8,128)(2,1)S(1)} collective-permute-done((bf16[2,272,128]{2,1,0:T(8,128)(2,1)S(1)}, bf16[2,272,128]{2,1,0:T(8,128)(2,1)S(1)}, u32[]{:S(2)}, u32[]{:S(2)}) %collective-permute-start.39) | collective-permute-done | bytes 139296 | tf_op jit(solution)/shard_map/ppermute | solution.py:58
  116.3 1.7 %collective-permute-start.40 = (bf16[1,272,128]{2,1,0:T(8,128)(2,1)S(1)}, bf16[1,272,128]{2,1,0:T(8,128)(2,1)S(1)}, u32[]{:S(2)}, u32[]{:S(2)}) collective-permute-start(bf16[1,272,128]{2,1,0:T(8,128)(2,1)S(1)} %get-tuple-element.156), channel_id=1, source_target_pairs={{0,16},{1,17},{2,18},{3,19},{4,20},{5,21},{6,22},{7,23},{8,24},{9,... | collective-permute-start | bytes 208904 | tf_op jit(solution)/shard_map/ppermute | solution.py:58
  119.3 2.6 %collective-permute-done.40.far = bf16[1,272,128]{2,1,0:T(8,128)(2,1)S(1)} collective-permute-done((bf16[1,272,128]{2,1,0:T(8,128)(2,1)S(1)}, bf16[1,272,128]{2,1,0:T(8,128)(2,1)S(1)}, u32[]{:S(2)}, u32[]{:S(2)}) %collective-permute-start.40) | collective-permute-done | bytes 69664 | tf_op jit(solution)/shard_map/ppermute | solution.py:58
  123.4 1.7 %shard_map.371 = (bf16[4,128,512]{2,1,0:T(8,128)(2,1)}, f32[4,128,512]{2,1,0:T(8,128)}) custom-call(s32[2]{0:T(128)S(1)} %pad_add_fusion.scal, f32[8,128]{1,0:T(8,128)S(1)} %get-tuple-element.157.done, bf16[128,512]{1,0:T(8,128)(2,1)S(1)} %get-tuple-element.158.res_k, f32[128,512]{1,0:T(8,128)S(1)} %get-tuple-element.159.gi_k, ...), custom_call_target="tpu_custom_call" | custom-call | flops 1000 | tf_op jit(solution)/shard_map/pallas_call | solution.py:641
  (132 shorter events, 39.9 us)
Async XLA Ops:
  2.8 29.6 %collective-permute-start = (bf16[4,128,512]{2,1,0:T(8,128)(2,1)S(1)}, bf16[4,128,512]{2,1,0:T(8,128)(2,1)S(1)}, u32[]{:S(2)}, u32[]{:S(2)}) collective-permute-start(bf16[4,128,512]{2,1,0:T(8,128)(2,1)S(1)} %get-tuple-element.104), channel_id=1, source_target_pairs={{0,2},{1,3},{2,0},{3,1},{4,6},{5,7},{6,4},{7,5},{8,10},{9,11},{10,... | collective-permute-start | bytes 1572872 | tf_op jit(solution)/shard_map/ppermute | solution.py:58
  11.4 8.1 %collective-permute-start.4 = (bf16[1,144,512]{2,1,0:T(8,128)(2,1)S(1)}, bf16[1,144,512]{2,1,0:T(8,128)(2,1)S(1)}, u32[]{:S(2)}, u32[]{:S(2)}) collective-permute-start(bf16[1,144,512]{2,1,0:T(8,128)(2,1)S(1)} %get-tuple-element.108.own), channel_id=1, source_target_pairs={{0,16},{1,17},{2,18},{3,19},{4,20},{5,21},{6,22},{7,23},{8,24},{9,... | collective-permute-start | bytes 442376 | tf_op jit(solution)/shard_map/ppermute | solution.py:58
  21.4 10.7 %collective-permute-start.10 = (bf16[4,272,128]{2,1,0:T(8,128)(2,1)S(1)}, bf16[4,272,128]{2,1,0:T(8,128)(2,1)S(1)}, u32[]{:S(2)}, u32[]{:S(2)}) collective-permute-start(bf16[4,272,128]{2,1,0:T(8,128)(2,1)S(1)} %shard_map.359.refs_5_), channel_id=1, source_target_pairs={{0,4},{1,5},{2,6},{3,7},{4,0},{5,1},{6,2},{7,3},{8,12},{9,13},{10,... | collective-permute-start | bytes 835592 | tf_op jit(solution)/shard_map/ppermute | solution.py:58
  22.9 9.6 %collective-permute-start.8 = (bf16[4,272,128]{2,1,0:T(8,128)(2,1)S(1)}, bf16[4,272,128]{2,1,0:T(8,128)(2,1)S(1)}, u32[]{:S(2)}, u32[]{:S(2)}) collective-permute-start(bf16[4,272,128]{2,1,0:T(8,128)(2,1)S(1)} %shard_map.359.refs_5_), channel_id=1, source_target_pairs={{0,2},{1,3},{2,0},{3,1},{4,6},{5,7},{6,4},{7,5},{8,10},{9,11},{10,... | collective-permute-start | bytes 835592 | tf_op jit(solution)/shard_map/ppermute | solution.py:58
  23.4 15.0 %collective-permute-start.12 = (bf16[4,272,128]{2,1,0:T(8,128)(2,1)S(1)}, bf16[4,272,128]{2,1,0:T(8,128)(2,1)S(1)}, u32[]{:S(2)}, u32[]{:S(2)}) collective-permute-start(bf16[4,272,128]{2,1,0:T(8,128)(2,1)S(1)} %shard_map.359.refs_5_), channel_id=1, source_target_pairs={{0,6},{1,7},{2,4},{3,5},{4,2},{5,3},{6,0},{7,1},{8,14},{9,15},{10,... | collective-permute-start | bytes 835592 | tf_op jit(solution)/shard_map/ppermute | solution.py:58
  32.5 14.0 %collective-permute-start.17 = (bf16[4,144,512]{2,1,0:T(8,128)(2,1)S(1)}, bf16[4,144,512]{2,1,0:T(8,128)(2,1)S(1)}, u32[]{:S(2)}, u32[]{:S(2)}) collective-permute-start(bf16[4,144,512]{2,1,0:T(8,128)(2,1)S(1)} %get-tuple-element.118.refs_8_), channel_id=1, source_target_pairs={{0,4},{1,5},{2,6},{3,7},{4,0},{5,1},{6,2},{7,3},{8,12},{9,13},{10,... | collective-permute-start | bytes 1769480 | tf_op jit(solution)/shard_map/ppermute | solution.py:58
  34.2 13.1 %collective-permute-start.15 = (bf16[4,144,512]{2,1,0:T(8,128)(2,1)S(1)}, bf16[4,144,512]{2,1,0:T(8,128)(2,1)S(1)}, u32[]{:S(2)}, u32[]{:S(2)}) collective-permute-start(bf16[4,144,512]{2,1,0:T(8,128)(2,1)S(1)} %get-tuple-element.118.refs_8_), channel_id=1, source_target_pairs={{0,2},{1,3},{2,0},{3,1},{4,6},{5,7},{6,4},{7,5},{8,10},{9,11},{10,... | collective-permute-start | bytes 1769480 | tf_op jit(solution)/shard_map/ppermute | solution.py:58
  46.5 8.7 %collective-permute-start.21 = (bf16[2,144,512]{2,1,0:T(8,128)(2,1)S(1)}, bf16[2,144,512]{2,1,0:T(8,128)(2,1)S(1)}, u32[]{:S(2)}, u32[]{:S(2)}) collective-permute-start(bf16[2,144,512]{2,1,0:T(8,128)(2,1)S(1)} %slice.54), channel_id=1, source_target_pairs={{0,2},{1,3},{2,0},{3,1},{4,6},{5,7},{6,4},{7,5},{8,10},{9,11},{10,... | collective-permute-start | bytes 884744 | tf_op jit(solution)/shard_map/ppermute | solution.py:58
  47.4 8.2 %collective-permute-start.19 = (bf16[2,144,512]{2,1,0:T(8,128)(2,1)S(1)}, bf16[2,144,512]{2,1,0:T(8,128)(2,1)S(1)}, u32[]{:S(2)}, u32[]{:S(2)}) collective-permute-start(bf16[2,144,512]{2,1,0:T(8,128)(2,1)S(1)} %slice.53), channel_id=1, source_target_pairs={{0,4},{1,5},{2,6},{3,7},{4,0},{5,1},{6,2},{7,3},{8,12},{9,13},{10,... | collective-permute-start | bytes 884744 | tf_op jit(solution)/shard_map/ppermute | solution.py:58
  48.8 7.3 %collective-permute-start.14 = (bf16[4,144,512]{2,1,0:T(8,128)(2,1)S(1)}, bf16[4,144,512]{2,1,0:T(8,128)(2,1)S(1)}, u32[]{:S(2)}, u32[]{:S(2)}) collective-permute-start(bf16[4,144,512]{2,1,0:T(8,128)(2,1)S(1)} %get-tuple-element.118.refs_8_), channel_id=1, source_target_pairs={{0,1},{1,0},{2,3},{3,2},{4,5},{5,4},{6,7},{7,6},{8,9},{9,8},{10,11... | collective-permute-start | bytes 1769480 | tf_op jit(solution)/shard_map/ppermute | solution.py:58
  48.8 7.3 %collective-permute-start.18 = (bf16[4,144,512]{2,1,0:T(8,128)(2,1)S(1)}, bf16[4,144,512]{2,1,0:T(8,128)(2,1)S(1)}, u32[]{:S(2)}, u32[]{:S(2)}) collective-permute-start(bf16[4,144,512]{2,1,0:T(8,128)(2,1)S(1)} %collective-permute-done.17.refs_12_), channel_id=1, source_target_pairs={{0,1},{1,0},{2,3},{3,2},{4,5},{5,4},{6,7},{7,6},{8,9},{9,8},{10,11... | collective-permute-start | bytes 1769480 | tf_op jit(solution)/shard_map/ppermute | solution.py:58
  69.5 18.5 %collective-permute-start.23 = (bf16[8,144,512]{2,1,0:T(8,128)(2,1)S(1)}, bf16[8,144,512]{2,1,0:T(8,128)(2,1)S(1)}, u32[]{:S(2)}, u32[]{:S(2)}) collective-permute-start(bf16[8,144,512]{2,1,0:T(8,128)(2,1)S(1)} %get-tuple-element.124), channel_id=1, source_target_pairs={{0,1},{1,0},{2,3},{3,2},{4,5},{5,4},{6,7},{7,6},{8,9},{9,8},{10,11... | collective-permute-start | bytes 3538952 | tf_op jit(solution)/shard_map/ppermute | solution.py:58
  71.1 15.4 %collective-permute-start.25 = (bf16[4,144,512]{2,1,0:T(8,128)(2,1)S(1)}, bf16[4,144,512]{2,1,0:T(8,128)(2,1)S(1)}, u32[]{:S(2)}, u32[]{:S(2)}) collective-permute-start(bf16[4,144,512]{2,1,0:T(8,128)(2,1)S(1)} %add_convert_fusion.1), channel_id=1, source_target_pairs={{0,2},{1,3},{2,0},{3,1},{4,6},{5,7},{6,4},{7,5},{8,10},{9,11},{10,... | collective-permute-start | bytes 1769480 | tf_op jit(solution)/shard_map/ppermute | solution.py:58
  72.8 15.2 %collective-permute-start.27 = (bf16[4,144,512]{2,1,0:T(8,128)(2,1)S(1)}, bf16[4,144,512]{2,1,0:T(8,128)(2,1)S(1)}, u32[]{:S(2)}, u32[]{:S(2)}) collective-permute-start(bf16[4,144,512]{2,1,0:T(8,128)(2,1)S(1)} %add_convert_fusion), channel_id=1, source_target_pairs={{0,4},{1,5},{2,6},{3,7},{4,0},{5,1},{6,2},{7,3},{8,12},{9,13},{10,... | collective-permute-start | bytes 1769480 | tf_op jit(solution)/shard_map/ppermute | solution.py:58
  86.5 17.0 %collective-permute-start.31 = (bf16[8,272,128]{2,1,0:T(8,128)(2,1)S(1)}, bf16[8,272,128]{2,1,0:T(8,128)(2,1)S(1)}, u32[]{:S(2)}, u32[]{:S(2)}) collective-permute-start(bf16[8,272,128]{2,1,0:T(8,128)(2,1)S(1)} %get-tuple-element.142), channel_id=1, source_target_pairs={{0,1},{1,0},{2,3},{3,2},{4,5},{5,4},{6,7},{7,6},{8,9},{9,8},{10,11... | collective-permute-start | bytes 1671176 | tf_op jit(solution)/shard_map/ppermute | solution.py:58
  88.2 10.0 %collective-permute-start.28 = (bf16[2,144,512]{2,1,0:T(8,128)(2,1)S(1)}, bf16[2,144,512]{2,1,0:T(8,128)(2,1)S(1)}, u32[]{:S(2)}, u32[]{:S(2)}) collective-permute-start(bf16[2,144,512]{2,1,0:T(8,128)(2,1)S(1)} %get-tuple-element.187), channel_id=1, source_target_pairs={{0,4},{1,5},{2,6},{3,7},{4,0},{5,1},{6,2},{7,3},{8,12},{9,13},{10,... | collective-permute-start | bytes 884744 | tf_op jit(solution)/shard_map/ppermute | solution.py:58
  89.8 9.9 %collective-permute-start.29 = (bf16[2,144,512]{2,1,0:T(8,128)(2,1)S(1)}, bf16[2,144,512]{2,1,0:T(8,128)(2,1)S(1)}, u32[]{:S(2)}, u32[]{:S(2)}) collective-permute-start(bf16[2,144,512]{2,1,0:T(8,128)(2,1)S(1)} %get-tuple-element.186), channel_id=1, source_target_pairs={{0,2},{1,3},{2,0},{3,1},{4,6},{5,7},{6,4},{7,5},{8,10},{9,11},{10,... | collective-permute-start | bytes 884744 | tf_op jit(solution)/shard_map/ppermute | solution.py:58
  90.8 12.7 %collective-permute-start.33 = (bf16[4,272,128]{2,1,0:T(8,128)(2,1)S(1)}, bf16[4,272,128]{2,1,0:T(8,128)(2,1)S(1)}, u32[]{:S(2)}, u32[]{:S(2)}) collective-permute-start(bf16[4,272,128]{2,1,0:T(8,128)(2,1)S(1)} %add_convert_fusion.5), channel_id=1, source_target_pairs={{0,2},{1,3},{2,0},{3,1},{4,6},{5,7},{6,4},{7,5},{8,10},{9,11},{10,... | collective-permute-start | bytes 835592 | tf_op jit(solution)/shard_map/ppermute | solution.py:58
  92.1 11.4 %collective-permute-start.35 = (bf16[4,272,128]{2,1,0:T(8,128)(2,1)S(1)}, bf16[4,272,128]{2,1,0:T(8,128)(2,1)S(1)}, u32[]{:S(2)}, u32[]{:S(2)}) collective-permute-start(bf16[4,272,128]{2,1,0:T(8,128)(2,1)S(1)} %add_convert_fusion.4), channel_id=1, source_target_pairs={{0,4},{1,5},{2,6},{3,7},{4,0},{5,1},{6,2},{7,3},{8,12},{9,13},{10,... | collective-permute-start | bytes 835592 | tf_op jit(solution)/shard_map/ppermute | solution.py:58
  100.0 9.2 %collective-permute-start.30 = (bf16[2,144,512]{2,1,0:T(8,128)(2,1)S(1)}, bf16[2,144,512]{2,1,0:T(8,128)(2,1)S(1)}, u32[]{:S(2)}, u32[]{:S(2)}) collective-permute-start(bf16[2,144,512]{2,1,0:T(8,128)(2,1)S(1)} %get-tuple-element.131), channel_id=1, source_target_pairs={{0,8},{1,9},{2,10},{3,11},{4,12},{5,13},{6,14},{7,15},{8,0},{9,1},... | collective-permute-start | bytes 884744 | tf_op jit(solution)/shard_map/ppermute | solution.py:58
  112.0 11.5 %collective-permute-start.43 = (bf16[2,128,512]{2,1,0:T(8,128)(2,1)S(1)}, bf16[2,128,512]{2,1,0:T(8,128)(2,1)S(1)}, u32[]{:S(2)}, u32[]{:S(2)}) collective-permute-start(bf16[2,128,512]{2,1,0:T(8,128)(2,1)S(1)} %get-tuple-element.164), channel_id=1, source_target_pairs={{0,2},{1,3},{2,0},{3,1},{4,6},{5,7},{6,4},{7,5},{8,10},{9,11},{10,... | collective-permute-start | bytes 786440 | tf_op jit(solution)/shard_map/ppermute | solution.py:58
  113.5 9.9 %collective-permute-start.44 = (bf16[2,128,512]{2,1,0:T(8,128)(2,1)S(1)}, bf16[2,128,512]{2,1,0:T(8,128)(2,1)S(1)}, u32[]{:S(2)}, u32[]{:S(2)}) collective-permute-start(bf16[2,128,512]{2,1,0:T(8,128)(2,1)S(1)} %get-tuple-element.165), channel_id=1, source_target_pairs={{0,3},{1,2},{2,1},{3,0},{4,7},{5,6},{6,5},{7,4},{8,11},{9,10},{10,... | collective-permute-start | bytes 786440 | tf_op jit(solution)/shard_map/ppermute | solution.py:58
  113.5 9.9 %collective-permute-start.41 = (bf16[1,128,512]{2,1,0:T(8,128)(2,1)S(1)}, bf16[1,128,512]{2,1,0:T(8,128)(2,1)S(1)}, u32[]{:S(2)}, u32[]{:S(2)}) collective-permute-start(bf16[1,128,512]{2,1,0:T(8,128)(2,1)S(1)} %get-tuple-element.160), channel_id=1, source_target_pairs={{0,1},{1,0},{2,3},{3,2},{4,5},{5,4},{6,7},{7,6},{8,9},{9,8},{10,11... | collective-permute-start | bytes 393224 | tf_op jit(solution)/shard_map/ppermute | solution.py:58
  116.3 7.1 %collective-permute-start.42 = (bf16[1,128,512]{2,1,0:T(8,128)(2,1)S(1)}, bf16[1,128,512]{2,1,0:T(8,128)(2,1)S(1)}, u32[]{:S(2)}, u32[]{:S(2)}) collective-permute-start(bf16[1,128,512]{2,1,0:T(8,128)(2,1)S(1)} %get-tuple-element.161), channel_id=1, source_target_pairs={{0,1},{1,0},{2,3},{3,2},{4,5},{5,4},{6,7},{7,6},{8,9},{9,8},{10,11... | collective-permute-start | bytes 393224 | tf_op jit(solution)/shard_map/ppermute | solution.py:58
  (40 other events, 227.6 us)
